TPU v7x, 128 devices: a whole 4x4x4 slice. The times are simulated.
128 devices in a mesh: gx: 8 (over y, core), gy: 16 (over z, x).
Axes of the slice: x: 4, y: 4, z: 4, core: 2. Of those that a mesh axis runs over, the one named last changes fastest.
Arguments:
- rhs: float32 [3, 20, 64, 2048], P(None, None, 'gx', 'gy'), may hold values from -6 to 6
- diag_block: bfloat16 [9, 20, 64, 2048], P(None, None, 'gx', 'gy'), may hold values from -0.5625 to 4.75
- mobility: bfloat16 [9, 20, 64, 2048], P(None, None, 'gx', 'gy'), may hold values from -0.34375 to 1.375
- trans: bfloat16 [3, 20, 64, 2048], P(None, None, 'gx', 'gy'), may hold values from 0.5 to 1
- perf_cell: int32 [128, 8, 128], P(('gx', 'gy')), may hold values from 0 to 20479, as said below
- perf_pi: float32 [128, 8, 128], P(('gx', 'gy')), may hold values from 0 to 0.6, as said below
- perf_seg: int32 [128, 8, 128], P(('gx', 'gy')), may hold values from 0 to 255
- seg_parent: int32 [32768], P(('gx', 'gy')), may hold values from -1 to 254, as said below
- seg_trans: float32 [32768], P(('gx', 'gy')), may hold values from 0.5 to 2
- seg_rhs: float32 [32768], P(('gx', 'gy')), may hold values from -6 to 6
Outputs:
- solution: float32 [3, 20, 64, 2048], P(None, None, 'gx', 'gy')
- seg_pressure: float32 [32768], P(('gx', 'gy'))
Inputs may be any that keep to these rules, and one draw needn't show every extreme that they name: `perf_cell`: the 8 slots of a sender-owner pair name consecutive cells along y in one layer and one x column. `perf_pi`: live slots of a sender-owner pair come first among its 8; every sender has one owner with all 8 slots live, and one owner receives all 8 from every sender; some of the owners, drawn from the seed, receive many more than the rest. `seg_parent`: A parent comes just before its segment on the same owner; segment 0 of every owner is at a well head.
All inputs are finite; a program needn't handle non-finite values.
Results may differ from a plain program's by a relative error of at most 0.0003.
Values may be sent and summed in bfloat16 or wider, within the bound.
No kernel may reach another device: no remote copies, remote signals or barrier semaphores. Data moves between devices by JAX's collectives and lax.ppermute only.
A program may use at most 128 MiB of HBM per device.

v0:
```python
import jax
import jax.numpy as jnp
from jax import lax
from jax.sharding import PartitionSpec as P

SWEEPS = 4
OUTER = 2


def extended(value, sides, width):
    for axis, dim in sides:
        count, length = (lax.axis_size(axis), value.shape[dim])
        up = [(i, (i + 1) % count) for i in range(count - 1)]
        down = [(j, i) for i, j in up]
        last = lax.slice_in_dim(value, length - width, length, axis=dim)
        leading = lax.slice_in_dim(value, 0, width, axis=dim)
        before = lax.ppermute(last, axis, up)
        after = lax.ppermute(leading, axis, down)
        value = jnp.concatenate([before, value, after], axis=dim)
    return value


def invert_blocks(mat):
    a, b, c, d, e, f, g, h, i = [mat[position] for position in range(9)]
    first = e * i - f * h
    second = f * g - d * i
    third = d * h - e * g
    determinant = a * first + b * second + c * third
    entries = [
        first,
        c * h - b * i,
        b * f - c * e,
        second,
        a * i - c * g,
        c * d - a * f,
        third,
        b * g - a * h,
        a * e - b * d,
    ]
    return jnp.stack([entry / determinant for entry in entries])


def block_apply(mat, vec):
    return jnp.stack(
        [
            mat[3 * row] * vec[0] + mat[3 * row + 1] * vec[1] + mat[3 * row + 2] * vec[2]
            for row in range(3)
        ]
    )


def child_total(values, parent, count):
    return jax.ops.segment_sum(
        jnp.where(parent >= 0, values, 0.0), jnp.maximum(parent, 0), num_segments=count
    )


def on_device(
    rhs, diag_block, mobility, trans, perf_cell, perf_pi, perf_seg, seg_parent, seg_trans, seg_rhs
):
    layers, rows_x, rows_y = (rhs.shape[1], rhs.shape[2], rhs.shape[3])
    dense = diag_block.astype(jnp.float32)
    mob_full = mobility.astype(jnp.float32)
    inverse = invert_blocks(dense)
    trans_f = trans.astype(jnp.float32)
    slots = perf_pi.shape[1]
    owners = perf_pi.shape[2]
    cells_count = layers * rows_x * rows_y
    cell_index = perf_cell[0].reshape(-1)
    weights = perf_pi[0]
    seg_index = perf_seg[0].reshape(-1)
    segments = seg_rhs.shape[0]
    fraction = mob_full[0::3]

    def to_owners(buffer):
        return lax.all_to_all(buffer, ("gx", "gy"), split_axis=1, concat_axis=1, tiled=True)

    weights_in = to_owners(weights)
    seg_diag = seg_trans + child_total(seg_trans, seg_parent, segments)
    seg_diag = seg_diag + jax.ops.segment_sum(
        weights_in.reshape(-1), seg_index, num_segments=segments
    )
    rims = extended(trans[:2], (("gx", 2), ("gy", 3)), 1).astype(jnp.float32)
    x_lower = rims[0, :, :-2, 1:-1] * trans_f[0]
    x_upper = trans_f[0] * rims[0, :, 2:, 1:-1]
    y_lower = rims[1, :, 1:-1, :-2] * trans_f[1]
    y_upper = trans_f[1] * rims[1, :, 1:-1, 2:]
    z_face = trans_f[2, :-1] * trans_f[2, 1:]
    rounds = SWEEPS
    solution = jnp.zeros_like(rhs)
    seg_pressure = jnp.zeros_like(seg_rhs)
    cell_res, seg_res = (rhs, seg_rhs)
    for outer in range(OUTER):
        field, seg_state = (solution, seg_pressure)
        cell_now, seg_now = (cell_res, seg_res)
        for sweep in range(rounds):
            advance_field = field
            advance_seg_state = seg_state
            advance_field = advance_field + block_apply(inverse, cell_now)
            seg_new = advance_seg_state + seg_now / seg_diag
            advance_seg_state = seg_new
            advance_slot_state = lax.all_to_all(
                seg_new[perf_seg[0]], ("gx", "gy"), split_axis=1, concat_axis=1, tiled=True
            )
            flows = weights.reshape(-1) * (
                advance_field[0].reshape(-1)[cell_index] - advance_slot_state.reshape(-1)
            )
            into_cells = (
                jnp.zeros((cells_count,), jnp.float32)
                .at[cell_index]
                .add(flows)
                .reshape(layers, rows_x, rows_y)
            )
            mob_vec = block_apply(mob_full, advance_field)
            rim = extended(mob_vec, (("gx", 2), ("gy", 3)), 1)
            total = x_lower * rim[:, :, :-2, 1:-1] + x_upper * rim[:, :, 2:, 1:-1]
            total = total + y_lower * rim[:, :, 1:-1, :-2] + y_upper * rim[:, :, 1:-1, 2:]
            zeros_layer = jnp.zeros_like(mob_vec[:, :1])
            below = jnp.concatenate([z_face * mob_vec[:, 1:], zeros_layer], axis=1)
            above = jnp.concatenate([zeros_layer, z_face * mob_vec[:, :-1]], axis=1)
            advance_cell_res = (
                rhs
                - block_apply(dense, advance_field)
                + (total + below + above)
                - fraction * into_cells
            )
            arrived = to_owners(flows.reshape(slots, owners))
            upper = jnp.where(seg_parent >= 0, advance_seg_state[jnp.maximum(seg_parent, 0)], 0.0)
            flux = seg_trans * (advance_seg_state - upper)
            into_segs = jax.ops.segment_sum(arrived.reshape(-1), seg_index, num_segments=segments)
            advance_seg_res = seg_rhs - flux + child_total(flux, seg_parent, segments) + into_segs
            field = advance_field
            seg_state = advance_seg_state
            cell_now = advance_cell_res
            seg_now = advance_seg_res
        cell_diff = cell_res - cell_now
        seg_diff = seg_res - seg_now
        local_numer = jnp.sum(cell_res * cell_diff) + jnp.sum(seg_res * seg_diff)
        local_denom = jnp.sum(cell_diff * cell_diff) + jnp.sum(seg_diff * seg_diff)
        numer, denom = lax.psum((local_numer, local_denom), ("gx", "gy"))
        omega = numer / denom
        solution = solution + omega * (field - solution)
        seg_pressure = seg_pressure + omega * (seg_state - seg_pressure)
        cell_res = cell_res - omega * cell_diff
        seg_res = seg_res - omega * seg_diff
    return (solution, seg_pressure)


def solution(mesh):
    return jax.shard_map(
        on_device,
        mesh=mesh,
        in_specs=(
            P(None, None, "gx", "gy"),
            P(None, None, "gx", "gy"),
            P(None, None, "gx", "gy"),
            P(None, None, "gx", "gy"),
            P(("gx", "gy"), None, None),
            P(("gx", "gy"), None, None),
            P(("gx", "gy"), None, None),
            P(("gx", "gy")),
            P(("gx", "gy")),
            P(("gx", "gy")),
        ),
        out_specs=(P(None, None, "gx", "gy"), P(("gx", "gy"))),
        check_vma=False,
    )
```

profile of v0, /device:TPU:1, one launch (start us, length us, event | category | flops | bytes accessed | tf_op | source)
XLA Modules:
  0.0 902.5 jit_solution(17539824280071425496)
XLA Ops:
  13.2 10.0 %all-to-all-start = ((f32[8,128,1]{0,2,1:T(1,128)}), f32[8,128,1]{0,2,1:T(1,128)S(1)}, u32[]{:S(2)}, u32[]{:S(2)}) async-start(f32[8,128,1]{0,2,1:T(1,128)} %copy.13), calls=%async_computation | async-start | bytes 131072 | tf_op jit(solution)/shard_map/all_to_all | solution.py:76
  43.4 7.6 scatter_custom_fusion.1
  51.0 6.8 gather_fusion.1
  58.6 9.5 %all-to-all-start.1 = ((f32[8,128,1]{0,2,1:T(1,128)}), f32[8,128,1]{0,2,1:T(1,128)S(1)}, u32[]{:S(2)}, u32[]{:S(2)}) async-start(f32[8,128,1]{0,2,1:T(1,128)} %copy.15), calls=%async_computation.1 | async-start | bytes 131072 | tf_op jit(solution)/shard_map/all_to_all | solution.py:102
  92.9 6.7 all-to-all-start.2
  102.6 6.7 all-to-all-done.2
  109.4 8.0 scatter_custom_fusion.4
  117.4 6.8 gather_fusion.4
  160.9 10.5 %gather_fusion.2 = f32[1024]{0:T(1024)} fusion(f32[20480]{0:T(1024)S(1)} %get-tuple-element.156, s32[1024]{0:T(1024)S(1)} %broadcast_clamp_fusion), kind=kCustom, calls=%fused_computation.2 | custom fusion | bytes 12288 | tf_op jit(solution)/shard_map/gather | solution.py:106
  172.8 12.0 %all-to-all-start.4 = ((f32[8,128,1]{0,2,1:T(1,128)}), f32[8,128,1]{0,2,1:T(1,128)S(1)}, u32[]{:S(2)}, u32[]{:S(2)}) async-start(f32[8,128,1]{0,2,1:T(1,128)} %copy.23), calls=%async_computation.4 | async-start | bytes 131072 | tf_op jit(solution)/shard_map/all_to_all | solution.py:76
  184.9 6.6 scatter_custom_fusion.5
  194.6 7.9 scatter_custom_fusion.7
  202.6 6.8 gather_fusion.7
  212.8 7.1 all-to-all-start.5
  249.8 10.5 %gather_fusion.5 = f32[1024]{0:T(1024)} fusion(f32[20480]{0:T(1024)S(1)} %get-tuple-element.150, s32[1024]{0:T(1024)S(1)} %broadcast_clamp_fusion), kind=kCustom, calls=%fused_computation.5 | custom fusion | bytes 12288 | tf_op jit(solution)/shard_map/gather | solution.py:106
  261.8 11.9 %all-to-all-start.6 = ((f32[8,128,1]{0,2,1:T(1,128)}), f32[8,128,1]{0,2,1:T(1,128)S(1)}, u32[]{:S(2)}, u32[]{:S(2)}) async-start(f32[8,128,1]{0,2,1:T(1,128)} %copy.28), calls=%async_computation.6 | async-start | bytes 131072 | tf_op jit(solution)/shard_map/all_to_all | solution.py:76
  273.7 6.6 scatter_custom_fusion.8
  283.5 7.9 scatter_custom_fusion.10
  291.5 6.8 gather_fusion.10
  301.7 7.1 all-to-all-start.7
  331.1 10.5 %gather_fusion.8 = f32[1024]{0:T(1024)} fusion(f32[20480]{0:T(1024)S(1)} %get-tuple-element.144, s32[1024]{0:T(1024)S(1)} %broadcast_clamp_fusion), kind=kCustom, calls=%fused_computation.8 | custom fusion | bytes 12288 | tf_op jit(solution)/shard_map/gather | solution.py:106
  351.7 12.4 %all-to-all-start.8 = ((f32[8,128,1]{0,2,1:T(1,128)}), f32[8,128,1]{0,2,1:T(1,128)}, u32[]{:S(2)}, u32[]{:S(2)}) async-start(f32[8,128,1]{0,2,1:T(1,128)} %copy.33), calls=%async_computation.8 | async-start | bytes 131072 | tf_op jit(solution)/shard_map/all_to_all | solution.py:76
  364.7 6.8 scatter_custom_fusion.11
  374.7 8.4 scatter_custom_fusion.13
  390.7 7.6 collective-permute-done.19
  404.4 69.9 %all-reduce.17 = (f32[]{:T(128)}, f32[]{:T(128)}) all-reduce(f32[]{:T(128)S(6)} %add.1196, f32[]{:T(128)S(6)} %add.1197), channel_id=1, replica_groups=mesh['gx'=8,'gy'=16] {'gx','gy'}, use_global_device_ids=true, to_apply=%region_16.17 | all-reduce | flops 2 | bytes 16 | tf_op jit(solution)/shard_map/psum | solution.py:140
  480.9 6.8 gather_fusion.13
  504.6 10.5 %gather_fusion.12 = f32[1024]{0:T(1024)} fusion(f32[20480]{0:T(1024)S(1)} %get-tuple-element.138, s32[1024]{0:T(1024)S(1)} %broadcast_clamp_fusion), kind=kCustom, calls=%fused_computation.12 | custom fusion | bytes 12288 | tf_op jit(solution)/shard_map/gather | solution.py:106
  519.7 9.6 %all-to-all-start.10 = ((f32[8,128,1]{0,2,1:T(1,128)}), f32[8,128,1]{0,2,1:T(1,128)S(1)}, u32[]{:S(2)}, u32[]{:S(2)}) async-start(f32[8,128,1]{0,2,1:T(1,128)} %copy.38), calls=%async_computation.10 | async-start | bytes 131072 | tf_op jit(solution)/shard_map/all_to_all | solution.py:76
  539.1 7.9 scatter_custom_fusion.16
  547.1 6.8 gather_fusion.16
  557.3 7.1 all-to-all-start.11
  594.7 10.5 %gather_fusion.14 = f32[1024]{0:T(1024)} fusion(f32[20480]{0:T(1024)S(1)} %get-tuple-element.132, s32[1024]{0:T(1024)S(1)} %broadcast_clamp_fusion), kind=kCustom, calls=%fused_computation.14 | custom fusion | bytes 12288 | tf_op jit(solution)/shard_map/gather | solution.py:106
  606.7 11.9 %all-to-all-start.12 = ((f32[8,128,1]{0,2,1:T(1,128)}), f32[8,128,1]{0,2,1:T(1,128)S(1)}, u32[]{:S(2)}, u32[]{:S(2)}) async-start(f32[8,128,1]{0,2,1:T(1,128)} %copy.43), calls=%async_computation.12 | async-start | bytes 131072 | tf_op jit(solution)/shard_map/all_to_all | solution.py:76
  618.6 6.6 scatter_custom_fusion.17
  628.4 7.9 scatter_custom_fusion.19
  636.3 6.8 gather_fusion.19
  646.5 7.1 all-to-all-start.13
  684.0 10.5 %gather_fusion.17 = f32[1024]{0:T(1024)} fusion(f32[20480]{0:T(1024)S(1)} %get-tuple-element.126, s32[1024]{0:T(1024)S(1)} %broadcast_clamp_fusion), kind=kCustom, calls=%fused_computation.17 | custom fusion | bytes 12288 | tf_op jit(solution)/shard_map/gather | solution.py:106
  695.9 11.9 %all-to-all-start.14 = ((f32[8,128,1]{0,2,1:T(1,128)}), f32[8,128,1]{0,2,1:T(1,128)S(1)}, u32[]{:S(2)}, u32[]{:S(2)}) async-start(f32[8,128,1]{0,2,1:T(1,128)} %copy.48), calls=%async_computation.14 | async-start | bytes 131072 | tf_op jit(solution)/shard_map/all_to_all | solution.py:76
  707.9 6.9 scatter_custom_fusion.20
  717.7 7.9 scatter_custom_fusion.22
  725.6 6.8 gather_fusion.22
  735.8 7.4 all-to-all-start.15
  780.7 11.9 %all-to-all-start.16 = ((f32[8,128,1]{0,2,1:T(1,128)}), f32[8,128,1]{0,2,1:T(1,128)S(1)}, u32[]{:S(2)}, u32[]{:S(2)}) async-start(f32[8,128,1]{0,2,1:T(1,128)} %copy.53), calls=%async_computation.16 | async-start | bytes 131072 | tf_op jit(solution)/shard_map/all_to_all | solution.py:76
  802.4 7.8 scatter_custom_fusion.25
  816.7 7.9 collective-permute-done.35
  829.3 69.0 %all-reduce.16 = (f32[]{:T(128)}, f32[]{:T(128)}) all-reduce(f32[]{:T(128)S(6)} %add.1306, f32[]{:T(128)S(6)} %add.1307), channel_id=1, replica_groups=mesh['gx'=8,'gy'=16] {'gx','gy'}, use_global_device_ids=true, to_apply=%region_34.35 | all-reduce | flops 2 | bytes 16 | tf_op jit(solution)/shard_map/psum | solution.py:140
  (613 shorter events, 363.6 us)
Async XLA Ops:
  5.8 126.4 %collective-permute-start.5 = (f32[3,20,1,128]{3,2,1,0:T(1,128)}, f32[3,20,1,128]{3,2,1,0:T(1,128)}, u32[]{:S(2)}, u32[]{:S(2)}) collective-permute-start(f32[3,20,1,128]{3,2,1,0:T(1,128)} %get-tuple-element.166), channel_id=1, source_target_pairs={{16,0},{32,16},{48,32},{64,48},{80,64},{96,80},{112,96},{17,1},{33... | collective-permute-start | bytes 92168 | tf_op jit(solution)/shard_map/ppermute | solution.py:18
  9.3 123.0 %collective-permute-start.4 = (f32[3,20,1,128]{3,2,1,0:T(1,128)}, f32[3,20,1,128]{3,2,1,0:T(1,128)}, u32[]{:S(2)}, u32[]{:S(2)}) collective-permute-start(f32[3,20,1,128]{3,2,1,0:T(1,128)} %get-tuple-element.165), channel_id=1, source_target_pairs={{0,16},{16,32},{32,48},{48,64},{64,80},{80,96},{96,112},{1,17},{17... | collective-permute-start | bytes 92168 | tf_op jit(solution)/shard_map/ppermute | solution.py:17
  13.2 30.1 %all-to-all-start = ((f32[8,128,1]{0,2,1:T(1,128)}), f32[8,128,1]{0,2,1:T(1,128)S(1)}, u32[]{:S(2)}, u32[]{:S(2)}) async-start(f32[8,128,1]{0,2,1:T(1,128)} %copy.13), calls=%async_computation | async-start | bytes 131072 | tf_op jit(solution)/shard_map/all_to_all | solution.py:76
  24.8 53.2 %collective-permute-start.1 = (bf16[2,20,1,128]{3,2,1,0:T(2,128)(2,1)}, bf16[2,20,1,128]{3,2,1,0:T(2,128)(2,1)}, u32[]{:S(2)}, u32[]{:S(2)}) collective-permute-start(bf16[2,20,1,128]{3,2,1,0:T(2,128)(2,1)} %get-tuple-element.170), channel_id=1, source_target_pairs={{16,0},{32,16},{48,32},{64,48},{80,64},{96,80},{112,96},{17,1},{33... | collective-permute-start | bytes 30728 | tf_op jit(solution)/shard_map/ppermute | solution.py:18
  27.8 50.2 %collective-permute-start = (bf16[2,20,1,128]{3,2,1,0:T(2,128)(2,1)}, bf16[2,20,1,128]{3,2,1,0:T(2,128)(2,1)}, u32[]{:S(2)}, u32[]{:S(2)}) collective-permute-start(bf16[2,20,1,128]{3,2,1,0:T(2,128)(2,1)} %get-tuple-element.169), channel_id=1, source_target_pairs={{0,16},{16,32},{32,48},{48,64},{64,80},{80,96},{96,112},{1,17},{17... | collective-permute-start | bytes 30728 | tf_op jit(solution)/shard_map/ppermute | solution.py:17
  58.6 19.3 %all-to-all-start.1 = ((f32[8,128,1]{0,2,1:T(1,128)}), f32[8,128,1]{0,2,1:T(1,128)S(1)}, u32[]{:S(2)}, u32[]{:S(2)}) async-start(f32[8,128,1]{0,2,1:T(1,128)} %copy.15), calls=%async_computation.1 | async-start | bytes 131072 | tf_op jit(solution)/shard_map/all_to_all | solution.py:102
  79.5 20.1 %collective-permute-start.3 = (bf16[2,20,10,1]{3,2,1,0:T(8,128)(2,1)}, bf16[2,20,10,1]{3,2,1,0:T(8,128)(2,1)S(1)}, u32[]{:S(2)}, u32[]{:S(2)}) collective-permute-start(bf16[2,20,10,1]{3,2,1,0:T(8,128)(2,1)} %get-tuple-element.168), channel_id=1, source_target_pairs={{1,0},{2,1},{3,2},{4,3},{5,4},{6,5},{7,6},{8,7},{9,8},{10,9},{11,1... | collective-permute-start | bytes 2408 | tf_op jit(solution)/shard_map/ppermute | solution.py:18
  80.8 19.4 %collective-permute-start.2 = (bf16[2,20,10,1]{3,2,1,0:T(8,128)(2,1)S(1)}, bf16[2,20,10,1]{3,2,1,0:T(8,128)(2,1)}, u32[]{:S(2)}, u32[]{:S(2)}) collective-permute-start(bf16[2,20,10,1]{3,2,1,0:T(8,128)(2,1)S(1)} %get-tuple-element.167), channel_id=1, source_target_pairs={{0,1},{1,2},{2,3},{3,4},{4,5},{5,6},{6,7},{7,8},{8,9},{9,10},{10,1... | collective-permute-start | bytes 2408 | tf_op jit(solution)/shard_map/ppermute | solution.py:17
  92.9 16.5 %all-to-all-start.2 = ((f32[8,128,1]{0,2,1:T(1,128)}), f32[8,128,1]{0,2,1:T(1,128)S(1)}, u32[]{:S(2)}, u32[]{:S(2)}) async-start(f32[8,128,1]{0,2,1:T(1,128)} %copy.18), calls=%async_computation.2 | async-start | bytes 131072 | tf_op jit(solution)/shard_map/all_to_all | solution.py:76
  127.1 15.7 %all-to-all-start.3 = ((f32[8,128,1]{0,2,1:T(1,128)}), f32[8,128,1]{0,2,1:T(1,128)}, u32[]{:S(2)}, u32[]{:S(2)}) async-start(f32[8,128,1]{0,2,1:T(1,128)} %copy.20), calls=%async_computation.3 | async-start | bytes 131072 | tf_op jit(solution)/shard_map/all_to_all | solution.py:102
  134.2 13.8 %collective-permute-start.7 = (f32[3,20,10,1]{3,2,1,0:T(8,128)}, f32[3,20,10,1]{3,2,1,0:T(8,128)}, u32[]{:S(2)}, u32[]{:S(2)}) collective-permute-start(f32[3,20,10,1]{3,2,1,0:T(8,128)} %get-tuple-element.103), channel_id=1, source_target_pairs={{1,0},{2,1},{3,2},{4,3},{5,4},{6,5},{7,6},{8,7},{9,8},{10,9},{11,1... | collective-permute-start | bytes 7208 | tf_op jit(solution)/shard_map/ppermute | solution.py:18
  152.4 67.5 %collective-permute-start.9 = (f32[3,20,1,128]{3,2,1,0:T(1,128)}, f32[3,20,1,128]{3,2,1,0:T(1,128)}, u32[]{:S(2)}, u32[]{:S(2)}) collective-permute-start(f32[3,20,1,128]{3,2,1,0:T(1,128)} %get-tuple-element.158), channel_id=1, source_target_pairs={{16,0},{32,16},{48,32},{64,48},{80,64},{96,80},{112,96},{17,1},{33... | collective-permute-start | bytes 92168 | tf_op jit(solution)/shard_map/ppermute | solution.py:18
  156.8 63.1 %collective-permute-start.8 = (f32[3,20,1,128]{3,2,1,0:T(1,128)}, f32[3,20,1,128]{3,2,1,0:T(1,128)}, u32[]{:S(2)}, u32[]{:S(2)}) collective-permute-start(f32[3,20,1,128]{3,2,1,0:T(1,128)} %get-tuple-element.157), channel_id=1, source_target_pairs={{0,16},{16,32},{32,48},{48,64},{64,80},{80,96},{96,112},{1,17},{17... | collective-permute-start | bytes 92168 | tf_op jit(solution)/shard_map/ppermute | solution.py:17
  172.8 21.8 %all-to-all-start.4 = ((f32[8,128,1]{0,2,1:T(1,128)}), f32[8,128,1]{0,2,1:T(1,128)S(1)}, u32[]{:S(2)}, u32[]{:S(2)}) async-start(f32[8,128,1]{0,2,1:T(1,128)} %copy.23), calls=%async_computation.4 | async-start | bytes 131072 | tf_op jit(solution)/shard_map/all_to_all | solution.py:76
  212.8 17.8 %all-to-all-start.5 = ((f32[8,128,1]{0,2,1:T(1,128)}), f32[8,128,1]{0,2,1:T(1,128)}, u32[]{:S(2)}, u32[]{:S(2)}) async-start(f32[8,128,1]{0,2,1:T(1,128)} %copy.25), calls=%async_computation.5 | async-start | bytes 131072 | tf_op jit(solution)/shard_map/all_to_all | solution.py:102
  222.0 13.9 %collective-permute-start.11 = (f32[3,20,10,1]{3,2,1,0:T(8,128)}, f32[3,20,10,1]{3,2,1,0:T(8,128)}, u32[]{:S(2)}, u32[]{:S(2)}) collective-permute-start(f32[3,20,10,1]{3,2,1,0:T(8,128)} %get-tuple-element.101), channel_id=1, source_target_pairs={{1,0},{2,1},{3,2},{4,3},{5,4},{6,5},{7,6},{8,7},{9,8},{10,9},{11,1... | collective-permute-start | bytes 7208 | tf_op jit(solution)/shard_map/ppermute | solution.py:18
  223.4 13.4 %collective-permute-start.10 = (f32[3,20,10,1]{3,2,1,0:T(8,128)}, f32[3,20,10,1]{3,2,1,0:T(8,128)}, u32[]{:S(2)}, u32[]{:S(2)}) collective-permute-start(f32[3,20,10,1]{3,2,1,0:T(8,128)} %get-tuple-element.100), channel_id=1, source_target_pairs={{0,1},{1,2},{2,3},{3,4},{4,5},{5,6},{6,7},{7,8},{8,9},{9,10},{10,1... | collective-permute-start | bytes 7208 | tf_op jit(solution)/shard_map/ppermute | solution.py:17
  241.2 67.6 %collective-permute-start.13 = (f32[3,20,1,128]{3,2,1,0:T(1,128)}, f32[3,20,1,128]{3,2,1,0:T(1,128)}, u32[]{:S(2)}, u32[]{:S(2)}) collective-permute-start(f32[3,20,1,128]{3,2,1,0:T(1,128)} %get-tuple-element.152), channel_id=1, source_target_pairs={{16,0},{32,16},{48,32},{64,48},{80,64},{96,80},{112,96},{17,1},{33... | collective-permute-start | bytes 92168 | tf_op jit(solution)/shard_map/ppermute | solution.py:18
  245.4 63.4 %collective-permute-start.12 = (f32[3,20,1,128]{3,2,1,0:T(1,128)}, f32[3,20,1,128]{3,2,1,0:T(1,128)}, u32[]{:S(2)}, u32[]{:S(2)}) collective-permute-start(f32[3,20,1,128]{3,2,1,0:T(1,128)} %get-tuple-element.151), channel_id=1, source_target_pairs={{0,16},{16,32},{32,48},{48,64},{64,80},{80,96},{96,112},{1,17},{17... | collective-permute-start | bytes 92168 | tf_op jit(solution)/shard_map/ppermute | solution.py:17
  261.8 21.7 %all-to-all-start.6 = ((f32[8,128,1]{0,2,1:T(1,128)}), f32[8,128,1]{0,2,1:T(1,128)S(1)}, u32[]{:S(2)}, u32[]{:S(2)}) async-start(f32[8,128,1]{0,2,1:T(1,128)} %copy.28), calls=%async_computation.6 | async-start | bytes 131072 | tf_op jit(solution)/shard_map/all_to_all | solution.py:76
  301.7 19.1 %all-to-all-start.7 = ((f32[8,128,1]{0,2,1:T(1,128)}), f32[8,128,1]{0,2,1:T(1,128)}, u32[]{:S(2)}, u32[]{:S(2)}) async-start(f32[8,128,1]{0,2,1:T(1,128)} %copy.30), calls=%async_computation.7 | async-start | bytes 131072 | tf_op jit(solution)/shard_map/all_to_all | solution.py:102
  311.0 13.9 %collective-permute-start.15 = (f32[3,20,10,1]{3,2,1,0:T(8,128)}, f32[3,20,10,1]{3,2,1,0:T(8,128)}, u32[]{:S(2)}, u32[]{:S(2)}) collective-permute-start(f32[3,20,10,1]{3,2,1,0:T(8,128)} %get-tuple-element.99), channel_id=1, source_target_pairs={{1,0},{2,1},{3,2},{4,3},{5,4},{6,5},{7,6},{8,7},{9,8},{10,9},{11,1... | collective-permute-start | bytes 7208 | tf_op jit(solution)/shard_map/ppermute | solution.py:18
  343.5 39.5 %collective-permute-start.17 = (f32[3,20,1,128]{3,2,1,0:T(1,128)}, f32[3,20,1,128]{3,2,1,0:T(1,128)}, u32[]{:S(2)}, u32[]{:S(2)}) collective-permute-start(f32[3,20,1,128]{3,2,1,0:T(1,128)} %get-tuple-element.146), channel_id=1, source_target_pairs={{16,0},{32,16},{48,32},{64,48},{80,64},{96,80},{112,96},{17,1},{33... | collective-permute-start | bytes 92168 | tf_op jit(solution)/shard_map/ppermute | solution.py:18
  347.8 35.2 %collective-permute-start.16 = (f32[3,20,1,128]{3,2,1,0:T(1,128)}, f32[3,20,1,128]{3,2,1,0:T(1,128)}, u32[]{:S(2)}, u32[]{:S(2)}) collective-permute-start(f32[3,20,1,128]{3,2,1,0:T(1,128)} %get-tuple-element.145), channel_id=1, source_target_pairs={{0,16},{16,32},{32,48},{48,64},{64,80},{80,96},{96,112},{1,17},{17... | collective-permute-start | bytes 92168 | tf_op jit(solution)/shard_map/ppermute | solution.py:17
  351.7 22.0 %all-to-all-start.8 = ((f32[8,128,1]{0,2,1:T(1,128)}), f32[8,128,1]{0,2,1:T(1,128)}, u32[]{:S(2)}, u32[]{:S(2)}) async-start(f32[8,128,1]{0,2,1:T(1,128)} %copy.33), calls=%async_computation.8 | async-start | bytes 131072 | tf_op jit(solution)/shard_map/all_to_all | solution.py:76
  384.4 13.9 %collective-permute-start.19 = (f32[3,20,10,1]{3,2,1,0:T(8,128)S(1)}, f32[3,20,10,1]{3,2,1,0:T(8,128)S(1)}, u32[]{:S(2)}, u32[]{:S(2)}) collective-permute-start(f32[3,20,10,1]{3,2,1,0:T(8,128)S(1)} %get-tuple-element.97), channel_id=1, source_target_pairs={{1,0},{2,1},{3,2},{4,3},{5,4},{6,5},{7,6},{8,7},{9,8},{10,9},{11,1... | collective-permute-start | bytes 7208 | tf_op jit(solution)/shard_map/ppermute | solution.py:18
  490.4 74.0 %collective-permute-start.21 = (f32[3,20,1,128]{3,2,1,0:T(1,128)}, f32[3,20,1,128]{3,2,1,0:T(1,128)}, u32[]{:S(2)}, u32[]{:S(2)}) collective-permute-start(f32[3,20,1,128]{3,2,1,0:T(1,128)} %get-tuple-element.140), channel_id=1, source_target_pairs={{16,0},{32,16},{48,32},{64,48},{80,64},{96,80},{112,96},{17,1},{33... | collective-permute-start | bytes 92168 | tf_op jit(solution)/shard_map/ppermute | solution.py:18
  492.9 71.5 %collective-permute-start.20 = (f32[3,20,1,128]{3,2,1,0:T(1,128)}, f32[3,20,1,128]{3,2,1,0:T(1,128)}, u32[]{:S(2)}, u32[]{:S(2)}) collective-permute-start(f32[3,20,1,128]{3,2,1,0:T(1,128)} %get-tuple-element.139), channel_id=1, source_target_pairs={{0,16},{16,32},{32,48},{48,64},{64,80},{80,96},{96,112},{1,17},{17... | collective-permute-start | bytes 92168 | tf_op jit(solution)/shard_map/ppermute | solution.py:17
  498.6 19.5 %all-to-all-start.9 = ((f32[8,128,1]{0,2,1:T(1,128)}), f32[8,128,1]{0,2,1:T(1,128)}, u32[]{:S(2)}, u32[]{:S(2)}) async-start(f32[8,128,1]{0,2,1:T(1,128)} %copy.35), calls=%async_computation.9 | async-start | bytes 131072 | tf_op jit(solution)/shard_map/all_to_all | solution.py:102
  519.7 19.4 %all-to-all-start.10 = ((f32[8,128,1]{0,2,1:T(1,128)}), f32[8,128,1]{0,2,1:T(1,128)S(1)}, u32[]{:S(2)}, u32[]{:S(2)}) async-start(f32[8,128,1]{0,2,1:T(1,128)} %copy.38), calls=%async_computation.10 | async-start | bytes 131072 | tf_op jit(solution)/shard_map/all_to_all | solution.py:76
  557.3 19.3 %all-to-all-start.11 = ((f32[8,128,1]{0,2,1:T(1,128)}), f32[8,128,1]{0,2,1:T(1,128)}, u32[]{:S(2)}, u32[]{:S(2)}) async-start(f32[8,128,1]{0,2,1:T(1,128)} %copy.40), calls=%async_computation.11 | async-start | bytes 131072 | tf_op jit(solution)/shard_map/all_to_all | solution.py:102
  566.6 13.9 %collective-permute-start.23 = (f32[3,20,10,1]{3,2,1,0:T(8,128)}, f32[3,20,10,1]{3,2,1,0:T(8,128)}, u32[]{:S(2)}, u32[]{:S(2)}) collective-permute-start(f32[3,20,10,1]{3,2,1,0:T(8,128)} %get-tuple-element.95), channel_id=1, source_target_pairs={{1,0},{2,1},{3,2},{4,3},{5,4},{6,5},{7,6},{8,7},{9,8},{10,9},{11,1... | collective-permute-start | bytes 7208 | tf_op jit(solution)/shard_map/ppermute | solution.py:18
  568.0 13.4 %collective-permute-start.22 = (f32[3,20,10,1]{3,2,1,0:T(8,128)}, f32[3,20,10,1]{3,2,1,0:T(8,128)}, u32[]{:S(2)}, u32[]{:S(2)}) collective-permute-start(f32[3,20,10,1]{3,2,1,0:T(8,128)} %get-tuple-element.94), channel_id=1, source_target_pairs={{0,1},{1,2},{2,3},{3,4},{4,5},{5,6},{6,7},{7,8},{8,9},{9,10},{10,1... | collective-permute-start | bytes 7208 | tf_op jit(solution)/shard_map/ppermute | solution.py:17
  586.5 67.2 %collective-permute-start.25 = (f32[3,20,1,128]{3,2,1,0:T(1,128)}, f32[3,20,1,128]{3,2,1,0:T(1,128)}, u32[]{:S(2)}, u32[]{:S(2)}) collective-permute-start(f32[3,20,1,128]{3,2,1,0:T(1,128)} %get-tuple-element.134), channel_id=1, source_target_pairs={{16,0},{32,16},{48,32},{64,48},{80,64},{96,80},{112,96},{17,1},{33... | collective-permute-start | bytes 92168 | tf_op jit(solution)/shard_map/ppermute | solution.py:18
  590.7 62.9 %collective-permute-start.24 = (f32[3,20,1,128]{3,2,1,0:T(1,128)}, f32[3,20,1,128]{3,2,1,0:T(1,128)}, u32[]{:S(2)}, u32[]{:S(2)}) collective-permute-start(f32[3,20,1,128]{3,2,1,0:T(1,128)} %get-tuple-element.133), channel_id=1, source_target_pairs={{0,16},{16,32},{32,48},{48,64},{64,80},{80,96},{96,112},{1,17},{17... | collective-permute-start | bytes 92168 | tf_op jit(solution)/shard_map/ppermute | solution.py:17
  606.7 21.7 %all-to-all-start.12 = ((f32[8,128,1]{0,2,1:T(1,128)}), f32[8,128,1]{0,2,1:T(1,128)S(1)}, u32[]{:S(2)}, u32[]{:S(2)}) async-start(f32[8,128,1]{0,2,1:T(1,128)} %copy.43), calls=%async_computation.12 | async-start | bytes 131072 | tf_op jit(solution)/shard_map/all_to_all | solution.py:76
  646.5 19.0 %all-to-all-start.13 = ((f32[8,128,1]{0,2,1:T(1,128)}), f32[8,128,1]{0,2,1:T(1,128)}, u32[]{:S(2)}, u32[]{:S(2)}) async-start(f32[8,128,1]{0,2,1:T(1,128)} %copy.45), calls=%async_computation.13 | async-start | bytes 131072 | tf_op jit(solution)/shard_map/all_to_all | solution.py:102
  655.8 13.9 %collective-permute-start.27 = (f32[3,20,10,1]{3,2,1,0:T(8,128)}, f32[3,20,10,1]{3,2,1,0:T(8,128)}, u32[]{:S(2)}, u32[]{:S(2)}) collective-permute-start(f32[3,20,10,1]{3,2,1,0:T(8,128)} %get-tuple-element.93), channel_id=1, source_target_pairs={{1,0},{2,1},{3,2},{4,3},{5,4},{6,5},{7,6},{8,7},{9,8},{10,9},{11,1... | collective-permute-start | bytes 7208 | tf_op jit(solution)/shard_map/ppermute | solution.py:18
  675.8 67.4 %collective-permute-start.29 = (f32[3,20,1,128]{3,2,1,0:T(1,128)}, f32[3,20,1,128]{3,2,1,0:T(1,128)}, u32[]{:S(2)}, u32[]{:S(2)}) collective-permute-start(f32[3,20,1,128]{3,2,1,0:T(1,128)} %get-tuple-element.128), channel_id=1, source_target_pairs={{16,0},{32,16},{48,32},{64,48},{80,64},{96,80},{112,96},{17,1},{33... | collective-permute-start | bytes 92168 | tf_op jit(solution)/shard_map/ppermute | solution.py:18
  680.0 63.2 %collective-permute-start.28 = (f32[3,20,1,128]{3,2,1,0:T(1,128)}, f32[3,20,1,128]{3,2,1,0:T(1,128)}, u32[]{:S(2)}, u32[]{:S(2)}) collective-permute-start(f32[3,20,1,128]{3,2,1,0:T(1,128)} %get-tuple-element.127), channel_id=1, source_target_pairs={{0,16},{16,32},{32,48},{48,64},{64,80},{80,96},{96,112},{1,17},{17... | collective-permute-start | bytes 92168 | tf_op jit(solution)/shard_map/ppermute | solution.py:17
  695.9 21.7 %all-to-all-start.14 = ((f32[8,128,1]{0,2,1:T(1,128)}), f32[8,128,1]{0,2,1:T(1,128)S(1)}, u32[]{:S(2)}, u32[]{:S(2)}) async-start(f32[8,128,1]{0,2,1:T(1,128)} %copy.48), calls=%async_computation.14 | async-start | bytes 131072 | tf_op jit(solution)/shard_map/all_to_all | solution.py:76
  735.8 19.3 %all-to-all-start.15 = ((f32[8,128,1]{0,2,1:T(1,128)}), f32[8,128,1]{0,2,1:T(1,128)}, u32[]{:S(2)}, u32[]{:S(2)}) async-start(f32[8,128,1]{0,2,1:T(1,128)} %copy.50), calls=%async_computation.15 | async-start | bytes 131072 | tf_op jit(solution)/shard_map/all_to_all | solution.py:102
  745.4 13.9 %collective-permute-start.31 = (f32[3,20,10,1]{3,2,1,0:T(8,128)}, f32[3,20,10,1]{3,2,1,0:T(8,128)}, u32[]{:S(2)}, u32[]{:S(2)}) collective-permute-start(f32[3,20,10,1]{3,2,1,0:T(8,128)} %get-tuple-element.91), channel_id=1, source_target_pairs={{1,0},{2,1},{3,2},{4,3},{5,4},{6,5},{7,6},{8,7},{9,8},{10,9},{11,1... | collective-permute-start | bytes 7208 | tf_op jit(solution)/shard_map/ppermute | solution.py:18
  772.5 37.7 %collective-permute-start.33 = (f32[3,20,1,128]{3,2,1,0:T(1,128)S(1)}, f32[3,20,1,128]{3,2,1,0:T(1,128)S(1)}, u32[]{:S(2)}, u32[]{:S(2)}) collective-permute-start(f32[3,20,1,128]{3,2,1,0:T(1,128)S(1)} %copy-done.150), channel_id=1, source_target_pairs={{16,0},{32,16},{48,32},{64,48},{80,64},{96,80},{112,96},{17,1},{33... | collective-permute-start | bytes 92168 | tf_op jit(solution)/shard_map/ppermute | solution.py:18
  776.7 33.5 %collective-permute-start.32 = (f32[3,20,1,128]{3,2,1,0:T(1,128)S(1)}, f32[3,20,1,128]{3,2,1,0:T(1,128)S(1)}, u32[]{:S(2)}, u32[]{:S(2)}) collective-permute-start(f32[3,20,1,128]{3,2,1,0:T(1,128)S(1)} %copy-done.149), channel_id=1, source_target_pairs={{0,16},{16,32},{32,48},{48,64},{64,80},{80,96},{96,112},{1,17},{17... | collective-permute-start | bytes 92168 | tf_op jit(solution)/shard_map/ppermute | solution.py:17
  780.7 21.7 %all-to-all-start.16 = ((f32[8,128,1]{0,2,1:T(1,128)}), f32[8,128,1]{0,2,1:T(1,128)S(1)}, u32[]{:S(2)}, u32[]{:S(2)}) async-start(f32[8,128,1]{0,2,1:T(1,128)} %copy.53), calls=%async_computation.16 | async-start | bytes 131072 | tf_op jit(solution)/shard_map/all_to_all | solution.py:76
  810.6 14.0 %collective-permute-start.35 = (f32[3,20,10,1]{3,2,1,0:T(8,128)S(1)}, f32[3,20,10,1]{3,2,1,0:T(8,128)S(1)}, u32[]{:S(2)}, u32[]{:S(2)}) collective-permute-start(f32[3,20,10,1]{3,2,1,0:T(8,128)S(1)} %get-tuple-element.89), channel_id=1, source_target_pairs={{1,0},{2,1},{3,2},{4,3},{5,4},{6,5},{7,6},{8,7},{9,8},{10,9},{11,1... | collective-permute-start | bytes 7208 | tf_op jit(solution)/shard_map/ppermute | solution.py:18
  812.0 13.5 %collective-permute-start.34 = (f32[3,20,10,1]{3,2,1,0:T(8,128)S(1)}, f32[3,20,10,1]{3,2,1,0:T(8,128)S(1)}, u32[]{:S(2)}, u32[]{:S(2)}) collective-permute-start(f32[3,20,10,1]{3,2,1,0:T(8,128)S(1)} %get-tuple-element.88), channel_id=1, source_target_pairs={{0,1},{1,2},{2,3},{3,4},{4,5},{5,6},{6,7},{7,8},{8,9},{9,10},{10,1... | collective-permute-start | bytes 7208 | tf_op jit(solution)/shard_map/ppermute | solution.py:17
  (173 other events, 1826.0 us)
where the time goes:
time: 915 us; the launch traced here: 903 us
  starting transfers between devices  271 us (30%)
  other arithmetic  210 us (23%)
  local copies, waits for them, and re-layouts  195 us (21%)
  blocking collectives  139 us (15%)
  waiting for transfers between devices  76.6 us (8%)
  between operations  11.3 us (1%)
    psum x2, blocking collectives, on_device(): numer, denom = lax.psum((local_numer, local_denom), ('gx', 'gy'))  139 us
    all_to_all x9, starting transfers between devices, to_owners(): lax.all_to_all(buffer, ('gx', 'gy'), split_axis=1, concat_axis=1, tiled=T...  98.4 us
    gather x8, local copies, waits for them, and re-layouts, on_device(): advance_field[0].reshape(-1)[cell_index] - advance_slot_state.reshape(-1)  75.4 us
    ppermute x18, starting transfers between devices, extended(): before = lax.ppermute(last, axis, up)  70.1 us
    scatter-add x8, other arithmetic, on_device(): jax.ops.segment_sum(arrived.reshape(-1), seg_index, num_segments=segments)  63.6 us
    all_to_all x8, starting transfers between devices, on_device(): lax.all_to_all(seg_new[perf_seg[0]], ('gx', 'gy'), split_axis=1, concat_a...  55.3 us
    gather x8, local copies, waits for them, and re-layouts, on_device(): seg_new[perf_seg[0]]  54.7 us
    scatter-add x8, other arithmetic, on_device(): into_cells = jnp.zeros((cells_count,), jnp.float32).at[cell_index].add(fl...  53.5 us
  transfers between devices with their start and end apart: 53, of which 25 were waited for; matrix products, arithmetic and copies ran while one was open for 36% of the time, Pallas kernels for 0%

commit v1 on v0

v1 whole, which is shorter than its diff:
```python
import functools

import jax
import jax.numpy as jnp
from jax import lax
from jax.experimental import pallas as pl
from jax.experimental.pallas import tpu as pltpu
from jax.sharding import PartitionSpec as P

F32 = jnp.float32
BF16 = jnp.bfloat16
AXES = ("gx", "gy")
NZ, CX, CY = 20, 8, 128
ROWS = NZ * CX
STEP = 16
CHUNKS = ROWS // STEP
PEERS = 128
CAP = 8


def lanes(shape):
    return lax.broadcasted_iota(jnp.int32, shape, 1)


def subs(shape):
    return lax.broadcasted_iota(jnp.int32, shape, 0)


def split3(x):
    high = x.astype(BF16)
    rest = x - high.astype(F32)
    mid = rest.astype(BF16)
    low = (rest - mid.astype(F32)).astype(BF16)
    return high, mid, low


def pick_rows(onehot, x):
    high, mid, low = split3(x)

    def dot(part):
        return lax.dot_general(onehot, part, (((1,), (0,)), ((), ())), preferred_element_type=F32)

    return (dot(low) + dot(mid)) + dot(high)


def slot_values(rows_of, start, first):
    lane = lanes((PEERS, CY))
    picked = pick_rows(rows_of, first)
    window = jnp.take_along_axis(picked, (start + lane) & (CY - 1), axis=1)
    return jnp.where(lane < CAP, window, 0.0)


def into_cells(rows_to, start, flows):
    lane = lanes((PEERS, CY))
    spread = jnp.take_along_axis(flows, (lane - start) & (CY - 1), axis=1)
    return pick_rows(rows_to, spread)


def segment_values(state, index):
    low = index & 127
    first = jnp.take_along_axis(jnp.broadcast_to(state[0:1], (8, 128)), low, axis=1)
    second = jnp.take_along_axis(jnp.broadcast_to(state[1:2], (8, 128)), low, axis=1)
    return jnp.where(index >= 128, second, first)


def into_segments(values, index, table):
    parts = [part.astype(F32) for part in split3(values)]
    sub = subs((16, 128))
    upper = (index >= 128).astype(jnp.int32)
    tiles = []
    for k in range(CAP):
        row = [jnp.broadcast_to(part[k : k + 1], (16, 128)) for part in parts]
        mine = jnp.broadcast_to(upper[k : k + 1], (16, 128)) == (sub & 1)
        tile = jnp.where(sub < 2, row[0], jnp.where(sub < 4, row[1], row[2]))
        tiles.append(jnp.where(mine & (sub < 6), tile, 0.0).astype(BF16))
    left = jnp.concatenate(tiles, axis=1)
    out = lax.dot_general(left, table, (((1,), (1,)), ((), ())), preferred_element_type=F32)[:8]
    total = (pltpu.roll(out, 4, 0) + pltpu.roll(out, 6, 0)) + out
    return jnp.where(subs((8, 128)) < 2, total, 0.0)


def previous(state):
    moved = pltpu.roll(state, 1, 1)
    return jnp.where(lanes((8, 128)) == 0, pltpu.roll(moved, 1, 0), moved)


def following(state):
    moved = pltpu.roll(state, 127, 1)
    return jnp.where(lanes((8, 128)) == 127, pltpu.roll(moved, 7, 0), moved)


def to_columns(values):
    tall = jnp.concatenate(
        [jnp.zeros((8, 128), F32), values, jnp.zeros((112, 128), F32)], axis=0
    )
    return tall.T


def chunk(t):
    return pl.ds(t * STEP, STEP)


def cell_setup(rhs, diag, cells, pi, inverse, first, message, rows_of, rows_to, start, weight, slots):
    for t in range(CHUNKS):
        rows = chunk(t)
        a, b, c, d, e, f, g, h, i = [diag[n, rows, :].astype(F32) for n in range(9)]
        p, q, s = e * i - f * h, f * g - d * i, d * h - e * g
        scale = 1.0 / (a * p + b * q + c * s)
        entries = [
            p, c * h - b * i, b * f - c * e,
            q, a * i - c * g, c * d - a * f,
            s, b * g - a * h, a * e - b * d,
        ]
        entries = [entry * scale for entry in entries]
        x, y, z = [rhs[n, rows, :] for n in range(3)]
        for n in range(9):
            inverse[n, rows, :] = entries[n]
        for n in range(3):
            first[n, rows, :] = entries[3 * n] * x + entries[3 * n + 1] * y + entries[3 * n + 2] * z
    base = cells[0:1, :]
    row = lax.shift_right_logical(base, 7)
    lane = lanes((PEERS, 128))
    info = jnp.concatenate(
        [pi[...], jnp.broadcast_to(row.astype(F32), (8, 128)),
         jnp.broadcast_to((base & 127).astype(F32), (8, 128)), jnp.zeros((104, 128), F32)],
        axis=0,
    ).T
    rows_to[...] = (subs((ROWS, PEERS)) == jnp.broadcast_to(row, (ROWS, PEERS))).astype(F32).astype(BF16)
    row_column = jnp.broadcast_to(info[:, 8:9], (PEERS, ROWS)).astype(jnp.int32)
    rows_of[...] = (lanes((PEERS, ROWS)) == row_column).astype(F32).astype(BF16)
    begin = jnp.broadcast_to(info[:, 16:17], (PEERS, 128)).astype(jnp.int32)
    start[...] = begin
    weights = jnp.where(lane < CAP, info, 0.0)
    weight[...] = weights
    values = slot_values(rows_of[...], begin, first[0])
    slots[...] = values
    message[...] = values + pltpu.roll(weights, 8, 1)


def well_setup(arrived, slots, index, parent, trans, rhs, message, weight, table, state, at_slots, fixed):
    turned = arrived[...].T
    pi = turned[8:16]
    weight[...] = pi
    number = index[...]
    low = number & 127
    for k in range(CAP):
        hit = subs((128, 128)) == jnp.broadcast_to(low[k : k + 1], (128, 128))
        table[:, 128 * k : 128 * (k + 1)] = hit.astype(F32).astype(BF16)
    zeros = jnp.zeros((6, 128), F32)
    linked = jnp.concatenate([(parent[...] >= 0).astype(F32), zeros], axis=0)
    across = jnp.concatenate([trans[...], zeros], axis=0)
    source = jnp.concatenate([rhs[...], zeros], axis=0)
    diagonal = across + following(linked * across) + into_segments(pi, number, table[...])
    diagonal = jnp.where(subs((8, 128)) < 2, diagonal, 1.0)
    fixed[0] = linked
    fixed[1] = across
    fixed[2] = source
    fixed[3] = diagonal
    now = source / diagonal
    state[...] = now
    values = segment_values(now, number)
    at_slots[...] = values
    message[...] = slots[...] + to_columns(values)


def borders(field, mobility, trans, weighted, toward_low, toward_high, sides, scratch):
    for t in range(CHUNKS):
        rows = chunk(t)
        x, y, z = [field[n, rows, :] for n in range(3)]
        along = trans[0, rows, :].astype(F32)
        for n in range(3):
            value = (
                mobility[3 * n, rows, :].astype(F32) * x
                + mobility[3 * n + 1, rows, :].astype(F32) * y
                + mobility[3 * n + 2, rows, :].astype(F32) * z
            )
            weighted[n, rows, :] = value
            scratch[pl.ds(n * ROWS + t * STEP, STEP), :] = along * value
    toward_low[...] = scratch[pl.ds(0, 3 * NZ, stride=CX), :]
    toward_high[...] = scratch[pl.ds(CX - 1, 3 * NZ, stride=CX), :]
    pair = lax.shift_right_logical(lanes((8, 128)), 1)
    packed = jnp.zeros((8, 128), F32)
    for t in range(CHUNKS):
        across = trans[1, chunk(t), :].astype(F32)
        for n in range(3):
            value = across * weighted[n, chunk(t), :]
            for half in range(2):
                j = n * NZ + 2 * t + half
                moved = pltpu.roll(value[8 * half : 8 * half + 8], (2 * j + 1) % 128, 1)
                packed = jnp.where(pair == j, moved, packed)
    sides[...] = packed


def interior(field, weighted, diag, trans, rhs, base, scratch):
    for n in range(3):
        scratch[n, 0:8, :] = jnp.zeros((8, 128), F32)
        scratch[n, ROWS + 8 : ROWS + 16, :] = jnp.zeros((8, 128), F32)
    for t in range(CHUNKS):
        up = trans[2, chunk(t), :].astype(F32)
        for n in range(3):
            scratch[n, pl.ds(8 + t * STEP, STEP), :] = up * weighted[n, chunk(t), :]
    lane = lanes((STEP, 128))
    sub = subs((STEP, 128)) & 7
    for t in range(CHUNKS):
        rows = chunk(t)
        x, y, z = [field[n, rows, :] for n in range(3)]
        tx, ty, tz = [trans[n, rows, :].astype(F32) for n in range(3)]
        for n in range(3):
            value = weighted[n, rows, :]
            px, py = tx * value, ty * value
            nx = jnp.where(sub == 0, 0.0, pltpu.roll(px, 1, 0)) + jnp.where(
                sub == 7, 0.0, pltpu.roll(px, STEP - 1, 0)
            )
            ny = jnp.where(lane == 0, 0.0, pltpu.roll(py, 1, 1)) + jnp.where(
                lane == 127, 0.0, pltpu.roll(py, 127, 1)
            )
            nz = scratch[n, pl.ds(t * STEP, STEP), :] + scratch[n, pl.ds(t * STEP + 16, STEP), :]
            near = tx * nx + ty * ny + tz * nz
            own = (
                diag[3 * n, rows, :].astype(F32) * x
                + diag[3 * n + 1, rows, :].astype(F32) * y
                + diag[3 * n + 2, rows, :].astype(F32) * z
            )
            base[n, rows, :] = (rhs[n, rows, :] - own) + near


MOVING = ("arrived", "base", "field", "from_low", "from_high", "side_low", "side_high",
          "slots", "at_slots", "state")
STEADY = ("inverse", "mobility", "trans", "rows_of", "rows_to", "start", "weight",
          "own_weight", "table", "index", "fixed")


def extras_of(last, final):
    if final:
        return ("rhs", "residual", "seg_residual", "omega")
    return ("rhs",) if last else ()


def results_of(blend, last, final):
    if final:
        return ("message",)
    names = ("field", "slots", "at_slots", "state", "message")
    return names + (("omega",) if blend else ()) + (("residual", "seg_residual") if last else ())


def spread_pair(two):
    return jnp.concatenate(
        [jnp.broadcast_to(two[h : h + 1], (8, 128)) for h in range(2)], axis=0
    )


def ratio(turned):
    numer = jnp.sum(turned[16:17], axis=1, keepdims=True)
    denom = jnp.sum(turned[17:18], axis=1, keepdims=True)
    return numer / denom


def sweep(blend, last, final, *refs):
    take = iter(refs)
    now = {name: next(take) for name in MOVING}
    early = {name: next(take) for name in MOVING} if blend else None
    fixed = {name: next(take) for name in STEADY}
    extra = {name: next(take) for name in extras_of(last, final)}
    out = {name: next(take) for name in results_of(blend, last, final)}
    if blend:
        omega = ratio(now["arrived"][...].T)
        out["omega"][...] = jnp.broadcast_to(omega, (8, 128))

    def get(name, *where):
        where = where or (Ellipsis,)
        value = now[name][where]
        if blend:
            old = early[name][where]
            value = old + omega * (value - old)
        return value

    arrived = get("arrived")
    turned = arrived.T
    pull = fixed["weight"][...] * (get("slots") - pltpu.roll(arrived, 120, 1))
    perforated = into_cells(fixed["rows_to"][...], fixed["start"][...], pull)

    state = get("state")
    linked, across, source, diagonal = [fixed["fixed"][n] for n in range(4)]
    push = fixed["own_weight"][...] * (turned[0:8] - get("at_slots"))
    number = fixed["index"][...]
    inflow = into_segments(push, number, fixed["table"][...])
    flux = across * (state - linked * previous(state))
    seg_res = source - flux + following(linked * flux) + inflow

    lane = lanes((STEP, 128))
    sub = subs((STEP, 128)) & 7
    odd = (lanes((8, 128)) & 1) == 1
    sides = jnp.where(
        odd, pltpu.roll(get("side_low"), 1, 1), pltpu.roll(get("side_high"), 127, 1)
    )
    numer = jnp.zeros((STEP, 128), F32)
    denom = jnp.zeros((STEP, 128), F32)
    if final:
        omega = extra["omega"][0:1, 0:1]
    for t in range(CHUNKS):
        rows = chunk(t)
        tx, ty = [fixed["trans"][n, rows, :].astype(F32) for n in range(2)]
        residual = []
        for n in range(3):
            j = n * NZ + 2 * t
            low = get("from_low", pl.ds(j, 2), slice(None))
            high = get("from_high", pl.ds(j, 2), slice(None))
            nx = jnp.where(sub == 0, spread_pair(low), jnp.where(sub == 7, spread_pair(high), 0.0))
            side = jnp.concatenate(
                [pltpu.roll(sides, (127 - 2 * (j + h)) % 128, 1) for h in range(2)], axis=0
            )
            ny = jnp.where((lane == 0) | (lane == 127), side, 0.0)
            share = fixed["mobility"][3 * n, rows, :].astype(F32)
            value = get("base", n, rows, slice(None)) + tx * nx + ty * ny
            residual.append(value - share * perforated[t * STEP : (t + 1) * STEP])
        for n in range(3):
            if last or final:
                before = extra["rhs"][n, rows, :]
                if final:
                    before = before + omega * (extra["residual"][n, rows, :] - before)
                change = before - residual[n]
                numer += before * change
                denom += change * change
            if last:
                out["residual"][n, rows, :] = residual[n]
            if not final:
                entry = [fixed["inverse"][3 * n + m, rows, :] for m in range(3)]
                out["field"][n, rows, :] = get("field", n, rows, slice(None)) + (
                    entry[0] * residual[0] + entry[1] * residual[1] + entry[2] * residual[2]
                )
    message = jnp.zeros((PEERS, 128), F32)
    if not final:
        advanced = state + seg_res / diagonal
        out["state"][...] = advanced
        values = segment_values(advanced, number)
        out["at_slots"][...] = values
        cells = slot_values(fixed["rows_of"][...], fixed["start"][...], out["field"][0])
        out["slots"][...] = cells
        message = cells + to_columns(values)
    if last or final:
        before = source
        if final:
            before = before + omega * (extra["seg_residual"][...] - before)
        change = before - seg_res
        above = jnp.sum(numer, keepdims=True) + jnp.sum(before * change, keepdims=True)
        below = jnp.sum(denom, keepdims=True) + jnp.sum(change * change, keepdims=True)
        place = lanes((PEERS, 128))
        message += jnp.where(place == 16, above, jnp.where(place == 17, below, 0.0))
    if last:
        out["seg_residual"][...] = seg_res
    out["message"][...] = message


def finish(arrived, omega, field_one, field_two, state_one, state_two, cells, segments):
    first = omega[0:1, 0:1]
    second = ratio(arrived[...].T)
    for n in range(3):
        for t in range(CHUNKS):
            kept = first * field_one[n, chunk(t), :]
            cells[n, chunk(t), :] = kept + second * (field_two[n, chunk(t), :] - kept)
    kept = first * state_one[0:2]
    segments[...] = kept + second * (state_two[0:2] - kept)


CELLS = ((3, ROWS, 128), F32)
PAIRS = ((PEERS, 128), F32)
TILE = ((8, 128), F32)
EDGE = ((3 * NZ, 128), F32)
SHAPES = {
    "field": CELLS, "residual": CELLS, "message": PAIRS, "slots": PAIRS,
    "at_slots": TILE, "state": TILE, "omega": TILE, "seg_residual": TILE,
}


def call(body, outs, args, scratch=(), name=None):
    moved = sum(a.size * a.dtype.itemsize for a in args)
    return pl.pallas_call(
        body,
        out_shape=[jax.ShapeDtypeStruct(*out) for out in outs],
        in_specs=[pl.BlockSpec(memory_space=pltpu.VMEM)] * len(args),
        out_specs=[pl.BlockSpec(memory_space=pltpu.VMEM)] * len(outs),
        scratch_shapes=list(scratch),
        compiler_params=pltpu.CompilerParams(vmem_limit_bytes=24 * 1024 * 1024),
        cost_estimate=pl.CostEstimate(flops=4_000_000, bytes_accessed=moved, transcendentals=0),
        name=name,
    )(*args)


def exchange(message):
    return lax.all_to_all(message, AXES, split_axis=0, concat_axis=0, tiled=True)


def neighbours(toward_low, toward_high, sides):
    up_x = [(i, i + 1) for i in range(lax.axis_size("gx") - 1)]
    up_y = [(i, i + 1) for i in range(lax.axis_size("gy") - 1)]
    down_x = [(b, a) for a, b in up_x]
    down_y = [(b, a) for a, b in up_y]
    return {
        "from_low": lax.ppermute(toward_high, "gx", up_x),
        "from_high": lax.ppermute(toward_low, "gx", down_x),
        "side_low": lax.ppermute(sides, "gy", up_y),
        "side_high": lax.ppermute(sides, "gy", down_y),
    }


def on_device(
    rhs, diag_block, mobility, trans, perf_cell, perf_pi, perf_seg, seg_parent, seg_trans, seg_rhs
):
    rhs = rhs.reshape(3, ROWS, 128)
    diag = diag_block.reshape(9, ROWS, 128)
    mobility = mobility.reshape(9, ROWS, 128)
    trans = trans.reshape(3, ROWS, 128)
    index = perf_seg[0]

    fixed = {"mobility": mobility, "trans": trans, "index": index}
    inverse, first, message, rows_of, rows_to, start, weight, slots = call(
        cell_setup,
        [((9, ROWS, 128), F32), CELLS, PAIRS, ((PEERS, ROWS), BF16), ((ROWS, PEERS), BF16),
         ((PEERS, 128), jnp.int32), PAIRS, PAIRS],
        [rhs, diag, perf_cell[0], perf_pi[0]],
        name="cell_setup",
    )
    fixed.update(inverse=inverse, rows_of=rows_of, rows_to=rows_to, start=start, weight=weight)
    arrived = exchange(message)

    def prepare(field):
        weighted, toward_low, toward_high, sides = call(
            borders,
            [CELLS, EDGE, EDGE, TILE],
            [field, mobility, trans],
            [pltpu.VMEM((3 * ROWS, 128), F32)],
            name="borders",
        )
        found = neighbours(toward_low, toward_high, sides)
        (found["base"],) = call(
            interior,
            [CELLS],
            [field, weighted, diag, trans, rhs],
            [pltpu.VMEM((3, ROWS + 16, 128), F32)],
            name="interior",
        )
        found["field"] = field
        return found

    now = prepare(first)
    message, own_weight, table, state, at_slots, constants = call(
        well_setup,
        [PAIRS, TILE, ((128, CAP * 128), BF16), TILE, TILE, ((4, 8, 128), F32)],
        [arrived, slots, index, seg_parent.reshape(2, 128), seg_trans.reshape(2, 128),
         seg_rhs.reshape(2, 128)],
        name="well_setup",
    )
    fixed.update(own_weight=own_weight, table=table, fixed=constants)
    now.update(arrived=exchange(message), slots=slots, at_slots=at_slots, state=state)

    def advance(now, early=None, last=False, final=False, extra=None):
        blend = early is not None
        args = [now[name] for name in MOVING]
        if blend:
            args += [early[name] for name in MOVING]
        args += [fixed[name] for name in STEADY]
        args += [extra[name] for name in extras_of(last, final)]
        names = results_of(blend, last, final)
        out = call(
            functools.partial(sweep, blend, last, final),
            [SHAPES[name] for name in names],
            args,
            name="sweep",
        )
        out = dict(zip(names, out))
        out["arrived"] = exchange(out.pop("message"))
        if not final:
            out.update(prepare(out["field"]))
        return out

    early = now
    now = advance(now)
    now = advance(now)
    one = advance(now)
    kept = advance(one, last=True, extra={"rhs": rhs})
    now = advance(kept, early=early)
    kept["omega"] = now["omega"]
    now = advance(now)
    two = advance(now)
    kept["rhs"] = rhs
    sums = advance(two, final=True, extra=kept)
    cells, segments = call(
        finish,
        [CELLS, ((2, 128), F32)],
        [sums["arrived"], kept["omega"], one["field"], two["field"], one["state"], two["state"]],
        name="finish",
    )
    return cells.reshape(3, NZ, CX, CY), segments.reshape(256)


def solution(mesh):
    grid = P(None, None, "gx", "gy")
    pairs = P(AXES, None, None)
    flat = P(AXES)
    return jax.shard_map(
        on_device,
        mesh=mesh,
        in_specs=(grid, grid, grid, grid, pairs, pairs, pairs, flat, flat, flat),
        out_specs=(grid, flat),
        check_vma=False,
    )
```

time: 915 us -> 319 us (0.35); the launches traced: 903 us -> 316 us
  other arithmetic: 210 us -> 0 us
  local copies, waits for them, and re-layouts: 195 us -> 73.7 us
  blocking collectives: 139 us -> 44.2 us
  starting transfers between devices: 271 us -> 182 us
  waiting for transfers between devices: 76.6 us -> 0.51 us
  Pallas kernels: 0 us -> 14 us
  between operations: 11.3 us -> 1.47 us
    gather x24 -> x0, local copies, waits for them, and re-layouts: 150 us -> none  [the longest x8 75.4 us: on_device(): advance_field[0].reshape(-1)[cell_index] - advance_slot_state.reshape(-1)]
    scatter-add x26 -> x0, other arithmetic: 146 us -> none  [the longest x8 63.6 us: on_device(): jax.ops.segment_sum(arrived.reshape(-1), seg_index, num_segments=segments)]
    psum x2 -> x0, blocking collectives: 139 us -> none  [on_device(): numer, denom = lax.psum((local_numer, local_denom), ('gx', 'gy'))]
    all_to_all x17 -> x8, starting transfers between devices: 154 us -> 96 us  [exchange(): lax.all_to_all(message, AXES, split_axis=0, concat_axis=0, tiled=True)]
    unnamed x336 -> x254, local copies, waits for them, and re-layouts: 16.2 us -> 73.7 us
    all_to_all x0 -> x2, blocking collectives: none -> 44.2 us  [exchange(): lax.all_to_all(message, AXES, split_axis=0, concat_axis=0, tiled=True)]
    ppermute x36 -> x32, waiting for transfers between devices: 44.4 us -> 0.49 us  [the longest x8 0.42 us: neighbours(): lax.ppermute(sides, 'gy', up_y)]
    all_to_all x17 -> x8, waiting for transfers between devices: 32.2 us -> 0.02 us  [exchange(): lax.all_to_all(message, AXES, split_axis=0, concat_axis=0, tiled=True)]
  transfers between devices with their start and end apart: 53 -> 40, of which waited for: 25 -> 1; matrix products, arithmetic and copies ran while one was open for 36% -> 0% of each run, Pallas kernels for 0% -> 1%
where the time goes in v1:
time: 319 us; the launch traced here: 316 us
  starting transfers between devices  182 us (57%)
  local copies, waits for them, and re-layouts  73.7 us (23%)
  blocking collectives  44.2 us (14%)
  Pallas kernels  14 us (4%)
    all_to_all x8, starting transfers between devices, exchange(): lax.all_to_all(message, AXES, split_axis=0, concat_axis=0, tiled=True)  96 us
    unnamed x254, local copies, waits for them, and re-layouts  73.7 us
    all_to_all x2, blocking collectives, exchange(): lax.all_to_all(message, AXES, split_axis=0, concat_axis=0, tiled=True)  44.2 us
    ppermute x8, starting transfers between devices, neighbours(): lax.ppermute(sides, 'gy', up_y)  31.9 us
    ppermute x8, starting transfers between devices, neighbours(): lax.ppermute(toward_high, 'gx', up_x)  28.5 us
    ppermute x8, starting transfers between devices, neighbours(): lax.ppermute(toward_low, 'gx', down_x)  15.4 us
    pallas_call x27, Pallas kernels, call(): pl.pallas_call(body, out_shape=[jax.ShapeDtypeStruct(*out) for out in out...  14 us
    ppermute x8, starting transfers between devices, neighbours(): lax.ppermute(sides, 'gy', down_y)  10.3 us
  transfers between devices with their start and end apart: 40, of which 1 were waited for; matrix products, arithmetic and copies ran while one was open for 0% of the time, Pallas kernels for 1%

profile of v1, /device:TPU:1, one launch (start us, length us, event | category | flops | bytes accessed | tf_op | source)
XLA Modules:
  0.0 315.9 jit_solution(1493952390595443863)
XLA Ops:
  1.3 1.0 copy-done.2
  2.3 0.9 copy-done.4
  4.5 21.1 %all_to_all.110 = f32[128,1,128]{2,1,0:T(1,128)S(1)} all-to-all(f32[128,1,128]{2,1,0:T(1,128)S(1)} %bitcast.138), channel_id=1, replica_groups=mesh['gx'=8,'gy'=16] {'gx','gy'}, dimensions={0} | all-to-all | bytes 131072 | tf_op jit(solution)/shard_map/all_to_all | solution.py:390
  26.3 1.1 well_setup.1
  27.4 4.3 %all-to-all-start.1 = ((f32[128,1,128]{2,1,0:T(1,128)}), f32[128,1,128]{2,1,0:T(1,128)S(1)}, u32[]{:S(2)}, u32[]{:S(2)}) async-start(f32[128,1,128]{2,1,0:T(1,128)} %bitcast.12), calls=%async_computation.1 | async-start | bytes 131072 | tf_op jit(solution)/shard_map/all_to_all | solution.py:390
  31.9 3.7 %collective-permute-start = (f32[60,128]{1,0:T(8,128)S(1)}, f32[60,128]{1,0:T(8,128)S(1)}, u32[]{:S(2)}, u32[]{:S(2)}) collective-permute-start(f32[60,128]{1,0:T(8,128)S(1)} %get-tuple-element.93), channel_id=1, source_target_pairs={{0,16},{16,32},{32,48},{48,64},{64,80},{80,96},{96,112},{1,17},{17... | collective-permute-start | bytes 92168 | tf_op jit(solution)/shard_map/ppermute | solution.py:399
  35.6 1.9 collective-permute-start.1
  37.5 1.3 collective-permute-start.3
  38.8 4.0 %collective-permute-start.2 = (f32[8,128]{1,0:T(8,128)S(1)}, f32[8,128]{1,0:T(8,128)S(1)}, u32[]{:S(2)}, u32[]{:S(2)}) collective-permute-start(f32[8,128]{1,0:T(8,128)S(1)} %get-tuple-element.95), channel_id=1, source_target_pairs={{0,1},{1,2},{2,3},{3,4},{4,5},{5,6},{6,7},{7,8},{8,9},{9,10},{10,1... | collective-permute-start | bytes 12296 | tf_op jit(solution)/shard_map/ppermute | solution.py:401
  44.1 1.4 sweep.8
  46.8 13.7 %all-to-all-start.2 = ((f32[128,1,128]{2,1,0:T(1,128)}), f32[128,1,128]{2,1,0:T(1,128)S(1)}, u32[]{:S(2)}, u32[]{:S(2)}) async-start(f32[128,1,128]{2,1,0:T(1,128)} %bitcast.17), calls=%async_computation.2 | async-start | bytes 131072 | tf_op jit(solution)/shard_map/all_to_all | solution.py:390
  60.6 3.5 %collective-permute-start.4 = (f32[60,128]{1,0:T(8,128)S(1)}, f32[60,128]{1,0:T(8,128)S(1)}, u32[]{:S(2)}, u32[]{:S(2)}) collective-permute-start(f32[60,128]{1,0:T(8,128)S(1)} %get-tuple-element.109), channel_id=1, source_target_pairs={{0,16},{16,32},{32,48},{48,64},{64,80},{80,96},{96,112},{1,17},{17... | collective-permute-start | bytes 92168 | tf_op jit(solution)/shard_map/ppermute | solution.py:399
  64.2 1.9 collective-permute-start.5
  66.1 1.3 collective-permute-start.7
  67.4 4.0 %collective-permute-start.6 = (f32[8,128]{1,0:T(8,128)S(1)}, f32[8,128]{1,0:T(8,128)S(1)}, u32[]{:S(2)}, u32[]{:S(2)}) collective-permute-start(f32[8,128]{1,0:T(8,128)S(1)} %get-tuple-element.111), channel_id=1, source_target_pairs={{0,1},{1,2},{2,3},{3,4},{4,5},{5,6},{6,7},{7,8},{8,9},{9,10},{10,1... | collective-permute-start | bytes 12296 | tf_op jit(solution)/shard_map/ppermute | solution.py:401
  84.1 12.8 %all-to-all-start.3 = ((f32[128,1,128]{2,1,0:T(1,128)}), f32[128,1,128]{2,1,0:T(1,128)S(1)}, u32[]{:S(2)}, u32[]{:S(2)}) async-start(f32[128,1,128]{2,1,0:T(1,128)} %bitcast.134), calls=%async_computation.3 | async-start | bytes 131072 | tf_op jit(solution)/shard_map/all_to_all | solution.py:390
  97.1 3.5 %collective-permute-start.8 = (f32[60,128]{1,0:T(8,128)S(1)}, f32[60,128]{1,0:T(8,128)S(1)}, u32[]{:S(2)}, u32[]{:S(2)}) collective-permute-start(f32[60,128]{1,0:T(8,128)S(1)} %get-tuple-element.118), channel_id=1, source_target_pairs={{0,16},{16,32},{32,48},{48,64},{64,80},{80,96},{96,112},{1,17},{17... | collective-permute-start | bytes 92168 | tf_op jit(solution)/shard_map/ppermute | solution.py:399
  100.6 1.9 collective-permute-start.9
  102.5 1.3 collective-permute-start.11
  103.8 4.0 %collective-permute-start.10 = (f32[8,128]{1,0:T(8,128)S(1)}, f32[8,128]{1,0:T(8,128)S(1)}, u32[]{:S(2)}, u32[]{:S(2)}) collective-permute-start(f32[8,128]{1,0:T(8,128)S(1)} %get-tuple-element.120), channel_id=1, source_target_pairs={{0,1},{1,2},{2,3},{3,4},{4,5},{5,6},{6,7},{7,8},{8,9},{9,10},{10,1... | collective-permute-start | bytes 12296 | tf_op jit(solution)/shard_map/ppermute | solution.py:401
  119.9 12.8 %all-to-all-start.4 = ((f32[128,1,128]{2,1,0:T(1,128)}), f32[128,1,128]{2,1,0:T(1,128)S(1)}, u32[]{:S(2)}, u32[]{:S(2)}) async-start(f32[128,1,128]{2,1,0:T(1,128)} %bitcast.135), calls=%async_computation.4 | async-start | bytes 131072 | tf_op jit(solution)/shard_map/all_to_all | solution.py:390
  132.9 3.5 %collective-permute-start.12 = (f32[60,128]{1,0:T(8,128)S(1)}, f32[60,128]{1,0:T(8,128)S(1)}, u32[]{:S(2)}, u32[]{:S(2)}) collective-permute-start(f32[60,128]{1,0:T(8,128)S(1)} %get-tuple-element.127), channel_id=1, source_target_pairs={{0,16},{16,32},{32,48},{48,64},{64,80},{80,96},{96,112},{1,17},{17... | collective-permute-start | bytes 92168 | tf_op jit(solution)/shard_map/ppermute | solution.py:399
  136.5 1.9 collective-permute-start.13
  138.4 1.3 collective-permute-start.15
  139.7 4.0 %collective-permute-start.14 = (f32[8,128]{1,0:T(8,128)S(1)}, f32[8,128]{1,0:T(8,128)S(1)}, u32[]{:S(2)}, u32[]{:S(2)}) collective-permute-start(f32[8,128]{1,0:T(8,128)S(1)} %get-tuple-element.129), channel_id=1, source_target_pairs={{0,1},{1,2},{2,3},{3,4},{4,5},{5,6},{6,7},{7,8},{8,9},{9,10},{10,1... | collective-permute-start | bytes 12296 | tf_op jit(solution)/shard_map/ppermute | solution.py:401
  157.0 12.8 %all-to-all-start.5 = ((f32[128,1,128]{2,1,0:T(1,128)}), f32[128,1,128]{2,1,0:T(1,128)S(1)}, u32[]{:S(2)}, u32[]{:S(2)}) async-start(f32[128,1,128]{2,1,0:T(1,128)} %bitcast.136), calls=%async_computation.5 | async-start | bytes 131072 | tf_op jit(solution)/shard_map/all_to_all | solution.py:390
  170.0 3.5 %collective-permute-start.16 = (f32[60,128]{1,0:T(8,128)S(1)}, f32[60,128]{1,0:T(8,128)S(1)}, u32[]{:S(2)}, u32[]{:S(2)}) collective-permute-start(f32[60,128]{1,0:T(8,128)S(1)} %get-tuple-element.136), channel_id=1, source_target_pairs={{0,16},{16,32},{32,48},{48,64},{64,80},{80,96},{96,112},{1,17},{17... | collective-permute-start | bytes 92168 | tf_op jit(solution)/shard_map/ppermute | solution.py:399
  173.6 1.9 collective-permute-start.17
  175.5 1.3 collective-permute-start.19
  176.8 4.0 %collective-permute-start.18 = (f32[8,128]{1,0:T(8,128)S(1)}, f32[8,128]{1,0:T(8,128)S(1)}, u32[]{:S(2)}, u32[]{:S(2)}) collective-permute-start(f32[8,128]{1,0:T(8,128)S(1)} %get-tuple-element.138), channel_id=1, source_target_pairs={{0,1},{1,2},{2,3},{3,4},{4,5},{5,6},{6,7},{7,8},{8,9},{9,10},{10,1... | collective-permute-start | bytes 12296 | tf_op jit(solution)/shard_map/ppermute | solution.py:401
  193.7 1.0 sweep.12
  198.5 12.8 %all-to-all-start.6 = ((f32[128,1,128]{2,1,0:T(1,128)}), f32[128,1,128]{2,1,0:T(1,128)S(1)}, u32[]{:S(2)}, u32[]{:S(2)}) async-start(f32[128,1,128]{2,1,0:T(1,128)} %bitcast.133), calls=%async_computation.6 | async-start | bytes 131072 | tf_op jit(solution)/shard_map/all_to_all | solution.py:390
  212.4 3.5 %collective-permute-start.20 = (f32[60,128]{1,0:T(8,128)S(1)}, f32[60,128]{1,0:T(8,128)S(1)}, u32[]{:S(2)}, u32[]{:S(2)}) collective-permute-start(f32[60,128]{1,0:T(8,128)S(1)} %get-tuple-element.145), channel_id=1, source_target_pairs={{0,16},{16,32},{32,48},{48,64},{64,80},{80,96},{96,112},{1,17},{17... | collective-permute-start | bytes 92168 | tf_op jit(solution)/shard_map/ppermute | solution.py:399
  215.9 1.9 collective-permute-start.21
  217.9 1.3 collective-permute-start.23
  219.2 4.0 %collective-permute-start.22 = (f32[8,128]{1,0:T(8,128)S(1)}, f32[8,128]{1,0:T(8,128)S(1)}, u32[]{:S(2)}, u32[]{:S(2)}) collective-permute-start(f32[8,128]{1,0:T(8,128)S(1)} %get-tuple-element.147), channel_id=1, source_target_pairs={{0,1},{1,2},{2,3},{3,4},{4,5},{5,6},{6,7},{7,8},{8,9},{9,10},{10,1... | collective-permute-start | bytes 12296 | tf_op jit(solution)/shard_map/ppermute | solution.py:401
  226.8 1.4 sweep.13
  230.0 13.5 %all-to-all-start.7 = ((f32[128,1,128]{2,1,0:T(1,128)}), f32[128,1,128]{2,1,0:T(1,128)S(1)}, u32[]{:S(2)}, u32[]{:S(2)}) async-start(f32[128,1,128]{2,1,0:T(1,128)} %bitcast.32), calls=%async_computation.7 | async-start | bytes 131072 | tf_op jit(solution)/shard_map/all_to_all | solution.py:390
  243.6 3.5 %collective-permute-start.24 = (f32[60,128]{1,0:T(8,128)S(1)}, f32[60,128]{1,0:T(8,128)S(1)}, u32[]{:S(2)}, u32[]{:S(2)}) collective-permute-start(f32[60,128]{1,0:T(8,128)S(1)} %get-tuple-element.154), channel_id=1, source_target_pairs={{0,16},{16,32},{32,48},{48,64},{64,80},{80,96},{96,112},{1,17},{17... | collective-permute-start | bytes 92168 | tf_op jit(solution)/shard_map/ppermute | solution.py:399
  247.2 1.9 collective-permute-start.25
  249.1 1.3 collective-permute-start.27
  250.4 4.0 %collective-permute-start.26 = (f32[8,128]{1,0:T(8,128)S(1)}, f32[8,128]{1,0:T(8,128)S(1)}, u32[]{:S(2)}, u32[]{:S(2)}) collective-permute-start(f32[8,128]{1,0:T(8,128)S(1)} %get-tuple-element.156), channel_id=1, source_target_pairs={{0,1},{1,2},{2,3},{3,4},{4,5},{5,6},{6,7},{7,8},{8,9},{9,10},{10,1... | collective-permute-start | bytes 12296 | tf_op jit(solution)/shard_map/ppermute | solution.py:401
  263.4 13.5 %all-to-all-start.8 = ((f32[128,1,128]{2,1,0:T(1,128)}), f32[128,1,128]{2,1,0:T(1,128)S(1)}, u32[]{:S(2)}, u32[]{:S(2)}) async-start(f32[128,1,128]{2,1,0:T(1,128)} %bitcast.137), calls=%async_computation.8 | async-start | bytes 131072 | tf_op jit(solution)/shard_map/all_to_all | solution.py:390
  277.0 3.5 %collective-permute-start.28 = (f32[60,128]{1,0:T(8,128)S(1)}, f32[60,128]{1,0:T(8,128)S(1)}, u32[]{:S(2)}, u32[]{:S(2)}) collective-permute-start(f32[60,128]{1,0:T(8,128)S(1)} %get-tuple-element.163), channel_id=1, source_target_pairs={{0,16},{16,32},{32,48},{48,64},{64,80},{80,96},{96,112},{1,17},{17... | collective-permute-start | bytes 92168 | tf_op jit(solution)/shard_map/ppermute | solution.py:399
  280.6 1.9 collective-permute-start.29
  282.5 1.3 collective-permute-start.31
  283.8 4.0 %collective-permute-start.30 = (f32[8,128]{1,0:T(8,128)S(1)}, f32[8,128]{1,0:T(8,128)S(1)}, u32[]{:S(2)}, u32[]{:S(2)}) collective-permute-start(f32[8,128]{1,0:T(8,128)S(1)} %get-tuple-element.165), channel_id=1, source_target_pairs={{0,1},{1,2},{2,3},{3,4},{4,5},{5,6},{6,7},{7,8},{8,9},{9,10},{10,1... | collective-permute-start | bytes 12296 | tf_op jit(solution)/shard_map/ppermute | solution.py:401
  292.0 23.1 %all_to_all.111 = f32[128,1,128]{2,1,0:T(1,128)S(1)} all-to-all(f32[128,1,128]{2,1,0:T(1,128)S(1)} %bitcast.129), channel_id=1, replica_groups=mesh['gx'=8,'gy'=16] {'gx','gy'}, dimensions={0} | all-to-all | bytes 131072 | tf_op jit(solution)/shard_map/all_to_all | solution.py:390
  (315 shorter events, 81.4 us)
Async XLA Ops:
  3.9 27.7 %copy-start = (bf16[9,20,8,128]{3,2,1,0:T(8,128)(2,1)S(1)}, bf16[9,20,8,128]{3,2,1,0:T(8,128)(2,1)}, u32[]{:S(2)}) copy-start(bf16[9,20,8,128]{3,2,1,0:T(8,128)(2,1)} %param.12) | copy-start | bytes 1105924
  26.3 5.4 %copy-start.1 = (bf16[3,20,8,128]{3,2,1,0:T(8,128)(2,1)S(1)}, bf16[3,20,8,128]{3,2,1,0:T(8,128)(2,1)}, u32[]{:S(2)}) copy-start(bf16[3,20,8,128]{3,2,1,0:T(8,128)(2,1)} %param.13) | copy-start | bytes 368644
  27.4 16.2 %copy-start.60 = (f32[8,128]{1,0:T(8,128)}, f32[8,128]{1,0:T(8,128)S(1)}, u32[]{:S(2)}) copy-start(f32[8,128]{1,0:T(8,128)S(1)} %get-tuple-element.96.refs_8_.refs_18_) | copy-start | bytes 12292
  27.4 16.2 %all-to-all-start.1 = ((f32[128,1,128]{2,1,0:T(1,128)}), f32[128,1,128]{2,1,0:T(1,128)S(1)}, u32[]{:S(2)}, u32[]{:S(2)}) async-start(f32[128,1,128]{2,1,0:T(1,128)} %bitcast.12), calls=%async_computation.1 | async-start | bytes 131072 | tf_op jit(solution)/shard_map/all_to_all | solution.py:390
  31.7 11.1 %copy-start.3 = (bf16[9,20,8,128]{3,2,1,0:T(8,128)(2,1)S(1)}, bf16[9,20,8,128]{3,2,1,0:T(8,128)(2,1)}, u32[]{:S(2)}) copy-start(bf16[9,20,8,128]{3,2,1,0:T(8,128)(2,1)} %param.11) | copy-start | bytes 1105924
  31.7 11.1 %copy-start.5 = (f32[3,20,8,128]{3,2,1,0:T(8,128)S(1)}, f32[3,20,8,128]{3,2,1,0:T(8,128)}, u32[]{:S(2)}) copy-start(f32[3,20,8,128]{3,2,1,0:T(8,128)} %param.10) | copy-start | bytes 737284
  31.9 11.6 %collective-permute-start = (f32[60,128]{1,0:T(8,128)S(1)}, f32[60,128]{1,0:T(8,128)S(1)}, u32[]{:S(2)}, u32[]{:S(2)}) collective-permute-start(f32[60,128]{1,0:T(8,128)S(1)} %get-tuple-element.93), channel_id=1, source_target_pairs={{0,16},{16,32},{32,48},{48,64},{64,80},{80,96},{96,112},{1,17},{17... | collective-permute-start | bytes 92168 | tf_op jit(solution)/shard_map/ppermute | solution.py:399
  35.6 8.0 %collective-permute-start.1 = (f32[60,128]{1,0:T(8,128)S(1)}, f32[60,128]{1,0:T(8,128)S(1)}, u32[]{:S(2)}, u32[]{:S(2)}) collective-permute-start(f32[60,128]{1,0:T(8,128)S(1)} %get-tuple-element.94), channel_id=1, source_target_pairs={{16,0},{32,16},{48,32},{64,48},{80,64},{96,80},{112,96},{17,1},{33... | collective-permute-start | bytes 92168 | tf_op jit(solution)/shard_map/ppermute | solution.py:400
  37.5 5.6 %collective-permute-start.3 = (f32[8,128]{1,0:T(8,128)S(1)}, f32[8,128]{1,0:T(8,128)S(1)}, u32[]{:S(2)}, u32[]{:S(2)}) collective-permute-start(f32[8,128]{1,0:T(8,128)S(1)} %get-tuple-element.95), channel_id=1, source_target_pairs={{1,0},{2,1},{3,2},{4,3},{5,4},{6,5},{7,6},{8,7},{9,8},{10,9},{11,1... | collective-permute-start | bytes 12296 | tf_op jit(solution)/shard_map/ppermute | solution.py:402
  38.8 4.7 %collective-permute-start.2 = (f32[8,128]{1,0:T(8,128)S(1)}, f32[8,128]{1,0:T(8,128)S(1)}, u32[]{:S(2)}, u32[]{:S(2)}) collective-permute-start(f32[8,128]{1,0:T(8,128)S(1)} %get-tuple-element.95), channel_id=1, source_target_pairs={{0,1},{1,2},{2,3},{3,4},{4,5},{5,6},{6,7},{7,8},{8,9},{9,10},{10,1... | collective-permute-start | bytes 12296 | tf_op jit(solution)/shard_map/ppermute | solution.py:401
  43.5 2.0 copy-start.19
  43.5 2.0 copy-start.21
  46.8 28.0 %all-to-all-start.2 = ((f32[128,1,128]{2,1,0:T(1,128)}), f32[128,1,128]{2,1,0:T(1,128)S(1)}, u32[]{:S(2)}, u32[]{:S(2)}) async-start(f32[128,1,128]{2,1,0:T(1,128)} %bitcast.17), calls=%async_computation.2 | async-start | bytes 131072 | tf_op jit(solution)/shard_map/all_to_all | solution.py:390
  60.6 13.0 %collective-permute-start.4 = (f32[60,128]{1,0:T(8,128)S(1)}, f32[60,128]{1,0:T(8,128)S(1)}, u32[]{:S(2)}, u32[]{:S(2)}) collective-permute-start(f32[60,128]{1,0:T(8,128)S(1)} %get-tuple-element.109), channel_id=1, source_target_pairs={{0,16},{16,32},{32,48},{48,64},{64,80},{80,96},{96,112},{1,17},{17... | collective-permute-start | bytes 92168 | tf_op jit(solution)/shard_map/ppermute | solution.py:399
  64.2 10.0 %collective-permute-start.5 = (f32[60,128]{1,0:T(8,128)S(1)}, f32[60,128]{1,0:T(8,128)S(1)}, u32[]{:S(2)}, u32[]{:S(2)}) collective-permute-start(f32[60,128]{1,0:T(8,128)S(1)} %get-tuple-element.110), channel_id=1, source_target_pairs={{16,0},{32,16},{48,32},{64,48},{80,64},{96,80},{112,96},{17,1},{33... | collective-permute-start | bytes 92168 | tf_op jit(solution)/shard_map/ppermute | solution.py:400
  66.1 6.3 %collective-permute-start.7 = (f32[8,128]{1,0:T(8,128)S(1)}, f32[8,128]{1,0:T(8,128)S(1)}, u32[]{:S(2)}, u32[]{:S(2)}) collective-permute-start(f32[8,128]{1,0:T(8,128)S(1)} %get-tuple-element.111), channel_id=1, source_target_pairs={{1,0},{2,1},{3,2},{4,3},{5,4},{6,5},{7,6},{8,7},{9,8},{10,9},{11,1... | collective-permute-start | bytes 12296 | tf_op jit(solution)/shard_map/ppermute | solution.py:402
  67.4 5.6 %collective-permute-start.6 = (f32[8,128]{1,0:T(8,128)S(1)}, f32[8,128]{1,0:T(8,128)S(1)}, u32[]{:S(2)}, u32[]{:S(2)}) collective-permute-start(f32[8,128]{1,0:T(8,128)S(1)} %get-tuple-element.111), channel_id=1, source_target_pairs={{0,1},{1,2},{2,3},{3,4},{4,5},{5,6},{6,7},{7,8},{8,9},{9,10},{10,1... | collective-permute-start | bytes 12296 | tf_op jit(solution)/shard_map/ppermute | solution.py:401
  84.1 27.2 %all-to-all-start.3 = ((f32[128,1,128]{2,1,0:T(1,128)}), f32[128,1,128]{2,1,0:T(1,128)S(1)}, u32[]{:S(2)}, u32[]{:S(2)}) async-start(f32[128,1,128]{2,1,0:T(1,128)} %bitcast.134), calls=%async_computation.3 | async-start | bytes 131072 | tf_op jit(solution)/shard_map/all_to_all | solution.py:390
  97.1 13.0 %collective-permute-start.8 = (f32[60,128]{1,0:T(8,128)S(1)}, f32[60,128]{1,0:T(8,128)S(1)}, u32[]{:S(2)}, u32[]{:S(2)}) collective-permute-start(f32[60,128]{1,0:T(8,128)S(1)} %get-tuple-element.118), channel_id=1, source_target_pairs={{0,16},{16,32},{32,48},{48,64},{64,80},{80,96},{96,112},{1,17},{17... | collective-permute-start | bytes 92168 | tf_op jit(solution)/shard_map/ppermute | solution.py:399
  100.6 10.0 %collective-permute-start.9 = (f32[60,128]{1,0:T(8,128)S(1)}, f32[60,128]{1,0:T(8,128)S(1)}, u32[]{:S(2)}, u32[]{:S(2)}) collective-permute-start(f32[60,128]{1,0:T(8,128)S(1)} %get-tuple-element.119), channel_id=1, source_target_pairs={{16,0},{32,16},{48,32},{64,48},{80,64},{96,80},{112,96},{17,1},{33... | collective-permute-start | bytes 92168 | tf_op jit(solution)/shard_map/ppermute | solution.py:400
  102.5 6.3 %collective-permute-start.11 = (f32[8,128]{1,0:T(8,128)S(1)}, f32[8,128]{1,0:T(8,128)S(1)}, u32[]{:S(2)}, u32[]{:S(2)}) collective-permute-start(f32[8,128]{1,0:T(8,128)S(1)} %get-tuple-element.120), channel_id=1, source_target_pairs={{1,0},{2,1},{3,2},{4,3},{5,4},{6,5},{7,6},{8,7},{9,8},{10,9},{11,1... | collective-permute-start | bytes 12296 | tf_op jit(solution)/shard_map/ppermute | solution.py:402
  103.8 5.6 %collective-permute-start.10 = (f32[8,128]{1,0:T(8,128)S(1)}, f32[8,128]{1,0:T(8,128)S(1)}, u32[]{:S(2)}, u32[]{:S(2)}) collective-permute-start(f32[8,128]{1,0:T(8,128)S(1)} %get-tuple-element.120), channel_id=1, source_target_pairs={{0,1},{1,2},{2,3},{3,4},{4,5},{5,6},{6,7},{7,8},{8,9},{9,10},{10,1... | collective-permute-start | bytes 12296 | tf_op jit(solution)/shard_map/ppermute | solution.py:401
  119.9 27.2 %all-to-all-start.4 = ((f32[128,1,128]{2,1,0:T(1,128)}), f32[128,1,128]{2,1,0:T(1,128)S(1)}, u32[]{:S(2)}, u32[]{:S(2)}) async-start(f32[128,1,128]{2,1,0:T(1,128)} %bitcast.135), calls=%async_computation.4 | async-start | bytes 131072 | tf_op jit(solution)/shard_map/all_to_all | solution.py:390
  132.9 13.0 %collective-permute-start.12 = (f32[60,128]{1,0:T(8,128)S(1)}, f32[60,128]{1,0:T(8,128)S(1)}, u32[]{:S(2)}, u32[]{:S(2)}) collective-permute-start(f32[60,128]{1,0:T(8,128)S(1)} %get-tuple-element.127), channel_id=1, source_target_pairs={{0,16},{16,32},{32,48},{48,64},{64,80},{80,96},{96,112},{1,17},{17... | collective-permute-start | bytes 92168 | tf_op jit(solution)/shard_map/ppermute | solution.py:399
  136.5 10.0 %collective-permute-start.13 = (f32[60,128]{1,0:T(8,128)S(1)}, f32[60,128]{1,0:T(8,128)S(1)}, u32[]{:S(2)}, u32[]{:S(2)}) collective-permute-start(f32[60,128]{1,0:T(8,128)S(1)} %get-tuple-element.128), channel_id=1, source_target_pairs={{16,0},{32,16},{48,32},{64,48},{80,64},{96,80},{112,96},{17,1},{33... | collective-permute-start | bytes 92168 | tf_op jit(solution)/shard_map/ppermute | solution.py:400
  138.4 6.3 %collective-permute-start.15 = (f32[8,128]{1,0:T(8,128)S(1)}, f32[8,128]{1,0:T(8,128)S(1)}, u32[]{:S(2)}, u32[]{:S(2)}) collective-permute-start(f32[8,128]{1,0:T(8,128)S(1)} %get-tuple-element.129), channel_id=1, source_target_pairs={{1,0},{2,1},{3,2},{4,3},{5,4},{6,5},{7,6},{8,7},{9,8},{10,9},{11,1... | collective-permute-start | bytes 12296 | tf_op jit(solution)/shard_map/ppermute | solution.py:402
  139.7 5.6 %collective-permute-start.14 = (f32[8,128]{1,0:T(8,128)S(1)}, f32[8,128]{1,0:T(8,128)S(1)}, u32[]{:S(2)}, u32[]{:S(2)}) collective-permute-start(f32[8,128]{1,0:T(8,128)S(1)} %get-tuple-element.129), channel_id=1, source_target_pairs={{0,1},{1,2},{2,3},{3,4},{4,5},{5,6},{6,7},{7,8},{8,9},{9,10},{10,1... | collective-permute-start | bytes 12296 | tf_op jit(solution)/shard_map/ppermute | solution.py:401
  157.0 27.1 %all-to-all-start.5 = ((f32[128,1,128]{2,1,0:T(1,128)}), f32[128,1,128]{2,1,0:T(1,128)S(1)}, u32[]{:S(2)}, u32[]{:S(2)}) async-start(f32[128,1,128]{2,1,0:T(1,128)} %bitcast.136), calls=%async_computation.5 | async-start | bytes 131072 | tf_op jit(solution)/shard_map/all_to_all | solution.py:390
  170.0 12.9 %collective-permute-start.16 = (f32[60,128]{1,0:T(8,128)S(1)}, f32[60,128]{1,0:T(8,128)S(1)}, u32[]{:S(2)}, u32[]{:S(2)}) collective-permute-start(f32[60,128]{1,0:T(8,128)S(1)} %get-tuple-element.136), channel_id=1, source_target_pairs={{0,16},{16,32},{32,48},{48,64},{64,80},{80,96},{96,112},{1,17},{17... | collective-permute-start | bytes 92168 | tf_op jit(solution)/shard_map/ppermute | solution.py:399
  173.6 10.0 %collective-permute-start.17 = (f32[60,128]{1,0:T(8,128)S(1)}, f32[60,128]{1,0:T(8,128)S(1)}, u32[]{:S(2)}, u32[]{:S(2)}) collective-permute-start(f32[60,128]{1,0:T(8,128)S(1)} %get-tuple-element.137), channel_id=1, source_target_pairs={{16,0},{32,16},{48,32},{64,48},{80,64},{96,80},{112,96},{17,1},{33... | collective-permute-start | bytes 92168 | tf_op jit(solution)/shard_map/ppermute | solution.py:400
  175.5 6.3 %collective-permute-start.19 = (f32[8,128]{1,0:T(8,128)S(1)}, f32[8,128]{1,0:T(8,128)S(1)}, u32[]{:S(2)}, u32[]{:S(2)}) collective-permute-start(f32[8,128]{1,0:T(8,128)S(1)} %get-tuple-element.138), channel_id=1, source_target_pairs={{1,0},{2,1},{3,2},{4,3},{5,4},{6,5},{7,6},{8,7},{9,8},{10,9},{11,1... | collective-permute-start | bytes 12296 | tf_op jit(solution)/shard_map/ppermute | solution.py:402
  176.8 5.6 %collective-permute-start.18 = (f32[8,128]{1,0:T(8,128)S(1)}, f32[8,128]{1,0:T(8,128)S(1)}, u32[]{:S(2)}, u32[]{:S(2)}) collective-permute-start(f32[8,128]{1,0:T(8,128)S(1)} %get-tuple-element.138), channel_id=1, source_target_pairs={{0,1},{1,2},{2,3},{3,4},{4,5},{5,6},{6,7},{7,8},{8,9},{9,10},{10,1... | collective-permute-start | bytes 12296 | tf_op jit(solution)/shard_map/ppermute | solution.py:401
  198.5 26.2 %all-to-all-start.6 = ((f32[128,1,128]{2,1,0:T(1,128)}), f32[128,1,128]{2,1,0:T(1,128)S(1)}, u32[]{:S(2)}, u32[]{:S(2)}) async-start(f32[128,1,128]{2,1,0:T(1,128)} %bitcast.133), calls=%async_computation.6 | async-start | bytes 131072 | tf_op jit(solution)/shard_map/all_to_all | solution.py:390
  212.4 12.3 %collective-permute-start.20 = (f32[60,128]{1,0:T(8,128)S(1)}, f32[60,128]{1,0:T(8,128)S(1)}, u32[]{:S(2)}, u32[]{:S(2)}) collective-permute-start(f32[60,128]{1,0:T(8,128)S(1)} %get-tuple-element.145), channel_id=1, source_target_pairs={{0,16},{16,32},{32,48},{48,64},{64,80},{80,96},{96,112},{1,17},{17... | collective-permute-start | bytes 92168 | tf_op jit(solution)/shard_map/ppermute | solution.py:399
  215.9 8.7 %collective-permute-start.21 = (f32[60,128]{1,0:T(8,128)S(1)}, f32[60,128]{1,0:T(8,128)S(1)}, u32[]{:S(2)}, u32[]{:S(2)}) collective-permute-start(f32[60,128]{1,0:T(8,128)S(1)} %get-tuple-element.146), channel_id=1, source_target_pairs={{16,0},{32,16},{48,32},{64,48},{80,64},{96,80},{112,96},{17,1},{33... | collective-permute-start | bytes 92168 | tf_op jit(solution)/shard_map/ppermute | solution.py:400
  217.9 5.6 %collective-permute-start.23 = (f32[8,128]{1,0:T(8,128)S(1)}, f32[8,128]{1,0:T(8,128)S(1)}, u32[]{:S(2)}, u32[]{:S(2)}) collective-permute-start(f32[8,128]{1,0:T(8,128)S(1)} %get-tuple-element.147), channel_id=1, source_target_pairs={{1,0},{2,1},{3,2},{4,3},{5,4},{6,5},{7,6},{8,7},{9,8},{10,9},{11,1... | collective-permute-start | bytes 12296 | tf_op jit(solution)/shard_map/ppermute | solution.py:402
  219.2 4.9 %collective-permute-start.22 = (f32[8,128]{1,0:T(8,128)S(1)}, f32[8,128]{1,0:T(8,128)S(1)}, u32[]{:S(2)}, u32[]{:S(2)}) collective-permute-start(f32[8,128]{1,0:T(8,128)S(1)} %get-tuple-element.147), channel_id=1, source_target_pairs={{0,1},{1,2},{2,3},{3,4},{4,5},{5,6},{6,7},{7,8},{8,9},{9,10},{10,1... | collective-permute-start | bytes 12296 | tf_op jit(solution)/shard_map/ppermute | solution.py:401
  230.0 27.1 %all-to-all-start.7 = ((f32[128,1,128]{2,1,0:T(1,128)}), f32[128,1,128]{2,1,0:T(1,128)S(1)}, u32[]{:S(2)}, u32[]{:S(2)}) async-start(f32[128,1,128]{2,1,0:T(1,128)} %bitcast.32), calls=%async_computation.7 | async-start | bytes 131072 | tf_op jit(solution)/shard_map/all_to_all | solution.py:390
  243.6 12.3 %collective-permute-start.24 = (f32[60,128]{1,0:T(8,128)S(1)}, f32[60,128]{1,0:T(8,128)S(1)}, u32[]{:S(2)}, u32[]{:S(2)}) collective-permute-start(f32[60,128]{1,0:T(8,128)S(1)} %get-tuple-element.154), channel_id=1, source_target_pairs={{0,16},{16,32},{32,48},{48,64},{64,80},{80,96},{96,112},{1,17},{17... | collective-permute-start | bytes 92168 | tf_op jit(solution)/shard_map/ppermute | solution.py:399
  247.2 9.3 %collective-permute-start.25 = (f32[60,128]{1,0:T(8,128)S(1)}, f32[60,128]{1,0:T(8,128)S(1)}, u32[]{:S(2)}, u32[]{:S(2)}) collective-permute-start(f32[60,128]{1,0:T(8,128)S(1)} %get-tuple-element.155), channel_id=1, source_target_pairs={{16,0},{32,16},{48,32},{64,48},{80,64},{96,80},{112,96},{17,1},{33... | collective-permute-start | bytes 92168 | tf_op jit(solution)/shard_map/ppermute | solution.py:400
  249.1 5.6 %collective-permute-start.27 = (f32[8,128]{1,0:T(8,128)S(1)}, f32[8,128]{1,0:T(8,128)S(1)}, u32[]{:S(2)}, u32[]{:S(2)}) collective-permute-start(f32[8,128]{1,0:T(8,128)S(1)} %get-tuple-element.156), channel_id=1, source_target_pairs={{1,0},{2,1},{3,2},{4,3},{5,4},{6,5},{7,6},{8,7},{9,8},{10,9},{11,1... | collective-permute-start | bytes 12296 | tf_op jit(solution)/shard_map/ppermute | solution.py:402
  250.4 4.9 %collective-permute-start.26 = (f32[8,128]{1,0:T(8,128)S(1)}, f32[8,128]{1,0:T(8,128)S(1)}, u32[]{:S(2)}, u32[]{:S(2)}) collective-permute-start(f32[8,128]{1,0:T(8,128)S(1)} %get-tuple-element.156), channel_id=1, source_target_pairs={{0,1},{1,2},{2,3},{3,4},{4,5},{5,6},{6,7},{7,8},{8,9},{9,10},{10,1... | collective-permute-start | bytes 12296 | tf_op jit(solution)/shard_map/ppermute | solution.py:401
  254.4 2.7 copy-start.30
  263.4 25.9 %all-to-all-start.8 = ((f32[128,1,128]{2,1,0:T(1,128)}), f32[128,1,128]{2,1,0:T(1,128)S(1)}, u32[]{:S(2)}, u32[]{:S(2)}) async-start(f32[128,1,128]{2,1,0:T(1,128)} %bitcast.137), calls=%async_computation.8 | async-start | bytes 131072 | tf_op jit(solution)/shard_map/all_to_all | solution.py:390
  277.0 12.3 %collective-permute-start.28 = (f32[60,128]{1,0:T(8,128)S(1)}, f32[60,128]{1,0:T(8,128)S(1)}, u32[]{:S(2)}, u32[]{:S(2)}) collective-permute-start(f32[60,128]{1,0:T(8,128)S(1)} %get-tuple-element.163), channel_id=1, source_target_pairs={{0,16},{16,32},{32,48},{48,64},{64,80},{80,96},{96,112},{1,17},{17... | collective-permute-start | bytes 92168 | tf_op jit(solution)/shard_map/ppermute | solution.py:399
  280.6 8.7 %collective-permute-start.29 = (f32[60,128]{1,0:T(8,128)S(1)}, f32[60,128]{1,0:T(8,128)S(1)}, u32[]{:S(2)}, u32[]{:S(2)}) collective-permute-start(f32[60,128]{1,0:T(8,128)S(1)} %get-tuple-element.164), channel_id=1, source_target_pairs={{16,0},{32,16},{48,32},{64,48},{80,64},{96,80},{112,96},{17,1},{33... | collective-permute-start | bytes 92168 | tf_op jit(solution)/shard_map/ppermute | solution.py:400
  282.5 5.6 %collective-permute-start.31 = (f32[8,128]{1,0:T(8,128)S(1)}, f32[8,128]{1,0:T(8,128)S(1)}, u32[]{:S(2)}, u32[]{:S(2)}) collective-permute-start(f32[8,128]{1,0:T(8,128)S(1)} %get-tuple-element.165), channel_id=1, source_target_pairs={{1,0},{2,1},{3,2},{4,3},{5,4},{6,5},{7,6},{8,7},{9,8},{10,9},{11,1... | collective-permute-start | bytes 12296 | tf_op jit(solution)/shard_map/ppermute | solution.py:402
  283.8 4.9 %collective-permute-start.30 = (f32[8,128]{1,0:T(8,128)S(1)}, f32[8,128]{1,0:T(8,128)S(1)}, u32[]{:S(2)}, u32[]{:S(2)}) collective-permute-start(f32[8,128]{1,0:T(8,128)S(1)} %get-tuple-element.165), channel_id=1, source_target_pairs={{0,1},{1,2},{2,3},{3,4},{4,5},{5,6},{6,7},{7,8},{8,9},{9,10},{10,1... | collective-permute-start | bytes 12296 | tf_op jit(solution)/shard_map/ppermute | solution.py:401
  (119 other events, 82.9 us)

commit v2 on v1

v2 whole, which is shorter than its diff:
```python
import functools

import jax
import jax.numpy as jnp
from jax import lax
from jax.experimental import pallas as pl
from jax.experimental.pallas import tpu as pltpu
from jax.sharding import PartitionSpec as P

F32 = jnp.float32
BF16 = jnp.bfloat16
AXES = ("gx", "gy")
NZ, CX, CY = 20, 8, 128
ROWS = NZ * CX
STEP = 16
CHUNKS = ROWS // STEP
PEERS = 128
CAP = 8


def lanes(shape):
    return lax.broadcasted_iota(jnp.int32, shape, 1)


def subs(shape):
    return lax.broadcasted_iota(jnp.int32, shape, 0)


def split3(x):
    high = x.astype(BF16)
    rest = x - high.astype(F32)
    mid = rest.astype(BF16)
    low = (rest - mid.astype(F32)).astype(BF16)
    return high, mid, low


def pick_rows(onehot, x):
    high, mid, low = split3(x)

    def dot(part):
        return lax.dot_general(onehot, part, (((1,), (0,)), ((), ())), preferred_element_type=F32)

    return (dot(low) + dot(mid)) + dot(high)


def is_slot(lane):
    return (lane & 63) >= 60


def slot_values(rows_of, start, first):
    lane = lanes((PEERS, CY))
    number = (lane & 3) + jnp.where(lane >= 64, 4, 0)
    picked = pick_rows(rows_of, first)
    window = jnp.take_along_axis(picked, (start + number) & (CY - 1), axis=1)
    return jnp.where(is_slot(lane), window, 0.0)


def into_cells(rows_to, start, flows):
    number = (lanes((PEERS, CY)) - start) & (CY - 1)
    place = jnp.where(number < 4, number + 60, jnp.where(number < CAP, number + 120, 0))
    return pick_rows(rows_to, jnp.take_along_axis(flows, place, axis=1))


def segment_values(state, index):
    low = index & 127
    first = jnp.take_along_axis(jnp.broadcast_to(state[0:1], (8, 128)), low, axis=1)
    second = jnp.take_along_axis(jnp.broadcast_to(state[1:2], (8, 128)), low, axis=1)
    return jnp.where(index >= 128, second, first)


def into_segments(values, index, table):
    parts = [part.astype(F32) for part in split3(values)]
    sub = subs((16, 128))
    upper = (index >= 128).astype(jnp.int32)
    tiles = []
    for k in range(CAP):
        row = [jnp.broadcast_to(part[k : k + 1], (16, 128)) for part in parts]
        mine = jnp.broadcast_to(upper[k : k + 1], (16, 128)) == (sub & 1)
        tile = jnp.where(sub < 2, row[0], jnp.where(sub < 4, row[1], row[2]))
        tiles.append(jnp.where(mine & (sub < 6), tile, 0.0).astype(BF16))
    left = jnp.concatenate(tiles, axis=1)
    out = lax.dot_general(left, table, (((1,), (1,)), ((), ())), preferred_element_type=F32)[:8]
    total = (pltpu.roll(out, 4, 0) + pltpu.roll(out, 6, 0)) + out
    return jnp.where(subs((8, 128)) < 2, total, 0.0)


def previous(state):
    moved = pltpu.roll(state, 1, 1)
    return jnp.where(lanes((8, 128)) == 0, pltpu.roll(moved, 1, 0), moved)


def following(state):
    moved = pltpu.roll(state, 127, 1)
    return jnp.where(lanes((8, 128)) == 127, pltpu.roll(moved, 7, 0), moved)


def to_columns(values):
    gap = jnp.zeros((60, 128), F32)
    return jnp.concatenate([gap, values[0:4], gap, values[4:8]], axis=0).T


def to_rows(columns):
    turned = columns.T
    return jnp.concatenate([turned[60:64], turned[124:128]], axis=0)


def block(n):
    return pl.ds(n, PEERS, stride=4)


def chunk(t):
    return pl.ds(t * STEP, STEP)


def me():
    return lax.axis_index("gx") * 16 + lax.axis_index("gy")


def peer_rows(shift):
    return pl.ds(4 * ((me() + shift) & (PEERS - 1)), 4)


def tile_to_rows(tile, pad):
    pad[0:8] = tile
    pad[8:16] = pltpu.roll(tile, 64, 1)
    even = pad[pl.ds(0, 4, stride=2), :]
    odd = pad[pl.ds(9, 4, stride=2), :]
    return jnp.where(lanes((4, 128)) < 64, even, odd)


def rows_to_tile(four, pad):
    pad[0:4] = four
    pad[8:16] = pltpu.roll(pad[0:8], 64, 1)
    low, high = pad[0:4], pad[8:12]
    pad[pl.ds(0, 4, stride=2), :] = low
    pad[pl.ds(1, 4, stride=2), :] = high
    return pad[0:8]


def mix(matrix, rows, vector):
    entry = [matrix[n, rows, :].astype(F32) for n in range(9)]
    x, y, z = vector
    return [entry[3 * n] * x + entry[3 * n + 1] * y + entry[3 * n + 2] * z for n in range(3)]


def borders(values, mobility, trans, weighted, along, t):
    rows = chunk(t)
    tx = trans[0, rows, :].astype(F32)
    for n, value in enumerate(mix(mobility, rows, values)):
        weighted[n, pl.ds(8 + t * STEP, STEP), :] = value
        along[pl.ds(n * ROWS + t * STEP, STEP), :] = tx * value


def interior(trans, weighted, along, near, toward_low, toward_high, message, pad):
    toward_low[...] = along[pl.ds(0, 3 * NZ, stride=CX), :]
    toward_high[...] = along[pl.ds(CX - 1, 3 * NZ, stride=CX), :]
    lane = lanes((STEP, 128))
    sub = subs((STEP, 128)) & 7
    small = lanes((8, 128))
    high = jnp.zeros((8, 128), F32)
    low = jnp.zeros((8, 128), F32)
    for n in range(3):
        weighted[n, 0:8, :] = jnp.zeros((8, 128), F32)
        weighted[n, ROWS + 8 : ROWS + 16, :] = jnp.zeros((8, 128), F32)
    up = [trans[2, chunk(t), :].astype(F32) for t in range(CHUNKS)]
    for t in range(CHUNKS):
        rows = chunk(t)
        tx, ty = [trans[n, rows, :].astype(F32) for n in range(2)]
        tz = up[t]
        zero = jnp.zeros((8, 128), F32)
        below = jnp.concatenate([up[t - 1][8:16] if t else zero, tz[0:8]], axis=0)
        above = jnp.concatenate([tz[8:16], up[t + 1][0:8] if t + 1 < CHUNKS else zero], axis=0)
        for n in range(3):
            px = along[pl.ds(n * ROWS + t * STEP, STEP), :]
            py = ty * weighted[n, pl.ds(8 + t * STEP, STEP), :]
            nx = jnp.where(sub == 0, 0.0, pltpu.roll(px, 1, 0)) + jnp.where(
                sub == 7, 0.0, pltpu.roll(px, STEP - 1, 0)
            )
            ny = jnp.where(lane == 0, 0.0, pltpu.roll(py, 1, 1)) + jnp.where(
                lane == 127, 0.0, pltpu.roll(py, 127, 1)
            )
            nz = below * weighted[n, pl.ds(t * STEP, STEP), :] + above * weighted[
                n, pl.ds(t * STEP + 16, STEP), :
            ]
            near[n, rows, :] = tx * nx + ty * ny + tz * nz
            for half in range(2):
                j = n * NZ + 2 * t + half
                moved = pltpu.roll(py[8 * half : 8 * half + 8], j + 1, 1)
                high = jnp.where(small == j, moved, high)
                low = jnp.where(small == j + 1, moved, low)
    low = pltpu.roll(low, 127, 1)
    mine = is_slot(lanes((4, 128)))
    for shift, tile in ((1, high), (-1, low)):
        rows = peer_rows(shift)
        packed = tile_to_rows(tile, pad)
        message[rows, :] = jnp.where(mine, message[rows, :], packed)


def cell_setup(rhs, diag, mobility, trans, cells, pi,
               inverse, first, rows_of, rows_to, start, weight, slots,
               near, toward_low, toward_high, message, weighted, along, pad):
    for t in range(CHUNKS):
        rows = chunk(t)
        a, b, c, d, e, f, g, h, i = [diag[n, rows, :].astype(F32) for n in range(9)]
        p, q, s = e * i - f * h, f * g - d * i, d * h - e * g
        scale = 1.0 / (a * p + b * q + c * s)
        entries = [
            p, c * h - b * i, b * f - c * e,
            q, a * i - c * g, c * d - a * f,
            s, b * g - a * h, a * e - b * d,
        ]
        entries = [entry * scale for entry in entries]
        x, y, z = [rhs[n, rows, :] for n in range(3)]
        for n in range(9):
            inverse[n, rows, :] = entries[n]
        values = [
            entries[3 * n] * x + entries[3 * n + 1] * y + entries[3 * n + 2] * z for n in range(3)
        ]
        for n in range(3):
            first[n, rows, :] = values[n]
        borders(values, mobility, trans, weighted, along, t)
    base = cells[0:1, :]
    row = lax.shift_right_logical(base, 7)
    live = pi[...]
    gap = jnp.zeros((44, 128), F32)
    info = jnp.concatenate(
        [jnp.broadcast_to(row.astype(F32), (8, 128)),
         jnp.broadcast_to((base & 127).astype(F32), (8, 128)),
         gap, live[0:4], gap, jnp.zeros((16, 128), F32), live[4:8]],
        axis=0,
    ).T
    rows_to[...] = (subs((ROWS, PEERS)) == jnp.broadcast_to(row, (ROWS, PEERS))).astype(F32).astype(BF16)
    row_column = jnp.broadcast_to(info[:, 0:1], (PEERS, ROWS)).astype(jnp.int32)
    rows_of[...] = (lanes((PEERS, ROWS)) == row_column).astype(F32).astype(BF16)
    begin = jnp.broadcast_to(info[:, 8:9], (PEERS, 128)).astype(jnp.int32)
    start[...] = begin
    weights = jnp.where(is_slot(lanes((PEERS, 128))), info, 0.0)
    weight[...] = weights
    values = slot_values(rows_of[...], begin, first[0])
    slots[...] = values
    message[block(0), :] = values
    message[block(1), :] = weights
    message[block(2), :] = jnp.zeros((PEERS, 128), F32)
    message[block(3), :] = jnp.zeros((PEERS, 128), F32)
    interior(trans, weighted, along, near, toward_low, toward_high, message, pad)


def well_setup(arrived, index, parent, trans, rhs, message, weight, table, state, at_slots, fixed):
    pi = to_rows(arrived[block(1), :])
    weight[...] = pi
    number = index[...]
    low = number & 127
    for k in range(CAP):
        hit = subs((128, 128)) == jnp.broadcast_to(low[k : k + 1], (128, 128))
        table[:, 128 * k : 128 * (k + 1)] = hit.astype(F32).astype(BF16)
    zeros = jnp.zeros((6, 128), F32)
    linked = jnp.concatenate([(parent[...] >= 0).astype(F32), zeros], axis=0)
    across = jnp.concatenate([trans[...], zeros], axis=0)
    source = jnp.concatenate([rhs[...], zeros], axis=0)
    diagonal = across + following(linked * across) + into_segments(pi, number, table[...])
    diagonal = jnp.where(subs((8, 128)) < 2, diagonal, 1.0)
    fixed[0] = linked
    fixed[1] = across
    fixed[2] = source
    fixed[3] = diagonal
    now = source / diagonal
    state[...] = now
    values = segment_values(now, number)
    at_slots[...] = values
    message[...] = to_columns(values)


def ratio(sums, place):
    total = jnp.sum(sums, axis=0, keepdims=True)
    lane = lanes((1, 128))
    numer = jnp.sum(jnp.where(lane == place, total, 0.0), axis=1, keepdims=True)
    denom = jnp.sum(jnp.where(lane == place + 1, total, 0.0), axis=1, keepdims=True)
    return numer / denom


def spread_pair(two):
    return jnp.concatenate(
        [jnp.broadcast_to(two[h : h + 1], (8, 128)) for h in range(2)], axis=0
    )


STEADY = ("first", "inverse", "mobility", "trans", "rows_of", "rows_to", "start", "weight",
          "own_weight", "table", "index", "fixed")
MOVING = ("arrived", "near", "from_low", "from_high", "slots", "at_slots", "state")
NEXT = ("near", "toward_low", "toward_high", "message", "slots", "at_slots", "state")
MORE_IN = {
    "first": ("pressures",), "plain": (), "keep": (), "last": ("diag", "rhs", "field"), "after": (),
    "final": ("diag", "rhs", "field", "change", "seg_change", "omega"),
}
MORE_OUT = {
    "first": (), "plain": (), "keep": ("field",), "last": ("change", "seg_change"),
    "after": ("omega",), "final": (),
}


def results_of(kind):
    return ("message",) if kind == "final" else NEXT + MORE_OUT[kind]


def sweep(kind, *refs):
    take = iter(refs)
    now = {name: next(take) for name in MOVING}
    fixed = {name: next(take) for name in STEADY}
    extra = {name: next(take) for name in MORE_IN[kind]}
    out = {name: next(take) for name in results_of(kind)}
    weighted, along, pad, forward = take
    final = kind == "final"
    gx, gy = lax.axis_index("gx"), lax.axis_index("gy")

    arrived = now["arrived"]
    pressures = extra["pressures"][...] if kind == "first" else arrived[block(1), :]
    pull = fixed["weight"][...] * (now["slots"][...] - pressures)
    perforated = into_cells(fixed["rows_to"][...], fixed["start"][...], pull)

    side_low = rows_to_tile(arrived[peer_rows(-1), :], pad)
    side_high = rows_to_tile(arrived[peer_rows(1), :], pad)
    side_low = jnp.where(gy == 0, 0.0, side_low)
    side_high = jnp.where(gy == lax.axis_size("gy") - 1, 0.0, side_high)
    open_low, open_high = gx > 0, gx < lax.axis_size("gx") - 1

    state = now["state"][...]
    linked, across, source, diagonal = [fixed["fixed"][n] for n in range(4)]
    push = fixed["own_weight"][...] * (to_rows(arrived[block(0), :]) - now["at_slots"][...])
    number = fixed["index"][...]
    inflow = into_segments(push, number, fixed["table"][...])
    flux = across * (state - linked * previous(state))
    seg_res = source - flux + following(linked * flux) + inflow

    lane = lanes((STEP, 128))
    sub = subs((STEP, 128)) & 7
    numer = jnp.zeros((STEP, 128), F32)
    denom = jnp.zeros((STEP, 128), F32)
    if final:
        omega = extra["omega"][0:1, 0:1]
    for t in range(CHUNKS):
        rows = chunk(t)
        tx, ty = [fixed["trans"][n, rows, :].astype(F32) for n in range(2)]
        terms = []
        for n in range(3):
            j = n * NZ + 2 * t
            low = jnp.where(open_low, now["from_low"][j : j + 2, :], 0.0)
            high = jnp.where(open_high, now["from_high"][j : j + 2, :], 0.0)
            nx = jnp.where(sub == 0, spread_pair(low), jnp.where(sub == 7, spread_pair(high), 0.0))
            before = [pltpu.roll(side_low, (128 - j - h) % 128, 1) for h in range(2)]
            behind = [pltpu.roll(side_high, 127 - j - h, 1) for h in range(2)]
            ny = jnp.where(
                lane == 0, jnp.concatenate(before, axis=0),
                jnp.where(lane == 127, jnp.concatenate(behind, axis=0), 0.0),
            )
            share = fixed["mobility"][3 * n, rows, :].astype(F32)
            value = now["near"][n, rows, :] + tx * nx + ty * ny
            terms.append(value - share * perforated[t * STEP : (t + 1) * STEP])
        if kind in ("last", "final"):
            own = mix(extra["diag"], rows, [extra["field"][n, rows, :] for n in range(3)])
            for n in range(3):
                change = own[n] - terms[n]
                before = extra["rhs"][n, rows, :]
                if final:
                    kept = extra["change"][n, rows, :]
                    before = before - omega * kept
                    change = kept + omega * (change - 2.0 * kept)
                else:
                    out["change"][n, rows, :] = change
                numer += before * change
                denom += change * change
        if not final:
            moves = mix(fixed["inverse"], rows, terms)
            values = [fixed["first"][n, rows, :] + moves[n] for n in range(3)]
            forward[rows, :] = values[0]
            if kind == "keep":
                for n in range(3):
                    out["field"][n, rows, :] = values[n]
            borders(values, fixed["mobility"], fixed["trans"], weighted, along, t)

    if kind in ("last", "final"):
        before = source
        change = source - seg_res
        if final:
            kept = extra["seg_change"][...]
            before = source - omega * kept
            change = kept + omega * (change - 2.0 * kept)
        else:
            out["seg_change"][...] = change
        above = jnp.sum(numer, keepdims=True) + jnp.sum(before * change, keepdims=True)
        below = jnp.sum(denom, keepdims=True) + jnp.sum(change * change, keepdims=True)
        place = lanes((PEERS, 128))
        sums = jnp.where(place == 60, above, jnp.where(place == 61, below, 0.0))
        if final:
            out["message"][...] = sums
            return
    else:
        sums = jnp.zeros((PEERS, 128), F32)
    message = out["message"]
    advanced = state + seg_res / diagonal
    out["state"][...] = advanced
    values = segment_values(advanced, number)
    out["at_slots"][...] = values
    cells = slot_values(fixed["rows_of"][...], fixed["start"][...], forward[...])
    out["slots"][...] = cells
    message[block(0), :] = cells
    message[block(1), :] = to_columns(values)
    message[block(2), :] = sums
    message[block(3), :] = jnp.zeros((PEERS, 128), F32)
    if kind == "after":
        out["omega"][...] = jnp.broadcast_to(ratio(arrived[block(2), :], 60), (8, 128))
    interior(
        fixed["trans"], weighted, along, out["near"], out["toward_low"], out["toward_high"],
        message, pad,
    )


def finish(arrived, omega, field_one, field_two, state_one, state_two, cells, segments):
    first = omega[0:1, 0:1]
    second = ratio(arrived[...], 60)

    def blend(one, two):
        kept = first * one
        return kept + second * (one + first * (two - one) - kept)

    for n in range(3):
        for t in range(CHUNKS):
            rows = chunk(t)
            cells[n, rows, :] = blend(field_one[n, rows, :], field_two[n, rows, :])
    segments[...] = blend(state_one[0:2], state_two[0:2])


CELLS = ((3, ROWS, 128), F32)
PAIRS = ((PEERS, 128), F32)
MESSAGE = ((4 * PEERS, 128), F32)
TILE = ((8, 128), F32)
EDGE = ((3 * NZ, 128), F32)
SHAPES = {
    "near": CELLS, "toward_low": EDGE, "toward_high": EDGE, "message": MESSAGE, "slots": PAIRS,
    "at_slots": TILE, "state": TILE, "omega": TILE, "field": CELLS, "change": CELLS,
    "seg_change": TILE,
}
SCRATCH = (
    pltpu.VMEM((3, ROWS + 16, 128), F32),
    pltpu.VMEM((3 * ROWS, 128), F32),
    pltpu.VMEM((16, 128), F32),
)


def call(body, outs, args, scratch=(), name=None):
    moved = sum(a.size * a.dtype.itemsize for a in args)
    return pl.pallas_call(
        body,
        out_shape=[jax.ShapeDtypeStruct(*out) for out in outs],
        in_specs=[pl.BlockSpec(memory_space=pltpu.VMEM)] * len(args),
        out_specs=[pl.BlockSpec(memory_space=pltpu.VMEM)] * len(outs),
        scratch_shapes=list(scratch),
        compiler_params=pltpu.CompilerParams(vmem_limit_bytes=24 * 1024 * 1024),
        cost_estimate=pl.CostEstimate(flops=4_000_000, bytes_accessed=moved, transcendentals=0),
        name=name,
    )(*args)


def exchange(message):
    return lax.all_to_all(message, AXES, split_axis=0, concat_axis=0, tiled=True)


def neighbours(toward_low, toward_high):
    count = lax.axis_size("gx")
    up = [(i, (i + 1) % count) for i in range(count)]
    down = [(b, a) for a, b in up]
    return {
        "from_low": lax.ppermute(toward_high, "gx", up),
        "from_high": lax.ppermute(toward_low, "gx", down),
    }


def on_device(
    rhs, diag_block, mobility, trans, perf_cell, perf_pi, perf_seg, seg_parent, seg_trans, seg_rhs
):
    rhs = rhs.reshape(3, ROWS, 128)
    diag = diag_block.reshape(9, ROWS, 128)
    mobility = mobility.reshape(9, ROWS, 128)
    trans = trans.reshape(3, ROWS, 128)
    index = perf_seg[0]

    fixed = {"mobility": mobility, "trans": trans, "index": index}
    (inverse, first, rows_of, rows_to, start, weight, slots, near, toward_low, toward_high,
     message) = call(
        cell_setup,
        [((9, ROWS, 128), F32), CELLS, ((PEERS, ROWS), BF16), ((ROWS, PEERS), BF16),
         ((PEERS, 128), jnp.int32), PAIRS, PAIRS, CELLS, EDGE, EDGE, MESSAGE],
        [rhs, diag, mobility, trans, perf_cell[0], perf_pi[0]],
        SCRATCH,
        name="cell_setup",
    )
    fixed.update(
        first=first, inverse=inverse, rows_of=rows_of, rows_to=rows_to, start=start, weight=weight
    )
    arrived = exchange(message)
    now = {"arrived": arrived, "near": near, "slots": slots}
    now.update(neighbours(toward_low, toward_high))
    message, own_weight, table, state, at_slots, constants = call(
        well_setup,
        [PAIRS, TILE, ((128, CAP * 128), BF16), TILE, TILE, ((4, 8, 128), F32)],
        [arrived, index, seg_parent.reshape(2, 128), seg_trans.reshape(2, 128),
         seg_rhs.reshape(2, 128)],
        name="well_setup",
    )
    fixed.update(own_weight=own_weight, table=table, fixed=constants)
    now.update(at_slots=at_slots, state=state)
    saved = {"pressures": exchange(message), "diag": diag, "rhs": rhs}

    def advance(kind, now):
        args = [now[name] for name in MOVING]
        args += [fixed[name] for name in STEADY]
        args += [saved[name] for name in MORE_IN[kind]]
        names = results_of(kind)
        out = call(
            functools.partial(sweep, kind),
            [PAIRS if kind == "final" else SHAPES[name] for name in names],
            args,
            SCRATCH + (pltpu.VMEM((ROWS, 128), F32),),
            name="sweep_" + kind,
        )
        out = dict(zip(names, out))
        out["arrived"] = exchange(out.pop("message"))
        if kind != "final":
            out.update(neighbours(out.pop("toward_low"), out.pop("toward_high")))
        return out

    now = advance("first", now)
    now = advance("plain", now)
    one = advance("keep", now)
    saved["field"] = one["field"]
    now = advance("last", one)
    saved.update(change=now["change"], seg_change=now["seg_change"])
    now = advance("after", now)
    saved["omega"] = now["omega"]
    now = advance("plain", now)
    two = advance("keep", now)
    saved["field"] = two["field"]
    sums = advance("final", two)
    cells, segments = call(
        finish,
        [CELLS, ((2, 128), F32)],
        [sums["arrived"], saved["omega"], one["field"], two["field"], one["state"], two["state"]],
        name="finish",
    )
    return cells.reshape(3, NZ, CX, CY), segments.reshape(256)


def solution(mesh):
    grid = P(None, None, "gx", "gy")
    pairs = P(AXES, None, None)
    flat = P(AXES)
    return jax.shard_map(
        on_device,
        mesh=mesh,
        in_specs=(grid, grid, grid, grid, pairs, pairs, pairs, flat, flat, flat),
        out_specs=(grid, flat),
        check_vma=False,
    )
```

time: 319 us -> 199 us (0.62)
  starting transfers between devices: 182 us -> 46 us
  waiting for transfers between devices: 0.51 us -> 74.8 us
  local copies, waits for them, and re-layouts: 73.7 us -> 25.5 us
  blocking collectives: 44.2 us -> 36.4 us
    ppermute x32 -> x16, starting transfers between devices: 86.1 us -> 13.5 us  [the longest x8 13.5 us: neighbours(): lax.ppermute(toward_high, 'gx', up)]
    all_to_all x8, starting transfers between devices: 96 us -> 32.5 us  [exchange(): lax.all_to_all(message, AXES, split_axis=0, concat_axis=0, tiled=True)]
    unnamed x254 -> x98, local copies, waits for them, and re-layouts: 73.7 us -> 25.5 us
    all_to_all x8, waiting for transfers between devices: 0.02 us -> 40.4 us  [exchange(): lax.all_to_all(message, AXES, split_axis=0, concat_axis=0, tiled=True)]
    ppermute x32 -> x16, waiting for transfers between devices: 0.49 us -> 34.4 us  [the longest x8 23.3 us: neighbours(): lax.ppermute(toward_low, 'gx', down)]
    all_to_all x2, blocking collectives: 44.2 us -> 36.4 us  [exchange(): lax.all_to_all(message, AXES, split_axis=0, concat_axis=0, tiled=True)]
    pallas_call x27 -> x11, Pallas kernels: 14 us -> 14.7 us  [call(): pl.pallas_call(body, out_shape=[jax.ShapeDtypeStruct(*out) for out in out...]
  transfers between devices with their start and end apart: 40 -> 24, of which waited for: 1 -> 24; matrix products, arithmetic and copies ran while one was open for 0% -> 0% of each run, Pallas kernels for 1% -> 0%
where the time goes in v2:
time: 199 us; the launch traced here: 198 us
  waiting for transfers between devices  74.8 us (38%)
  starting transfers between devices  46 us (23%)
  blocking collectives  36.4 us (18%)
  local copies, waits for them, and re-layouts  25.5 us (13%)
  Pallas kernels  14.7 us (7%)
    all_to_all x8, waiting for transfers between devices, exchange(): lax.all_to_all(message, AXES, split_axis=0, concat_axis=0, tiled=True)  40.4 us
    all_to_all x2, blocking collectives, exchange(): lax.all_to_all(message, AXES, split_axis=0, concat_axis=0, tiled=True)  36.4 us
    all_to_all x8, starting transfers between devices, exchange(): lax.all_to_all(message, AXES, split_axis=0, concat_axis=0, tiled=True)  32.5 us
    unnamed x98, local copies, waits for them, and re-layouts  25.5 us
    ppermute x8, waiting for transfers between devices, neighbours(): lax.ppermute(toward_low, 'gx', down)  23.3 us
    pallas_call x11, Pallas kernels, call(): pl.pallas_call(body, out_shape=[jax.ShapeDtypeStruct(*out) for out in out...  14.7 us
    ppermute x8, starting transfers between devices, neighbours(): lax.ppermute(toward_high, 'gx', up)  13.5 us
    ppermute x8, waiting for transfers between devices, neighbours(): lax.ppermute(toward_high, 'gx', up)  11.1 us
  transfers between devices with their start and end apart: 24, of which 24 were waited for; matrix products, arithmetic and copies ran while one was open for 0% of the time, Pallas kernels for 0%

profile of v2, /device:TPU:1, one launch (start us, length us, event | category | flops | bytes accessed | tf_op | source)
XLA Modules:
  0.0 198.1 jit_solution(6301980600533446666)
XLA Ops:
  6.0 22.8 %all_to_all.110 = f32[128,4,128]{2,1,0:T(4,128)S(1)} all-to-all(f32[128,4,128]{2,1,0:T(4,128)S(1)} %bitcast.81), channel_id=1, replica_groups=mesh['gx'=8,'gy'=16] {'gx','gy'}, dimensions={0} | all-to-all | bytes 524288 | tf_op jit(solution)/shard_map/all_to_all | solution.py:464
  29.4 1.1 well_setup.1
  30.5 4.0 %all-to-all-start.1 = ((f32[128,1,128]{2,1,0:T(1,128)}), f32[128,1,128]{2,1,0:T(1,128)S(1)}, u32[]{:S(2)}, u32[]{:S(2)}) async-start(f32[128,1,128]{2,1,0:T(1,128)} %bitcast.13), calls=%async_computation.1 | async-start | bytes 131072 | tf_op jit(solution)/shard_map/all_to_all | solution.py:464
  34.5 1.7 collective-permute-start
  37.2 2.7 %collective-permute-done.1.refs_3_ = f32[60,128]{1,0:T(8,128)S(1)} collective-permute-done((f32[60,128]{1,0:T(8,128)S(1)}, f32[60,128]{1,0:T(8,128)S(1)}, u32[]{:S(2)}, u32[]{:S(2)}) %collective-permute-start.1) | collective-permute-done | bytes 30752 | tf_op jit(solution)/shard_map/ppermute | solution.py:473
  39.9 4.4 %all-to-all-done.1 = f32[128,1,128]{2,1,0:T(1,128)S(1)} async-done(((f32[128,1,128]{2,1,0:T(1,128)}), f32[128,1,128]{2,1,0:T(1,128)S(1)}, u32[]{:S(2)}, u32[]{:S(2)}) %all-to-all-start.1) | async-done | bytes 65568 | tf_op jit(solution)/shard_map/all_to_all | solution.py:464
  44.4 1.7 sweep_first.1
  46.1 4.5 %all-to-all-start.2 = ((f32[128,4,128]{2,1,0:T(4,128)}), f32[128,4,128]{2,1,0:T(4,128)S(1)}, u32[]{:S(2)}, u32[]{:S(2)}) async-start(f32[128,4,128]{2,1,0:T(4,128)} %bitcast.15), calls=%async_computation.2 | async-start | bytes 524288 | tf_op jit(solution)/shard_map/all_to_all | solution.py:464
  50.6 1.6 collective-permute-start.2
  52.2 1.3 collective-permute-done.2.refs_2_
  53.5 3.1 %collective-permute-done.3.refs_3_ = f32[60,128]{1,0:T(8,128)S(1)} collective-permute-done((f32[60,128]{1,0:T(8,128)S(1)}, f32[60,128]{1,0:T(8,128)S(1)}, u32[]{:S(2)}, u32[]{:S(2)}) %collective-permute-start.3) | collective-permute-done | bytes 30752 | tf_op jit(solution)/shard_map/ppermute | solution.py:473
  56.6 5.4 %all-to-all-done.2 = f32[128,4,128]{2,1,0:T(4,128)S(1)} async-done(((f32[128,4,128]{2,1,0:T(4,128)}), f32[128,4,128]{2,1,0:T(4,128)S(1)}, u32[]{:S(2)}, u32[]{:S(2)}) %all-to-all-start.2) | async-done | bytes 262176 | tf_op jit(solution)/shard_map/all_to_all | solution.py:464
  62.1 1.7 sweep_plain.2
  63.8 4.0 %all-to-all-start.3 = ((f32[128,4,128]{2,1,0:T(4,128)}), f32[128,4,128]{2,1,0:T(4,128)S(1)}, u32[]{:S(2)}, u32[]{:S(2)}) async-start(f32[128,4,128]{2,1,0:T(4,128)} %bitcast.17), calls=%async_computation.3 | async-start | bytes 524288 | tf_op jit(solution)/shard_map/all_to_all | solution.py:464
  67.8 1.6 collective-permute-start.4
  69.4 1.3 collective-permute-done.4.refs_2_
  70.7 3.1 %collective-permute-done.5.refs_3_ = f32[60,128]{1,0:T(8,128)S(1)} collective-permute-done((f32[60,128]{1,0:T(8,128)S(1)}, f32[60,128]{1,0:T(8,128)S(1)}, u32[]{:S(2)}, u32[]{:S(2)}) %collective-permute-start.5) | collective-permute-done | bytes 30752 | tf_op jit(solution)/shard_map/ppermute | solution.py:473
  73.8 5.4 %all-to-all-done.3 = f32[128,4,128]{2,1,0:T(4,128)S(1)} async-done(((f32[128,4,128]{2,1,0:T(4,128)}), f32[128,4,128]{2,1,0:T(4,128)S(1)}, u32[]{:S(2)}, u32[]{:S(2)}) %all-to-all-start.3) | async-done | bytes 262176 | tf_op jit(solution)/shard_map/all_to_all | solution.py:464
  79.3 1.7 sweep_keep.2
  82.3 4.0 %all-to-all-start.4 = ((f32[128,4,128]{2,1,0:T(4,128)}), f32[128,4,128]{2,1,0:T(4,128)S(1)}, u32[]{:S(2)}, u32[]{:S(2)}) async-start(f32[128,4,128]{2,1,0:T(4,128)} %bitcast.19), calls=%async_computation.4 | async-start | bytes 524288 | tf_op jit(solution)/shard_map/all_to_all | solution.py:464
  86.3 1.6 collective-permute-start.6
  88.0 1.5 collective-permute-done.6.refs_2_
  89.5 2.9 %collective-permute-done.7.refs_3_ = f32[60,128]{1,0:T(8,128)S(1)} collective-permute-done((f32[60,128]{1,0:T(8,128)S(1)}, f32[60,128]{1,0:T(8,128)S(1)}, u32[]{:S(2)}, u32[]{:S(2)}) %collective-permute-start.7) | collective-permute-done | bytes 30752 | tf_op jit(solution)/shard_map/ppermute | solution.py:473
  93.0 4.8 %all-to-all-done.4 = f32[128,4,128]{2,1,0:T(4,128)S(1)} async-done(((f32[128,4,128]{2,1,0:T(4,128)}), f32[128,4,128]{2,1,0:T(4,128)S(1)}, u32[]{:S(2)}, u32[]{:S(2)}) %all-to-all-start.4) | async-done | bytes 262176 | tf_op jit(solution)/shard_map/all_to_all | solution.py:464
  99.5 2.0 sweep_last.1
  103.4 4.0 %all-to-all-start.5 = ((f32[128,4,128]{2,1,0:T(4,128)}), f32[128,4,128]{2,1,0:T(4,128)S(1)}, u32[]{:S(2)}, u32[]{:S(2)}) async-start(f32[128,4,128]{2,1,0:T(4,128)} %bitcast.21), calls=%async_computation.5 | async-start | bytes 524288 | tf_op jit(solution)/shard_map/all_to_all | solution.py:464
  107.4 1.7 collective-permute-start.8
  109.1 1.5 collective-permute-done.8.refs_2_
  110.6 2.8 %collective-permute-done.9.refs_3_ = f32[60,128]{1,0:T(8,128)S(1)} collective-permute-done((f32[60,128]{1,0:T(8,128)S(1)}, f32[60,128]{1,0:T(8,128)S(1)}, u32[]{:S(2)}, u32[]{:S(2)}) %collective-permute-start.9) | collective-permute-done | bytes 30752 | tf_op jit(solution)/shard_map/ppermute | solution.py:473
  114.1 4.9 %all-to-all-done.5 = f32[128,4,128]{2,1,0:T(4,128)S(1)} async-done(((f32[128,4,128]{2,1,0:T(4,128)}), f32[128,4,128]{2,1,0:T(4,128)S(1)}, u32[]{:S(2)}, u32[]{:S(2)}) %all-to-all-start.5) | async-done | bytes 262176 | tf_op jit(solution)/shard_map/all_to_all | solution.py:464
  119.7 1.7 sweep_after.1
  122.7 4.0 %all-to-all-start.6 = ((f32[128,4,128]{2,1,0:T(4,128)}), f32[128,4,128]{2,1,0:T(4,128)S(1)}, u32[]{:S(2)}, u32[]{:S(2)}) async-start(f32[128,4,128]{2,1,0:T(4,128)} %bitcast.23), calls=%async_computation.6 | async-start | bytes 524288 | tf_op jit(solution)/shard_map/all_to_all | solution.py:464
  126.7 1.7 collective-permute-start.10
  128.5 1.5 collective-permute-done.10.refs_2_
  130.0 2.8 %collective-permute-done.11.refs_3_ = f32[60,128]{1,0:T(8,128)S(1)} collective-permute-done((f32[60,128]{1,0:T(8,128)S(1)}, f32[60,128]{1,0:T(8,128)S(1)}, u32[]{:S(2)}, u32[]{:S(2)}) %collective-permute-start.11) | collective-permute-done | bytes 30752 | tf_op jit(solution)/shard_map/ppermute | solution.py:473
  133.4 4.9 %all-to-all-done.6 = f32[128,4,128]{2,1,0:T(4,128)S(1)} async-done(((f32[128,4,128]{2,1,0:T(4,128)}), f32[128,4,128]{2,1,0:T(4,128)S(1)}, u32[]{:S(2)}, u32[]{:S(2)}) %all-to-all-start.6) | async-done | bytes 262176 | tf_op jit(solution)/shard_map/all_to_all | solution.py:464
  143.3 4.1 %all-to-all-start.7 = ((f32[128,4,128]{2,1,0:T(4,128)}), f32[128,4,128]{2,1,0:T(4,128)S(1)}, u32[]{:S(2)}, u32[]{:S(2)}) async-start(f32[128,4,128]{2,1,0:T(4,128)} %bitcast.80), calls=%async_computation.7 | async-start | bytes 524288 | tf_op jit(solution)/shard_map/all_to_all | solution.py:464
  147.4 1.7 collective-permute-start.12
  149.1 1.3 collective-permute-done.12.refs_2_
  150.4 3.0 %collective-permute-done.13.refs_3_ = f32[60,128]{1,0:T(8,128)S(1)} collective-permute-done((f32[60,128]{1,0:T(8,128)S(1)}, f32[60,128]{1,0:T(8,128)S(1)}, u32[]{:S(2)}, u32[]{:S(2)}) %collective-permute-start.13) | collective-permute-done | bytes 30752 | tf_op jit(solution)/shard_map/ppermute | solution.py:473
  154.1 4.9 %all-to-all-done.7 = f32[128,4,128]{2,1,0:T(4,128)S(1)} async-done(((f32[128,4,128]{2,1,0:T(4,128)}), f32[128,4,128]{2,1,0:T(4,128)S(1)}, u32[]{:S(2)}, u32[]{:S(2)}) %all-to-all-start.7) | async-done | bytes 262176 | tf_op jit(solution)/shard_map/all_to_all | solution.py:464
  161.4 1.4 sweep_keep.3
  164.8 4.0 %all-to-all-start.8 = ((f32[128,4,128]{2,1,0:T(4,128)}), f32[128,4,128]{2,1,0:T(4,128)S(1)}, u32[]{:S(2)}, u32[]{:S(2)}) async-start(f32[128,4,128]{2,1,0:T(4,128)} %bitcast.79), calls=%async_computation.8 | async-start | bytes 524288 | tf_op jit(solution)/shard_map/all_to_all | solution.py:464
  168.8 1.7 collective-permute-start.14
  170.5 1.5 collective-permute-done.14.refs_2_
  172.0 2.8 %collective-permute-done.15.refs_3_ = f32[60,128]{1,0:T(8,128)S(1)} collective-permute-done((f32[60,128]{1,0:T(8,128)S(1)}, f32[60,128]{1,0:T(8,128)S(1)}, u32[]{:S(2)}, u32[]{:S(2)}) %collective-permute-start.15) | collective-permute-done | bytes 30752 | tf_op jit(solution)/shard_map/ppermute | solution.py:473
  174.8 5.5 %all-to-all-done.8 = f32[128,4,128]{2,1,0:T(4,128)S(1)} async-done(((f32[128,4,128]{2,1,0:T(4,128)}), f32[128,4,128]{2,1,0:T(4,128)S(1)}, u32[]{:S(2)}, u32[]{:S(2)}) %all-to-all-start.8) | async-done | bytes 262176 | tf_op jit(solution)/shard_map/all_to_all | solution.py:464
  183.7 13.6 %all_to_all.111 = f32[128,1,128]{2,1,0:T(1,128)S(1)} all-to-all(f32[128,1,128]{2,1,0:T(1,128)S(1)} %bitcast.83), channel_id=1, replica_groups=mesh['gx'=8,'gy'=16] {'gx','gy'}, dimensions={0} | all-to-all | bytes 131072 | tf_op jit(solution)/shard_map/all_to_all | solution.py:464
  (111 shorter events, 29.8 us)
Async XLA Ops:
  1.3 1.0 copy-start
  2.3 0.9 copy-start.2
  3.2 1.0 copy-start.4
  4.2 0.9 copy-start.6
  5.9 22.8 %copy-start.36 = (f32[256]{0:T(256)S(1)}, f32[256]{0:T(256)}, u32[]{:S(2)}) copy-start(f32[256]{0:T(256)} %param.18) | copy-start | bytes 3076
  5.9 22.8 %copy-start.37 = (f32[256]{0:T(256)S(1)}, f32[256]{0:T(256)}, u32[]{:S(2)}) copy-start(f32[256]{0:T(256)} %param.19) | copy-start | bytes 3076
  5.9 38.4 %copy-start.1 = (bf16[9,20,8,128]{3,2,1,0:T(8,128)(2,1)S(1)}, bf16[9,20,8,128]{3,2,1,0:T(8,128)(2,1)}, u32[]{:S(2)}) copy-start(bf16[9,20,8,128]{3,2,1,0:T(8,128)(2,1)} %param.12) | copy-start | bytes 1105924
  30.5 13.9 %copy-start.3 = (bf16[3,20,8,128]{3,2,1,0:T(8,128)(2,1)S(1)}, bf16[3,20,8,128]{3,2,1,0:T(8,128)(2,1)}, u32[]{:S(2)}) copy-start(bf16[3,20,8,128]{3,2,1,0:T(8,128)(2,1)} %param.13) | copy-start | bytes 368644
  30.5 13.9 %all-to-all-start.1 = ((f32[128,1,128]{2,1,0:T(1,128)}), f32[128,1,128]{2,1,0:T(1,128)S(1)}, u32[]{:S(2)}, u32[]{:S(2)}) async-start(f32[128,1,128]{2,1,0:T(1,128)} %bitcast.13), calls=%async_computation.1 | async-start | bytes 131072 | tf_op jit(solution)/shard_map/all_to_all | solution.py:464
  34.5 2.7 %collective-permute-start = (f32[60,128]{1,0:T(8,128)S(1)}, f32[60,128]{1,0:T(8,128)S(1)}, u32[]{:S(2)}, u32[]{:S(2)}) collective-permute-start(f32[60,128]{1,0:T(8,128)S(1)} %get-tuple-element.77), channel_id=1, source_target_pairs={{0,16},{16,32},{32,48},{48,64},{64,80},{80,96},{96,112},{112,0},{1... | collective-permute-start | bytes 92168 | tf_op jit(solution)/shard_map/ppermute | solution.py:472
  36.2 3.7 %collective-permute-start.1 = (f32[60,128]{1,0:T(8,128)S(1)}, f32[60,128]{1,0:T(8,128)S(1)}, u32[]{:S(2)}, u32[]{:S(2)}) collective-permute-start(f32[60,128]{1,0:T(8,128)S(1)} %get-tuple-element.78), channel_id=1, source_target_pairs={{16,0},{32,16},{48,32},{64,48},{80,64},{96,80},{112,96},{0,112},{1... | collective-permute-start | bytes 92168 | tf_op jit(solution)/shard_map/ppermute | solution.py:473
  46.1 16.0 %all-to-all-start.2 = ((f32[128,4,128]{2,1,0:T(4,128)}), f32[128,4,128]{2,1,0:T(4,128)S(1)}, u32[]{:S(2)}, u32[]{:S(2)}) async-start(f32[128,4,128]{2,1,0:T(4,128)} %bitcast.15), calls=%async_computation.2 | async-start | bytes 524288 | tf_op jit(solution)/shard_map/all_to_all | solution.py:464
  50.6 3.0 %collective-permute-start.2 = (f32[60,128]{1,0:T(8,128)S(1)}, f32[60,128]{1,0:T(8,128)S(1)}, u32[]{:S(2)}, u32[]{:S(2)}) collective-permute-start(f32[60,128]{1,0:T(8,128)S(1)} %get-tuple-element.94), channel_id=1, source_target_pairs={{0,16},{16,32},{32,48},{48,64},{64,80},{80,96},{96,112},{112,0},{1... | collective-permute-start | bytes 92168 | tf_op jit(solution)/shard_map/ppermute | solution.py:472
  52.2 4.4 %collective-permute-start.3 = (f32[60,128]{1,0:T(8,128)S(1)}, f32[60,128]{1,0:T(8,128)S(1)}, u32[]{:S(2)}, u32[]{:S(2)}) collective-permute-start(f32[60,128]{1,0:T(8,128)S(1)} %get-tuple-element.95), channel_id=1, source_target_pairs={{16,0},{32,16},{48,32},{64,48},{80,64},{96,80},{112,96},{0,112},{1... | collective-permute-start | bytes 92168 | tf_op jit(solution)/shard_map/ppermute | solution.py:473
  63.8 15.5 %all-to-all-start.3 = ((f32[128,4,128]{2,1,0:T(4,128)}), f32[128,4,128]{2,1,0:T(4,128)S(1)}, u32[]{:S(2)}, u32[]{:S(2)}) async-start(f32[128,4,128]{2,1,0:T(4,128)} %bitcast.17), calls=%async_computation.3 | async-start | bytes 524288 | tf_op jit(solution)/shard_map/all_to_all | solution.py:464
  67.8 3.0 %collective-permute-start.4 = (f32[60,128]{1,0:T(8,128)S(1)}, f32[60,128]{1,0:T(8,128)S(1)}, u32[]{:S(2)}, u32[]{:S(2)}) collective-permute-start(f32[60,128]{1,0:T(8,128)S(1)} %get-tuple-element.101), channel_id=1, source_target_pairs={{0,16},{16,32},{32,48},{48,64},{64,80},{80,96},{96,112},{112,0},{1... | collective-permute-start | bytes 92168 | tf_op jit(solution)/shard_map/ppermute | solution.py:472
  69.4 4.4 %collective-permute-start.5 = (f32[60,128]{1,0:T(8,128)S(1)}, f32[60,128]{1,0:T(8,128)S(1)}, u32[]{:S(2)}, u32[]{:S(2)}) collective-permute-start(f32[60,128]{1,0:T(8,128)S(1)} %get-tuple-element.102), channel_id=1, source_target_pairs={{16,0},{32,16},{48,32},{64,48},{80,64},{96,80},{112,96},{0,112},{1... | collective-permute-start | bytes 92168 | tf_op jit(solution)/shard_map/ppermute | solution.py:473
  79.3 18.5 %copy-start.7 = (f32[3,20,8,128]{3,2,1,0:T(8,128)S(1)}, f32[3,20,8,128]{3,2,1,0:T(8,128)}, u32[]{:S(2)}) copy-start(f32[3,20,8,128]{3,2,1,0:T(8,128)} %param.10) | copy-start | bytes 737284
  81.7 16.1 %copy-start.5 = (bf16[9,20,8,128]{3,2,1,0:T(8,128)(2,1)S(1)}, bf16[9,20,8,128]{3,2,1,0:T(8,128)(2,1)}, u32[]{:S(2)}) copy-start(bf16[9,20,8,128]{3,2,1,0:T(8,128)(2,1)} %param.11) | copy-start | bytes 1105924
  82.3 15.5 %all-to-all-start.4 = ((f32[128,4,128]{2,1,0:T(4,128)}), f32[128,4,128]{2,1,0:T(4,128)S(1)}, u32[]{:S(2)}, u32[]{:S(2)}) async-start(f32[128,4,128]{2,1,0:T(4,128)} %bitcast.19), calls=%async_computation.4 | async-start | bytes 524288 | tf_op jit(solution)/shard_map/all_to_all | solution.py:464
  86.3 3.2 %collective-permute-start.6 = (f32[60,128]{1,0:T(8,128)}, f32[60,128]{1,0:T(8,128)S(1)}, u32[]{:S(2)}, u32[]{:S(2)}) collective-permute-start(f32[60,128]{1,0:T(8,128)} %copy-done.46), channel_id=1, source_target_pairs={{0,16},{16,32},{32,48},{48,64},{64,80},{80,96},{96,112},{112,0},{1... | collective-permute-start | bytes 92168 | tf_op jit(solution)/shard_map/ppermute | solution.py:472
  88.0 4.4 %collective-permute-start.7 = (f32[60,128]{1,0:T(8,128)S(1)}, f32[60,128]{1,0:T(8,128)S(1)}, u32[]{:S(2)}, u32[]{:S(2)}) collective-permute-start(f32[60,128]{1,0:T(8,128)S(1)} %get-tuple-element.109), channel_id=1, source_target_pairs={{16,0},{32,16},{48,32},{64,48},{80,64},{96,80},{112,96},{0,112},{1... | collective-permute-start | bytes 92168 | tf_op jit(solution)/shard_map/ppermute | solution.py:473
  97.8 0.9 copy-start.16
  98.8 0.8 copy-start.22
  103.4 5.7 %copy-start.39 = (f32[60,128]{1,0:T(8,128)S(1)}, f32[60,128]{1,0:T(8,128)}, u32[]{:S(2)}) copy-start(f32[60,128]{1,0:T(8,128)} %copy-done.38) | copy-start | bytes 92164
  103.4 15.6 %all-to-all-start.5 = ((f32[128,4,128]{2,1,0:T(4,128)}), f32[128,4,128]{2,1,0:T(4,128)S(1)}, u32[]{:S(2)}, u32[]{:S(2)}) async-start(f32[128,4,128]{2,1,0:T(4,128)} %bitcast.21), calls=%async_computation.5 | async-start | bytes 524288 | tf_op jit(solution)/shard_map/all_to_all | solution.py:464
  107.4 3.2 %collective-permute-start.8 = (f32[60,128]{1,0:T(8,128)}, f32[60,128]{1,0:T(8,128)S(1)}, u32[]{:S(2)}, u32[]{:S(2)}) collective-permute-start(f32[60,128]{1,0:T(8,128)} %get-tuple-element.116), channel_id=1, source_target_pairs={{0,16},{16,32},{32,48},{48,64},{64,80},{80,96},{96,112},{112,0},{1... | collective-permute-start | bytes 92168 | tf_op jit(solution)/shard_map/ppermute | solution.py:472
  109.1 4.4 %collective-permute-start.9 = (f32[60,128]{1,0:T(8,128)S(1)}, f32[60,128]{1,0:T(8,128)S(1)}, u32[]{:S(2)}, u32[]{:S(2)}) collective-permute-start(f32[60,128]{1,0:T(8,128)S(1)} %copy-done.39), channel_id=1, source_target_pairs={{16,0},{32,16},{48,32},{64,48},{80,64},{96,80},{112,96},{0,112},{1... | collective-permute-start | bytes 92168 | tf_op jit(solution)/shard_map/ppermute | solution.py:473
  119.0 0.8 copy-start.26
  122.7 5.7 %copy-start.41 = (f32[60,128]{1,0:T(8,128)S(1)}, f32[60,128]{1,0:T(8,128)}, u32[]{:S(2)}) copy-start(f32[60,128]{1,0:T(8,128)} %copy-done.40) | copy-start | bytes 92164
  122.7 15.6 %copy-start.12 = (f32[3,160,128]{2,1,0:T(8,128)S(1)}, f32[3,160,128]{2,1,0:T(8,128)}, u32[]{:S(2)}) copy-start(f32[3,160,128]{2,1,0:T(8,128)} %copy-done.11) | copy-start | bytes 737284
  122.7 15.6 %all-to-all-start.6 = ((f32[128,4,128]{2,1,0:T(4,128)}), f32[128,4,128]{2,1,0:T(4,128)S(1)}, u32[]{:S(2)}, u32[]{:S(2)}) async-start(f32[128,4,128]{2,1,0:T(4,128)} %bitcast.23), calls=%async_computation.6 | async-start | bytes 524288 | tf_op jit(solution)/shard_map/all_to_all | solution.py:464
  126.7 3.2 %collective-permute-start.10 = (f32[60,128]{1,0:T(8,128)}, f32[60,128]{1,0:T(8,128)S(1)}, u32[]{:S(2)}, u32[]{:S(2)}) collective-permute-start(f32[60,128]{1,0:T(8,128)} %get-tuple-element.123), channel_id=1, source_target_pairs={{0,16},{16,32},{32,48},{48,64},{64,80},{80,96},{96,112},{112,0},{1... | collective-permute-start | bytes 92168 | tf_op jit(solution)/shard_map/ppermute | solution.py:472
  128.5 4.4 %collective-permute-start.11 = (f32[60,128]{1,0:T(8,128)S(1)}, f32[60,128]{1,0:T(8,128)S(1)}, u32[]{:S(2)}, u32[]{:S(2)}) collective-permute-start(f32[60,128]{1,0:T(8,128)S(1)} %copy-done.41), channel_id=1, source_target_pairs={{16,0},{32,16},{48,32},{64,48},{80,64},{96,80},{112,96},{0,112},{1... | collective-permute-start | bytes 92168 | tf_op jit(solution)/shard_map/ppermute | solution.py:473
  138.4 0.8 copy-start.28
  142.7 4.6 %copy-start.48 = (f32[60,128]{1,0:T(8,128)S(1)}, f32[60,128]{1,0:T(8,128)}, u32[]{:S(2)}) copy-start(f32[60,128]{1,0:T(8,128)} %copy-done.47) | copy-start | bytes 92164
  142.7 6.4 %copy-start.45 = (f32[60,128]{1,0:T(8,128)S(1)}, f32[60,128]{1,0:T(8,128)}, u32[]{:S(2)}) copy-start(f32[60,128]{1,0:T(8,128)} %copy-done.44) | copy-start | bytes 92164
  143.3 15.7 %all-to-all-start.7 = ((f32[128,4,128]{2,1,0:T(4,128)}), f32[128,4,128]{2,1,0:T(4,128)S(1)}, u32[]{:S(2)}, u32[]{:S(2)}) async-start(f32[128,4,128]{2,1,0:T(4,128)} %bitcast.80), calls=%async_computation.7 | async-start | bytes 524288 | tf_op jit(solution)/shard_map/all_to_all | solution.py:464
  147.4 3.1 %collective-permute-start.12 = (f32[60,128]{1,0:T(8,128)S(1)}, f32[60,128]{1,0:T(8,128)S(1)}, u32[]{:S(2)}, u32[]{:S(2)}) collective-permute-start(f32[60,128]{1,0:T(8,128)S(1)} %copy-done.48), channel_id=1, source_target_pairs={{0,16},{16,32},{32,48},{48,64},{64,80},{80,96},{96,112},{112,0},{1... | collective-permute-start | bytes 92168 | tf_op jit(solution)/shard_map/ppermute | solution.py:472
  149.1 4.4 %collective-permute-start.13 = (f32[60,128]{1,0:T(8,128)S(1)}, f32[60,128]{1,0:T(8,128)S(1)}, u32[]{:S(2)}, u32[]{:S(2)}) collective-permute-start(f32[60,128]{1,0:T(8,128)S(1)} %copy-done.45), channel_id=1, source_target_pairs={{16,0},{32,16},{48,32},{64,48},{80,64},{96,80},{112,96},{0,112},{1... | collective-permute-start | bytes 92168 | tf_op jit(solution)/shard_map/ppermute | solution.py:473
  159.7 0.9 copy-start.14
  160.6 0.8 copy-start.24
  164.8 5.7 %copy-start.43 = (f32[60,128]{1,0:T(8,128)S(1)}, f32[60,128]{1,0:T(8,128)}, u32[]{:S(2)}) copy-start(f32[60,128]{1,0:T(8,128)} %copy-done.42) | copy-start | bytes 92164
  164.8 15.6 %all-to-all-start.8 = ((f32[128,4,128]{2,1,0:T(4,128)}), f32[128,4,128]{2,1,0:T(4,128)S(1)}, u32[]{:S(2)}, u32[]{:S(2)}) async-start(f32[128,4,128]{2,1,0:T(4,128)} %bitcast.79), calls=%async_computation.8 | async-start | bytes 524288 | tf_op jit(solution)/shard_map/all_to_all | solution.py:464
  168.8 3.2 %collective-permute-start.14 = (f32[60,128]{1,0:T(8,128)}, f32[60,128]{1,0:T(8,128)S(1)}, u32[]{:S(2)}, u32[]{:S(2)}) collective-permute-start(f32[60,128]{1,0:T(8,128)} %get-tuple-element.137), channel_id=1, source_target_pairs={{0,16},{16,32},{32,48},{48,64},{64,80},{80,96},{96,112},{112,0},{1... | collective-permute-start | bytes 92168 | tf_op jit(solution)/shard_map/ppermute | solution.py:472
  170.5 4.4 %collective-permute-start.15 = (f32[60,128]{1,0:T(8,128)S(1)}, f32[60,128]{1,0:T(8,128)S(1)}, u32[]{:S(2)}, u32[]{:S(2)}) collective-permute-start(f32[60,128]{1,0:T(8,128)S(1)} %copy-done.43), channel_id=1, source_target_pairs={{16,0},{32,16},{48,32},{64,48},{80,64},{96,80},{112,96},{0,112},{1... | collective-permute-start | bytes 92168 | tf_op jit(solution)/shard_map/ppermute | solution.py:473
  181.1 0.9 copy-start.18
  182.0 0.9 copy-start.20
  (25 other events, 16.2 us)

commit v3 on v2

--- a/solution.py
+++ b/solution.py
@@ -141,6 +141,18 @@
     entry = [matrix[n, rows, :].astype(F32) for n in range(9)]
     x, y, z = vector
     return [entry[3 * n] * x + entry[3 * n + 1] * y + entry[3 * n + 2] * z for n in range(3)]
+
+
+def solve(diag, rows, vector):
+    a, b, c, d, e, f, g, h, i = [diag[n, rows, :].astype(F32) for n in range(9)]
+    x, y, z = vector
+    p, q, s = e * i - f * h, f * g - d * i, d * h - e * g
+    scale = 1.0 / (a * p + b * q + c * s)
+    return [
+        (p * x + (c * h - b * i) * y + (b * f - c * e) * z) * scale,
+        (q * x + (a * i - c * g) * y + (c * d - a * f) * z) * scale,
+        (s * x + (b * g - a * h) * y + (a * e - b * d) * z) * scale,
+    ]
 
 
 def borders(values, mobility, trans, weighted, along, t):
@@ -196,28 +208,21 @@
         message[rows, :] = jnp.where(mine, message[rows, :], packed)
 
 
-def cell_setup(rhs, diag, mobility, trans, cells, pi,
-               inverse, first, rows_of, rows_to, start, weight, slots,
-               near, toward_low, toward_high, message, weighted, along, pad):
+def cell_setup(rhs_in, diag_in, mobility_in, trans_in, cells_in, pi_in,
+               rows_of, rows_to, start, weight, slots,
+               near, toward_low, toward_high, message, weighted, along, pad, forward,
+               rhs, diag, mobility, trans, cells, pi, sems):
+    pairs = ((rhs_in, rhs), (diag_in, diag), (cells_in, cells), (pi_in, pi),
+             (mobility_in, mobility), (trans_in, trans))
+    copies = [pltpu.make_async_copy(a, b, sems.at[n]) for n, (a, b) in enumerate(pairs)]
+    for copy in copies:
+        copy.start()
+    for copy in copies:
+        copy.wait()
     for t in range(CHUNKS):
         rows = chunk(t)
-        a, b, c, d, e, f, g, h, i = [diag[n, rows, :].astype(F32) for n in range(9)]
-        p, q, s = e * i - f * h, f * g - d * i, d * h - e * g
-        scale = 1.0 / (a * p + b * q + c * s)
-        entries = [
-            p, c * h - b * i, b * f - c * e,
-            q, a * i - c * g, c * d - a * f,
-            s, b * g - a * h, a * e - b * d,
-        ]
-        entries = [entry * scale for entry in entries]
-        x, y, z = [rhs[n, rows, :] for n in range(3)]
-        for n in range(9):
-            inverse[n, rows, :] = entries[n]
-        values = [
-            entries[3 * n] * x + entries[3 * n + 1] * y + entries[3 * n + 2] * z for n in range(3)
-        ]
-        for n in range(3):
-            first[n, rows, :] = values[n]
+        values = solve(diag, rows, [rhs[n, rows, :] for n in range(3)])
+        forward[rows, :] = values[0]
         borders(values, mobility, trans, weighted, along, t)
     base = cells[0:1, :]
     row = lax.shift_right_logical(base, 7)
@@ -236,7 +241,7 @@
     start[...] = begin
     weights = jnp.where(is_slot(lanes((PEERS, 128))), info, 0.0)
     weight[...] = weights
-    values = slot_values(rows_of[...], begin, first[0])
+    values = slot_values(rows_of[...], begin, forward[...])
     slots[...] = values
     message[block(0), :] = values
     message[block(1), :] = weights
@@ -245,25 +250,28 @@
     interior(trans, weighted, along, near, toward_low, toward_high, message, pad)
 
 
-def well_setup(arrived, index, parent, trans, rhs, message, weight, table, state, at_slots, fixed):
-    pi = to_rows(arrived[block(1), :])
-    weight[...] = pi
-    number = index[...]
-    low = number & 127
+def well_tables(index, parent, trans, rhs, table, fixed):
+    low = index[...] & 127
     for k in range(CAP):
         hit = subs((128, 128)) == jnp.broadcast_to(low[k : k + 1], (128, 128))
         table[:, 128 * k : 128 * (k + 1)] = hit.astype(F32).astype(BF16)
     zeros = jnp.zeros((6, 128), F32)
     linked = jnp.concatenate([(parent[...] >= 0).astype(F32), zeros], axis=0)
     across = jnp.concatenate([trans[...], zeros], axis=0)
-    source = jnp.concatenate([rhs[...], zeros], axis=0)
-    diagonal = across + following(linked * across) + into_segments(pi, number, table[...])
-    diagonal = jnp.where(subs((8, 128)) < 2, diagonal, 1.0)
     fixed[0] = linked
     fixed[1] = across
-    fixed[2] = source
-    fixed[3] = diagonal
-    now = source / diagonal
+    fixed[2] = jnp.concatenate([rhs[...], zeros], axis=0)
+    fixed[3] = across + following(linked * across)
+
+
+def well_setup(arrived, index, table, fixed, message, weight, state, at_slots, diagonal):
+    pi = to_rows(arrived[block(1), :])
+    weight[...] = pi
+    number = index[...]
+    total = fixed[3] + into_segments(pi, number, table[...])
+    total = jnp.where(subs((8, 128)) < 2, total, 1.0)
+    diagonal[...] = total
+    now = fixed[2] / total
     state[...] = now
     values = segment_values(now, number)
     at_slots[...] = values
@@ -284,13 +292,13 @@
     )
 
 
-STEADY = ("first", "inverse", "mobility", "trans", "rows_of", "rows_to", "start", "weight",
-          "own_weight", "table", "index", "fixed")
+STEADY = ("rhs", "diag", "mobility", "trans", "rows_of", "rows_to", "start", "weight",
+          "own_weight", "table", "index", "fixed", "diagonal")
 MOVING = ("arrived", "near", "from_low", "from_high", "slots", "at_slots", "state")
 NEXT = ("near", "toward_low", "toward_high", "message", "slots", "at_slots", "state")
 MORE_IN = {
-    "first": ("pressures",), "plain": (), "keep": (), "last": ("diag", "rhs", "field"), "after": (),
-    "final": ("diag", "rhs", "field", "change", "seg_change", "omega"),
+    "first": ("pressures",), "plain": (), "keep": (), "last": ("field",), "after": (),
+    "final": ("field", "change", "seg_change", "omega"),
 }
 MORE_OUT = {
     "first": (), "plain": (), "keep": ("field",), "last": ("change", "seg_change"),
@@ -324,7 +332,7 @@
     open_low, open_high = gx > 0, gx < lax.axis_size("gx") - 1
 
     state = now["state"][...]
-    linked, across, source, diagonal = [fixed["fixed"][n] for n in range(4)]
+    linked, across, source = [fixed["fixed"][n] for n in range(3)]
     push = fixed["own_weight"][...] * (to_rows(arrived[block(0), :]) - now["at_slots"][...])
     number = fixed["index"][...]
     inflow = into_segments(push, number, fixed["table"][...])
@@ -356,10 +364,10 @@
             value = now["near"][n, rows, :] + tx * nx + ty * ny
             terms.append(value - share * perforated[t * STEP : (t + 1) * STEP])
         if kind in ("last", "final"):
-            own = mix(extra["diag"], rows, [extra["field"][n, rows, :] for n in range(3)])
+            own = mix(fixed["diag"], rows, [extra["field"][n, rows, :] for n in range(3)])
             for n in range(3):
                 change = own[n] - terms[n]
-                before = extra["rhs"][n, rows, :]
+                before = fixed["rhs"][n, rows, :]
                 if final:
                     kept = extra["change"][n, rows, :]
                     before = before - omega * kept
@@ -369,8 +377,8 @@
                 numer += before * change
                 denom += change * change
         if not final:
-            moves = mix(fixed["inverse"], rows, terms)
-            values = [fixed["first"][n, rows, :] + moves[n] for n in range(3)]
+            total = [fixed["rhs"][n, rows, :] + terms[n] for n in range(3)]
+            values = solve(fixed["diag"], rows, total)
             forward[rows, :] = values[0]
             if kind == "keep":
                 for n in range(3):
@@ -396,7 +404,7 @@
     else:
         sums = jnp.zeros((PEERS, 128), F32)
     message = out["message"]
-    advanced = state + seg_res / diagonal
+    advanced = state + seg_res / fixed["diagonal"][...]
     out["state"][...] = advanced
     values = segment_values(advanced, number)
     out["at_slots"][...] = values
@@ -443,15 +451,16 @@
     pltpu.VMEM((3, ROWS + 16, 128), F32),
     pltpu.VMEM((3 * ROWS, 128), F32),
     pltpu.VMEM((16, 128), F32),
+    pltpu.VMEM((ROWS, 128), F32),
 )
 
 
-def call(body, outs, args, scratch=(), name=None):
+def call(body, outs, args, scratch=(), name=None, space=pltpu.VMEM):
     moved = sum(a.size * a.dtype.itemsize for a in args)
     return pl.pallas_call(
         body,
         out_shape=[jax.ShapeDtypeStruct(*out) for out in outs],
-        in_specs=[pl.BlockSpec(memory_space=pltpu.VMEM)] * len(args),
+        in_specs=[pl.BlockSpec(memory_space=space)] * len(args),
         out_specs=[pl.BlockSpec(memory_space=pltpu.VMEM)] * len(outs),
         scratch_shapes=list(scratch),
         compiler_params=pltpu.CompilerParams(vmem_limit_bytes=24 * 1024 * 1024),
@@ -483,32 +492,37 @@
     trans = trans.reshape(3, ROWS, 128)
     index = perf_seg[0]
 
-    fixed = {"mobility": mobility, "trans": trans, "index": index}
-    (inverse, first, rows_of, rows_to, start, weight, slots, near, toward_low, toward_high,
-     message) = call(
+    fixed = {"rhs": rhs, "diag": diag, "mobility": mobility, "trans": trans, "index": index}
+    inputs = [rhs, diag, mobility, trans, perf_cell[0], perf_pi[0]]
+    (rows_of, rows_to, start, weight, slots, near, toward_low, toward_high, message) = call(
         cell_setup,
-        [((9, ROWS, 128), F32), CELLS, ((PEERS, ROWS), BF16), ((ROWS, PEERS), BF16),
+        [((PEERS, ROWS), BF16), ((ROWS, PEERS), BF16),
          ((PEERS, 128), jnp.int32), PAIRS, PAIRS, CELLS, EDGE, EDGE, MESSAGE],
-        [rhs, diag, mobility, trans, perf_cell[0], perf_pi[0]],
-        SCRATCH,
+        inputs,
+        SCRATCH + tuple(pltpu.VMEM(a.shape, a.dtype) for a in inputs)
+        + (pltpu.SemaphoreType.DMA((6,)),),
         name="cell_setup",
-    )
-    fixed.update(
-        first=first, inverse=inverse, rows_of=rows_of, rows_to=rows_to, start=start, weight=weight
+        space=pltpu.HBM,
     )
     arrived = exchange(message)
+    table, constants = call(
+        well_tables,
+        [((128, CAP * 128), BF16), ((4, 8, 128), F32)],
+        [index, seg_parent.reshape(2, 128), seg_trans.reshape(2, 128), seg_rhs.reshape(2, 128)],
+        name="well_tables",
+    )
+    fixed.update(rows_of=rows_of, rows_to=rows_to, start=start, weight=weight)
     now = {"arrived": arrived, "near": near, "slots": slots}
     now.update(neighbours(toward_low, toward_high))
-    message, own_weight, table, state, at_slots, constants = call(
+    message, own_weight, state, at_slots, diagonal = call(
         well_setup,
-        [PAIRS, TILE, ((128, CAP * 128), BF16), TILE, TILE, ((4, 8, 128), F32)],
-        [arrived, index, seg_parent.reshape(2, 128), seg_trans.reshape(2, 128),
-         seg_rhs.reshape(2, 128)],
+        [PAIRS, TILE, TILE, TILE, TILE],
+        [arrived, index, table, constants],
         name="well_setup",
     )
-    fixed.update(own_weight=own_weight, table=table, fixed=constants)
+    fixed.update(own_weight=own_weight, table=table, fixed=constants, diagonal=diagonal)
     now.update(at_slots=at_slots, state=state)
-    saved = {"pressures": exchange(message), "diag": diag, "rhs": rhs}
+    saved = {"pressures": exchange(message)}
 
     def advance(kind, now):
         args = [now[name] for name in MOVING]
@@ -519,7 +533,7 @@
             functools.partial(sweep, kind),
             [PAIRS if kind == "final" else SHAPES[name] for name in names],
             args,
-            SCRATCH + (pltpu.VMEM((ROWS, 128), F32),),
+            SCRATCH,
             name="sweep_" + kind,
         )
         out = dict(zip(names, out))

time: 199 us -> 183 us (0.920)
  blocking collectives: 36.4 us -> 13.6 us
  local copies, waits for them, and re-layouts: 25.5 us -> 4.55 us
  waiting for transfers between devices: 74.8 us -> 88.1 us
  starting transfers between devices: 46 us -> 57.2 us
  Pallas kernels: 14.7 us -> 17.8 us
    all_to_all x2 -> x1, blocking collectives: 36.4 us -> 13.6 us  [exchange(): lax.all_to_all(message, AXES, split_axis=0, concat_axis=0, tiled=True)]
    unnamed x98 -> x28, local copies, waits for them, and re-layouts: 25.5 us -> 4.55 us
    all_to_all x8 -> x9, waiting for transfers between devices: 40.4 us -> 53.6 us  [exchange(): lax.all_to_all(message, AXES, split_axis=0, concat_axis=0, tiled=True)]
    all_to_all x8 -> x9, starting transfers between devices: 32.5 us -> 44 us  [exchange(): lax.all_to_all(message, AXES, split_axis=0, concat_axis=0, tiled=True)]
    pallas_call x11 -> x12, Pallas kernels: 14.7 us -> 17.8 us  [call(): pl.pallas_call(body, out_shape=[jax.ShapeDtypeStruct(*out) for out in out...]
  transfers between devices with their start and end apart: 24 -> 25, of which waited for: 24 -> 25; matrix products, arithmetic and copies ran while one was open for 0% -> 0% of each run, Pallas kernels for 0% -> 0%
where the time goes in v3:
time: 183 us; the launch traced here: 182 us
  waiting for transfers between devices  88.1 us (48%)
  starting transfers between devices  57.2 us (31%)
  Pallas kernels  17.8 us (10%)
  blocking collectives  13.6 us (7%)
  local copies, waits for them, and re-layouts  4.55 us (2%)
    all_to_all x9, waiting for transfers between devices, exchange(): lax.all_to_all(message, AXES, split_axis=0, concat_axis=0, tiled=True)  53.6 us
    all_to_all x9, starting transfers between devices, exchange(): lax.all_to_all(message, AXES, split_axis=0, concat_axis=0, tiled=True)  44 us
    ppermute x8, waiting for transfers between devices, neighbours(): lax.ppermute(toward_low, 'gx', down)  24.3 us
    pallas_call x12, Pallas kernels, call(): pl.pallas_call(body, out_shape=[jax.ShapeDtypeStruct(*out) for out in out...  17.8 us
    all_to_all x1, blocking collectives, exchange(): lax.all_to_all(message, AXES, split_axis=0, concat_axis=0, tiled=True)  13.6 us
    ppermute x8, starting transfers between devices, neighbours(): lax.ppermute(toward_high, 'gx', up)  13.2 us
    ppermute x8, waiting for transfers between devices, neighbours(): lax.ppermute(toward_high, 'gx', up)  10.2 us
    unnamed x28, local copies, waits for them, and re-layouts  4.55 us
  transfers between devices with their start and end apart: 25, of which 25 were waited for; matrix products, arithmetic and copies ran while one was open for 0% of the time, Pallas kernels for 0%

profile of v3, /device:TPU:1, one launch (start us, length us, event | category | flops | bytes accessed | tf_op | source)
XLA Modules:
  0.0 182.1 jit_solution(6866575448227211822)
XLA Ops:
  5.2 2.2 %cell_setup.1 = (bf16[128,160]{1,0:T(8,128)(2,1)S(1)}, bf16[160,128]{1,0:T(8,128)(2,1)S(1)}, s32[128,128]{1,0:T(8,128)S(1)}, f32[128,128]{1,0:T(8,128)S(1)}, f32...) custom-call(f32[3,160,128]{2,1,0:T(8,128)S(1)} %bitcast.54, ...), custom_call_target="tpu_custom_call" | custom-call | flops 4000000 | bytes 1114112 | tf_op jit(solution)/shard_map/cell_setup/pallas_call | solution.py:460
  7.5 11.5 %all-to-all-start = ((f32[128,4,128]{2,1,0:T(4,128)}), f32[128,4,128]{2,1,0:T(4,128)S(1)}, u32[]{:S(2)}, u32[]{:S(2)}) async-start(f32[128,4,128]{2,1,0:T(4,128)} %bitcast.6), calls=%async_computation | async-start | bytes 524288 | tf_op jit(solution)/shard_map/all_to_all | solution.py:473
  19.2 11.3 %all-to-all-done = f32[128,4,128]{2,1,0:T(4,128)S(1)} async-done(((f32[128,4,128]{2,1,0:T(4,128)}), f32[128,4,128]{2,1,0:T(4,128)S(1)}, u32[]{:S(2)}, u32[]{:S(2)}) %all-to-all-start) | async-done | bytes 262176 | tf_op jit(solution)/shard_map/all_to_all | solution.py:473
  31.5 4.0 %all-to-all-start.1 = ((f32[128,1,128]{2,1,0:T(1,128)}), f32[128,1,128]{2,1,0:T(1,128)S(1)}, u32[]{:S(2)}, u32[]{:S(2)}) async-start(f32[128,1,128]{2,1,0:T(1,128)} %bitcast.13), calls=%async_computation.1 | async-start | bytes 131072 | tf_op jit(solution)/shard_map/all_to_all | solution.py:473
  35.5 1.6 collective-permute-start
  38.2 2.7 %collective-permute-done.1.refs_3_ = f32[60,128]{1,0:T(8,128)S(1)} collective-permute-done((f32[60,128]{1,0:T(8,128)S(1)}, f32[60,128]{1,0:T(8,128)S(1)}, u32[]{:S(2)}, u32[]{:S(2)}) %collective-permute-start.1) | collective-permute-done | bytes 30752 | tf_op jit(solution)/shard_map/ppermute | solution.py:482
  40.9 4.3 %all-to-all-done.1 = f32[128,1,128]{2,1,0:T(1,128)S(1)} async-done(((f32[128,1,128]{2,1,0:T(1,128)}), f32[128,1,128]{2,1,0:T(1,128)S(1)}, u32[]{:S(2)}, u32[]{:S(2)}) %all-to-all-start.1) | async-done | bytes 65568 | tf_op jit(solution)/shard_map/all_to_all | solution.py:473
  45.2 1.8 sweep_first.1
  47.1 4.5 %all-to-all-start.2 = ((f32[128,4,128]{2,1,0:T(4,128)}), f32[128,4,128]{2,1,0:T(4,128)S(1)}, u32[]{:S(2)}, u32[]{:S(2)}) async-start(f32[128,4,128]{2,1,0:T(4,128)} %bitcast.15), calls=%async_computation.2 | async-start | bytes 524288 | tf_op jit(solution)/shard_map/all_to_all | solution.py:473
  51.5 1.6 collective-permute-start.2
  54.5 3.1 %collective-permute-done.3.refs_3_ = f32[60,128]{1,0:T(8,128)S(1)} collective-permute-done((f32[60,128]{1,0:T(8,128)S(1)}, f32[60,128]{1,0:T(8,128)S(1)}, u32[]{:S(2)}, u32[]{:S(2)}) %collective-permute-start.3) | collective-permute-done | bytes 30752 | tf_op jit(solution)/shard_map/ppermute | solution.py:482
  57.6 5.4 %all-to-all-done.2 = f32[128,4,128]{2,1,0:T(4,128)S(1)} async-done(((f32[128,4,128]{2,1,0:T(4,128)}), f32[128,4,128]{2,1,0:T(4,128)S(1)}, u32[]{:S(2)}, u32[]{:S(2)}) %all-to-all-start.2) | async-done | bytes 262176 | tf_op jit(solution)/shard_map/all_to_all | solution.py:473
  63.0 1.8 sweep_plain.2
  64.8 4.0 %all-to-all-start.3 = ((f32[128,4,128]{2,1,0:T(4,128)}), f32[128,4,128]{2,1,0:T(4,128)S(1)}, u32[]{:S(2)}, u32[]{:S(2)}) async-start(f32[128,4,128]{2,1,0:T(4,128)} %bitcast.17), calls=%async_computation.3 | async-start | bytes 524288 | tf_op jit(solution)/shard_map/all_to_all | solution.py:473
  68.8 1.6 collective-permute-start.4
  71.8 3.1 %collective-permute-done.5.refs_3_ = f32[60,128]{1,0:T(8,128)S(1)} collective-permute-done((f32[60,128]{1,0:T(8,128)S(1)}, f32[60,128]{1,0:T(8,128)S(1)}, u32[]{:S(2)}, u32[]{:S(2)}) %collective-permute-start.5) | collective-permute-done | bytes 30752 | tf_op jit(solution)/shard_map/ppermute | solution.py:482
  74.9 5.4 %all-to-all-done.3 = f32[128,4,128]{2,1,0:T(4,128)S(1)} async-done(((f32[128,4,128]{2,1,0:T(4,128)}), f32[128,4,128]{2,1,0:T(4,128)S(1)}, u32[]{:S(2)}, u32[]{:S(2)}) %all-to-all-start.3) | async-done | bytes 262176 | tf_op jit(solution)/shard_map/all_to_all | solution.py:473
  80.3 1.8 sweep_keep.2
  82.1 4.0 %all-to-all-start.4 = ((f32[128,4,128]{2,1,0:T(4,128)}), f32[128,4,128]{2,1,0:T(4,128)S(1)}, u32[]{:S(2)}, u32[]{:S(2)}) async-start(f32[128,4,128]{2,1,0:T(4,128)} %bitcast.19), calls=%async_computation.4 | async-start | bytes 524288 | tf_op jit(solution)/shard_map/all_to_all | solution.py:473
  86.1 1.6 collective-permute-start.6
  87.8 1.3 collective-permute-done.6.refs_2_
  89.1 3.1 %collective-permute-done.7.refs_3_ = f32[60,128]{1,0:T(8,128)S(1)} collective-permute-done((f32[60,128]{1,0:T(8,128)S(1)}, f32[60,128]{1,0:T(8,128)S(1)}, u32[]{:S(2)}, u32[]{:S(2)}) %collective-permute-start.7) | collective-permute-done | bytes 30752 | tf_op jit(solution)/shard_map/ppermute | solution.py:482
  92.2 5.4 %all-to-all-done.4 = f32[128,4,128]{2,1,0:T(4,128)S(1)} async-done(((f32[128,4,128]{2,1,0:T(4,128)}), f32[128,4,128]{2,1,0:T(4,128)S(1)}, u32[]{:S(2)}, u32[]{:S(2)}) %all-to-all-start.4) | async-done | bytes 262176 | tf_op jit(solution)/shard_map/all_to_all | solution.py:473
  97.6 2.0 %sweep_last.1 = (f32[3,160,128]{2,1,0:T(8,128)S(1)}, f32[60,128]{1,0:T(8,128)S(1)}, f32[60,128]{1,0:T(8,128)S(1)}, f32[512,128]{1,0:T(8,128)}, f32[128,128]{1,0:...) custom-call(f32[512,128]{1,0:T(8,128)S(1)} %bitcast.75, ...), custom_call_target="tpu_custom_call" | custom-call | flops 4000000 | bytes 2498560 | tf_op jit(solution)/shard_map/sweep_last/pallas_call | solution.py:460
  99.6 4.0 %all-to-all-start.5 = ((f32[128,4,128]{2,1,0:T(4,128)}), f32[128,4,128]{2,1,0:T(4,128)S(1)}, u32[]{:S(2)}, u32[]{:S(2)}) async-start(f32[128,4,128]{2,1,0:T(4,128)} %bitcast.21), calls=%async_computation.5 | async-start | bytes 524288 | tf_op jit(solution)/shard_map/all_to_all | solution.py:473
  103.6 1.6 collective-permute-start.8
  105.3 1.3 collective-permute-done.8.refs_2_
  106.6 3.1 %collective-permute-done.9.refs_3_ = f32[60,128]{1,0:T(8,128)S(1)} collective-permute-done((f32[60,128]{1,0:T(8,128)S(1)}, f32[60,128]{1,0:T(8,128)S(1)}, u32[]{:S(2)}, u32[]{:S(2)}) %collective-permute-start.9) | collective-permute-done | bytes 30752 | tf_op jit(solution)/shard_map/ppermute | solution.py:482
  109.7 5.4 %all-to-all-done.5 = f32[128,4,128]{2,1,0:T(4,128)S(1)} async-done(((f32[128,4,128]{2,1,0:T(4,128)}), f32[128,4,128]{2,1,0:T(4,128)S(1)}, u32[]{:S(2)}, u32[]{:S(2)}) %all-to-all-start.5) | async-done | bytes 262176 | tf_op jit(solution)/shard_map/all_to_all | solution.py:473
  115.1 1.8 sweep_after.1
  116.9 4.0 %all-to-all-start.6 = ((f32[128,4,128]{2,1,0:T(4,128)}), f32[128,4,128]{2,1,0:T(4,128)S(1)}, u32[]{:S(2)}, u32[]{:S(2)}) async-start(f32[128,4,128]{2,1,0:T(4,128)} %bitcast.23), calls=%async_computation.6 | async-start | bytes 524288 | tf_op jit(solution)/shard_map/all_to_all | solution.py:473
  120.9 1.6 collective-permute-start.10
  122.5 1.3 collective-permute-done.10.refs_2_
  123.8 3.1 %collective-permute-done.11.refs_3_ = f32[60,128]{1,0:T(8,128)S(1)} collective-permute-done((f32[60,128]{1,0:T(8,128)S(1)}, f32[60,128]{1,0:T(8,128)S(1)}, u32[]{:S(2)}, u32[]{:S(2)}) %collective-permute-start.11) | collective-permute-done | bytes 30752 | tf_op jit(solution)/shard_map/ppermute | solution.py:482
  126.9 5.4 %all-to-all-done.6 = f32[128,4,128]{2,1,0:T(4,128)S(1)} async-done(((f32[128,4,128]{2,1,0:T(4,128)}), f32[128,4,128]{2,1,0:T(4,128)S(1)}, u32[]{:S(2)}, u32[]{:S(2)}) %all-to-all-start.6) | async-done | bytes 262176 | tf_op jit(solution)/shard_map/all_to_all | solution.py:473
  132.4 1.8 sweep_plain.3
  134.2 4.0 %all-to-all-start.7 = ((f32[128,4,128]{2,1,0:T(4,128)}), f32[128,4,128]{2,1,0:T(4,128)S(1)}, u32[]{:S(2)}, u32[]{:S(2)}) async-start(f32[128,4,128]{2,1,0:T(4,128)} %bitcast.25), calls=%async_computation.7 | async-start | bytes 524288 | tf_op jit(solution)/shard_map/all_to_all | solution.py:473
  138.2 1.6 collective-permute-start.12
  139.8 1.3 collective-permute-done.12.refs_2_
  141.1 3.1 %collective-permute-done.13.refs_3_ = f32[60,128]{1,0:T(8,128)S(1)} collective-permute-done((f32[60,128]{1,0:T(8,128)S(1)}, f32[60,128]{1,0:T(8,128)S(1)}, u32[]{:S(2)}, u32[]{:S(2)}) %collective-permute-start.13) | collective-permute-done | bytes 30752 | tf_op jit(solution)/shard_map/ppermute | solution.py:482
  144.2 5.4 %all-to-all-done.7 = f32[128,4,128]{2,1,0:T(4,128)S(1)} async-done(((f32[128,4,128]{2,1,0:T(4,128)}), f32[128,4,128]{2,1,0:T(4,128)S(1)}, u32[]{:S(2)}, u32[]{:S(2)}) %all-to-all-start.7) | async-done | bytes 262176 | tf_op jit(solution)/shard_map/all_to_all | solution.py:473
  149.6 1.8 sweep_keep.3
  151.5 4.0 %all-to-all-start.8 = ((f32[128,4,128]{2,1,0:T(4,128)}), f32[128,4,128]{2,1,0:T(4,128)S(1)}, u32[]{:S(2)}, u32[]{:S(2)}) async-start(f32[128,4,128]{2,1,0:T(4,128)} %bitcast.27), calls=%async_computation.8 | async-start | bytes 524288 | tf_op jit(solution)/shard_map/all_to_all | solution.py:473
  155.5 1.6 collective-permute-start.14
  157.1 1.3 collective-permute-done.14.refs_2_
  158.4 3.1 %collective-permute-done.15.refs_3_ = f32[60,128]{1,0:T(8,128)S(1)} collective-permute-done((f32[60,128]{1,0:T(8,128)S(1)}, f32[60,128]{1,0:T(8,128)S(1)}, u32[]{:S(2)}, u32[]{:S(2)}) %collective-permute-start.15) | collective-permute-done | bytes 30752 | tf_op jit(solution)/shard_map/ppermute | solution.py:482
  161.5 5.4 %all-to-all-done.8 = f32[128,4,128]{2,1,0:T(4,128)S(1)} async-done(((f32[128,4,128]{2,1,0:T(4,128)}), f32[128,4,128]{2,1,0:T(4,128)S(1)}, u32[]{:S(2)}, u32[]{:S(2)}) %all-to-all-start.8) | async-done | bytes 262176 | tf_op jit(solution)/shard_map/all_to_all | solution.py:473
  167.7 13.6 %all_to_all.110 = f32[128,1,128]{2,1,0:T(1,128)S(1)} all-to-all(f32[128,1,128]{2,1,0:T(1,128)S(1)} %bitcast.92), channel_id=1, replica_groups=mesh['gx'=8,'gy'=16] {'gx','gy'}, dimensions={0} | all-to-all | bytes 131072 | tf_op jit(solution)/shard_map/all_to_all | solution.py:473
  (43 shorter events, 11.0 us)
Async XLA Ops:
  0.6 0.7 copy-start.10
  0.6 0.7 copy-start.9
  1.3 1.0 copy-start
  2.3 1.0 copy-start.2
  3.3 0.9 copy-start.4
  4.3 0.9 copy-start.6
  7.4 11.6 %copy-start.8 = (s32[1,8,128]{2,1,0:T(8,128)S(1)}, s32[1,8,128]{2,1,0:T(8,128)}, u32[]{:S(2)}) copy-start(s32[1,8,128]{2,1,0:T(8,128)} %param.16) | copy-start | bytes 12292
  7.4 11.6 %copy-start.11 = (s32[256]{0:T(256)S(1)}, s32[256]{0:T(256)}, u32[]{:S(2)}) copy-start(s32[256]{0:T(256)} %param.17) | copy-start | bytes 3076
  7.4 11.6 %copy-start.12 = (f32[256]{0:T(256)S(1)}, f32[256]{0:T(256)}, u32[]{:S(2)}) copy-start(f32[256]{0:T(256)} %param.18) | copy-start | bytes 3076
  7.4 11.6 %copy-start.13 = (f32[256]{0:T(256)S(1)}, f32[256]{0:T(256)}, u32[]{:S(2)}) copy-start(f32[256]{0:T(256)} %param.19) | copy-start | bytes 3076
  7.4 37.8 %copy-start.3 = (bf16[9,20,8,128]{3,2,1,0:T(8,128)(2,1)S(1)}, bf16[9,20,8,128]{3,2,1,0:T(8,128)(2,1)}, u32[]{:S(2)}) copy-start(bf16[9,20,8,128]{3,2,1,0:T(8,128)(2,1)} %param.12) | copy-start | bytes 1105924
  7.5 37.8 %copy-start.7 = (bf16[3,20,8,128]{3,2,1,0:T(8,128)(2,1)S(1)}, bf16[3,20,8,128]{3,2,1,0:T(8,128)(2,1)}, u32[]{:S(2)}) copy-start(bf16[3,20,8,128]{3,2,1,0:T(8,128)(2,1)} %param.13) | copy-start | bytes 368644
  7.5 23.0 %all-to-all-start = ((f32[128,4,128]{2,1,0:T(4,128)}), f32[128,4,128]{2,1,0:T(4,128)S(1)}, u32[]{:S(2)}, u32[]{:S(2)}) async-start(f32[128,4,128]{2,1,0:T(4,128)} %bitcast.6), calls=%async_computation | async-start | bytes 524288 | tf_op jit(solution)/shard_map/all_to_all | solution.py:473
  19.0 26.3 %copy-start.1 = (bf16[9,20,8,128]{3,2,1,0:T(8,128)(2,1)S(1)}, bf16[9,20,8,128]{3,2,1,0:T(8,128)(2,1)}, u32[]{:S(2)}) copy-start(bf16[9,20,8,128]{3,2,1,0:T(8,128)(2,1)} %param.11) | copy-start | bytes 1105924
  30.4 14.8 %copy-start.5 = (f32[3,20,8,128]{3,2,1,0:T(8,128)S(1)}, f32[3,20,8,128]{3,2,1,0:T(8,128)}, u32[]{:S(2)}) copy-start(f32[3,20,8,128]{3,2,1,0:T(8,128)} %param.10) | copy-start | bytes 737284
  31.5 13.7 %all-to-all-start.1 = ((f32[128,1,128]{2,1,0:T(1,128)}), f32[128,1,128]{2,1,0:T(1,128)S(1)}, u32[]{:S(2)}, u32[]{:S(2)}) async-start(f32[128,1,128]{2,1,0:T(1,128)} %bitcast.13), calls=%async_computation.1 | async-start | bytes 131072 | tf_op jit(solution)/shard_map/all_to_all | solution.py:473
  35.5 2.7 %collective-permute-start = (f32[60,128]{1,0:T(8,128)S(1)}, f32[60,128]{1,0:T(8,128)S(1)}, u32[]{:S(2)}, u32[]{:S(2)}) collective-permute-start(f32[60,128]{1,0:T(8,128)S(1)} %get-tuple-element.76), channel_id=1, source_target_pairs={{0,16},{16,32},{32,48},{48,64},{64,80},{80,96},{96,112},{112,0},{1... | collective-permute-start | bytes 92168 | tf_op jit(solution)/shard_map/ppermute | solution.py:481
  37.2 3.7 %collective-permute-start.1 = (f32[60,128]{1,0:T(8,128)S(1)}, f32[60,128]{1,0:T(8,128)S(1)}, u32[]{:S(2)}, u32[]{:S(2)}) collective-permute-start(f32[60,128]{1,0:T(8,128)S(1)} %get-tuple-element.77), channel_id=1, source_target_pairs={{16,0},{32,16},{48,32},{64,48},{80,64},{96,80},{112,96},{0,112},{1... | collective-permute-start | bytes 92168 | tf_op jit(solution)/shard_map/ppermute | solution.py:482
  47.1 16.0 %all-to-all-start.2 = ((f32[128,4,128]{2,1,0:T(4,128)}), f32[128,4,128]{2,1,0:T(4,128)S(1)}, u32[]{:S(2)}, u32[]{:S(2)}) async-start(f32[128,4,128]{2,1,0:T(4,128)} %bitcast.15), calls=%async_computation.2 | async-start | bytes 524288 | tf_op jit(solution)/shard_map/all_to_all | solution.py:473
  51.5 3.0 %collective-permute-start.2 = (f32[60,128]{1,0:T(8,128)S(1)}, f32[60,128]{1,0:T(8,128)S(1)}, u32[]{:S(2)}, u32[]{:S(2)}) collective-permute-start(f32[60,128]{1,0:T(8,128)S(1)} %get-tuple-element.92), channel_id=1, source_target_pairs={{0,16},{16,32},{32,48},{48,64},{64,80},{80,96},{96,112},{112,0},{1... | collective-permute-start | bytes 92168 | tf_op jit(solution)/shard_map/ppermute | solution.py:481
  53.2 4.4 %collective-permute-start.3 = (f32[60,128]{1,0:T(8,128)S(1)}, f32[60,128]{1,0:T(8,128)S(1)}, u32[]{:S(2)}, u32[]{:S(2)}) collective-permute-start(f32[60,128]{1,0:T(8,128)S(1)} %get-tuple-element.93), channel_id=1, source_target_pairs={{16,0},{32,16},{48,32},{64,48},{80,64},{96,80},{112,96},{0,112},{1... | collective-permute-start | bytes 92168 | tf_op jit(solution)/shard_map/ppermute | solution.py:482
  64.8 15.5 %all-to-all-start.3 = ((f32[128,4,128]{2,1,0:T(4,128)}), f32[128,4,128]{2,1,0:T(4,128)S(1)}, u32[]{:S(2)}, u32[]{:S(2)}) async-start(f32[128,4,128]{2,1,0:T(4,128)} %bitcast.17), calls=%async_computation.3 | async-start | bytes 524288 | tf_op jit(solution)/shard_map/all_to_all | solution.py:473
  68.8 3.0 %collective-permute-start.4 = (f32[60,128]{1,0:T(8,128)S(1)}, f32[60,128]{1,0:T(8,128)S(1)}, u32[]{:S(2)}, u32[]{:S(2)}) collective-permute-start(f32[60,128]{1,0:T(8,128)S(1)} %get-tuple-element.99), channel_id=1, source_target_pairs={{0,16},{16,32},{32,48},{48,64},{64,80},{80,96},{96,112},{112,0},{1... | collective-permute-start | bytes 92168 | tf_op jit(solution)/shard_map/ppermute | solution.py:481
  70.5 4.4 %collective-permute-start.5 = (f32[60,128]{1,0:T(8,128)S(1)}, f32[60,128]{1,0:T(8,128)S(1)}, u32[]{:S(2)}, u32[]{:S(2)}) collective-permute-start(f32[60,128]{1,0:T(8,128)S(1)} %get-tuple-element.100), channel_id=1, source_target_pairs={{16,0},{32,16},{48,32},{64,48},{80,64},{96,80},{112,96},{0,112},{1... | collective-permute-start | bytes 92168 | tf_op jit(solution)/shard_map/ppermute | solution.py:482
  82.1 15.5 %all-to-all-start.4 = ((f32[128,4,128]{2,1,0:T(4,128)}), f32[128,4,128]{2,1,0:T(4,128)S(1)}, u32[]{:S(2)}, u32[]{:S(2)}) async-start(f32[128,4,128]{2,1,0:T(4,128)} %bitcast.19), calls=%async_computation.4 | async-start | bytes 524288 | tf_op jit(solution)/shard_map/all_to_all | solution.py:473
  86.1 3.0 %collective-permute-start.6 = (f32[60,128]{1,0:T(8,128)S(1)}, f32[60,128]{1,0:T(8,128)S(1)}, u32[]{:S(2)}, u32[]{:S(2)}) collective-permute-start(f32[60,128]{1,0:T(8,128)S(1)} %get-tuple-element.106), channel_id=1, source_target_pairs={{0,16},{16,32},{32,48},{48,64},{64,80},{80,96},{96,112},{112,0},{1... | collective-permute-start | bytes 92168 | tf_op jit(solution)/shard_map/ppermute | solution.py:481
  87.8 4.4 %collective-permute-start.7 = (f32[60,128]{1,0:T(8,128)S(1)}, f32[60,128]{1,0:T(8,128)S(1)}, u32[]{:S(2)}, u32[]{:S(2)}) collective-permute-start(f32[60,128]{1,0:T(8,128)S(1)} %get-tuple-element.107), channel_id=1, source_target_pairs={{16,0},{32,16},{48,32},{64,48},{80,64},{96,80},{112,96},{0,112},{1... | collective-permute-start | bytes 92168 | tf_op jit(solution)/shard_map/ppermute | solution.py:482
  99.6 15.5 %all-to-all-start.5 = ((f32[128,4,128]{2,1,0:T(4,128)}), f32[128,4,128]{2,1,0:T(4,128)S(1)}, u32[]{:S(2)}, u32[]{:S(2)}) async-start(f32[128,4,128]{2,1,0:T(4,128)} %bitcast.21), calls=%async_computation.5 | async-start | bytes 524288 | tf_op jit(solution)/shard_map/all_to_all | solution.py:473
  103.6 3.0 %collective-permute-start.8 = (f32[60,128]{1,0:T(8,128)S(1)}, f32[60,128]{1,0:T(8,128)S(1)}, u32[]{:S(2)}, u32[]{:S(2)}) collective-permute-start(f32[60,128]{1,0:T(8,128)S(1)} %get-tuple-element.114), channel_id=1, source_target_pairs={{0,16},{16,32},{32,48},{48,64},{64,80},{80,96},{96,112},{112,0},{1... | collective-permute-start | bytes 92168 | tf_op jit(solution)/shard_map/ppermute | solution.py:481
  105.3 4.4 %collective-permute-start.9 = (f32[60,128]{1,0:T(8,128)S(1)}, f32[60,128]{1,0:T(8,128)S(1)}, u32[]{:S(2)}, u32[]{:S(2)}) collective-permute-start(f32[60,128]{1,0:T(8,128)S(1)} %get-tuple-element.115), channel_id=1, source_target_pairs={{16,0},{32,16},{48,32},{64,48},{80,64},{96,80},{112,96},{0,112},{1... | collective-permute-start | bytes 92168 | tf_op jit(solution)/shard_map/ppermute | solution.py:482
  116.9 15.5 %all-to-all-start.6 = ((f32[128,4,128]{2,1,0:T(4,128)}), f32[128,4,128]{2,1,0:T(4,128)S(1)}, u32[]{:S(2)}, u32[]{:S(2)}) async-start(f32[128,4,128]{2,1,0:T(4,128)} %bitcast.23), calls=%async_computation.6 | async-start | bytes 524288 | tf_op jit(solution)/shard_map/all_to_all | solution.py:473
  120.9 3.0 %collective-permute-start.10 = (f32[60,128]{1,0:T(8,128)S(1)}, f32[60,128]{1,0:T(8,128)S(1)}, u32[]{:S(2)}, u32[]{:S(2)}) collective-permute-start(f32[60,128]{1,0:T(8,128)S(1)} %get-tuple-element.121), channel_id=1, source_target_pairs={{0,16},{16,32},{32,48},{48,64},{64,80},{80,96},{96,112},{112,0},{1... | collective-permute-start | bytes 92168 | tf_op jit(solution)/shard_map/ppermute | solution.py:481
  122.5 4.4 %collective-permute-start.11 = (f32[60,128]{1,0:T(8,128)S(1)}, f32[60,128]{1,0:T(8,128)S(1)}, u32[]{:S(2)}, u32[]{:S(2)}) collective-permute-start(f32[60,128]{1,0:T(8,128)S(1)} %get-tuple-element.122), channel_id=1, source_target_pairs={{16,0},{32,16},{48,32},{64,48},{80,64},{96,80},{112,96},{0,112},{1... | collective-permute-start | bytes 92168 | tf_op jit(solution)/shard_map/ppermute | solution.py:482
  134.2 15.5 %all-to-all-start.7 = ((f32[128,4,128]{2,1,0:T(4,128)}), f32[128,4,128]{2,1,0:T(4,128)S(1)}, u32[]{:S(2)}, u32[]{:S(2)}) async-start(f32[128,4,128]{2,1,0:T(4,128)} %bitcast.25), calls=%async_computation.7 | async-start | bytes 524288 | tf_op jit(solution)/shard_map/all_to_all | solution.py:473
  138.2 3.0 %collective-permute-start.12 = (f32[60,128]{1,0:T(8,128)S(1)}, f32[60,128]{1,0:T(8,128)S(1)}, u32[]{:S(2)}, u32[]{:S(2)}) collective-permute-start(f32[60,128]{1,0:T(8,128)S(1)} %get-tuple-element.128), channel_id=1, source_target_pairs={{0,16},{16,32},{32,48},{48,64},{64,80},{80,96},{96,112},{112,0},{1... | collective-permute-start | bytes 92168 | tf_op jit(solution)/shard_map/ppermute | solution.py:481
  139.8 4.4 %collective-permute-start.13 = (f32[60,128]{1,0:T(8,128)S(1)}, f32[60,128]{1,0:T(8,128)S(1)}, u32[]{:S(2)}, u32[]{:S(2)}) collective-permute-start(f32[60,128]{1,0:T(8,128)S(1)} %get-tuple-element.129), channel_id=1, source_target_pairs={{16,0},{32,16},{48,32},{64,48},{80,64},{96,80},{112,96},{0,112},{1... | collective-permute-start | bytes 92168 | tf_op jit(solution)/shard_map/ppermute | solution.py:482
  151.5 15.5 %all-to-all-start.8 = ((f32[128,4,128]{2,1,0:T(4,128)}), f32[128,4,128]{2,1,0:T(4,128)S(1)}, u32[]{:S(2)}, u32[]{:S(2)}) async-start(f32[128,4,128]{2,1,0:T(4,128)} %bitcast.27), calls=%async_computation.8 | async-start | bytes 524288 | tf_op jit(solution)/shard_map/all_to_all | solution.py:473
  155.5 3.0 %collective-permute-start.14 = (f32[60,128]{1,0:T(8,128)S(1)}, f32[60,128]{1,0:T(8,128)S(1)}, u32[]{:S(2)}, u32[]{:S(2)}) collective-permute-start(f32[60,128]{1,0:T(8,128)S(1)} %get-tuple-element.135), channel_id=1, source_target_pairs={{0,16},{16,32},{32,48},{48,64},{64,80},{80,96},{96,112},{112,0},{1... | collective-permute-start | bytes 92168 | tf_op jit(solution)/shard_map/ppermute | solution.py:481
  157.1 4.4 %collective-permute-start.15 = (f32[60,128]{1,0:T(8,128)S(1)}, f32[60,128]{1,0:T(8,128)S(1)}, u32[]{:S(2)}, u32[]{:S(2)}) collective-permute-start(f32[60,128]{1,0:T(8,128)S(1)} %get-tuple-element.136), channel_id=1, source_target_pairs={{16,0},{32,16},{48,32},{64,48},{80,64},{96,80},{112,96},{0,112},{1... | collective-permute-start | bytes 92168 | tf_op jit(solution)/shard_map/ppermute | solution.py:482

commit v4 on v3

--- a/solution.py
+++ b/solution.py
@@ -159,42 +159,20 @@
     rows = chunk(t)
     tx = trans[0, rows, :].astype(F32)
     for n, value in enumerate(mix(mobility, rows, values)):
-        weighted[n, pl.ds(8 + t * STEP, STEP), :] = value
+        weighted[n, rows, :] = value
         along[pl.ds(n * ROWS + t * STEP, STEP), :] = tx * value
 
 
-def interior(trans, weighted, along, near, toward_low, toward_high, message, pad):
+def send_borders(trans, weighted, along, toward_low, toward_high, message, pad):
     toward_low[...] = along[pl.ds(0, 3 * NZ, stride=CX), :]
     toward_high[...] = along[pl.ds(CX - 1, 3 * NZ, stride=CX), :]
-    lane = lanes((STEP, 128))
-    sub = subs((STEP, 128)) & 7
     small = lanes((8, 128))
     high = jnp.zeros((8, 128), F32)
     low = jnp.zeros((8, 128), F32)
-    for n in range(3):
-        weighted[n, 0:8, :] = jnp.zeros((8, 128), F32)
-        weighted[n, ROWS + 8 : ROWS + 16, :] = jnp.zeros((8, 128), F32)
-    up = [trans[2, chunk(t), :].astype(F32) for t in range(CHUNKS)]
     for t in range(CHUNKS):
-        rows = chunk(t)
-        tx, ty = [trans[n, rows, :].astype(F32) for n in range(2)]
-        tz = up[t]
-        zero = jnp.zeros((8, 128), F32)
-        below = jnp.concatenate([up[t - 1][8:16] if t else zero, tz[0:8]], axis=0)
-        above = jnp.concatenate([tz[8:16], up[t + 1][0:8] if t + 1 < CHUNKS else zero], axis=0)
+        ty = trans[1, chunk(t), :].astype(F32)
         for n in range(3):
-            px = along[pl.ds(n * ROWS + t * STEP, STEP), :]
-            py = ty * weighted[n, pl.ds(8 + t * STEP, STEP), :]
-            nx = jnp.where(sub == 0, 0.0, pltpu.roll(px, 1, 0)) + jnp.where(
-                sub == 7, 0.0, pltpu.roll(px, STEP - 1, 0)
-            )
-            ny = jnp.where(lane == 0, 0.0, pltpu.roll(py, 1, 1)) + jnp.where(
-                lane == 127, 0.0, pltpu.roll(py, 127, 1)
-            )
-            nz = below * weighted[n, pl.ds(t * STEP, STEP), :] + above * weighted[
-                n, pl.ds(t * STEP + 16, STEP), :
-            ]
-            near[n, rows, :] = tx * nx + ty * ny + tz * nz
+            py = ty * weighted[n, chunk(t), :]
             for half in range(2):
                 j = n * NZ + 2 * t + half
                 moved = pltpu.roll(py[8 * half : 8 * half + 8], j + 1, 1)
@@ -208,9 +186,38 @@
         message[rows, :] = jnp.where(mine, message[rows, :], packed)
 
 
+def interior(weighted, trans, near):
+    lane = lanes((STEP, 128))
+    sub = subs((STEP, 128)) & 7
+    zero = jnp.zeros((8, 128), F32)
+    up = [trans[2, chunk(t), :].astype(F32) for t in range(CHUNKS)]
+    for t in range(CHUNKS):
+        rows = chunk(t)
+        tx, ty = [trans[n, rows, :].astype(F32) for n in range(2)]
+        tz = up[t]
+        for n in range(3):
+            value = weighted[n, rows, :]
+            px, py = tx * value, ty * value
+            nx = jnp.where(sub == 0, 0.0, pltpu.roll(px, 1, 0)) + jnp.where(
+                sub == 7, 0.0, pltpu.roll(px, STEP - 1, 0)
+            )
+            ny = jnp.where(lane == 0, 0.0, pltpu.roll(py, 1, 1)) + jnp.where(
+                lane == 127, 0.0, pltpu.roll(py, 127, 1)
+            )
+            pz = tz * value
+            below = zero
+            above = zero
+            if t:
+                below = up[t - 1][8:16] * weighted[n, pl.ds(t * STEP - 8, 8), :]
+            if t + 1 < CHUNKS:
+                above = up[t + 1][0:8] * weighted[n, pl.ds(t * STEP + STEP, 8), :]
+            nz = jnp.concatenate([below + pz[8:16], pz[0:8] + above], axis=0)
+            near[n, rows, :] = tx * nx + ty * ny + tz * nz
+
+
 def cell_setup(rhs_in, diag_in, mobility_in, trans_in, cells_in, pi_in,
                rows_of, rows_to, start, weight, slots,
-               near, toward_low, toward_high, message, weighted, along, pad, forward,
+               weighted, toward_low, toward_high, message, along, pad, forward,
                rhs, diag, mobility, trans, cells, pi, sems):
     pairs = ((rhs_in, rhs), (diag_in, diag), (cells_in, cells), (pi_in, pi),
              (mobility_in, mobility), (trans_in, trans))
@@ -247,7 +254,7 @@
     message[block(1), :] = weights
     message[block(2), :] = jnp.zeros((PEERS, 128), F32)
     message[block(3), :] = jnp.zeros((PEERS, 128), F32)
-    interior(trans, weighted, along, near, toward_low, toward_high, message, pad)
+    send_borders(trans, weighted, along, toward_low, toward_high, message, pad)
 
 
 def well_tables(index, parent, trans, rhs, table, fixed):
@@ -295,7 +302,7 @@
 STEADY = ("rhs", "diag", "mobility", "trans", "rows_of", "rows_to", "start", "weight",
           "own_weight", "table", "index", "fixed", "diagonal")
 MOVING = ("arrived", "near", "from_low", "from_high", "slots", "at_slots", "state")
-NEXT = ("near", "toward_low", "toward_high", "message", "slots", "at_slots", "state")
+NEXT = ("weighted", "toward_low", "toward_high", "message", "slots", "at_slots", "state")
 MORE_IN = {
     "first": ("pressures",), "plain": (), "keep": (), "last": ("field",), "after": (),
     "final": ("field", "change", "seg_change", "omega"),
@@ -316,7 +323,8 @@
     fixed = {name: next(take) for name in STEADY}
     extra = {name: next(take) for name in MORE_IN[kind]}
     out = {name: next(take) for name in results_of(kind)}
-    weighted, along, pad, forward = take
+    along, pad, forward = take
+    weighted = out.get("weighted")
     final = kind == "final"
     gx, gy = lax.axis_index("gx"), lax.axis_index("gy")
 
@@ -416,9 +424,8 @@
     message[block(3), :] = jnp.zeros((PEERS, 128), F32)
     if kind == "after":
         out["omega"][...] = jnp.broadcast_to(ratio(arrived[block(2), :], 60), (8, 128))
-    interior(
-        fixed["trans"], weighted, along, out["near"], out["toward_low"], out["toward_high"],
-        message, pad,
+    send_borders(
+        fixed["trans"], weighted, along, out["toward_low"], out["toward_high"], message, pad
     )
 
 
@@ -443,19 +450,18 @@
 TILE = ((8, 128), F32)
 EDGE = ((3 * NZ, 128), F32)
 SHAPES = {
-    "near": CELLS, "toward_low": EDGE, "toward_high": EDGE, "message": MESSAGE, "slots": PAIRS,
+    "weighted": CELLS, "toward_low": EDGE, "toward_high": EDGE, "message": MESSAGE, "slots": PAIRS,
     "at_slots": TILE, "state": TILE, "omega": TILE, "field": CELLS, "change": CELLS,
     "seg_change": TILE,
 }
 SCRATCH = (
-    pltpu.VMEM((3, ROWS + 16, 128), F32),
     pltpu.VMEM((3 * ROWS, 128), F32),
     pltpu.VMEM((16, 128), F32),
     pltpu.VMEM((ROWS, 128), F32),
 )
 
 
-def call(body, outs, args, scratch=(), name=None, space=pltpu.VMEM):
+def call(body, outs, args, scratch=(), name=None, space=pltpu.VMEM, grant=24 * 1024 * 1024):
     moved = sum(a.size * a.dtype.itemsize for a in args)
     return pl.pallas_call(
         body,
@@ -463,7 +469,7 @@
         in_specs=[pl.BlockSpec(memory_space=space)] * len(args),
         out_specs=[pl.BlockSpec(memory_space=pltpu.VMEM)] * len(outs),
         scratch_shapes=list(scratch),
-        compiler_params=pltpu.CompilerParams(vmem_limit_bytes=24 * 1024 * 1024),
+        compiler_params=pltpu.CompilerParams(vmem_limit_bytes=grant),
         cost_estimate=pl.CostEstimate(flops=4_000_000, bytes_accessed=moved, transcendentals=0),
         name=name,
     )(*args)
@@ -494,7 +500,7 @@
 
     fixed = {"rhs": rhs, "diag": diag, "mobility": mobility, "trans": trans, "index": index}
     inputs = [rhs, diag, mobility, trans, perf_cell[0], perf_pi[0]]
-    (rows_of, rows_to, start, weight, slots, near, toward_low, toward_high, message) = call(
+    (rows_of, rows_to, start, weight, slots, weighted, toward_low, toward_high, message) = call(
         cell_setup,
         [((PEERS, ROWS), BF16), ((ROWS, PEERS), BF16),
          ((PEERS, 128), jnp.int32), PAIRS, PAIRS, CELLS, EDGE, EDGE, MESSAGE],
@@ -503,8 +509,13 @@
         + (pltpu.SemaphoreType.DMA((6,)),),
         name="cell_setup",
         space=pltpu.HBM,
+        grant=64 * 1024 * 1024 - 256 * 1024,
     )
     arrived = exchange(message)
+
+    def inside(weighted):
+        return call(interior, [CELLS], [weighted, trans], name="interior")[0]
+
     table, constants = call(
         well_tables,
         [((128, CAP * 128), BF16), ((4, 8, 128), F32)],
@@ -512,7 +523,7 @@
         name="well_tables",
     )
     fixed.update(rows_of=rows_of, rows_to=rows_to, start=start, weight=weight)
-    now = {"arrived": arrived, "near": near, "slots": slots}
+    now = {"arrived": arrived, "near": inside(weighted), "slots": slots}
     now.update(neighbours(toward_low, toward_high))
     message, own_weight, state, at_slots, diagonal = call(
         well_setup,
@@ -540,6 +551,7 @@
         out["arrived"] = exchange(out.pop("message"))
         if kind != "final":
             out.update(neighbours(out.pop("toward_low"), out.pop("toward_high")))
+            out["near"] = inside(out.pop("weighted"))
         return out
 
     now = advance("first", now)

time: 183 us -> 179 us (0.978)
  local copies, waits for them, and re-layouts: 4.55 us -> 0.73 us
  waiting for transfers between devices: 88.1 us -> 85.8 us
  Pallas kernels: 17.8 us -> 19.8 us
    unnamed x28 -> x32, local copies, waits for them, and re-layouts: 4.55 us -> 0.73 us
    pallas_call x12 -> x20, Pallas kernels: 17.8 us -> 19.8 us  [call(): pl.pallas_call(body, out_shape=[jax.ShapeDtypeStruct(*out) for out in out...]
  transfers between devices with their start and end apart: 25 -> 25, of which waited for: 25 -> 25; matrix products, arithmetic and copies ran while one was open for 0% -> 0% of each run, Pallas kernels for 0% -> 1%
where the time goes in v4:
time: 179 us; the launch traced here: 178 us
  waiting for transfers between devices  85.8 us (48%)
  starting transfers between devices  57.1 us (32%)
  Pallas kernels  19.8 us (11%)
  blocking collectives  13.6 us (8%)
    all_to_all x9, waiting for transfers between devices, exchange(): lax.all_to_all(message, AXES, split_axis=0, concat_axis=0, tiled=True)  53.2 us
    all_to_all x9, starting transfers between devices, exchange(): lax.all_to_all(message, AXES, split_axis=0, concat_axis=0, tiled=True)  43.9 us
    ppermute x8, waiting for transfers between devices, neighbours(): lax.ppermute(toward_low, 'gx', down)  24.3 us
    pallas_call x20, Pallas kernels, call(): pl.pallas_call(body, out_shape=[jax.ShapeDtypeStruct(*out) for out in out...  19.8 us
    all_to_all x1, blocking collectives, exchange(): lax.all_to_all(message, AXES, split_axis=0, concat_axis=0, tiled=True)  13.6 us
    ppermute x8, starting transfers between devices, neighbours(): lax.ppermute(toward_high, 'gx', up)  13.2 us
    ppermute x8, waiting for transfers between devices, neighbours(): lax.ppermute(toward_high, 'gx', up)  8.41 us
  transfers between devices with their start and end apart: 25, of which 25 were waited for; matrix products, arithmetic and copies ran while one was open for 0% of the time, Pallas kernels for 1%

profile of v4, /device:TPU:1, one launch (start us, length us, event | category | flops | bytes accessed | tf_op | source)
XLA Modules:
  0.0 178.1 jit_solution(14376536257117526215)
XLA Ops:
  0.6 2.6 %cell_setup.1 = (bf16[128,160]{1,0:T(8,128)(2,1)}, bf16[160,128]{1,0:T(8,128)(2,1)}, s32[128,128]{1,0:T(8,128)}, f32[128,128]{1,0:T(8,128)}, f32[128,128]{1,0:T(...) custom-call(f32[3,160,128]{2,1,0:T(8,128)} %bitcast.71, ...), custom_call_target="tpu_custom_call" | custom-call | flops 4000000 | bytes 1114112 | tf_op jit(solution)/shard_map/cell_setup/pallas_call | solution.py:466
  3.4 11.5 %all-to-all-start = ((f32[128,4,128]{2,1,0:T(4,128)}), f32[128,4,128]{2,1,0:T(4,128)S(1)}, u32[]{:S(2)}, u32[]{:S(2)}) async-start(f32[128,4,128]{2,1,0:T(4,128)} %bitcast.105), calls=%async_computation | async-start | bytes 524288 | tf_op jit(solution)/shard_map/all_to_all | solution.py:479
  15.7 10.6 %all-to-all-done = f32[128,4,128]{2,1,0:T(4,128)S(1)} async-done(((f32[128,4,128]{2,1,0:T(4,128)}), f32[128,4,128]{2,1,0:T(4,128)S(1)}, u32[]{:S(2)}, u32[]{:S(2)}) %all-to-all-start) | async-done | bytes 262176 | tf_op jit(solution)/shard_map/all_to_all | solution.py:479
  27.4 4.0 %all-to-all-start.1 = ((f32[128,1,128]{2,1,0:T(1,128)}), f32[128,1,128]{2,1,0:T(1,128)S(1)}, u32[]{:S(2)}, u32[]{:S(2)}) async-start(f32[128,1,128]{2,1,0:T(1,128)} %bitcast.13), calls=%async_computation.1 | async-start | bytes 131072 | tf_op jit(solution)/shard_map/all_to_all | solution.py:479
  31.4 1.6 collective-permute-start
  34.1 2.7 %collective-permute-done.1.refs_3_ = f32[60,128]{1,0:T(8,128)S(1)} collective-permute-done((f32[60,128]{1,0:T(8,128)S(1)}, f32[60,128]{1,0:T(8,128)S(1)}, u32[]{:S(2)}, u32[]{:S(2)}) %collective-permute-start.1) | collective-permute-done | bytes 30752 | tf_op jit(solution)/shard_map/ppermute | solution.py:488
  36.8 4.4 %all-to-all-done.1 = f32[128,1,128]{2,1,0:T(1,128)S(1)} async-done(((f32[128,1,128]{2,1,0:T(1,128)}), f32[128,1,128]{2,1,0:T(1,128)S(1)}, u32[]{:S(2)}, u32[]{:S(2)}) %all-to-all-start.1) | async-done | bytes 65568 | tf_op jit(solution)/shard_map/all_to_all | solution.py:479
  41.3 1.8 %sweep_first.1 = (f32[3,160,128]{2,1,0:T(8,128)S(1)}, f32[60,128]{1,0:T(8,128)S(1)}, f32[60,128]{1,0:T(8,128)S(1)}, f32[512,128]{1,0:T(8,128)}, f32[128,128]{1,0...) custom-call(f32[512,128]{1,0:T(8,128)S(1)} %bitcast.81, f32[3,160,128]{2,1,0:T(8,128)S(1)} %interior.8.refs_1_, ...), custom_call_target="tpu_custom_call" | custom-call | flops 4000000 | bytes 2318336 | tf_op jit(solution)/shard_map/sweep_first/pallas_call | solution.py:466
  43.1 4.4 %all-to-all-start.2 = ((f32[128,4,128]{2,1,0:T(4,128)}), f32[128,4,128]{2,1,0:T(4,128)S(1)}, u32[]{:S(2)}, u32[]{:S(2)}) async-start(f32[128,4,128]{2,1,0:T(4,128)} %bitcast.15), calls=%async_computation.2 | async-start | bytes 524288 | tf_op jit(solution)/shard_map/all_to_all | solution.py:479
  47.6 1.6 collective-permute-start.2
  49.4 1.1 collective-permute-done.2.refs_2_
  50.5 3.1 %collective-permute-done.3.refs_3_ = f32[60,128]{1,0:T(8,128)S(1)} collective-permute-done((f32[60,128]{1,0:T(8,128)S(1)}, f32[60,128]{1,0:T(8,128)S(1)}, u32[]{:S(2)}, u32[]{:S(2)}) %collective-permute-start.3) | collective-permute-done | bytes 30752 | tf_op jit(solution)/shard_map/ppermute | solution.py:488
  53.6 5.4 %all-to-all-done.2 = f32[128,4,128]{2,1,0:T(4,128)S(1)} async-done(((f32[128,4,128]{2,1,0:T(4,128)}), f32[128,4,128]{2,1,0:T(4,128)S(1)}, u32[]{:S(2)}, u32[]{:S(2)}) %all-to-all-start.2) | async-done | bytes 262176 | tf_op jit(solution)/shard_map/all_to_all | solution.py:479
  59.0 1.8 %sweep_plain.2 = (f32[3,160,128]{2,1,0:T(8,128)S(1)}, f32[60,128]{1,0:T(8,128)S(1)}, f32[60,128]{1,0:T(8,128)S(1)}, f32[512,128]{1,0:T(8,128)}, f32[128,128]{1,0...) custom-call(f32[512,128]{1,0:T(8,128)S(1)} %bitcast.85, f32[3,160,128]{2,1,0:T(8,128)S(1)} %interior.9.refs_1_, ...), custom_call_target="tpu_custom_call" | custom-call | flops 4000000 | bytes 2252800 | tf_op jit(solution)/shard_map/sweep_plain/pallas_call | solution.py:466
  60.8 4.0 %all-to-all-start.3 = ((f32[128,4,128]{2,1,0:T(4,128)}), f32[128,4,128]{2,1,0:T(4,128)S(1)}, u32[]{:S(2)}, u32[]{:S(2)}) async-start(f32[128,4,128]{2,1,0:T(4,128)} %bitcast.17), calls=%async_computation.3 | async-start | bytes 524288 | tf_op jit(solution)/shard_map/all_to_all | solution.py:479
  64.8 1.6 collective-permute-start.4
  66.7 1.1 collective-permute-done.4.refs_2_
  67.8 3.1 %collective-permute-done.5.refs_3_ = f32[60,128]{1,0:T(8,128)S(1)} collective-permute-done((f32[60,128]{1,0:T(8,128)S(1)}, f32[60,128]{1,0:T(8,128)S(1)}, u32[]{:S(2)}, u32[]{:S(2)}) %collective-permute-start.5) | collective-permute-done | bytes 30752 | tf_op jit(solution)/shard_map/ppermute | solution.py:488
  70.9 5.5 %all-to-all-done.3 = f32[128,4,128]{2,1,0:T(4,128)S(1)} async-done(((f32[128,4,128]{2,1,0:T(4,128)}), f32[128,4,128]{2,1,0:T(4,128)S(1)}, u32[]{:S(2)}, u32[]{:S(2)}) %all-to-all-start.3) | async-done | bytes 262176 | tf_op jit(solution)/shard_map/all_to_all | solution.py:479
  76.3 1.8 %sweep_keep.2 = (f32[3,160,128]{2,1,0:T(8,128)S(1)}, f32[60,128]{1,0:T(8,128)S(1)}, f32[60,128]{1,0:T(8,128)S(1)}, f32[512,128]{1,0:T(8,128)}, f32[128,128]{1,0:...) custom-call(f32[512,128]{1,0:T(8,128)S(1)} %bitcast.82, ...), custom_call_target="tpu_custom_call" | custom-call | flops 4000000 | bytes 2252800 | tf_op jit(solution)/shard_map/sweep_keep/pallas_call | solution.py:466
  78.1 4.0 %all-to-all-start.4 = ((f32[128,4,128]{2,1,0:T(4,128)}), f32[128,4,128]{2,1,0:T(4,128)S(1)}, u32[]{:S(2)}, u32[]{:S(2)}) async-start(f32[128,4,128]{2,1,0:T(4,128)} %bitcast.19), calls=%async_computation.4 | async-start | bytes 524288 | tf_op jit(solution)/shard_map/all_to_all | solution.py:479
  82.1 1.6 collective-permute-start.6
  84.0 1.1 collective-permute-done.6.refs_2_
  85.1 3.1 %collective-permute-done.7.refs_3_ = f32[60,128]{1,0:T(8,128)S(1)} collective-permute-done((f32[60,128]{1,0:T(8,128)S(1)}, f32[60,128]{1,0:T(8,128)S(1)}, u32[]{:S(2)}, u32[]{:S(2)}) %collective-permute-start.7) | collective-permute-done | bytes 30752 | tf_op jit(solution)/shard_map/ppermute | solution.py:488
  88.2 5.5 %all-to-all-done.4 = f32[128,4,128]{2,1,0:T(4,128)S(1)} async-done(((f32[128,4,128]{2,1,0:T(4,128)}), f32[128,4,128]{2,1,0:T(4,128)S(1)}, u32[]{:S(2)}, u32[]{:S(2)}) %all-to-all-start.4) | async-done | bytes 262176 | tf_op jit(solution)/shard_map/all_to_all | solution.py:479
  93.6 1.9 %sweep_last.1 = (f32[3,160,128]{2,1,0:T(8,128)S(1)}, f32[60,128]{1,0:T(8,128)S(1)}, f32[60,128]{1,0:T(8,128)S(1)}, f32[512,128]{1,0:T(8,128)}, f32[128,128]{1,0:...) custom-call(f32[512,128]{1,0:T(8,128)S(1)} %bitcast.83, ...), custom_call_target="tpu_custom_call" | custom-call | flops 4000000 | bytes 2498560 | tf_op jit(solution)/shard_map/sweep_last/pallas_call | solution.py:466
  95.5 4.0 %all-to-all-start.5 = ((f32[128,4,128]{2,1,0:T(4,128)}), f32[128,4,128]{2,1,0:T(4,128)S(1)}, u32[]{:S(2)}, u32[]{:S(2)}) async-start(f32[128,4,128]{2,1,0:T(4,128)} %bitcast.21), calls=%async_computation.5 | async-start | bytes 524288 | tf_op jit(solution)/shard_map/all_to_all | solution.py:479
  99.5 1.6 collective-permute-start.8
  101.4 1.1 collective-permute-done.8.refs_2_
  102.5 3.1 %collective-permute-done.9.refs_3_ = f32[60,128]{1,0:T(8,128)S(1)} collective-permute-done((f32[60,128]{1,0:T(8,128)S(1)}, f32[60,128]{1,0:T(8,128)S(1)}, u32[]{:S(2)}, u32[]{:S(2)}) %collective-permute-start.9) | collective-permute-done | bytes 30752 | tf_op jit(solution)/shard_map/ppermute | solution.py:488
  105.6 5.5 %all-to-all-done.5 = f32[128,4,128]{2,1,0:T(4,128)S(1)} async-done(((f32[128,4,128]{2,1,0:T(4,128)}), f32[128,4,128]{2,1,0:T(4,128)S(1)}, u32[]{:S(2)}, u32[]{:S(2)}) %all-to-all-start.5) | async-done | bytes 262176 | tf_op jit(solution)/shard_map/all_to_all | solution.py:479
  111.0 1.8 %sweep_after.1 = (f32[3,160,128]{2,1,0:T(8,128)S(1)}, f32[60,128]{1,0:T(8,128)S(1)}, f32[60,128]{1,0:T(8,128)S(1)}, f32[512,128]{1,0:T(8,128)}, f32[128,128]{1,0...) custom-call(f32[512,128]{1,0:T(8,128)S(1)} %bitcast.86, ...), custom_call_target="tpu_custom_call" | custom-call | flops 4000000 | bytes 2252800 | tf_op jit(solution)/shard_map/sweep_after/pallas_call | solution.py:466
  112.8 4.0 %all-to-all-start.6 = ((f32[128,4,128]{2,1,0:T(4,128)}), f32[128,4,128]{2,1,0:T(4,128)S(1)}, u32[]{:S(2)}, u32[]{:S(2)}) async-start(f32[128,4,128]{2,1,0:T(4,128)} %bitcast.23), calls=%async_computation.6 | async-start | bytes 524288 | tf_op jit(solution)/shard_map/all_to_all | solution.py:479
  116.8 1.6 collective-permute-start.10
  118.7 1.1 collective-permute-done.10.refs_2_
  119.8 3.0 %collective-permute-done.11.refs_3_ = f32[60,128]{1,0:T(8,128)S(1)} collective-permute-done((f32[60,128]{1,0:T(8,128)S(1)}, f32[60,128]{1,0:T(8,128)S(1)}, u32[]{:S(2)}, u32[]{:S(2)}) %collective-permute-start.11) | collective-permute-done | bytes 30752 | tf_op jit(solution)/shard_map/ppermute | solution.py:488
  122.8 5.5 %all-to-all-done.6 = f32[128,4,128]{2,1,0:T(4,128)S(1)} async-done(((f32[128,4,128]{2,1,0:T(4,128)}), f32[128,4,128]{2,1,0:T(4,128)S(1)}, u32[]{:S(2)}, u32[]{:S(2)}) %all-to-all-start.6) | async-done | bytes 262176 | tf_op jit(solution)/shard_map/all_to_all | solution.py:479
  128.3 1.8 %sweep_plain.3 = (f32[3,160,128]{2,1,0:T(8,128)S(1)}, f32[60,128]{1,0:T(8,128)S(1)}, f32[60,128]{1,0:T(8,128)S(1)}, f32[512,128]{1,0:T(8,128)}, f32[128,128]{1,0...) custom-call(f32[512,128]{1,0:T(8,128)S(1)} %bitcast.87, f32[3,160,128]{2,1,0:T(8,128)S(1)} %interior.13.refs_1_, ...), custom_call_target="tpu_custom_call" | custom-call | flops 4000000 | bytes 2252800 | tf_op jit(solution)/shard_map/sweep_plain/pallas_call | solution.py:466
  130.1 4.0 %all-to-all-start.7 = ((f32[128,4,128]{2,1,0:T(4,128)}), f32[128,4,128]{2,1,0:T(4,128)S(1)}, u32[]{:S(2)}, u32[]{:S(2)}) async-start(f32[128,4,128]{2,1,0:T(4,128)} %bitcast.25), calls=%async_computation.7 | async-start | bytes 524288 | tf_op jit(solution)/shard_map/all_to_all | solution.py:479
  134.1 1.6 collective-permute-start.12
  137.1 3.1 %collective-permute-done.13.refs_3_ = f32[60,128]{1,0:T(8,128)S(1)} collective-permute-done((f32[60,128]{1,0:T(8,128)S(1)}, f32[60,128]{1,0:T(8,128)S(1)}, u32[]{:S(2)}, u32[]{:S(2)}) %collective-permute-start.13) | collective-permute-done | bytes 30752 | tf_op jit(solution)/shard_map/ppermute | solution.py:488
  140.1 5.5 %all-to-all-done.7 = f32[128,4,128]{2,1,0:T(4,128)S(1)} async-done(((f32[128,4,128]{2,1,0:T(4,128)}), f32[128,4,128]{2,1,0:T(4,128)S(1)}, u32[]{:S(2)}, u32[]{:S(2)}) %all-to-all-start.7) | async-done | bytes 262176 | tf_op jit(solution)/shard_map/all_to_all | solution.py:479
  145.6 1.8 %sweep_keep.3 = (f32[3,160,128]{2,1,0:T(8,128)S(1)}, f32[60,128]{1,0:T(8,128)S(1)}, f32[60,128]{1,0:T(8,128)S(1)}, f32[512,128]{1,0:T(8,128)}, f32[128,128]{1,0:...) custom-call(f32[512,128]{1,0:T(8,128)S(1)} %bitcast.84, ...), custom_call_target="tpu_custom_call" | custom-call | flops 4000000 | bytes 2252800 | tf_op jit(solution)/shard_map/sweep_keep/pallas_call | solution.py:466
  147.4 4.0 %all-to-all-start.8 = ((f32[128,4,128]{2,1,0:T(4,128)}), f32[128,4,128]{2,1,0:T(4,128)S(1)}, u32[]{:S(2)}, u32[]{:S(2)}) async-start(f32[128,4,128]{2,1,0:T(4,128)} %bitcast.27), calls=%async_computation.8 | async-start | bytes 524288 | tf_op jit(solution)/shard_map/all_to_all | solution.py:479
  151.4 1.6 collective-permute-start.14
  154.4 3.1 %collective-permute-done.15.refs_3_ = f32[60,128]{1,0:T(8,128)S(1)} collective-permute-done((f32[60,128]{1,0:T(8,128)S(1)}, f32[60,128]{1,0:T(8,128)S(1)}, u32[]{:S(2)}, u32[]{:S(2)}) %collective-permute-start.15) | collective-permute-done | bytes 30752 | tf_op jit(solution)/shard_map/ppermute | solution.py:488
  157.5 5.5 %all-to-all-done.8 = f32[128,4,128]{2,1,0:T(4,128)S(1)} async-done(((f32[128,4,128]{2,1,0:T(4,128)}), f32[128,4,128]{2,1,0:T(4,128)S(1)}, u32[]{:S(2)}, u32[]{:S(2)}) %all-to-all-start.8) | async-done | bytes 262176 | tf_op jit(solution)/shard_map/all_to_all | solution.py:479
  163.7 13.6 %all_to_all.110 = f32[128,1,128]{2,1,0:T(1,128)S(1)} all-to-all(f32[128,1,128]{2,1,0:T(1,128)S(1)} %bitcast.100), channel_id=1, replica_groups=mesh['gx'=8,'gy'=16] {'gx','gy'}, dimensions={0} | all-to-all | bytes 131072 | tf_op jit(solution)/shard_map/all_to_all | solution.py:479
  (55 shorter events, 8.2 us)
Async XLA Ops:
  3.3 11.6 %copy-start.12 = (f32[256]{0:T(256)S(1)}, f32[256]{0:T(256)}, u32[]{:S(2)}) copy-start(f32[256]{0:T(256)} %param.18) | copy-start | bytes 3076
  3.3 11.6 %copy-start.13 = (f32[256]{0:T(256)S(1)}, f32[256]{0:T(256)}, u32[]{:S(2)}) copy-start(f32[256]{0:T(256)} %param.19) | copy-start | bytes 3076
  3.3 28.1 %copy-start.15 = (f32[60,128]{1,0:T(8,128)S(1)}, f32[60,128]{1,0:T(8,128)}, u32[]{:S(2)}) copy-start(f32[60,128]{1,0:T(8,128)} %get-tuple-element.76) | copy-start | bytes 92164
  3.3 29.8 %copy-start.14 = (f32[60,128]{1,0:T(8,128)S(1)}, f32[60,128]{1,0:T(8,128)}, u32[]{:S(2)}) copy-start(f32[60,128]{1,0:T(8,128)} %get-tuple-element.77) | copy-start | bytes 92164
  3.3 29.8 %copy-start.9 = (f32[3,160,128]{2,1,0:T(8,128)S(1)}, f32[3,160,128]{2,1,0:T(8,128)}, u32[]{:S(2)}) copy-start(f32[3,160,128]{2,1,0:T(8,128)} %get-tuple-element.75.weighted) | copy-start | bytes 737284
  3.3 37.9 %copy-start.7 = (bf16[160,128]{1,0:T(8,128)(2,1)S(1)}, bf16[160,128]{1,0:T(8,128)(2,1)}, u32[]{:S(2)}) copy-start(bf16[160,128]{1,0:T(8,128)(2,1)} %get-tuple-element.84.refs_12_) | copy-start | bytes 122884
  3.3 37.9 %copy-start.10 = (f32[128,128]{1,0:T(8,128)S(1)}, f32[128,128]{1,0:T(8,128)}, u32[]{:S(2)}) copy-start(f32[128,128]{1,0:T(8,128)} %get-tuple-element.78.refs_4_) | copy-start | bytes 196612
  3.4 23.0 %all-to-all-start = ((f32[128,4,128]{2,1,0:T(4,128)}), f32[128,4,128]{2,1,0:T(4,128)S(1)}, u32[]{:S(2)}, u32[]{:S(2)}) async-start(f32[128,4,128]{2,1,0:T(4,128)} %bitcast.105), calls=%async_computation | async-start | bytes 524288 | tf_op jit(solution)/shard_map/all_to_all | solution.py:479
  14.9 0.7 copy-start.8
  14.9 0.7 copy-start.11
  15.6 25.7 %copy-start.6 = (f32[128,128]{1,0:T(8,128)S(1)}, f32[128,128]{1,0:T(8,128)}, u32[]{:S(2)}) copy-start(f32[128,128]{1,0:T(8,128)} %get-tuple-element.86.refs_14_) | copy-start | bytes 196612
  26.3 14.9 %copy-start.2 = (bf16[9,20,8,128]{3,2,1,0:T(8,128)(2,1)S(1)}, bf16[9,20,8,128]{3,2,1,0:T(8,128)(2,1)}, u32[]{:S(2)}) copy-start(bf16[9,20,8,128]{3,2,1,0:T(8,128)(2,1)} %param.12) | copy-start | bytes 1105924
  26.3 14.9 %copy-start.4 = (bf16[128,160]{1,0:T(8,128)(2,1)S(1)}, bf16[128,160]{1,0:T(8,128)(2,1)}, u32[]{:S(2)}) copy-start(bf16[128,160]{1,0:T(8,128)(2,1)} %get-tuple-element.83.refs_11_) | copy-start | bytes 122884
  26.3 14.9 %copy-start.5 = (s32[128,128]{1,0:T(8,128)S(1)}, s32[128,128]{1,0:T(8,128)}, u32[]{:S(2)}) copy-start(s32[128,128]{1,0:T(8,128)} %get-tuple-element.85.refs_13_) | copy-start | bytes 196612
  27.4 5.7 %copy-start = (bf16[3,20,8,128]{3,2,1,0:T(8,128)(2,1)S(1)}, bf16[3,20,8,128]{3,2,1,0:T(8,128)(2,1)}, u32[]{:S(2)}) copy-start(bf16[3,20,8,128]{3,2,1,0:T(8,128)(2,1)} %param.13) | copy-start | bytes 368644
  27.4 13.9 %copy-start.1 = (bf16[9,20,8,128]{3,2,1,0:T(8,128)(2,1)S(1)}, bf16[9,20,8,128]{3,2,1,0:T(8,128)(2,1)}, u32[]{:S(2)}) copy-start(bf16[9,20,8,128]{3,2,1,0:T(8,128)(2,1)} %param.11) | copy-start | bytes 1105924
  27.4 13.8 %all-to-all-start.1 = ((f32[128,1,128]{2,1,0:T(1,128)}), f32[128,1,128]{2,1,0:T(1,128)S(1)}, u32[]{:S(2)}, u32[]{:S(2)}) async-start(f32[128,1,128]{2,1,0:T(1,128)} %bitcast.13), calls=%async_computation.1 | async-start | bytes 131072 | tf_op jit(solution)/shard_map/all_to_all | solution.py:479
  31.4 2.7 %collective-permute-start = (f32[60,128]{1,0:T(8,128)S(1)}, f32[60,128]{1,0:T(8,128)S(1)}, u32[]{:S(2)}, u32[]{:S(2)}) collective-permute-start(f32[60,128]{1,0:T(8,128)S(1)} %copy-done.15), channel_id=1, source_target_pairs={{0,16},{16,32},{32,48},{48,64},{64,80},{80,96},{96,112},{112,0},{1... | collective-permute-start | bytes 92168 | tf_op jit(solution)/shard_map/ppermute | solution.py:487
  33.1 3.7 %collective-permute-start.1 = (f32[60,128]{1,0:T(8,128)S(1)}, f32[60,128]{1,0:T(8,128)S(1)}, u32[]{:S(2)}, u32[]{:S(2)}) collective-permute-start(f32[60,128]{1,0:T(8,128)S(1)} %copy-done.14), channel_id=1, source_target_pairs={{16,0},{32,16},{48,32},{64,48},{80,64},{96,80},{112,96},{0,112},{1... | collective-permute-start | bytes 92168 | tf_op jit(solution)/shard_map/ppermute | solution.py:488
  33.1 8.2 %copy-start.3 = (f32[3,20,8,128]{3,2,1,0:T(8,128)S(1)}, f32[3,20,8,128]{3,2,1,0:T(8,128)}, u32[]{:S(2)}) copy-start(f32[3,20,8,128]{3,2,1,0:T(8,128)} %param.10) | copy-start | bytes 737284
  43.1 15.9 %all-to-all-start.2 = ((f32[128,4,128]{2,1,0:T(4,128)}), f32[128,4,128]{2,1,0:T(4,128)S(1)}, u32[]{:S(2)}, u32[]{:S(2)}) async-start(f32[128,4,128]{2,1,0:T(4,128)} %bitcast.15), calls=%async_computation.2 | async-start | bytes 524288 | tf_op jit(solution)/shard_map/all_to_all | solution.py:479
  47.6 3.0 %collective-permute-start.2 = (f32[60,128]{1,0:T(8,128)S(1)}, f32[60,128]{1,0:T(8,128)S(1)}, u32[]{:S(2)}, u32[]{:S(2)}) collective-permute-start(f32[60,128]{1,0:T(8,128)S(1)} %get-tuple-element.92), channel_id=1, source_target_pairs={{0,16},{16,32},{32,48},{48,64},{64,80},{80,96},{96,112},{112,0},{1... | collective-permute-start | bytes 92168 | tf_op jit(solution)/shard_map/ppermute | solution.py:487
  49.2 4.4 %collective-permute-start.3 = (f32[60,128]{1,0:T(8,128)S(1)}, f32[60,128]{1,0:T(8,128)S(1)}, u32[]{:S(2)}, u32[]{:S(2)}) collective-permute-start(f32[60,128]{1,0:T(8,128)S(1)} %get-tuple-element.93), channel_id=1, source_target_pairs={{16,0},{32,16},{48,32},{64,48},{80,64},{96,80},{112,96},{0,112},{1... | collective-permute-start | bytes 92168 | tf_op jit(solution)/shard_map/ppermute | solution.py:488
  60.8 15.5 %all-to-all-start.3 = ((f32[128,4,128]{2,1,0:T(4,128)}), f32[128,4,128]{2,1,0:T(4,128)S(1)}, u32[]{:S(2)}, u32[]{:S(2)}) async-start(f32[128,4,128]{2,1,0:T(4,128)} %bitcast.17), calls=%async_computation.3 | async-start | bytes 524288 | tf_op jit(solution)/shard_map/all_to_all | solution.py:479
  64.8 3.0 %collective-permute-start.4 = (f32[60,128]{1,0:T(8,128)S(1)}, f32[60,128]{1,0:T(8,128)S(1)}, u32[]{:S(2)}, u32[]{:S(2)}) collective-permute-start(f32[60,128]{1,0:T(8,128)S(1)} %get-tuple-element.99), channel_id=1, source_target_pairs={{0,16},{16,32},{32,48},{48,64},{64,80},{80,96},{96,112},{112,0},{1... | collective-permute-start | bytes 92168 | tf_op jit(solution)/shard_map/ppermute | solution.py:487
  66.5 4.4 %collective-permute-start.5 = (f32[60,128]{1,0:T(8,128)S(1)}, f32[60,128]{1,0:T(8,128)S(1)}, u32[]{:S(2)}, u32[]{:S(2)}) collective-permute-start(f32[60,128]{1,0:T(8,128)S(1)} %get-tuple-element.100), channel_id=1, source_target_pairs={{16,0},{32,16},{48,32},{64,48},{80,64},{96,80},{112,96},{0,112},{1... | collective-permute-start | bytes 92168 | tf_op jit(solution)/shard_map/ppermute | solution.py:488
  78.1 15.5 %all-to-all-start.4 = ((f32[128,4,128]{2,1,0:T(4,128)}), f32[128,4,128]{2,1,0:T(4,128)S(1)}, u32[]{:S(2)}, u32[]{:S(2)}) async-start(f32[128,4,128]{2,1,0:T(4,128)} %bitcast.19), calls=%async_computation.4 | async-start | bytes 524288 | tf_op jit(solution)/shard_map/all_to_all | solution.py:479
  82.1 3.0 %collective-permute-start.6 = (f32[60,128]{1,0:T(8,128)S(1)}, f32[60,128]{1,0:T(8,128)S(1)}, u32[]{:S(2)}, u32[]{:S(2)}) collective-permute-start(f32[60,128]{1,0:T(8,128)S(1)} %get-tuple-element.106), channel_id=1, source_target_pairs={{0,16},{16,32},{32,48},{48,64},{64,80},{80,96},{96,112},{112,0},{1... | collective-permute-start | bytes 92168 | tf_op jit(solution)/shard_map/ppermute | solution.py:487
  83.8 4.4 %collective-permute-start.7 = (f32[60,128]{1,0:T(8,128)S(1)}, f32[60,128]{1,0:T(8,128)S(1)}, u32[]{:S(2)}, u32[]{:S(2)}) collective-permute-start(f32[60,128]{1,0:T(8,128)S(1)} %get-tuple-element.107), channel_id=1, source_target_pairs={{16,0},{32,16},{48,32},{64,48},{80,64},{96,80},{112,96},{0,112},{1... | collective-permute-start | bytes 92168 | tf_op jit(solution)/shard_map/ppermute | solution.py:488
  95.5 15.5 %all-to-all-start.5 = ((f32[128,4,128]{2,1,0:T(4,128)}), f32[128,4,128]{2,1,0:T(4,128)S(1)}, u32[]{:S(2)}, u32[]{:S(2)}) async-start(f32[128,4,128]{2,1,0:T(4,128)} %bitcast.21), calls=%async_computation.5 | async-start | bytes 524288 | tf_op jit(solution)/shard_map/all_to_all | solution.py:479
  99.5 3.0 %collective-permute-start.8 = (f32[60,128]{1,0:T(8,128)S(1)}, f32[60,128]{1,0:T(8,128)S(1)}, u32[]{:S(2)}, u32[]{:S(2)}) collective-permute-start(f32[60,128]{1,0:T(8,128)S(1)} %get-tuple-element.114), channel_id=1, source_target_pairs={{0,16},{16,32},{32,48},{48,64},{64,80},{80,96},{96,112},{112,0},{1... | collective-permute-start | bytes 92168 | tf_op jit(solution)/shard_map/ppermute | solution.py:487
  101.2 4.4 %collective-permute-start.9 = (f32[60,128]{1,0:T(8,128)S(1)}, f32[60,128]{1,0:T(8,128)S(1)}, u32[]{:S(2)}, u32[]{:S(2)}) collective-permute-start(f32[60,128]{1,0:T(8,128)S(1)} %get-tuple-element.115), channel_id=1, source_target_pairs={{16,0},{32,16},{48,32},{64,48},{80,64},{96,80},{112,96},{0,112},{1... | collective-permute-start | bytes 92168 | tf_op jit(solution)/shard_map/ppermute | solution.py:488
  112.8 15.5 %all-to-all-start.6 = ((f32[128,4,128]{2,1,0:T(4,128)}), f32[128,4,128]{2,1,0:T(4,128)S(1)}, u32[]{:S(2)}, u32[]{:S(2)}) async-start(f32[128,4,128]{2,1,0:T(4,128)} %bitcast.23), calls=%async_computation.6 | async-start | bytes 524288 | tf_op jit(solution)/shard_map/all_to_all | solution.py:479
  116.8 3.0 %collective-permute-start.10 = (f32[60,128]{1,0:T(8,128)S(1)}, f32[60,128]{1,0:T(8,128)S(1)}, u32[]{:S(2)}, u32[]{:S(2)}) collective-permute-start(f32[60,128]{1,0:T(8,128)S(1)} %get-tuple-element.121), channel_id=1, source_target_pairs={{0,16},{16,32},{32,48},{48,64},{64,80},{80,96},{96,112},{112,0},{1... | collective-permute-start | bytes 92168 | tf_op jit(solution)/shard_map/ppermute | solution.py:487
  118.5 4.4 %collective-permute-start.11 = (f32[60,128]{1,0:T(8,128)S(1)}, f32[60,128]{1,0:T(8,128)S(1)}, u32[]{:S(2)}, u32[]{:S(2)}) collective-permute-start(f32[60,128]{1,0:T(8,128)S(1)} %get-tuple-element.122), channel_id=1, source_target_pairs={{16,0},{32,16},{48,32},{64,48},{80,64},{96,80},{112,96},{0,112},{1... | collective-permute-start | bytes 92168 | tf_op jit(solution)/shard_map/ppermute | solution.py:488
  130.1 15.5 %all-to-all-start.7 = ((f32[128,4,128]{2,1,0:T(4,128)}), f32[128,4,128]{2,1,0:T(4,128)S(1)}, u32[]{:S(2)}, u32[]{:S(2)}) async-start(f32[128,4,128]{2,1,0:T(4,128)} %bitcast.25), calls=%async_computation.7 | async-start | bytes 524288 | tf_op jit(solution)/shard_map/all_to_all | solution.py:479
  134.1 3.0 %collective-permute-start.12 = (f32[60,128]{1,0:T(8,128)S(1)}, f32[60,128]{1,0:T(8,128)S(1)}, u32[]{:S(2)}, u32[]{:S(2)}) collective-permute-start(f32[60,128]{1,0:T(8,128)S(1)} %get-tuple-element.128), channel_id=1, source_target_pairs={{0,16},{16,32},{32,48},{48,64},{64,80},{80,96},{96,112},{112,0},{1... | collective-permute-start | bytes 92168 | tf_op jit(solution)/shard_map/ppermute | solution.py:487
  135.8 4.4 %collective-permute-start.13 = (f32[60,128]{1,0:T(8,128)S(1)}, f32[60,128]{1,0:T(8,128)S(1)}, u32[]{:S(2)}, u32[]{:S(2)}) collective-permute-start(f32[60,128]{1,0:T(8,128)S(1)} %get-tuple-element.129), channel_id=1, source_target_pairs={{16,0},{32,16},{48,32},{64,48},{80,64},{96,80},{112,96},{0,112},{1... | collective-permute-start | bytes 92168 | tf_op jit(solution)/shard_map/ppermute | solution.py:488
  147.4 15.5 %all-to-all-start.8 = ((f32[128,4,128]{2,1,0:T(4,128)}), f32[128,4,128]{2,1,0:T(4,128)S(1)}, u32[]{:S(2)}, u32[]{:S(2)}) async-start(f32[128,4,128]{2,1,0:T(4,128)} %bitcast.27), calls=%async_computation.8 | async-start | bytes 524288 | tf_op jit(solution)/shard_map/all_to_all | solution.py:479
  151.4 3.0 %collective-permute-start.14 = (f32[60,128]{1,0:T(8,128)S(1)}, f32[60,128]{1,0:T(8,128)S(1)}, u32[]{:S(2)}, u32[]{:S(2)}) collective-permute-start(f32[60,128]{1,0:T(8,128)S(1)} %get-tuple-element.135), channel_id=1, source_target_pairs={{0,16},{16,32},{32,48},{48,64},{64,80},{80,96},{96,112},{112,0},{1... | collective-permute-start | bytes 92168 | tf_op jit(solution)/shard_map/ppermute | solution.py:487
  153.1 4.4 %collective-permute-start.15 = (f32[60,128]{1,0:T(8,128)S(1)}, f32[60,128]{1,0:T(8,128)S(1)}, u32[]{:S(2)}, u32[]{:S(2)}) collective-permute-start(f32[60,128]{1,0:T(8,128)S(1)} %get-tuple-element.136), channel_id=1, source_target_pairs={{16,0},{32,16},{48,32},{64,48},{80,64},{96,80},{112,96},{0,112},{1... | collective-permute-start | bytes 92168 | tf_op jit(solution)/shard_map/ppermute | solution.py:488

commit v5 on v4

--- a/solution.py
+++ b/solution.py
@@ -106,6 +106,11 @@
 
 def block(n):
     return pl.ds(n, PEERS, stride=4)
+
+
+def halves(x):
+    high = x.astype(BF16).astype(F32)
+    return high, x - high
 
 
 def chunk(t):
@@ -307,6 +312,7 @@
     "first": ("pressures",), "plain": (), "keep": (), "last": ("field",), "after": (),
     "final": ("field", "change", "seg_change", "omega"),
 }
+NARROW = ("first", "plain", "keep", "after")
 MORE_OUT = {
     "first": (), "plain": (), "keep": ("field",), "last": ("change", "seg_change"),
     "after": ("omega",), "final": (),
@@ -323,13 +329,21 @@
     fixed = {name: next(take) for name in STEADY}
     extra = {name: next(take) for name in MORE_IN[kind]}
     out = {name: next(take) for name in results_of(kind)}
-    along, pad, forward = take
+    along, pad, forward, wide = take
+    narrow = kind in NARROW
     weighted = out.get("weighted")
     final = kind == "final"
     gx, gy = lax.axis_index("gx"), lax.axis_index("gy")
 
     arrived = now["arrived"]
-    pressures = extra["pressures"][...] if kind == "first" else arrived[block(1), :]
+    if arrived.dtype == BF16:
+        wide[...] = arrived[...].astype(F32)
+        arrived = wide
+        pressures = arrived[block(1), :] + arrived[block(3), :]
+        heads = arrived[block(0), :] + arrived[block(2), :]
+    else:
+        pressures = extra["pressures"][...] if kind == "first" else arrived[block(1), :]
+        heads = arrived[block(0), :]
     pull = fixed["weight"][...] * (now["slots"][...] - pressures)
     perforated = into_cells(fixed["rows_to"][...], fixed["start"][...], pull)
 
@@ -341,7 +355,7 @@
 
     state = now["state"][...]
     linked, across, source = [fixed["fixed"][n] for n in range(3)]
-    push = fixed["own_weight"][...] * (to_rows(arrived[block(0), :]) - now["at_slots"][...])
+    push = fixed["own_weight"][...] * (to_rows(heads) - now["at_slots"][...])
     number = fixed["index"][...]
     inflow = into_segments(push, number, fixed["table"][...])
     flux = across * (state - linked * previous(state))
@@ -409,24 +423,29 @@
         if final:
             out["message"][...] = sums
             return
-    else:
-        sums = jnp.zeros((PEERS, 128), F32)
-    message = out["message"]
+    if kind == "after":
+        out["omega"][...] = jnp.broadcast_to(ratio(arrived[block(2), :], 60), (8, 128))
+    message = wide if narrow else out["message"]
     advanced = state + seg_res / fixed["diagonal"][...]
     out["state"][...] = advanced
     values = segment_values(advanced, number)
     out["at_slots"][...] = values
     cells = slot_values(fixed["rows_of"][...], fixed["start"][...], forward[...])
     out["slots"][...] = cells
-    message[block(0), :] = cells
-    message[block(1), :] = to_columns(values)
-    message[block(2), :] = sums
-    message[block(3), :] = jnp.zeros((PEERS, 128), F32)
-    if kind == "after":
-        out["omega"][...] = jnp.broadcast_to(ratio(arrived[block(2), :], 60), (8, 128))
+    columns = to_columns(values)
+    if narrow:
+        message[block(0), :], message[block(2), :] = halves(cells)
+        message[block(1), :], message[block(3), :] = halves(columns)
+    else:
+        message[block(0), :] = cells
+        message[block(1), :] = columns
+        message[block(2), :] = sums
+        message[block(3), :] = jnp.zeros((PEERS, 128), F32)
     send_borders(
         fixed["trans"], weighted, along, out["toward_low"], out["toward_high"], message, pad
     )
+    if narrow:
+        out["message"][...] = message[...].astype(BF16)
 
 
 def finish(arrived, omega, field_one, field_two, state_one, state_two, cells, segments):
@@ -454,6 +473,16 @@
     "at_slots": TILE, "state": TILE, "omega": TILE, "field": CELLS, "change": CELLS,
     "seg_change": TILE,
 }
+
+
+def shape_of(kind, name):
+    if name != "message":
+        return SHAPES[name]
+    if kind == "final":
+        return PAIRS
+    return (MESSAGE[0], BF16) if kind in NARROW else MESSAGE
+
+
 SCRATCH = (
     pltpu.VMEM((3 * ROWS, 128), F32),
     pltpu.VMEM((16, 128), F32),
@@ -542,9 +571,9 @@
         names = results_of(kind)
         out = call(
             functools.partial(sweep, kind),
-            [PAIRS if kind == "final" else SHAPES[name] for name in names],
+            [shape_of(kind, name) for name in names],
             args,
-            SCRATCH,
+            SCRATCH + (pltpu.VMEM(*MESSAGE),),
             name="sweep_" + kind,
         )
         out = dict(zip(names, out))

time: 179 us -> 171 us (0.955)
  waiting for transfers between devices: 85.8 us -> 78.2 us
    all_to_all x9, waiting for transfers between devices: 53.2 us -> 48.3 us  [exchange(): lax.all_to_all(message, AXES, split_axis=0, concat_axis=0, tiled=True)]
where the time goes in v5:
time: 171 us; the launch traced here: 170 us
  waiting for transfers between devices  78.2 us (46%)
  starting transfers between devices  57.2 us (33%)
  Pallas kernels  19.6 us (11%)
  blocking collectives  13.6 us (8%)
    all_to_all x9, waiting for transfers between devices, exchange(): lax.all_to_all(message, AXES, split_axis=0, concat_axis=0, tiled=True)  48.3 us
    all_to_all x9, starting transfers between devices, exchange(): lax.all_to_all(message, AXES, split_axis=0, concat_axis=0, tiled=True)  44 us
    ppermute x8, waiting for transfers between devices, neighbours(): lax.ppermute(toward_low, 'gx', down)  23.2 us
    pallas_call x20, Pallas kernels, call(): pl.pallas_call(body, out_shape=[jax.ShapeDtypeStruct(*out) for out in out...  19.6 us
    all_to_all x1, blocking collectives, exchange(): lax.all_to_all(message, AXES, split_axis=0, concat_axis=0, tiled=True)  13.6 us
    ppermute x8, starting transfers between devices, neighbours(): lax.ppermute(toward_high, 'gx', up)  13.2 us
    ppermute x8, waiting for transfers between devices, neighbours(): lax.ppermute(toward_high, 'gx', up)  6.63 us
  transfers between devices with their start and end apart: 25, of which 25 were waited for; matrix products, arithmetic and copies ran while one was open for 0% of the time, Pallas kernels for 1%

profile of v5, /device:TPU:1, one launch (start us, length us, event | category | flops | bytes accessed | tf_op | source)
XLA Modules:
  0.0 170.2 jit_solution(15325394097730084245)
XLA Ops:
  0.6 2.6 %cell_setup.1 = (bf16[128,160]{1,0:T(8,128)(2,1)}, bf16[160,128]{1,0:T(8,128)(2,1)}, s32[128,128]{1,0:T(8,128)}, f32[128,128]{1,0:T(8,128)}, f32[128,128]{1,0:T(...) custom-call(f32[3,160,128]{2,1,0:T(8,128)} %bitcast.71, ...), custom_call_target="tpu_custom_call" | custom-call | flops 4000000 | bytes 1114112 | tf_op jit(solution)/shard_map/cell_setup/pallas_call | solution.py:495
  3.4 11.5 %all-to-all-start = ((f32[128,4,128]{2,1,0:T(4,128)}), f32[128,4,128]{2,1,0:T(4,128)S(1)}, u32[]{:S(2)}, u32[]{:S(2)}) async-start(f32[128,4,128]{2,1,0:T(4,128)} %bitcast.105), calls=%async_computation | async-start | bytes 524288 | tf_op jit(solution)/shard_map/all_to_all | solution.py:508
  15.7 10.6 %all-to-all-done = f32[128,4,128]{2,1,0:T(4,128)S(1)} async-done(((f32[128,4,128]{2,1,0:T(4,128)}), f32[128,4,128]{2,1,0:T(4,128)S(1)}, u32[]{:S(2)}, u32[]{:S(2)}) %all-to-all-start) | async-done | bytes 262176 | tf_op jit(solution)/shard_map/all_to_all | solution.py:508
  26.3 1.1 well_setup.1
  27.4 4.0 %all-to-all-start.1 = ((f32[128,1,128]{2,1,0:T(1,128)}), f32[128,1,128]{2,1,0:T(1,128)S(1)}, u32[]{:S(2)}, u32[]{:S(2)}) async-start(f32[128,1,128]{2,1,0:T(1,128)} %bitcast.13), calls=%async_computation.1 | async-start | bytes 131072 | tf_op jit(solution)/shard_map/all_to_all | solution.py:508
  31.4 1.6 collective-permute-start
  34.1 2.7 %collective-permute-done.1.refs_3_ = f32[60,128]{1,0:T(8,128)S(1)} collective-permute-done((f32[60,128]{1,0:T(8,128)S(1)}, f32[60,128]{1,0:T(8,128)S(1)}, u32[]{:S(2)}, u32[]{:S(2)}) %collective-permute-start.1) | collective-permute-done | bytes 30752 | tf_op jit(solution)/shard_map/ppermute | solution.py:517
  36.8 4.4 %all-to-all-done.1 = f32[128,1,128]{2,1,0:T(1,128)S(1)} async-done(((f32[128,1,128]{2,1,0:T(1,128)}), f32[128,1,128]{2,1,0:T(1,128)S(1)}, u32[]{:S(2)}, u32[]{:S(2)}) %all-to-all-start.1) | async-done | bytes 65568 | tf_op jit(solution)/shard_map/all_to_all | solution.py:508
  41.3 1.8 %sweep_first.1 = (f32[3,160,128]{2,1,0:T(8,128)S(1)}, f32[60,128]{1,0:T(8,128)S(1)}, f32[60,128]{1,0:T(8,128)S(1)}, bf16[512,128]{1,0:T(8,128)(2,1)}, f32[128,12...) custom-call(f32[512,128]{1,0:T(8,128)S(1)} %bitcast.81, f32[3,160,128]{2,1,0:T(8,128)S(1)} %interior.8.refs_1_, ...), custom_call_target="tpu_custom_call" | custom-call | flops 4000000 | bytes 2318336 | tf_op jit(solution)/shard_map/sweep_first/pallas_call | solution.py:495
  43.0 4.4 %all-to-all-start.2 = ((bf16[128,4,128]{2,1,0:T(4,128)(2,1)}), bf16[128,4,128]{2,1,0:T(4,128)(2,1)S(1)}, u32[]{:S(2)}, u32[]{:S(2)}) async-start(bf16[128,4,128]{2,1,0:T(4,128)(2,1)} %bitcast.15), calls=%async_computation.2 | async-start | bytes 262144 | tf_op jit(solution)/shard_map/all_to_all | solution.py:508
  47.5 1.6 collective-permute-start.2
  49.4 0.8 collective-permute-done.2.refs_2_
  50.2 2.9 %collective-permute-done.3.refs_3_ = f32[60,128]{1,0:T(8,128)S(1)} collective-permute-done((f32[60,128]{1,0:T(8,128)S(1)}, f32[60,128]{1,0:T(8,128)S(1)}, u32[]{:S(2)}, u32[]{:S(2)}) %collective-permute-start.3) | collective-permute-done | bytes 30752 | tf_op jit(solution)/shard_map/ppermute | solution.py:517
  53.1 4.6 %all-to-all-done.2 = bf16[128,4,128]{2,1,0:T(4,128)(2,1)S(1)} async-done(((bf16[128,4,128]{2,1,0:T(4,128)(2,1)}), bf16[128,4,128]{2,1,0:T(4,128)(2,1)S(1)}, u32[]{:S(2)}, u32[]{:S(2)}) %all-to-all-start.2) | async-done | bytes 131104 | tf_op jit(solution)/shard_map/all_to_all | solution.py:508
  57.7 1.8 %sweep_plain.2 = (f32[3,160,128]{2,1,0:T(8,128)S(1)}, f32[60,128]{1,0:T(8,128)S(1)}, f32[60,128]{1,0:T(8,128)S(1)}, bf16[512,128]{1,0:T(8,128)(2,1)}, f32[128,12...) custom-call(bf16[512,128]{1,0:T(8,128)(2,1)S(1)} %bitcast.86, f32[3,160,128]{2,1,0:T(8,128)S(1)} %interior.9.refs_1_, ...), custom_call_target="tpu_custom_call" | custom-call | flops 4000000 | bytes 2121728 | tf_op jit(solution)/shard_map/sweep_plain/pallas_call | solution.py:495
  59.5 4.0 %all-to-all-start.3 = ((bf16[128,4,128]{2,1,0:T(4,128)(2,1)}), bf16[128,4,128]{2,1,0:T(4,128)(2,1)S(1)}, u32[]{:S(2)}, u32[]{:S(2)}) async-start(bf16[128,4,128]{2,1,0:T(4,128)(2,1)} %bitcast.17), calls=%async_computation.3 | async-start | bytes 262144 | tf_op jit(solution)/shard_map/all_to_all | solution.py:508
  63.5 1.6 collective-permute-start.4
  66.2 2.9 %collective-permute-done.5.refs_3_ = f32[60,128]{1,0:T(8,128)S(1)} collective-permute-done((f32[60,128]{1,0:T(8,128)S(1)}, f32[60,128]{1,0:T(8,128)S(1)}, u32[]{:S(2)}, u32[]{:S(2)}) %collective-permute-start.5) | collective-permute-done | bytes 30752 | tf_op jit(solution)/shard_map/ppermute | solution.py:517
  69.1 4.6 %all-to-all-done.3 = bf16[128,4,128]{2,1,0:T(4,128)(2,1)S(1)} async-done(((bf16[128,4,128]{2,1,0:T(4,128)(2,1)}), bf16[128,4,128]{2,1,0:T(4,128)(2,1)S(1)}, u32[]{:S(2)}, u32[]{:S(2)}) %all-to-all-start.3) | async-done | bytes 131104 | tf_op jit(solution)/shard_map/all_to_all | solution.py:508
  73.7 1.8 %sweep_keep.2 = (f32[3,160,128]{2,1,0:T(8,128)S(1)}, f32[60,128]{1,0:T(8,128)S(1)}, f32[60,128]{1,0:T(8,128)S(1)}, bf16[512,128]{1,0:T(8,128)(2,1)}, f32[128,128...) custom-call(bf16[512,128]{1,0:T(8,128)(2,1)S(1)} %bitcast.83, ...), custom_call_target="tpu_custom_call" | custom-call | flops 4000000 | bytes 2121728 | tf_op jit(solution)/shard_map/sweep_keep/pallas_call | solution.py:495
  75.4 4.0 %all-to-all-start.4 = ((bf16[128,4,128]{2,1,0:T(4,128)(2,1)}), bf16[128,4,128]{2,1,0:T(4,128)(2,1)S(1)}, u32[]{:S(2)}, u32[]{:S(2)}) async-start(bf16[128,4,128]{2,1,0:T(4,128)(2,1)} %bitcast.19), calls=%async_computation.4 | async-start | bytes 262144 | tf_op jit(solution)/shard_map/all_to_all | solution.py:508
  79.5 1.6 collective-permute-start.6
  81.3 0.8 collective-permute-done.6.refs_2_
  82.1 2.9 %collective-permute-done.7.refs_3_ = f32[60,128]{1,0:T(8,128)S(1)} collective-permute-done((f32[60,128]{1,0:T(8,128)S(1)}, f32[60,128]{1,0:T(8,128)S(1)}, u32[]{:S(2)}, u32[]{:S(2)}) %collective-permute-start.7) | collective-permute-done | bytes 30752 | tf_op jit(solution)/shard_map/ppermute | solution.py:517
  85.0 4.6 %all-to-all-done.4 = bf16[128,4,128]{2,1,0:T(4,128)(2,1)S(1)} async-done(((bf16[128,4,128]{2,1,0:T(4,128)(2,1)}), bf16[128,4,128]{2,1,0:T(4,128)(2,1)S(1)}, u32[]{:S(2)}, u32[]{:S(2)}) %all-to-all-start.4) | async-done | bytes 131104 | tf_op jit(solution)/shard_map/all_to_all | solution.py:508
  89.7 1.9 %sweep_last.1 = (f32[3,160,128]{2,1,0:T(8,128)S(1)}, f32[60,128]{1,0:T(8,128)S(1)}, f32[60,128]{1,0:T(8,128)S(1)}, f32[512,128]{1,0:T(8,128)}, f32[128,128]{1,0:...) custom-call(bf16[512,128]{1,0:T(8,128)(2,1)S(1)} %bitcast.84, ...), custom_call_target="tpu_custom_call" | custom-call | flops 4000000 | bytes 2367488 | tf_op jit(solution)/shard_map/sweep_last/pallas_call | solution.py:495
  91.6 4.0 %all-to-all-start.5 = ((f32[128,4,128]{2,1,0:T(4,128)}), f32[128,4,128]{2,1,0:T(4,128)S(1)}, u32[]{:S(2)}, u32[]{:S(2)}) async-start(f32[128,4,128]{2,1,0:T(4,128)} %bitcast.21), calls=%async_computation.5 | async-start | bytes 524288 | tf_op jit(solution)/shard_map/all_to_all | solution.py:508
  95.6 1.6 collective-permute-start.8
  97.5 1.1 collective-permute-done.8.refs_2_
  98.6 3.1 %collective-permute-done.9.refs_3_ = f32[60,128]{1,0:T(8,128)S(1)} collective-permute-done((f32[60,128]{1,0:T(8,128)S(1)}, f32[60,128]{1,0:T(8,128)S(1)}, u32[]{:S(2)}, u32[]{:S(2)}) %collective-permute-start.9) | collective-permute-done | bytes 30752 | tf_op jit(solution)/shard_map/ppermute | solution.py:517
  101.6 5.4 %all-to-all-done.5 = f32[128,4,128]{2,1,0:T(4,128)S(1)} async-done(((f32[128,4,128]{2,1,0:T(4,128)}), f32[128,4,128]{2,1,0:T(4,128)S(1)}, u32[]{:S(2)}, u32[]{:S(2)}) %all-to-all-start.5) | async-done | bytes 262176 | tf_op jit(solution)/shard_map/all_to_all | solution.py:508
  107.1 1.7 %sweep_after.1 = (f32[3,160,128]{2,1,0:T(8,128)S(1)}, f32[60,128]{1,0:T(8,128)S(1)}, f32[60,128]{1,0:T(8,128)S(1)}, bf16[512,128]{1,0:T(8,128)(2,1)}, f32[128,12...) custom-call(f32[512,128]{1,0:T(8,128)S(1)} %bitcast.82, ...), custom_call_target="tpu_custom_call" | custom-call | flops 4000000 | bytes 2252800 | tf_op jit(solution)/shard_map/sweep_after/pallas_call | solution.py:495
  108.8 4.0 %all-to-all-start.6 = ((bf16[128,4,128]{2,1,0:T(4,128)(2,1)}), bf16[128,4,128]{2,1,0:T(4,128)(2,1)S(1)}, u32[]{:S(2)}, u32[]{:S(2)}) async-start(bf16[128,4,128]{2,1,0:T(4,128)(2,1)} %bitcast.23), calls=%async_computation.6 | async-start | bytes 262144 | tf_op jit(solution)/shard_map/all_to_all | solution.py:508
  112.8 1.6 collective-permute-start.10
  115.5 2.9 %collective-permute-done.11.refs_3_ = f32[60,128]{1,0:T(8,128)S(1)} collective-permute-done((f32[60,128]{1,0:T(8,128)S(1)}, f32[60,128]{1,0:T(8,128)S(1)}, u32[]{:S(2)}, u32[]{:S(2)}) %collective-permute-start.11) | collective-permute-done | bytes 30752 | tf_op jit(solution)/shard_map/ppermute | solution.py:517
  118.4 4.7 %all-to-all-done.6 = bf16[128,4,128]{2,1,0:T(4,128)(2,1)S(1)} async-done(((bf16[128,4,128]{2,1,0:T(4,128)(2,1)}), bf16[128,4,128]{2,1,0:T(4,128)(2,1)S(1)}, u32[]{:S(2)}, u32[]{:S(2)}) %all-to-all-start.6) | async-done | bytes 131104 | tf_op jit(solution)/shard_map/all_to_all | solution.py:508
  123.1 1.8 %sweep_plain.3 = (f32[3,160,128]{2,1,0:T(8,128)S(1)}, f32[60,128]{1,0:T(8,128)S(1)}, f32[60,128]{1,0:T(8,128)S(1)}, bf16[512,128]{1,0:T(8,128)(2,1)}, f32[128,12...) custom-call(bf16[512,128]{1,0:T(8,128)(2,1)S(1)} %bitcast.87, f32[3,160,128]{2,1,0:T(8,128)S(1)} %interior.13.refs_1_, ...), custom_call_target="tpu_custom_call" | custom-call | flops 4000000 | bytes 2121728 | tf_op jit(solution)/shard_map/sweep_plain/pallas_call | solution.py:495
  124.8 4.0 %all-to-all-start.7 = ((bf16[128,4,128]{2,1,0:T(4,128)(2,1)}), bf16[128,4,128]{2,1,0:T(4,128)(2,1)S(1)}, u32[]{:S(2)}, u32[]{:S(2)}) async-start(bf16[128,4,128]{2,1,0:T(4,128)(2,1)} %bitcast.25), calls=%async_computation.7 | async-start | bytes 262144 | tf_op jit(solution)/shard_map/all_to_all | solution.py:508
  128.8 1.6 collective-permute-start.12
  131.5 2.9 %collective-permute-done.13.refs_3_ = f32[60,128]{1,0:T(8,128)S(1)} collective-permute-done((f32[60,128]{1,0:T(8,128)S(1)}, f32[60,128]{1,0:T(8,128)S(1)}, u32[]{:S(2)}, u32[]{:S(2)}) %collective-permute-start.13) | collective-permute-done | bytes 30752 | tf_op jit(solution)/shard_map/ppermute | solution.py:517
  134.4 4.6 %all-to-all-done.7 = bf16[128,4,128]{2,1,0:T(4,128)(2,1)S(1)} async-done(((bf16[128,4,128]{2,1,0:T(4,128)(2,1)}), bf16[128,4,128]{2,1,0:T(4,128)(2,1)S(1)}, u32[]{:S(2)}, u32[]{:S(2)}) %all-to-all-start.7) | async-done | bytes 131104 | tf_op jit(solution)/shard_map/all_to_all | solution.py:508
  139.0 1.8 %sweep_keep.3 = (f32[3,160,128]{2,1,0:T(8,128)S(1)}, f32[60,128]{1,0:T(8,128)S(1)}, f32[60,128]{1,0:T(8,128)S(1)}, bf16[512,128]{1,0:T(8,128)(2,1)}, f32[128,128...) custom-call(bf16[512,128]{1,0:T(8,128)(2,1)S(1)} %bitcast.85, ...), custom_call_target="tpu_custom_call" | custom-call | flops 4000000 | bytes 2121728 | tf_op jit(solution)/shard_map/sweep_keep/pallas_call | solution.py:495
  140.8 4.0 %all-to-all-start.8 = ((bf16[128,4,128]{2,1,0:T(4,128)(2,1)}), bf16[128,4,128]{2,1,0:T(4,128)(2,1)S(1)}, u32[]{:S(2)}, u32[]{:S(2)}) async-start(bf16[128,4,128]{2,1,0:T(4,128)(2,1)} %bitcast.27), calls=%async_computation.8 | async-start | bytes 262144 | tf_op jit(solution)/shard_map/all_to_all | solution.py:508
  144.8 1.6 collective-permute-start.14
  147.5 2.9 %collective-permute-done.15.refs_3_ = f32[60,128]{1,0:T(8,128)S(1)} collective-permute-done((f32[60,128]{1,0:T(8,128)S(1)}, f32[60,128]{1,0:T(8,128)S(1)}, u32[]{:S(2)}, u32[]{:S(2)}) %collective-permute-start.15) | collective-permute-done | bytes 30752 | tf_op jit(solution)/shard_map/ppermute | solution.py:517
  150.4 4.6 %all-to-all-done.8 = bf16[128,4,128]{2,1,0:T(4,128)(2,1)S(1)} async-done(((bf16[128,4,128]{2,1,0:T(4,128)(2,1)}), bf16[128,4,128]{2,1,0:T(4,128)(2,1)S(1)}, u32[]{:S(2)}, u32[]{:S(2)}) %all-to-all-start.8) | async-done | bytes 131104 | tf_op jit(solution)/shard_map/all_to_all | solution.py:508
  155.8 13.6 %all_to_all.110 = f32[128,1,128]{2,1,0:T(1,128)S(1)} all-to-all(f32[128,1,128]{2,1,0:T(1,128)S(1)} %bitcast.100), channel_id=1, replica_groups=mesh['gx'=8,'gy'=16] {'gx','gy'}, dimensions={0} | all-to-all | bytes 131072 | tf_op jit(solution)/shard_map/all_to_all | solution.py:508
  169.4 0.8 finish.1
  (55 shorter events, 7.3 us)
Async XLA Ops:
  3.3 11.6 %copy-start.12 = (f32[256]{0:T(256)S(1)}, f32[256]{0:T(256)}, u32[]{:S(2)}) copy-start(f32[256]{0:T(256)} %param.18) | copy-start | bytes 3076
  3.3 11.6 %copy-start.13 = (f32[256]{0:T(256)S(1)}, f32[256]{0:T(256)}, u32[]{:S(2)}) copy-start(f32[256]{0:T(256)} %param.19) | copy-start | bytes 3076
  3.3 28.1 %copy-start.15 = (f32[60,128]{1,0:T(8,128)S(1)}, f32[60,128]{1,0:T(8,128)}, u32[]{:S(2)}) copy-start(f32[60,128]{1,0:T(8,128)} %get-tuple-element.76) | copy-start | bytes 92164
  3.3 29.8 %copy-start.14 = (f32[60,128]{1,0:T(8,128)S(1)}, f32[60,128]{1,0:T(8,128)}, u32[]{:S(2)}) copy-start(f32[60,128]{1,0:T(8,128)} %get-tuple-element.77) | copy-start | bytes 92164
  3.3 29.8 %copy-start.9 = (f32[3,160,128]{2,1,0:T(8,128)S(1)}, f32[3,160,128]{2,1,0:T(8,128)}, u32[]{:S(2)}) copy-start(f32[3,160,128]{2,1,0:T(8,128)} %get-tuple-element.75.weighted) | copy-start | bytes 737284
  3.3 37.9 %copy-start.7 = (bf16[160,128]{1,0:T(8,128)(2,1)S(1)}, bf16[160,128]{1,0:T(8,128)(2,1)}, u32[]{:S(2)}) copy-start(bf16[160,128]{1,0:T(8,128)(2,1)} %get-tuple-element.84.refs_12_) | copy-start | bytes 122884
  3.3 37.9 %copy-start.10 = (f32[128,128]{1,0:T(8,128)S(1)}, f32[128,128]{1,0:T(8,128)}, u32[]{:S(2)}) copy-start(f32[128,128]{1,0:T(8,128)} %get-tuple-element.78.refs_4_) | copy-start | bytes 196612
  3.4 23.0 %all-to-all-start = ((f32[128,4,128]{2,1,0:T(4,128)}), f32[128,4,128]{2,1,0:T(4,128)S(1)}, u32[]{:S(2)}, u32[]{:S(2)}) async-start(f32[128,4,128]{2,1,0:T(4,128)} %bitcast.105), calls=%async_computation | async-start | bytes 524288 | tf_op jit(solution)/shard_map/all_to_all | solution.py:508
  14.9 0.7 copy-start.8
  14.9 0.7 copy-start.11
  15.6 25.7 %copy-start.6 = (f32[128,128]{1,0:T(8,128)S(1)}, f32[128,128]{1,0:T(8,128)}, u32[]{:S(2)}) copy-start(f32[128,128]{1,0:T(8,128)} %get-tuple-element.86.refs_14_) | copy-start | bytes 196612
  26.3 14.9 %copy-start.2 = (bf16[9,20,8,128]{3,2,1,0:T(8,128)(2,1)S(1)}, bf16[9,20,8,128]{3,2,1,0:T(8,128)(2,1)}, u32[]{:S(2)}) copy-start(bf16[9,20,8,128]{3,2,1,0:T(8,128)(2,1)} %param.12) | copy-start | bytes 1105924
  26.3 14.9 %copy-start.4 = (bf16[128,160]{1,0:T(8,128)(2,1)S(1)}, bf16[128,160]{1,0:T(8,128)(2,1)}, u32[]{:S(2)}) copy-start(bf16[128,160]{1,0:T(8,128)(2,1)} %get-tuple-element.83.refs_11_) | copy-start | bytes 122884
  26.3 14.9 %copy-start.5 = (s32[128,128]{1,0:T(8,128)S(1)}, s32[128,128]{1,0:T(8,128)}, u32[]{:S(2)}) copy-start(s32[128,128]{1,0:T(8,128)} %get-tuple-element.85.refs_13_) | copy-start | bytes 196612
  27.4 5.7 %copy-start = (bf16[3,20,8,128]{3,2,1,0:T(8,128)(2,1)S(1)}, bf16[3,20,8,128]{3,2,1,0:T(8,128)(2,1)}, u32[]{:S(2)}) copy-start(bf16[3,20,8,128]{3,2,1,0:T(8,128)(2,1)} %param.13) | copy-start | bytes 368644
  27.4 13.9 %copy-start.1 = (bf16[9,20,8,128]{3,2,1,0:T(8,128)(2,1)S(1)}, bf16[9,20,8,128]{3,2,1,0:T(8,128)(2,1)}, u32[]{:S(2)}) copy-start(bf16[9,20,8,128]{3,2,1,0:T(8,128)(2,1)} %param.11) | copy-start | bytes 1105924
  27.4 13.8 %all-to-all-start.1 = ((f32[128,1,128]{2,1,0:T(1,128)}), f32[128,1,128]{2,1,0:T(1,128)S(1)}, u32[]{:S(2)}, u32[]{:S(2)}) async-start(f32[128,1,128]{2,1,0:T(1,128)} %bitcast.13), calls=%async_computation.1 | async-start | bytes 131072 | tf_op jit(solution)/shard_map/all_to_all | solution.py:508
  31.4 2.7 %collective-permute-start = (f32[60,128]{1,0:T(8,128)S(1)}, f32[60,128]{1,0:T(8,128)S(1)}, u32[]{:S(2)}, u32[]{:S(2)}) collective-permute-start(f32[60,128]{1,0:T(8,128)S(1)} %copy-done.15), channel_id=1, source_target_pairs={{0,16},{16,32},{32,48},{48,64},{64,80},{80,96},{96,112},{112,0},{1... | collective-permute-start | bytes 92168 | tf_op jit(solution)/shard_map/ppermute | solution.py:516
  33.1 3.7 %collective-permute-start.1 = (f32[60,128]{1,0:T(8,128)S(1)}, f32[60,128]{1,0:T(8,128)S(1)}, u32[]{:S(2)}, u32[]{:S(2)}) collective-permute-start(f32[60,128]{1,0:T(8,128)S(1)} %copy-done.14), channel_id=1, source_target_pairs={{16,0},{32,16},{48,32},{64,48},{80,64},{96,80},{112,96},{0,112},{1... | collective-permute-start | bytes 92168 | tf_op jit(solution)/shard_map/ppermute | solution.py:517
  33.1 8.2 %copy-start.3 = (f32[3,20,8,128]{3,2,1,0:T(8,128)S(1)}, f32[3,20,8,128]{3,2,1,0:T(8,128)}, u32[]{:S(2)}) copy-start(f32[3,20,8,128]{3,2,1,0:T(8,128)} %param.10) | copy-start | bytes 737284
  43.0 14.7 %all-to-all-start.2 = ((bf16[128,4,128]{2,1,0:T(4,128)(2,1)}), bf16[128,4,128]{2,1,0:T(4,128)(2,1)S(1)}, u32[]{:S(2)}, u32[]{:S(2)}) async-start(bf16[128,4,128]{2,1,0:T(4,128)(2,1)} %bitcast.15), calls=%async_computation.2 | async-start | bytes 262144 | tf_op jit(solution)/shard_map/all_to_all | solution.py:508
  47.5 2.7 %collective-permute-start.2 = (f32[60,128]{1,0:T(8,128)S(1)}, f32[60,128]{1,0:T(8,128)S(1)}, u32[]{:S(2)}, u32[]{:S(2)}) collective-permute-start(f32[60,128]{1,0:T(8,128)S(1)} %get-tuple-element.92), channel_id=1, source_target_pairs={{0,16},{16,32},{32,48},{48,64},{64,80},{80,96},{96,112},{112,0},{1... | collective-permute-start | bytes 92168 | tf_op jit(solution)/shard_map/ppermute | solution.py:516
  49.1 3.9 %collective-permute-start.3 = (f32[60,128]{1,0:T(8,128)S(1)}, f32[60,128]{1,0:T(8,128)S(1)}, u32[]{:S(2)}, u32[]{:S(2)}) collective-permute-start(f32[60,128]{1,0:T(8,128)S(1)} %get-tuple-element.93), channel_id=1, source_target_pairs={{16,0},{32,16},{48,32},{64,48},{80,64},{96,80},{112,96},{0,112},{1... | collective-permute-start | bytes 92168 | tf_op jit(solution)/shard_map/ppermute | solution.py:517
  59.5 14.2 %all-to-all-start.3 = ((bf16[128,4,128]{2,1,0:T(4,128)(2,1)}), bf16[128,4,128]{2,1,0:T(4,128)(2,1)S(1)}, u32[]{:S(2)}, u32[]{:S(2)}) async-start(bf16[128,4,128]{2,1,0:T(4,128)(2,1)} %bitcast.17), calls=%async_computation.3 | async-start | bytes 262144 | tf_op jit(solution)/shard_map/all_to_all | solution.py:508
  63.5 2.7 %collective-permute-start.4 = (f32[60,128]{1,0:T(8,128)S(1)}, f32[60,128]{1,0:T(8,128)S(1)}, u32[]{:S(2)}, u32[]{:S(2)}) collective-permute-start(f32[60,128]{1,0:T(8,128)S(1)} %get-tuple-element.99), channel_id=1, source_target_pairs={{0,16},{16,32},{32,48},{48,64},{64,80},{80,96},{96,112},{112,0},{1... | collective-permute-start | bytes 92168 | tf_op jit(solution)/shard_map/ppermute | solution.py:516
  65.1 3.9 %collective-permute-start.5 = (f32[60,128]{1,0:T(8,128)S(1)}, f32[60,128]{1,0:T(8,128)S(1)}, u32[]{:S(2)}, u32[]{:S(2)}) collective-permute-start(f32[60,128]{1,0:T(8,128)S(1)} %get-tuple-element.100), channel_id=1, source_target_pairs={{16,0},{32,16},{48,32},{64,48},{80,64},{96,80},{112,96},{0,112},{1... | collective-permute-start | bytes 92168 | tf_op jit(solution)/shard_map/ppermute | solution.py:517
  75.4 14.2 %all-to-all-start.4 = ((bf16[128,4,128]{2,1,0:T(4,128)(2,1)}), bf16[128,4,128]{2,1,0:T(4,128)(2,1)S(1)}, u32[]{:S(2)}, u32[]{:S(2)}) async-start(bf16[128,4,128]{2,1,0:T(4,128)(2,1)} %bitcast.19), calls=%async_computation.4 | async-start | bytes 262144 | tf_op jit(solution)/shard_map/all_to_all | solution.py:508
  79.5 2.7 %collective-permute-start.6 = (f32[60,128]{1,0:T(8,128)S(1)}, f32[60,128]{1,0:T(8,128)S(1)}, u32[]{:S(2)}, u32[]{:S(2)}) collective-permute-start(f32[60,128]{1,0:T(8,128)S(1)} %get-tuple-element.106), channel_id=1, source_target_pairs={{0,16},{16,32},{32,48},{48,64},{64,80},{80,96},{96,112},{112,0},{1... | collective-permute-start | bytes 92168 | tf_op jit(solution)/shard_map/ppermute | solution.py:516
  81.1 3.9 %collective-permute-start.7 = (f32[60,128]{1,0:T(8,128)S(1)}, f32[60,128]{1,0:T(8,128)S(1)}, u32[]{:S(2)}, u32[]{:S(2)}) collective-permute-start(f32[60,128]{1,0:T(8,128)S(1)} %get-tuple-element.107), channel_id=1, source_target_pairs={{16,0},{32,16},{48,32},{64,48},{80,64},{96,80},{112,96},{0,112},{1... | collective-permute-start | bytes 92168 | tf_op jit(solution)/shard_map/ppermute | solution.py:517
  91.6 15.5 %all-to-all-start.5 = ((f32[128,4,128]{2,1,0:T(4,128)}), f32[128,4,128]{2,1,0:T(4,128)S(1)}, u32[]{:S(2)}, u32[]{:S(2)}) async-start(f32[128,4,128]{2,1,0:T(4,128)} %bitcast.21), calls=%async_computation.5 | async-start | bytes 524288 | tf_op jit(solution)/shard_map/all_to_all | solution.py:508
  95.6 3.0 %collective-permute-start.8 = (f32[60,128]{1,0:T(8,128)S(1)}, f32[60,128]{1,0:T(8,128)S(1)}, u32[]{:S(2)}, u32[]{:S(2)}) collective-permute-start(f32[60,128]{1,0:T(8,128)S(1)} %get-tuple-element.114), channel_id=1, source_target_pairs={{0,16},{16,32},{32,48},{48,64},{64,80},{80,96},{96,112},{112,0},{1... | collective-permute-start | bytes 92168 | tf_op jit(solution)/shard_map/ppermute | solution.py:516
  97.2 4.4 %collective-permute-start.9 = (f32[60,128]{1,0:T(8,128)S(1)}, f32[60,128]{1,0:T(8,128)S(1)}, u32[]{:S(2)}, u32[]{:S(2)}) collective-permute-start(f32[60,128]{1,0:T(8,128)S(1)} %get-tuple-element.115), channel_id=1, source_target_pairs={{16,0},{32,16},{48,32},{64,48},{80,64},{96,80},{112,96},{0,112},{1... | collective-permute-start | bytes 92168 | tf_op jit(solution)/shard_map/ppermute | solution.py:517
  108.8 14.3 %all-to-all-start.6 = ((bf16[128,4,128]{2,1,0:T(4,128)(2,1)}), bf16[128,4,128]{2,1,0:T(4,128)(2,1)S(1)}, u32[]{:S(2)}, u32[]{:S(2)}) async-start(bf16[128,4,128]{2,1,0:T(4,128)(2,1)} %bitcast.23), calls=%async_computation.6 | async-start | bytes 262144 | tf_op jit(solution)/shard_map/all_to_all | solution.py:508
  112.8 2.7 %collective-permute-start.10 = (f32[60,128]{1,0:T(8,128)S(1)}, f32[60,128]{1,0:T(8,128)S(1)}, u32[]{:S(2)}, u32[]{:S(2)}) collective-permute-start(f32[60,128]{1,0:T(8,128)S(1)} %get-tuple-element.121), channel_id=1, source_target_pairs={{0,16},{16,32},{32,48},{48,64},{64,80},{80,96},{96,112},{112,0},{1... | collective-permute-start | bytes 92168 | tf_op jit(solution)/shard_map/ppermute | solution.py:516
  114.5 3.9 %collective-permute-start.11 = (f32[60,128]{1,0:T(8,128)S(1)}, f32[60,128]{1,0:T(8,128)S(1)}, u32[]{:S(2)}, u32[]{:S(2)}) collective-permute-start(f32[60,128]{1,0:T(8,128)S(1)} %get-tuple-element.122), channel_id=1, source_target_pairs={{16,0},{32,16},{48,32},{64,48},{80,64},{96,80},{112,96},{0,112},{1... | collective-permute-start | bytes 92168 | tf_op jit(solution)/shard_map/ppermute | solution.py:517
  124.8 14.2 %all-to-all-start.7 = ((bf16[128,4,128]{2,1,0:T(4,128)(2,1)}), bf16[128,4,128]{2,1,0:T(4,128)(2,1)S(1)}, u32[]{:S(2)}, u32[]{:S(2)}) async-start(bf16[128,4,128]{2,1,0:T(4,128)(2,1)} %bitcast.25), calls=%async_computation.7 | async-start | bytes 262144 | tf_op jit(solution)/shard_map/all_to_all | solution.py:508
  128.8 2.7 %collective-permute-start.12 = (f32[60,128]{1,0:T(8,128)S(1)}, f32[60,128]{1,0:T(8,128)S(1)}, u32[]{:S(2)}, u32[]{:S(2)}) collective-permute-start(f32[60,128]{1,0:T(8,128)S(1)} %get-tuple-element.128), channel_id=1, source_target_pairs={{0,16},{16,32},{32,48},{48,64},{64,80},{80,96},{96,112},{112,0},{1... | collective-permute-start | bytes 92168 | tf_op jit(solution)/shard_map/ppermute | solution.py:516
  130.5 3.9 %collective-permute-start.13 = (f32[60,128]{1,0:T(8,128)S(1)}, f32[60,128]{1,0:T(8,128)S(1)}, u32[]{:S(2)}, u32[]{:S(2)}) collective-permute-start(f32[60,128]{1,0:T(8,128)S(1)} %get-tuple-element.129), channel_id=1, source_target_pairs={{16,0},{32,16},{48,32},{64,48},{80,64},{96,80},{112,96},{0,112},{1... | collective-permute-start | bytes 92168 | tf_op jit(solution)/shard_map/ppermute | solution.py:517
  140.8 14.2 %all-to-all-start.8 = ((bf16[128,4,128]{2,1,0:T(4,128)(2,1)}), bf16[128,4,128]{2,1,0:T(4,128)(2,1)S(1)}, u32[]{:S(2)}, u32[]{:S(2)}) async-start(bf16[128,4,128]{2,1,0:T(4,128)(2,1)} %bitcast.27), calls=%async_computation.8 | async-start | bytes 262144 | tf_op jit(solution)/shard_map/all_to_all | solution.py:508
  144.8 2.7 %collective-permute-start.14 = (f32[60,128]{1,0:T(8,128)S(1)}, f32[60,128]{1,0:T(8,128)S(1)}, u32[]{:S(2)}, u32[]{:S(2)}) collective-permute-start(f32[60,128]{1,0:T(8,128)S(1)} %get-tuple-element.135), channel_id=1, source_target_pairs={{0,16},{16,32},{32,48},{48,64},{64,80},{80,96},{96,112},{112,0},{1... | collective-permute-start | bytes 92168 | tf_op jit(solution)/shard_map/ppermute | solution.py:516
  146.5 3.9 %collective-permute-start.15 = (f32[60,128]{1,0:T(8,128)S(1)}, f32[60,128]{1,0:T(8,128)S(1)}, u32[]{:S(2)}, u32[]{:S(2)}) collective-permute-start(f32[60,128]{1,0:T(8,128)S(1)} %get-tuple-element.136), channel_id=1, source_target_pairs={{16,0},{32,16},{48,32},{64,48},{80,64},{96,80},{112,96},{0,112},{1... | collective-permute-start | bytes 92168 | tf_op jit(solution)/shard_map/ppermute | solution.py:517

commit v6 on v5

--- a/solution.py
+++ b/solution.py
@@ -222,20 +222,15 @@
 
 def cell_setup(rhs_in, diag_in, mobility_in, trans_in, cells_in, pi_in,
                rows_of, rows_to, start, weight, slots,
-               weighted, toward_low, toward_high, message, along, pad, forward,
+               weighted, toward_low, toward_high, message, along, pad, forward, wide,
                rhs, diag, mobility, trans, cells, pi, sems):
-    pairs = ((rhs_in, rhs), (diag_in, diag), (cells_in, cells), (pi_in, pi),
+    pairs = ((cells_in, cells), (pi_in, pi), (rhs_in, rhs), (diag_in, diag),
              (mobility_in, mobility), (trans_in, trans))
     copies = [pltpu.make_async_copy(a, b, sems.at[n]) for n, (a, b) in enumerate(pairs)]
     for copy in copies:
         copy.start()
-    for copy in copies:
+    for copy in copies[:2]:
         copy.wait()
-    for t in range(CHUNKS):
-        rows = chunk(t)
-        values = solve(diag, rows, [rhs[n, rows, :] for n in range(3)])
-        forward[rows, :] = values[0]
-        borders(values, mobility, trans, weighted, along, t)
     base = cells[0:1, :]
     row = lax.shift_right_logical(base, 7)
     live = pi[...]
@@ -253,13 +248,25 @@
     start[...] = begin
     weights = jnp.where(is_slot(lanes((PEERS, 128))), info, 0.0)
     weight[...] = weights
+    wide[block(1), :], wide[block(3), :] = halves(weights)
+    for copy in copies[2:4]:
+        copy.wait()
+    for t in range(CHUNKS):
+        rows = chunk(t)
+        values = solve(diag, rows, [rhs[n, rows, :] for n in range(3)])
+        forward[rows, :] = values[0]
+        for n in range(3):
+            weighted[n, rows, :] = values[n]
     values = slot_values(rows_of[...], begin, forward[...])
     slots[...] = values
-    message[block(0), :] = values
-    message[block(1), :] = weights
-    message[block(2), :] = jnp.zeros((PEERS, 128), F32)
-    message[block(3), :] = jnp.zeros((PEERS, 128), F32)
-    send_borders(trans, weighted, along, toward_low, toward_high, message, pad)
+    wide[block(0), :], wide[block(2), :] = halves(values)
+    for copy in copies[4:]:
+        copy.wait()
+    for t in range(CHUNKS):
+        values = [weighted[n, chunk(t), :] for n in range(3)]
+        borders(values, mobility, trans, weighted, along, t)
+    send_borders(trans, weighted, along, toward_low, toward_high, wide, pad)
+    message[...] = wide[...].astype(BF16)
 
 
 def well_tables(index, parent, trans, rhs, table, fixed):
@@ -276,8 +283,9 @@
     fixed[3] = across + following(linked * across)
 
 
-def well_setup(arrived, index, table, fixed, message, weight, state, at_slots, diagonal):
-    pi = to_rows(arrived[block(1), :])
+def well_setup(arrived, index, table, fixed, message, weight, state, at_slots, diagonal, wide):
+    wide[...] = arrived[...].astype(F32)
+    pi = to_rows(wide[block(1), :] + wide[block(3), :])
     weight[...] = pi
     number = index[...]
     total = fixed[3] + into_segments(pi, number, table[...])
@@ -339,11 +347,13 @@
     if arrived.dtype == BF16:
         wide[...] = arrived[...].astype(F32)
         arrived = wide
-        pressures = arrived[block(1), :] + arrived[block(3), :]
         heads = arrived[block(0), :] + arrived[block(2), :]
+        if kind == "first":
+            pressures = extra["pressures"][...]
+        else:
+            pressures = arrived[block(1), :] + arrived[block(3), :]
     else:
-        pressures = extra["pressures"][...] if kind == "first" else arrived[block(1), :]
-        heads = arrived[block(0), :]
+        heads, pressures = arrived[block(0), :], arrived[block(1), :]
     pull = fixed["weight"][...] * (now["slots"][...] - pressures)
     perforated = into_cells(fixed["rows_to"][...], fixed["start"][...], pull)
 
@@ -351,6 +361,9 @@
     side_high = rows_to_tile(arrived[peer_rows(1), :], pad)
     side_low = jnp.where(gy == 0, 0.0, side_low)
     side_high = jnp.where(gy == lax.axis_size("gy") - 1, 0.0, side_high)
+    small = lanes((8, 128))
+    ahead = pltpu.roll(side_high, 127, 1)
+    sides = [jnp.where((small & 1) == odd, side_low, ahead) for odd in range(2)]
     open_low, open_high = gx > 0, gx < lax.axis_size("gx") - 1
 
     state = now["state"][...]
@@ -370,17 +383,18 @@
     for t in range(CHUNKS):
         rows = chunk(t)
         tx, ty = [fixed["trans"][n, rows, :].astype(F32) for n in range(2)]
+        tx = jnp.where(
+            sub == 0, jnp.where(open_low, tx, 0.0),
+            jnp.where((sub == 7) & open_high, tx, 0.0),
+        )
+        ty = jnp.where((lane == 0) | (lane == 127), ty, 0.0)
         terms = []
         for n in range(3):
             j = n * NZ + 2 * t
-            low = jnp.where(open_low, now["from_low"][j : j + 2, :], 0.0)
-            high = jnp.where(open_high, now["from_high"][j : j + 2, :], 0.0)
-            nx = jnp.where(sub == 0, spread_pair(low), jnp.where(sub == 7, spread_pair(high), 0.0))
-            before = [pltpu.roll(side_low, (128 - j - h) % 128, 1) for h in range(2)]
-            behind = [pltpu.roll(side_high, 127 - j - h, 1) for h in range(2)]
-            ny = jnp.where(
-                lane == 0, jnp.concatenate(before, axis=0),
-                jnp.where(lane == 127, jnp.concatenate(behind, axis=0), 0.0),
+            low, high = now["from_low"][j : j + 2, :], now["from_high"][j : j + 2, :]
+            nx = jnp.where(sub == 0, spread_pair(low), spread_pair(high))
+            ny = jnp.concatenate(
+                [pltpu.roll(sides[(j + h) & 1], (128 - j - h) % 128, 1) for h in range(2)], axis=0
             )
             share = fixed["mobility"][3 * n, rows, :].astype(F32)
             value = now["near"][n, rows, :] + tx * nx + ty * ny
@@ -529,12 +543,13 @@
 
     fixed = {"rhs": rhs, "diag": diag, "mobility": mobility, "trans": trans, "index": index}
     inputs = [rhs, diag, mobility, trans, perf_cell[0], perf_pi[0]]
+    packed = (MESSAGE[0], BF16)
     (rows_of, rows_to, start, weight, slots, weighted, toward_low, toward_high, message) = call(
         cell_setup,
         [((PEERS, ROWS), BF16), ((ROWS, PEERS), BF16),
-         ((PEERS, 128), jnp.int32), PAIRS, PAIRS, CELLS, EDGE, EDGE, MESSAGE],
+         ((PEERS, 128), jnp.int32), PAIRS, PAIRS, CELLS, EDGE, EDGE, packed],
         inputs,
-        SCRATCH + tuple(pltpu.VMEM(a.shape, a.dtype) for a in inputs)
+        SCRATCH + (pltpu.VMEM(*MESSAGE),) + tuple(pltpu.VMEM(a.shape, a.dtype) for a in inputs)
         + (pltpu.SemaphoreType.DMA((6,)),),
         name="cell_setup",
         space=pltpu.HBM,
@@ -558,6 +573,7 @@
         well_setup,
         [PAIRS, TILE, TILE, TILE, TILE],
         [arrived, index, table, constants],
+        [pltpu.VMEM(*MESSAGE)],
         name="well_setup",
     )
     fixed.update(own_weight=own_weight, table=table, fixed=constants, diagonal=diagonal)

time: 171 us -> 169 us (0.988)
  waiting for transfers between devices: 78.2 us -> 76 us
where the time goes in v6:
time: 169 us
  waiting for transfers between devices  76 us (45%)
  starting transfers between devices  57.4 us (34%)
  Pallas kernels  19.3 us (11%)
  blocking collectives  13.6 us (8%)
    all_to_all x9, waiting for transfers between devices, exchange(): lax.all_to_all(message, AXES, split_axis=0, concat_axis=0, tiled=True)  46.9 us
    all_to_all x9, starting transfers between devices, exchange(): lax.all_to_all(message, AXES, split_axis=0, concat_axis=0, tiled=True)  44.2 us
    ppermute x8, waiting for transfers between devices, neighbours(): lax.ppermute(toward_low, 'gx', down)  23.1 us
    pallas_call x20, Pallas kernels, call(): pl.pallas_call(body, out_shape=[jax.ShapeDtypeStruct(*out) for out in out...  19.3 us
    all_to_all x1, blocking collectives, exchange(): lax.all_to_all(message, AXES, split_axis=0, concat_axis=0, tiled=True)  13.6 us
    ppermute x8, starting transfers between devices, neighbours(): lax.ppermute(toward_high, 'gx', up)  13.2 us
    ppermute x8, waiting for transfers between devices, neighbours(): lax.ppermute(toward_high, 'gx', up)  6.03 us
  transfers between devices with their start and end apart: 25, of which 25 were waited for; matrix products, arithmetic and copies ran while one was open for 0% of the time, Pallas kernels for 1%

profile of v6, /device:TPU:1, one launch (start us, length us, event | category | flops | bytes accessed | tf_op | source)
XLA Modules:
  0.0 168.9 jit_solution(12270570810357814844)
XLA Ops:
  0.6 2.6 %cell_setup.1 = (bf16[128,160]{1,0:T(8,128)(2,1)}, bf16[160,128]{1,0:T(8,128)(2,1)}, s32[128,128]{1,0:T(8,128)}, f32[128,128]{1,0:T(8,128)}, f32[128,128]{1,0:T(...) custom-call(f32[3,160,128]{2,1,0:T(8,128)} %bitcast.71, ...), custom_call_target="tpu_custom_call" | custom-call | flops 4000000 | bytes 1114112 | tf_op jit(solution)/shard_map/cell_setup/pallas_call | solution.py:509
  3.3 11.5 %all-to-all-start = ((bf16[128,4,128]{2,1,0:T(4,128)(2,1)}), bf16[128,4,128]{2,1,0:T(4,128)(2,1)S(1)}, u32[]{:S(2)}, u32[]{:S(2)}) async-start(bf16[128,4,128]{2,1,0:T(4,128)(2,1)} %bitcast.105), calls=%async_computation | async-start | bytes 262144 | tf_op jit(solution)/shard_map/all_to_all | solution.py:522
  15.7 9.4 %all-to-all-done = bf16[128,4,128]{2,1,0:T(4,128)(2,1)S(1)} async-done(((bf16[128,4,128]{2,1,0:T(4,128)(2,1)}), bf16[128,4,128]{2,1,0:T(4,128)(2,1)S(1)}, u32[]{:S(2)}, u32[]{:S(2)}) %all-to-all-start) | async-done | bytes 131104 | tf_op jit(solution)/shard_map/all_to_all | solution.py:522
  25.1 1.1 well_setup.1
  26.1 4.0 %all-to-all-start.1 = ((f32[128,1,128]{2,1,0:T(1,128)}), f32[128,1,128]{2,1,0:T(1,128)S(1)}, u32[]{:S(2)}, u32[]{:S(2)}) async-start(f32[128,1,128]{2,1,0:T(1,128)} %bitcast.13), calls=%async_computation.1 | async-start | bytes 131072 | tf_op jit(solution)/shard_map/all_to_all | solution.py:522
  30.2 1.6 collective-permute-start
  31.8 0.9 copy-done.9
  33.1 2.6 %collective-permute-done.1.refs_3_ = f32[60,128]{1,0:T(8,128)S(1)} collective-permute-done((f32[60,128]{1,0:T(8,128)}, f32[60,128]{1,0:T(8,128)S(1)}, u32[]{:S(2)}, u32[]{:S(2)}) %collective-permute-start.1) | collective-permute-done | bytes 30752 | tf_op jit(solution)/shard_map/ppermute | solution.py:531
  35.7 4.2 %all-to-all-done.1 = f32[128,1,128]{2,1,0:T(1,128)S(1)} async-done(((f32[128,1,128]{2,1,0:T(1,128)}), f32[128,1,128]{2,1,0:T(1,128)S(1)}, u32[]{:S(2)}, u32[]{:S(2)}) %all-to-all-start.1) | async-done | bytes 65568 | tf_op jit(solution)/shard_map/all_to_all | solution.py:522
  40.0 1.7 %sweep_first.1 = (f32[3,160,128]{2,1,0:T(8,128)S(1)}, f32[60,128]{1,0:T(8,128)S(1)}, f32[60,128]{1,0:T(8,128)S(1)}, bf16[512,128]{1,0:T(8,128)(2,1)}, f32[128,12...) custom-call(bf16[512,128]{1,0:T(8,128)(2,1)S(1)} %bitcast.81, f32[3,160,128]{2,1,0:T(8,128)S(1)} %interior.8.refs_1_, ...), custom_call_target="tpu_custom_call" | custom-call | flops 4000000 | bytes 2187264 | tf_op jit(solution)/shard_map/sweep_first/pallas_call | solution.py:509
  41.7 4.6 %all-to-all-start.2 = ((bf16[128,4,128]{2,1,0:T(4,128)(2,1)}), bf16[128,4,128]{2,1,0:T(4,128)(2,1)S(1)}, u32[]{:S(2)}, u32[]{:S(2)}) async-start(bf16[128,4,128]{2,1,0:T(4,128)(2,1)} %bitcast.15), calls=%async_computation.2 | async-start | bytes 262144 | tf_op jit(solution)/shard_map/all_to_all | solution.py:522
  46.4 1.6 collective-permute-start.2
  48.3 0.8 collective-permute-done.2.refs_2_
  49.1 2.9 %collective-permute-done.3.refs_3_ = f32[60,128]{1,0:T(8,128)S(1)} collective-permute-done((f32[60,128]{1,0:T(8,128)S(1)}, f32[60,128]{1,0:T(8,128)S(1)}, u32[]{:S(2)}, u32[]{:S(2)}) %collective-permute-start.3) | collective-permute-done | bytes 30752 | tf_op jit(solution)/shard_map/ppermute | solution.py:531
  52.0 4.6 %all-to-all-done.2 = bf16[128,4,128]{2,1,0:T(4,128)(2,1)S(1)} async-done(((bf16[128,4,128]{2,1,0:T(4,128)(2,1)}), bf16[128,4,128]{2,1,0:T(4,128)(2,1)S(1)}, u32[]{:S(2)}, u32[]{:S(2)}) %all-to-all-start.2) | async-done | bytes 131104 | tf_op jit(solution)/shard_map/all_to_all | solution.py:522
  56.6 1.7 %sweep_plain.2 = (f32[3,160,128]{2,1,0:T(8,128)S(1)}, f32[60,128]{1,0:T(8,128)S(1)}, f32[60,128]{1,0:T(8,128)S(1)}, bf16[512,128]{1,0:T(8,128)(2,1)}, f32[128,12...) custom-call(bf16[512,128]{1,0:T(8,128)(2,1)S(1)} %bitcast.86, f32[3,160,128]{2,1,0:T(8,128)S(1)} %interior.9.refs_1_, ...), custom_call_target="tpu_custom_call" | custom-call | flops 4000000 | bytes 2121728 | tf_op jit(solution)/shard_map/sweep_plain/pallas_call | solution.py:509
  58.3 4.0 %all-to-all-start.3 = ((bf16[128,4,128]{2,1,0:T(4,128)(2,1)}), bf16[128,4,128]{2,1,0:T(4,128)(2,1)S(1)}, u32[]{:S(2)}, u32[]{:S(2)}) async-start(bf16[128,4,128]{2,1,0:T(4,128)(2,1)} %bitcast.17), calls=%async_computation.3 | async-start | bytes 262144 | tf_op jit(solution)/shard_map/all_to_all | solution.py:522
  62.3 1.6 collective-permute-start.4
  65.0 2.9 %collective-permute-done.5.refs_3_ = f32[60,128]{1,0:T(8,128)S(1)} collective-permute-done((f32[60,128]{1,0:T(8,128)S(1)}, f32[60,128]{1,0:T(8,128)S(1)}, u32[]{:S(2)}, u32[]{:S(2)}) %collective-permute-start.5) | collective-permute-done | bytes 30752 | tf_op jit(solution)/shard_map/ppermute | solution.py:531
  67.9 4.6 %all-to-all-done.3 = bf16[128,4,128]{2,1,0:T(4,128)(2,1)S(1)} async-done(((bf16[128,4,128]{2,1,0:T(4,128)(2,1)}), bf16[128,4,128]{2,1,0:T(4,128)(2,1)S(1)}, u32[]{:S(2)}, u32[]{:S(2)}) %all-to-all-start.3) | async-done | bytes 131104 | tf_op jit(solution)/shard_map/all_to_all | solution.py:522
  72.6 1.7 %sweep_keep.2 = (f32[3,160,128]{2,1,0:T(8,128)S(1)}, f32[60,128]{1,0:T(8,128)S(1)}, f32[60,128]{1,0:T(8,128)S(1)}, bf16[512,128]{1,0:T(8,128)(2,1)}, f32[128,128...) custom-call(bf16[512,128]{1,0:T(8,128)(2,1)S(1)} %bitcast.83, ...), custom_call_target="tpu_custom_call" | custom-call | flops 4000000 | bytes 2121728 | tf_op jit(solution)/shard_map/sweep_keep/pallas_call | solution.py:509
  74.3 4.0 %all-to-all-start.4 = ((bf16[128,4,128]{2,1,0:T(4,128)(2,1)}), bf16[128,4,128]{2,1,0:T(4,128)(2,1)S(1)}, u32[]{:S(2)}, u32[]{:S(2)}) async-start(bf16[128,4,128]{2,1,0:T(4,128)(2,1)} %bitcast.19), calls=%async_computation.4 | async-start | bytes 262144 | tf_op jit(solution)/shard_map/all_to_all | solution.py:522
  78.3 1.6 collective-permute-start.6
  81.0 2.9 %collective-permute-done.7.refs_3_ = f32[60,128]{1,0:T(8,128)S(1)} collective-permute-done((f32[60,128]{1,0:T(8,128)S(1)}, f32[60,128]{1,0:T(8,128)S(1)}, u32[]{:S(2)}, u32[]{:S(2)}) %collective-permute-start.7) | collective-permute-done | bytes 30752 | tf_op jit(solution)/shard_map/ppermute | solution.py:531
  83.9 4.6 %all-to-all-done.4 = bf16[128,4,128]{2,1,0:T(4,128)(2,1)S(1)} async-done(((bf16[128,4,128]{2,1,0:T(4,128)(2,1)}), bf16[128,4,128]{2,1,0:T(4,128)(2,1)S(1)}, u32[]{:S(2)}, u32[]{:S(2)}) %all-to-all-start.4) | async-done | bytes 131104 | tf_op jit(solution)/shard_map/all_to_all | solution.py:522
  88.5 1.9 %sweep_last.1 = (f32[3,160,128]{2,1,0:T(8,128)S(1)}, f32[60,128]{1,0:T(8,128)S(1)}, f32[60,128]{1,0:T(8,128)S(1)}, f32[512,128]{1,0:T(8,128)}, f32[128,128]{1,0:...) custom-call(bf16[512,128]{1,0:T(8,128)(2,1)S(1)} %bitcast.84, ...), custom_call_target="tpu_custom_call" | custom-call | flops 4000000 | bytes 2367488 | tf_op jit(solution)/shard_map/sweep_last/pallas_call | solution.py:509
  90.4 4.0 %all-to-all-start.5 = ((f32[128,4,128]{2,1,0:T(4,128)}), f32[128,4,128]{2,1,0:T(4,128)S(1)}, u32[]{:S(2)}, u32[]{:S(2)}) async-start(f32[128,4,128]{2,1,0:T(4,128)} %bitcast.21), calls=%async_computation.5 | async-start | bytes 524288 | tf_op jit(solution)/shard_map/all_to_all | solution.py:522
  94.4 1.6 collective-permute-start.8
  96.3 1.1 collective-permute-done.8.refs_2_
  97.4 3.1 %collective-permute-done.9.refs_3_ = f32[60,128]{1,0:T(8,128)S(1)} collective-permute-done((f32[60,128]{1,0:T(8,128)S(1)}, f32[60,128]{1,0:T(8,128)S(1)}, u32[]{:S(2)}, u32[]{:S(2)}) %collective-permute-start.9) | collective-permute-done | bytes 30752 | tf_op jit(solution)/shard_map/ppermute | solution.py:531
  100.4 5.4 %all-to-all-done.5 = f32[128,4,128]{2,1,0:T(4,128)S(1)} async-done(((f32[128,4,128]{2,1,0:T(4,128)}), f32[128,4,128]{2,1,0:T(4,128)S(1)}, u32[]{:S(2)}, u32[]{:S(2)}) %all-to-all-start.5) | async-done | bytes 262176 | tf_op jit(solution)/shard_map/all_to_all | solution.py:522
  105.9 1.7 %sweep_after.1 = (f32[3,160,128]{2,1,0:T(8,128)S(1)}, f32[60,128]{1,0:T(8,128)S(1)}, f32[60,128]{1,0:T(8,128)S(1)}, bf16[512,128]{1,0:T(8,128)(2,1)}, f32[128,12...) custom-call(f32[512,128]{1,0:T(8,128)S(1)} %bitcast.82, ...), custom_call_target="tpu_custom_call" | custom-call | flops 4000000 | bytes 2252800 | tf_op jit(solution)/shard_map/sweep_after/pallas_call | solution.py:509
  107.6 4.0 %all-to-all-start.6 = ((bf16[128,4,128]{2,1,0:T(4,128)(2,1)}), bf16[128,4,128]{2,1,0:T(4,128)(2,1)S(1)}, u32[]{:S(2)}, u32[]{:S(2)}) async-start(bf16[128,4,128]{2,1,0:T(4,128)(2,1)} %bitcast.23), calls=%async_computation.6 | async-start | bytes 262144 | tf_op jit(solution)/shard_map/all_to_all | solution.py:522
  111.6 1.6 collective-permute-start.10
  114.3 2.9 %collective-permute-done.11.refs_3_ = f32[60,128]{1,0:T(8,128)S(1)} collective-permute-done((f32[60,128]{1,0:T(8,128)S(1)}, f32[60,128]{1,0:T(8,128)S(1)}, u32[]{:S(2)}, u32[]{:S(2)}) %collective-permute-start.11) | collective-permute-done | bytes 30752 | tf_op jit(solution)/shard_map/ppermute | solution.py:531
  117.2 4.7 %all-to-all-done.6 = bf16[128,4,128]{2,1,0:T(4,128)(2,1)S(1)} async-done(((bf16[128,4,128]{2,1,0:T(4,128)(2,1)}), bf16[128,4,128]{2,1,0:T(4,128)(2,1)S(1)}, u32[]{:S(2)}, u32[]{:S(2)}) %all-to-all-start.6) | async-done | bytes 131104 | tf_op jit(solution)/shard_map/all_to_all | solution.py:522
  121.8 1.7 %sweep_plain.3 = (f32[3,160,128]{2,1,0:T(8,128)S(1)}, f32[60,128]{1,0:T(8,128)S(1)}, f32[60,128]{1,0:T(8,128)S(1)}, bf16[512,128]{1,0:T(8,128)(2,1)}, f32[128,12...) custom-call(bf16[512,128]{1,0:T(8,128)(2,1)S(1)} %bitcast.87, f32[3,160,128]{2,1,0:T(8,128)S(1)} %interior.13.refs_1_, ...), custom_call_target="tpu_custom_call" | custom-call | flops 4000000 | bytes 2121728 | tf_op jit(solution)/shard_map/sweep_plain/pallas_call | solution.py:509
  123.6 4.0 %all-to-all-start.7 = ((bf16[128,4,128]{2,1,0:T(4,128)(2,1)}), bf16[128,4,128]{2,1,0:T(4,128)(2,1)S(1)}, u32[]{:S(2)}, u32[]{:S(2)}) async-start(bf16[128,4,128]{2,1,0:T(4,128)(2,1)} %bitcast.25), calls=%async_computation.7 | async-start | bytes 262144 | tf_op jit(solution)/shard_map/all_to_all | solution.py:522
  127.6 1.6 collective-permute-start.12
  130.2 2.9 %collective-permute-done.13.refs_3_ = f32[60,128]{1,0:T(8,128)S(1)} collective-permute-done((f32[60,128]{1,0:T(8,128)S(1)}, f32[60,128]{1,0:T(8,128)S(1)}, u32[]{:S(2)}, u32[]{:S(2)}) %collective-permute-start.13) | collective-permute-done | bytes 30752 | tf_op jit(solution)/shard_map/ppermute | solution.py:531
  133.2 4.6 %all-to-all-done.7 = bf16[128,4,128]{2,1,0:T(4,128)(2,1)S(1)} async-done(((bf16[128,4,128]{2,1,0:T(4,128)(2,1)}), bf16[128,4,128]{2,1,0:T(4,128)(2,1)S(1)}, u32[]{:S(2)}, u32[]{:S(2)}) %all-to-all-start.7) | async-done | bytes 131104 | tf_op jit(solution)/shard_map/all_to_all | solution.py:522
  137.8 1.7 %sweep_keep.3 = (f32[3,160,128]{2,1,0:T(8,128)S(1)}, f32[60,128]{1,0:T(8,128)S(1)}, f32[60,128]{1,0:T(8,128)S(1)}, bf16[512,128]{1,0:T(8,128)(2,1)}, f32[128,128...) custom-call(bf16[512,128]{1,0:T(8,128)(2,1)S(1)} %bitcast.85, ...), custom_call_target="tpu_custom_call" | custom-call | flops 4000000 | bytes 2121728 | tf_op jit(solution)/shard_map/sweep_keep/pallas_call | solution.py:509
  139.5 4.0 %all-to-all-start.8 = ((bf16[128,4,128]{2,1,0:T(4,128)(2,1)}), bf16[128,4,128]{2,1,0:T(4,128)(2,1)S(1)}, u32[]{:S(2)}, u32[]{:S(2)}) async-start(bf16[128,4,128]{2,1,0:T(4,128)(2,1)} %bitcast.27), calls=%async_computation.8 | async-start | bytes 262144 | tf_op jit(solution)/shard_map/all_to_all | solution.py:522
  143.5 1.6 collective-permute-start.14
  146.2 2.9 %collective-permute-done.15.refs_3_ = f32[60,128]{1,0:T(8,128)S(1)} collective-permute-done((f32[60,128]{1,0:T(8,128)S(1)}, f32[60,128]{1,0:T(8,128)S(1)}, u32[]{:S(2)}, u32[]{:S(2)}) %collective-permute-start.15) | collective-permute-done | bytes 30752 | tf_op jit(solution)/shard_map/ppermute | solution.py:531
  149.1 4.6 %all-to-all-done.8 = bf16[128,4,128]{2,1,0:T(4,128)(2,1)S(1)} async-done(((bf16[128,4,128]{2,1,0:T(4,128)(2,1)}), bf16[128,4,128]{2,1,0:T(4,128)(2,1)S(1)}, u32[]{:S(2)}, u32[]{:S(2)}) %all-to-all-start.8) | async-done | bytes 131104 | tf_op jit(solution)/shard_map/all_to_all | solution.py:522
  154.5 13.6 %all_to_all.110 = f32[128,1,128]{2,1,0:T(1,128)S(1)} all-to-all(f32[128,1,128]{2,1,0:T(1,128)S(1)} %bitcast.100), channel_id=1, replica_groups=mesh['gx'=8,'gy'=16] {'gx','gy'}, dimensions={0} | all-to-all | bytes 131072 | tf_op jit(solution)/shard_map/all_to_all | solution.py:522
  168.1 0.8 finish.1
  (51 shorter events, 7.5 us)
Async XLA Ops:
  3.3 11.6 %copy-start.12 = (f32[256]{0:T(256)S(1)}, f32[256]{0:T(256)}, u32[]{:S(2)}) copy-start(f32[256]{0:T(256)} %param.18) | copy-start | bytes 3076
  3.3 11.6 %copy-start.13 = (f32[256]{0:T(256)S(1)}, f32[256]{0:T(256)}, u32[]{:S(2)}) copy-start(f32[256]{0:T(256)} %param.19) | copy-start | bytes 3076
  3.3 36.7 %copy-start.5 = (s32[128,128]{1,0:T(8,128)S(1)}, s32[128,128]{1,0:T(8,128)}, u32[]{:S(2)}) copy-start(s32[128,128]{1,0:T(8,128)} %get-tuple-element.85.refs_13_) | copy-start | bytes 196612
  3.3 36.7 %copy-start.6 = (f32[128,128]{1,0:T(8,128)S(1)}, f32[128,128]{1,0:T(8,128)}, u32[]{:S(2)}) copy-start(f32[128,128]{1,0:T(8,128)} %get-tuple-element.86.refs_14_) | copy-start | bytes 196612
  3.3 36.7 %copy-start.7 = (bf16[160,128]{1,0:T(8,128)(2,1)S(1)}, bf16[160,128]{1,0:T(8,128)(2,1)}, u32[]{:S(2)}) copy-start(bf16[160,128]{1,0:T(8,128)(2,1)} %get-tuple-element.84.refs_12_) | copy-start | bytes 122884
  3.3 36.7 %copy-start.10 = (f32[128,128]{1,0:T(8,128)S(1)}, f32[128,128]{1,0:T(8,128)}, u32[]{:S(2)}) copy-start(f32[128,128]{1,0:T(8,128)} %get-tuple-element.78.refs_4_) | copy-start | bytes 196612
  3.3 21.7 %all-to-all-start = ((bf16[128,4,128]{2,1,0:T(4,128)(2,1)}), bf16[128,4,128]{2,1,0:T(4,128)(2,1)S(1)}, u32[]{:S(2)}, u32[]{:S(2)}) async-start(bf16[128,4,128]{2,1,0:T(4,128)(2,1)} %bitcast.105), calls=%async_computation | async-start | bytes 262144 | tf_op jit(solution)/shard_map/all_to_all | solution.py:522
  14.8 0.7 copy-start.8
  14.9 0.7 copy-start.11
  15.5 24.4 %copy-start.4 = (bf16[128,160]{1,0:T(8,128)(2,1)S(1)}, bf16[128,160]{1,0:T(8,128)(2,1)}, u32[]{:S(2)}) copy-start(bf16[128,160]{1,0:T(8,128)(2,1)} %get-tuple-element.83.refs_11_) | copy-start | bytes 122884
  25.1 15.0 %copy-start.2 = (bf16[9,20,8,128]{3,2,1,0:T(8,128)(2,1)S(1)}, bf16[9,20,8,128]{3,2,1,0:T(8,128)(2,1)}, u32[]{:S(2)}) copy-start(bf16[9,20,8,128]{3,2,1,0:T(8,128)(2,1)} %param.12) | copy-start | bytes 1105924
  26.1 5.7 %copy-start = (bf16[3,20,8,128]{3,2,1,0:T(8,128)(2,1)S(1)}, bf16[3,20,8,128]{3,2,1,0:T(8,128)(2,1)}, u32[]{:S(2)}) copy-start(bf16[3,20,8,128]{3,2,1,0:T(8,128)(2,1)} %param.13) | copy-start | bytes 368644
  26.1 13.9 %copy-start.1 = (bf16[9,20,8,128]{3,2,1,0:T(8,128)(2,1)S(1)}, bf16[9,20,8,128]{3,2,1,0:T(8,128)(2,1)}, u32[]{:S(2)}) copy-start(bf16[9,20,8,128]{3,2,1,0:T(8,128)(2,1)} %param.11) | copy-start | bytes 1105924
  26.1 13.8 %all-to-all-start.1 = ((f32[128,1,128]{2,1,0:T(1,128)}), f32[128,1,128]{2,1,0:T(1,128)S(1)}, u32[]{:S(2)}, u32[]{:S(2)}) async-start(f32[128,1,128]{2,1,0:T(1,128)} %bitcast.13), calls=%async_computation.1 | async-start | bytes 131072 | tf_op jit(solution)/shard_map/all_to_all | solution.py:522
  30.2 3.0 %collective-permute-start = (f32[60,128]{1,0:T(8,128)}, f32[60,128]{1,0:T(8,128)S(1)}, u32[]{:S(2)}, u32[]{:S(2)}) collective-permute-start(f32[60,128]{1,0:T(8,128)} %get-tuple-element.76), channel_id=1, source_target_pairs={{0,16},{16,32},{32,48},{48,64},{64,80},{80,96},{96,112},{112,0},{1... | collective-permute-start | bytes 92168 | tf_op jit(solution)/shard_map/ppermute | solution.py:530
  31.8 3.9 %collective-permute-start.1 = (f32[60,128]{1,0:T(8,128)}, f32[60,128]{1,0:T(8,128)S(1)}, u32[]{:S(2)}, u32[]{:S(2)}) collective-permute-start(f32[60,128]{1,0:T(8,128)} %get-tuple-element.77), channel_id=1, source_target_pairs={{16,0},{32,16},{48,32},{64,48},{80,64},{96,80},{112,96},{0,112},{1... | collective-permute-start | bytes 92168 | tf_op jit(solution)/shard_map/ppermute | solution.py:531
  31.8 0.9 copy-start.9
  32.8 7.3 %copy-start.3 = (f32[3,20,8,128]{3,2,1,0:T(8,128)S(1)}, f32[3,20,8,128]{3,2,1,0:T(8,128)}, u32[]{:S(2)}) copy-start(f32[3,20,8,128]{3,2,1,0:T(8,128)} %param.10) | copy-start | bytes 737284
  41.7 14.9 %all-to-all-start.2 = ((bf16[128,4,128]{2,1,0:T(4,128)(2,1)}), bf16[128,4,128]{2,1,0:T(4,128)(2,1)S(1)}, u32[]{:S(2)}, u32[]{:S(2)}) async-start(bf16[128,4,128]{2,1,0:T(4,128)(2,1)} %bitcast.15), calls=%async_computation.2 | async-start | bytes 262144 | tf_op jit(solution)/shard_map/all_to_all | solution.py:522
  46.4 2.7 %collective-permute-start.2 = (f32[60,128]{1,0:T(8,128)S(1)}, f32[60,128]{1,0:T(8,128)S(1)}, u32[]{:S(2)}, u32[]{:S(2)}) collective-permute-start(f32[60,128]{1,0:T(8,128)S(1)} %get-tuple-element.92), channel_id=1, source_target_pairs={{0,16},{16,32},{32,48},{48,64},{64,80},{80,96},{96,112},{112,0},{1... | collective-permute-start | bytes 92168 | tf_op jit(solution)/shard_map/ppermute | solution.py:530
  48.0 3.9 %collective-permute-start.3 = (f32[60,128]{1,0:T(8,128)S(1)}, f32[60,128]{1,0:T(8,128)S(1)}, u32[]{:S(2)}, u32[]{:S(2)}) collective-permute-start(f32[60,128]{1,0:T(8,128)S(1)} %get-tuple-element.93), channel_id=1, source_target_pairs={{16,0},{32,16},{48,32},{64,48},{80,64},{96,80},{112,96},{0,112},{1... | collective-permute-start | bytes 92168 | tf_op jit(solution)/shard_map/ppermute | solution.py:531
  58.3 14.2 %all-to-all-start.3 = ((bf16[128,4,128]{2,1,0:T(4,128)(2,1)}), bf16[128,4,128]{2,1,0:T(4,128)(2,1)S(1)}, u32[]{:S(2)}, u32[]{:S(2)}) async-start(bf16[128,4,128]{2,1,0:T(4,128)(2,1)} %bitcast.17), calls=%async_computation.3 | async-start | bytes 262144 | tf_op jit(solution)/shard_map/all_to_all | solution.py:522
  62.3 2.7 %collective-permute-start.4 = (f32[60,128]{1,0:T(8,128)S(1)}, f32[60,128]{1,0:T(8,128)S(1)}, u32[]{:S(2)}, u32[]{:S(2)}) collective-permute-start(f32[60,128]{1,0:T(8,128)S(1)} %get-tuple-element.99), channel_id=1, source_target_pairs={{0,16},{16,32},{32,48},{48,64},{64,80},{80,96},{96,112},{112,0},{1... | collective-permute-start | bytes 92168 | tf_op jit(solution)/shard_map/ppermute | solution.py:530
  64.0 3.9 %collective-permute-start.5 = (f32[60,128]{1,0:T(8,128)S(1)}, f32[60,128]{1,0:T(8,128)S(1)}, u32[]{:S(2)}, u32[]{:S(2)}) collective-permute-start(f32[60,128]{1,0:T(8,128)S(1)} %get-tuple-element.100), channel_id=1, source_target_pairs={{16,0},{32,16},{48,32},{64,48},{80,64},{96,80},{112,96},{0,112},{1... | collective-permute-start | bytes 92168 | tf_op jit(solution)/shard_map/ppermute | solution.py:531
  74.3 14.2 %all-to-all-start.4 = ((bf16[128,4,128]{2,1,0:T(4,128)(2,1)}), bf16[128,4,128]{2,1,0:T(4,128)(2,1)S(1)}, u32[]{:S(2)}, u32[]{:S(2)}) async-start(bf16[128,4,128]{2,1,0:T(4,128)(2,1)} %bitcast.19), calls=%async_computation.4 | async-start | bytes 262144 | tf_op jit(solution)/shard_map/all_to_all | solution.py:522
  78.3 2.7 %collective-permute-start.6 = (f32[60,128]{1,0:T(8,128)S(1)}, f32[60,128]{1,0:T(8,128)S(1)}, u32[]{:S(2)}, u32[]{:S(2)}) collective-permute-start(f32[60,128]{1,0:T(8,128)S(1)} %get-tuple-element.106), channel_id=1, source_target_pairs={{0,16},{16,32},{32,48},{48,64},{64,80},{80,96},{96,112},{112,0},{1... | collective-permute-start | bytes 92168 | tf_op jit(solution)/shard_map/ppermute | solution.py:530
  80.0 3.9 %collective-permute-start.7 = (f32[60,128]{1,0:T(8,128)S(1)}, f32[60,128]{1,0:T(8,128)S(1)}, u32[]{:S(2)}, u32[]{:S(2)}) collective-permute-start(f32[60,128]{1,0:T(8,128)S(1)} %get-tuple-element.107), channel_id=1, source_target_pairs={{16,0},{32,16},{48,32},{64,48},{80,64},{96,80},{112,96},{0,112},{1... | collective-permute-start | bytes 92168 | tf_op jit(solution)/shard_map/ppermute | solution.py:531
  90.4 15.5 %all-to-all-start.5 = ((f32[128,4,128]{2,1,0:T(4,128)}), f32[128,4,128]{2,1,0:T(4,128)S(1)}, u32[]{:S(2)}, u32[]{:S(2)}) async-start(f32[128,4,128]{2,1,0:T(4,128)} %bitcast.21), calls=%async_computation.5 | async-start | bytes 524288 | tf_op jit(solution)/shard_map/all_to_all | solution.py:522
  94.4 3.0 %collective-permute-start.8 = (f32[60,128]{1,0:T(8,128)S(1)}, f32[60,128]{1,0:T(8,128)S(1)}, u32[]{:S(2)}, u32[]{:S(2)}) collective-permute-start(f32[60,128]{1,0:T(8,128)S(1)} %get-tuple-element.114), channel_id=1, source_target_pairs={{0,16},{16,32},{32,48},{48,64},{64,80},{80,96},{96,112},{112,0},{1... | collective-permute-start | bytes 92168 | tf_op jit(solution)/shard_map/ppermute | solution.py:530
  96.0 4.4 %collective-permute-start.9 = (f32[60,128]{1,0:T(8,128)S(1)}, f32[60,128]{1,0:T(8,128)S(1)}, u32[]{:S(2)}, u32[]{:S(2)}) collective-permute-start(f32[60,128]{1,0:T(8,128)S(1)} %get-tuple-element.115), channel_id=1, source_target_pairs={{16,0},{32,16},{48,32},{64,48},{80,64},{96,80},{112,96},{0,112},{1... | collective-permute-start | bytes 92168 | tf_op jit(solution)/shard_map/ppermute | solution.py:531
  107.6 14.3 %all-to-all-start.6 = ((bf16[128,4,128]{2,1,0:T(4,128)(2,1)}), bf16[128,4,128]{2,1,0:T(4,128)(2,1)S(1)}, u32[]{:S(2)}, u32[]{:S(2)}) async-start(bf16[128,4,128]{2,1,0:T(4,128)(2,1)} %bitcast.23), calls=%async_computation.6 | async-start | bytes 262144 | tf_op jit(solution)/shard_map/all_to_all | solution.py:522
  111.6 2.7 %collective-permute-start.10 = (f32[60,128]{1,0:T(8,128)S(1)}, f32[60,128]{1,0:T(8,128)S(1)}, u32[]{:S(2)}, u32[]{:S(2)}) collective-permute-start(f32[60,128]{1,0:T(8,128)S(1)} %get-tuple-element.121), channel_id=1, source_target_pairs={{0,16},{16,32},{32,48},{48,64},{64,80},{80,96},{96,112},{112,0},{1... | collective-permute-start | bytes 92168 | tf_op jit(solution)/shard_map/ppermute | solution.py:530
  113.2 3.9 %collective-permute-start.11 = (f32[60,128]{1,0:T(8,128)S(1)}, f32[60,128]{1,0:T(8,128)S(1)}, u32[]{:S(2)}, u32[]{:S(2)}) collective-permute-start(f32[60,128]{1,0:T(8,128)S(1)} %get-tuple-element.122), channel_id=1, source_target_pairs={{16,0},{32,16},{48,32},{64,48},{80,64},{96,80},{112,96},{0,112},{1... | collective-permute-start | bytes 92168 | tf_op jit(solution)/shard_map/ppermute | solution.py:531
  123.6 14.2 %all-to-all-start.7 = ((bf16[128,4,128]{2,1,0:T(4,128)(2,1)}), bf16[128,4,128]{2,1,0:T(4,128)(2,1)S(1)}, u32[]{:S(2)}, u32[]{:S(2)}) async-start(bf16[128,4,128]{2,1,0:T(4,128)(2,1)} %bitcast.25), calls=%async_computation.7 | async-start | bytes 262144 | tf_op jit(solution)/shard_map/all_to_all | solution.py:522
  127.6 2.7 %collective-permute-start.12 = (f32[60,128]{1,0:T(8,128)S(1)}, f32[60,128]{1,0:T(8,128)S(1)}, u32[]{:S(2)}, u32[]{:S(2)}) collective-permute-start(f32[60,128]{1,0:T(8,128)S(1)} %get-tuple-element.128), channel_id=1, source_target_pairs={{0,16},{16,32},{32,48},{48,64},{64,80},{80,96},{96,112},{112,0},{1... | collective-permute-start | bytes 92168 | tf_op jit(solution)/shard_map/ppermute | solution.py:530
  129.2 3.9 %collective-permute-start.13 = (f32[60,128]{1,0:T(8,128)S(1)}, f32[60,128]{1,0:T(8,128)S(1)}, u32[]{:S(2)}, u32[]{:S(2)}) collective-permute-start(f32[60,128]{1,0:T(8,128)S(1)} %get-tuple-element.129), channel_id=1, source_target_pairs={{16,0},{32,16},{48,32},{64,48},{80,64},{96,80},{112,96},{0,112},{1... | collective-permute-start | bytes 92168 | tf_op jit(solution)/shard_map/ppermute | solution.py:531
  139.5 14.2 %all-to-all-start.8 = ((bf16[128,4,128]{2,1,0:T(4,128)(2,1)}), bf16[128,4,128]{2,1,0:T(4,128)(2,1)S(1)}, u32[]{:S(2)}, u32[]{:S(2)}) async-start(bf16[128,4,128]{2,1,0:T(4,128)(2,1)} %bitcast.27), calls=%async_computation.8 | async-start | bytes 262144 | tf_op jit(solution)/shard_map/all_to_all | solution.py:522
  143.5 2.7 %collective-permute-start.14 = (f32[60,128]{1,0:T(8,128)S(1)}, f32[60,128]{1,0:T(8,128)S(1)}, u32[]{:S(2)}, u32[]{:S(2)}) collective-permute-start(f32[60,128]{1,0:T(8,128)S(1)} %get-tuple-element.135), channel_id=1, source_target_pairs={{0,16},{16,32},{32,48},{48,64},{64,80},{80,96},{96,112},{112,0},{1... | collective-permute-start | bytes 92168 | tf_op jit(solution)/shard_map/ppermute | solution.py:530
  145.2 3.9 %collective-permute-start.15 = (f32[60,128]{1,0:T(8,128)S(1)}, f32[60,128]{1,0:T(8,128)S(1)}, u32[]{:S(2)}, u32[]{:S(2)}) collective-permute-start(f32[60,128]{1,0:T(8,128)S(1)} %get-tuple-element.136), channel_id=1, source_target_pairs={{16,0},{32,16},{48,32},{64,48},{80,64},{96,80},{112,96},{0,112},{1... | collective-permute-start | bytes 92168 | tf_op jit(solution)/shard_map/ppermute | solution.py:531

commit v7 on v6

--- a/solution.py
+++ b/solution.py
@@ -104,6 +104,10 @@
     return jnp.concatenate([turned[60:64], turned[124:128]], axis=0)
 
 
+def field(n):
+    return pl.ds(n, PEERS, stride=8)
+
+
 def block(n):
     return pl.ds(n, PEERS, stride=4)
 
@@ -121,8 +125,8 @@
     return lax.axis_index("gx") * 16 + lax.axis_index("gy")
 
 
-def peer_rows(shift):
-    return pl.ds(4 * ((me() + shift) & (PEERS - 1)), 4)
+def peer_rows(shift, pitch=4):
+    return pl.ds(pitch * ((me() + shift) & (PEERS - 1)), 4)
 
 
 def tile_to_rows(tile, pad):
@@ -168,7 +172,7 @@
         along[pl.ds(n * ROWS + t * STEP, STEP), :] = tx * value
 
 
-def send_borders(trans, weighted, along, toward_low, toward_high, message, pad):
+def send_borders(trans, weighted, along, toward_low, toward_high, message, pad, pitch=4):
     toward_low[...] = along[pl.ds(0, 3 * NZ, stride=CX), :]
     toward_high[...] = along[pl.ds(CX - 1, 3 * NZ, stride=CX), :]
     small = lanes((8, 128))
@@ -186,7 +190,7 @@
     low = pltpu.roll(low, 127, 1)
     mine = is_slot(lanes((4, 128)))
     for shift, tile in ((1, high), (-1, low)):
-        rows = peer_rows(shift)
+        rows = peer_rows(shift, pitch)
         packed = tile_to_rows(tile, pad)
         message[rows, :] = jnp.where(mine, message[rows, :], packed)
 
@@ -220,17 +224,33 @@
             near[n, rows, :] = tx * nx + ty * ny + tz * nz
 
 
-def cell_setup(rhs_in, diag_in, mobility_in, trans_in, cells_in, pi_in,
-               rows_of, rows_to, start, weight, slots,
-               weighted, toward_low, toward_high, message, along, pad, forward, wide,
-               rhs, diag, mobility, trans, cells, pi, sems):
-    pairs = ((cells_in, cells), (pi_in, pi), (rhs_in, rhs), (diag_in, diag),
+def cell_setup(rhs_in, diag_in, mobility_in, trans_in, cells_in, pi_in, index_in, parent_in,
+               across_in, source_in,
+               rows_of, rows_to, start, weight, slots, fixed,
+               weighted, toward_low, toward_high, message, along, pad, forward, own,
+               rhs, diag, mobility, trans, cells, pi, index, parent, across, source, sems):
+    pairs = ((cells_in, cells), (pi_in, pi), (index_in, index), (parent_in, parent),
+             (across_in, across), (source_in, source), (rhs_in, rhs), (diag_in, diag),
              (mobility_in, mobility), (trans_in, trans))
     copies = [pltpu.make_async_copy(a, b, sems.at[n]) for n, (a, b) in enumerate(pairs)]
     for copy in copies:
         copy.start()
-    for copy in copies[:2]:
+    for copy in copies[:6]:
         copy.wait()
+    zeros = jnp.zeros((6, 128), F32)
+    linked = jnp.concatenate([(parent[...] >= 0).astype(F32), zeros], axis=0)
+    moving = jnp.concatenate([across[...], zeros], axis=0)
+    given = jnp.concatenate([source[...], zeros], axis=0)
+    partial = moving + following(linked * moving)
+    fixed[0] = linked
+    fixed[1] = moving
+    fixed[2] = given
+    fixed[3] = partial
+    number = index[...]
+    own[field(1), :], own[field(3), :] = halves(to_columns(segment_values(given, number)))
+    own[field(4), :], own[field(5), :] = halves(to_columns(segment_values(partial, number)))
+    own[field(6), :] = jnp.zeros((PEERS, 128), F32)
+    own[field(7), :] = jnp.zeros((PEERS, 128), F32)
     base = cells[0:1, :]
     row = lax.shift_right_logical(base, 7)
     live = pi[...]
@@ -248,8 +268,11 @@
     start[...] = begin
     weights = jnp.where(is_slot(lanes((PEERS, 128))), info, 0.0)
     weight[...] = weights
-    wide[block(1), :], wide[block(3), :] = halves(weights)
-    for copy in copies[2:4]:
+    high, low = halves(live)
+    common = jnp.concatenate([low, number.astype(F32)], axis=0).astype(BF16)
+    for d in range(PEERS):
+        message[pl.ds(32 * d + 16, 16), :] = common
+    for copy in copies[6:8]:
         copy.wait()
     for t in range(CHUNKS):
         rows = chunk(t)
@@ -259,33 +282,52 @@
             weighted[n, rows, :] = values[n]
     values = slot_values(rows_of[...], begin, forward[...])
     slots[...] = values
-    wide[block(0), :], wide[block(2), :] = halves(values)
-    for copy in copies[4:]:
+    own[field(0), :], own[field(2), :] = halves(values)
+    for copy in copies[8:]:
         copy.wait()
     for t in range(CHUNKS):
         values = [weighted[n, chunk(t), :] for n in range(3)]
         borders(values, mobility, trans, weighted, along, t)
-    send_borders(trans, weighted, along, toward_low, toward_high, wide, pad)
-    message[...] = wide[...].astype(BF16)
-
-
-def well_tables(index, parent, trans, rhs, table, fixed):
+    send_borders(trans, weighted, along, toward_low, toward_high, own, pad, 8)
+    for d in range(PEERS):
+        both = jnp.concatenate([own[pl.ds(8 * d, 8), :], high], axis=0)
+        message[pl.ds(32 * d, 16), :] = both.astype(BF16)
+
+
+def well_tables(index, table):
     low = index[...] & 127
     for k in range(CAP):
         hit = subs((128, 128)) == jnp.broadcast_to(low[k : k + 1], (128, 128))
         table[:, 128 * k : 128 * (k + 1)] = hit.astype(F32).astype(BF16)
-    zeros = jnp.zeros((6, 128), F32)
-    linked = jnp.concatenate([(parent[...] >= 0).astype(F32), zeros], axis=0)
-    across = jnp.concatenate([trans[...], zeros], axis=0)
-    fixed[0] = linked
-    fixed[1] = across
-    fixed[2] = jnp.concatenate([rhs[...], zeros], axis=0)
-    fixed[3] = across + following(linked * across)
-
-
-def well_setup(arrived, index, table, fixed, message, weight, state, at_slots, diagonal, wide):
+
+
+def well_setup(arrived, index, table, fixed, message, weight, state, at_slots, diagonal,
+               wide, turned):
     wide[...] = arrived[...].astype(F32)
-    pi = to_rows(wide[block(1), :] + wide[block(3), :])
+
+    def part(n):
+        return wide[pl.ds(n, PEERS, stride=32), :]
+
+    lane = lanes((PEERS, 128))
+    mine = lane == me()
+    for k in range(CAP):
+        turned[k] = (part(8 + k) + part(16 + k)).T
+    total = part(4) + part(5)
+    for k in range(CAP):
+        target = jnp.sum(jnp.where(mine, part(24 + k), 0.0), axis=1, keepdims=True)
+        target = jnp.broadcast_to(target, (PEERS, 128))
+        found = jnp.zeros((PEERS, 128), F32)
+        for m in range(CAP):
+            found += jnp.where(part(24 + m) == target, turned[m], 0.0)
+        place = 60 + k if k < 4 else 120 + k
+        total += jnp.where(lane == place, jnp.sum(found, axis=1, keepdims=True), 0.0)
+    slot = is_slot(lane)
+    pressures = (part(1) + part(3)) / jnp.where(slot, total, 1.0)
+    message[block(0), :] = jnp.where(slot, part(0) + part(2), part(0))
+    message[block(1), :] = jnp.where(slot, pressures, part(1))
+    message[block(2), :] = part(2)
+    message[block(3), :] = part(3)
+    pi = jnp.concatenate([turned[k, pl.ds(me(), 1), :] for k in range(CAP)], axis=0)
     weight[...] = pi
     number = index[...]
     total = fixed[3] + into_segments(pi, number, table[...])
@@ -293,9 +335,7 @@
     diagonal[...] = total
     now = fixed[2] / total
     state[...] = now
-    values = segment_values(now, number)
-    at_slots[...] = values
-    message[...] = to_columns(values)
+    at_slots[...] = segment_values(now, number)
 
 
 def ratio(sums, place):
@@ -317,12 +357,12 @@
 MOVING = ("arrived", "near", "from_low", "from_high", "slots", "at_slots", "state")
 NEXT = ("weighted", "toward_low", "toward_high", "message", "slots", "at_slots", "state")
 MORE_IN = {
-    "first": ("pressures",), "plain": (), "keep": (), "last": ("field",), "after": (),
+    "plain": (), "keep": (), "last": ("field",), "after": (),
     "final": ("field", "change", "seg_change", "omega"),
 }
-NARROW = ("first", "plain", "keep", "after")
+NARROW = ("plain", "keep", "after")
 MORE_OUT = {
-    "first": (), "plain": (), "keep": ("field",), "last": ("change", "seg_change"),
+    "plain": (), "keep": ("field",), "last": ("change", "seg_change"),
     "after": ("omega",), "final": (),
 }
 
@@ -348,10 +388,7 @@
         wide[...] = arrived[...].astype(F32)
         arrived = wide
         heads = arrived[block(0), :] + arrived[block(2), :]
-        if kind == "first":
-            pressures = extra["pressures"][...]
-        else:
-            pressures = arrived[block(1), :] + arrived[block(3), :]
+        pressures = arrived[block(1), :] + arrived[block(3), :]
     else:
         heads, pressures = arrived[block(0), :], arrived[block(1), :]
     pull = fixed["weight"][...] * (now["slots"][...] - pressures)
@@ -542,15 +579,17 @@
     index = perf_seg[0]
 
     fixed = {"rhs": rhs, "diag": diag, "mobility": mobility, "trans": trans, "index": index}
-    inputs = [rhs, diag, mobility, trans, perf_cell[0], perf_pi[0]]
-    packed = (MESSAGE[0], BF16)
-    (rows_of, rows_to, start, weight, slots, weighted, toward_low, toward_high, message) = call(
+    inputs = [rhs, diag, mobility, trans, perf_cell[0], perf_pi[0], index]
+    inputs += [a.reshape(2, 128) for a in (seg_parent, seg_trans, seg_rhs)]
+    (rows_of, rows_to, start, weight, slots, constants, weighted, toward_low, toward_high,
+     message) = call(
         cell_setup,
         [((PEERS, ROWS), BF16), ((ROWS, PEERS), BF16),
-         ((PEERS, 128), jnp.int32), PAIRS, PAIRS, CELLS, EDGE, EDGE, packed],
+         ((PEERS, 128), jnp.int32), PAIRS, PAIRS, ((4, 8, 128), F32), CELLS, EDGE, EDGE,
+         ((32 * PEERS, 128), BF16)],
         inputs,
-        SCRATCH + (pltpu.VMEM(*MESSAGE),) + tuple(pltpu.VMEM(a.shape, a.dtype) for a in inputs)
-        + (pltpu.SemaphoreType.DMA((6,)),),
+        SCRATCH + (pltpu.VMEM((8 * PEERS, 128), F32),)
+        + tuple(pltpu.VMEM(a.shape, a.dtype) for a in inputs) + (pltpu.SemaphoreType.DMA((10,)),),
         name="cell_setup",
         space=pltpu.HBM,
         grant=64 * 1024 * 1024 - 256 * 1024,
@@ -560,25 +599,20 @@
     def inside(weighted):
         return call(interior, [CELLS], [weighted, trans], name="interior")[0]
 
-    table, constants = call(
-        well_tables,
-        [((128, CAP * 128), BF16), ((4, 8, 128), F32)],
-        [index, seg_parent.reshape(2, 128), seg_trans.reshape(2, 128), seg_rhs.reshape(2, 128)],
-        name="well_tables",
-    )
+    (table,) = call(well_tables, [((128, CAP * 128), BF16)], [index], name="well_tables")
     fixed.update(rows_of=rows_of, rows_to=rows_to, start=start, weight=weight)
-    now = {"arrived": arrived, "near": inside(weighted), "slots": slots}
+    now = {"near": inside(weighted), "slots": slots}
     now.update(neighbours(toward_low, toward_high))
-    message, own_weight, state, at_slots, diagonal = call(
+    now["arrived"], own_weight, state, at_slots, diagonal = call(
         well_setup,
-        [PAIRS, TILE, TILE, TILE, TILE],
+        [MESSAGE, TILE, TILE, TILE, TILE],
         [arrived, index, table, constants],
-        [pltpu.VMEM(*MESSAGE)],
+        [pltpu.VMEM((32 * PEERS, 128), F32), pltpu.VMEM((CAP, PEERS, 128), F32)],
         name="well_setup",
     )
     fixed.update(own_weight=own_weight, table=table, fixed=constants, diagonal=diagonal)
     now.update(at_slots=at_slots, state=state)
-    saved = {"pressures": exchange(message)}
+    saved = {}
 
     def advance(kind, now):
         args = [now[name] for name in MOVING]
@@ -599,7 +633,7 @@
             out["near"] = inside(out.pop("weighted"))
         return out
 
-    now = advance("first", now)
+    now = advance("plain", now)
     now = advance("plain", now)
     one = advance("keep", now)
     saved["field"] = one["field"]

time: 169 us -> 166 us (0.982)
  starting transfers between devices: 57.4 us -> 53.2 us
    all_to_all x9 -> x8, starting transfers between devices: 44.2 us -> 39.9 us  [exchange(): lax.all_to_all(message, AXES, split_axis=0, concat_axis=0, tiled=True)]
    all_to_all x9 -> x8, waiting for transfers between devices: 46.9 us -> 49.9 us  [exchange(): lax.all_to_all(message, AXES, split_axis=0, concat_axis=0, tiled=True)]
    ppermute x8, waiting for transfers between devices: 23.1 us -> 20.5 us  [neighbours(): lax.ppermute(toward_low, 'gx', down)]
  transfers between devices with their start and end apart: 25 -> 24, of which waited for: 25 -> 22; matrix products, arithmetic and copies ran while one was open for 0% -> 0% of each run, Pallas kernels for 1% -> 2%
where the time goes in v7:
time: 166 us
  waiting for transfers between devices  76.3 us (46%)
  starting transfers between devices  53.2 us (32%)
  Pallas kernels  20.8 us (13%)
  blocking collectives  13.6 us (8%)
    all_to_all x8, waiting for transfers between devices, exchange(): lax.all_to_all(message, AXES, split_axis=0, concat_axis=0, tiled=True)  49.9 us
    all_to_all x8, starting transfers between devices, exchange(): lax.all_to_all(message, AXES, split_axis=0, concat_axis=0, tiled=True)  39.9 us
    pallas_call x20, Pallas kernels, call(): pl.pallas_call(body, out_shape=[jax.ShapeDtypeStruct(*out) for out in out...  20.8 us
    ppermute x8, waiting for transfers between devices, neighbours(): lax.ppermute(toward_low, 'gx', down)  20.5 us
    all_to_all x1, blocking collectives, exchange(): lax.all_to_all(message, AXES, split_axis=0, concat_axis=0, tiled=True)  13.6 us
    ppermute x8, starting transfers between devices, neighbours(): lax.ppermute(toward_high, 'gx', up)  13.3 us
    ppermute x8, waiting for transfers between devices, neighbours(): lax.ppermute(toward_high, 'gx', up)  5.88 us
  transfers between devices with their start and end apart: 24, of which 22 were waited for; matrix products, arithmetic and copies ran while one was open for 0% of the time, Pallas kernels for 2%

profile of v7, /device:TPU:1, one launch (start us, length us, event | category | flops | bytes accessed | tf_op | source)
XLA Modules:
  0.0 165.7 jit_solution(10259452642870439883)
XLA Ops:
  0.6 3.1 %cell_setup.1 = (bf16[128,160]{1,0:T(8,128)(2,1)}, bf16[160,128]{1,0:T(8,128)(2,1)}, s32[128,128]{1,0:T(8,128)}, f32[128,128]{1,0:T(8,128)}, f32[128,128]{1,0:T(...) custom-call(f32[3,160,128]{2,1,0:T(8,128)} %bitcast.67, ...), custom_call_target="tpu_custom_call" | custom-call | flops 4000000 | bytes 1121280 | tf_op jit(solution)/shard_map/cell_setup/pallas_call | solution.py:546
  3.8 11.5 %all-to-all-start = ((bf16[128,32,128]{2,1,0:T(8,128)(2,1)}), bf16[128,32,128]{2,1,0:T(8,128)(2,1)S(1)}, u32[]{:S(2)}, u32[]{:S(2)}) async-start(bf16[128,32,128]{2,1,0:T(8,128)(2,1)} %bitcast.97), calls=%async_computation | async-start | bytes 2097152 | tf_op jit(solution)/shard_map/all_to_all | solution.py:559
  15.3 1.6 collective-permute-start
  17.1 0.8 copy-done
  18.1 16.5 %all-to-all-done = bf16[128,32,128]{2,1,0:T(8,128)(2,1)S(1)} async-done(((bf16[128,32,128]{2,1,0:T(8,128)(2,1)}), bf16[128,32,128]{2,1,0:T(8,128)(2,1)S(1)}, u32[]{:S(2)}, u32[]{:S(2)}) %all-to-all-start) | async-done | bytes 1048608 | tf_op jit(solution)/shard_map/all_to_all | solution.py:559
  34.7 2.1 %well_setup.1 = (f32[512,128]{1,0:T(8,128)S(1)}, f32[8,128]{1,0:T(8,128)S(1)}, f32[8,128]{1,0:T(8,128)S(1)}, f32[8,128]{1,0:T(8,128)S(1)}, f32[8,128]{1,0:T(8,128)S(1)}) custom-call(bf16[4096,128]{1,0:T(8,128)(2,1)S(1)} %bitcast.76, s32[8,128]{1,0:T(8,128)S(1)} %bitcast.86, bf16[128,1024]{1,0:T(8,128)(2,1)S(1)} %well_tables.1.table.refs_16_, ...), custom_call_target="tpu_custom_call" | custom-call | flops 4000000 | bytes 1331200 | tf_op jit(solution)/shard_map/well_setup/pallas_call | solution.py:546
  36.9 1.7 %sweep_plain.3 = (f32[3,160,128]{2,1,0:T(8,128)S(1)}, f32[60,128]{1,0:T(8,128)S(1)}, f32[60,128]{1,0:T(8,128)S(1)}, bf16[512,128]{1,0:T(8,128)(2,1)}, f32[128,12...) custom-call(f32[512,128]{1,0:T(8,128)S(1)} %get-tuple-element.75.refs_0_, ...), custom_call_target="tpu_custom_call" | custom-call | flops 4000000 | bytes 2252800 | tf_op jit(solution)/shard_map/sweep_plain/pallas_call | solution.py:546
  38.6 4.2 %all-to-all-start.1 = ((bf16[128,4,128]{2,1,0:T(4,128)(2,1)}), bf16[128,4,128]{2,1,0:T(4,128)(2,1)S(1)}, u32[]{:S(2)}, u32[]{:S(2)}) async-start(bf16[128,4,128]{2,1,0:T(4,128)(2,1)} %bitcast.12), calls=%async_computation.1 | async-start | bytes 262144 | tf_op jit(solution)/shard_map/all_to_all | solution.py:559
  42.9 1.7 %collective-permute-start.2 = (f32[60,128]{1,0:T(8,128)S(1)}, f32[60,128]{1,0:T(8,128)S(1)}, u32[]{:S(2)}, u32[]{:S(2)}) collective-permute-start(f32[60,128]{1,0:T(8,128)S(1)} %get-tuple-element.90), channel_id=1, source_target_pairs={{0,16},{16,32},{32,48},{48,64},{64,80},{80,96},{96,112},{112,0},{1... | collective-permute-start | bytes 92168 | tf_op jit(solution)/shard_map/ppermute | solution.py:567
  45.6 2.9 %collective-permute-done.3.refs_3_ = f32[60,128]{1,0:T(8,128)S(1)} collective-permute-done((f32[60,128]{1,0:T(8,128)S(1)}, f32[60,128]{1,0:T(8,128)S(1)}, u32[]{:S(2)}, u32[]{:S(2)}) %collective-permute-start.3) | collective-permute-done | bytes 30752 | tf_op jit(solution)/shard_map/ppermute | solution.py:568
  48.5 4.7 %all-to-all-done.1 = bf16[128,4,128]{2,1,0:T(4,128)(2,1)S(1)} async-done(((bf16[128,4,128]{2,1,0:T(4,128)(2,1)}), bf16[128,4,128]{2,1,0:T(4,128)(2,1)S(1)}, u32[]{:S(2)}, u32[]{:S(2)}) %all-to-all-start.1) | async-done | bytes 131104 | tf_op jit(solution)/shard_map/all_to_all | solution.py:559
  53.2 1.7 %sweep_plain.4 = (f32[3,160,128]{2,1,0:T(8,128)S(1)}, f32[60,128]{1,0:T(8,128)S(1)}, f32[60,128]{1,0:T(8,128)S(1)}, bf16[512,128]{1,0:T(8,128)(2,1)}, f32[128,12...) custom-call(bf16[512,128]{1,0:T(8,128)(2,1)S(1)} %bitcast.81, f32[3,160,128]{2,1,0:T(8,128)S(1)} %interior.9.refs_1_, ...), custom_call_target="tpu_custom_call" | custom-call | flops 4000000 | bytes 2121728 | tf_op jit(solution)/shard_map/sweep_plain/pallas_call | solution.py:546
  54.9 4.0 %all-to-all-start.2 = ((bf16[128,4,128]{2,1,0:T(4,128)(2,1)}), bf16[128,4,128]{2,1,0:T(4,128)(2,1)S(1)}, u32[]{:S(2)}, u32[]{:S(2)}) async-start(bf16[128,4,128]{2,1,0:T(4,128)(2,1)} %bitcast.14), calls=%async_computation.2 | async-start | bytes 262144 | tf_op jit(solution)/shard_map/all_to_all | solution.py:559
  59.0 1.6 collective-permute-start.4
  60.8 0.8 collective-permute-done.4.refs_2_
  61.6 2.9 %collective-permute-done.5.refs_3_ = f32[60,128]{1,0:T(8,128)S(1)} collective-permute-done((f32[60,128]{1,0:T(8,128)S(1)}, f32[60,128]{1,0:T(8,128)S(1)}, u32[]{:S(2)}, u32[]{:S(2)}) %collective-permute-start.5) | collective-permute-done | bytes 30752 | tf_op jit(solution)/shard_map/ppermute | solution.py:568
  64.5 4.6 %all-to-all-done.2 = bf16[128,4,128]{2,1,0:T(4,128)(2,1)S(1)} async-done(((bf16[128,4,128]{2,1,0:T(4,128)(2,1)}), bf16[128,4,128]{2,1,0:T(4,128)(2,1)S(1)}, u32[]{:S(2)}, u32[]{:S(2)}) %all-to-all-start.2) | async-done | bytes 131104 | tf_op jit(solution)/shard_map/all_to_all | solution.py:559
  69.2 1.7 %sweep_keep.2 = (f32[3,160,128]{2,1,0:T(8,128)S(1)}, f32[60,128]{1,0:T(8,128)S(1)}, f32[60,128]{1,0:T(8,128)S(1)}, bf16[512,128]{1,0:T(8,128)(2,1)}, f32[128,128...) custom-call(bf16[512,128]{1,0:T(8,128)(2,1)S(1)} %bitcast.78, ...), custom_call_target="tpu_custom_call" | custom-call | flops 4000000 | bytes 2121728 | tf_op jit(solution)/shard_map/sweep_keep/pallas_call | solution.py:546
  70.9 4.0 %all-to-all-start.3 = ((bf16[128,4,128]{2,1,0:T(4,128)(2,1)}), bf16[128,4,128]{2,1,0:T(4,128)(2,1)S(1)}, u32[]{:S(2)}, u32[]{:S(2)}) async-start(bf16[128,4,128]{2,1,0:T(4,128)(2,1)} %bitcast.16), calls=%async_computation.3 | async-start | bytes 262144 | tf_op jit(solution)/shard_map/all_to_all | solution.py:559
  74.9 1.6 collective-permute-start.6
  76.8 0.8 collective-permute-done.6.refs_2_
  77.6 2.9 %collective-permute-done.7.refs_3_ = f32[60,128]{1,0:T(8,128)S(1)} collective-permute-done((f32[60,128]{1,0:T(8,128)S(1)}, f32[60,128]{1,0:T(8,128)S(1)}, u32[]{:S(2)}, u32[]{:S(2)}) %collective-permute-start.7) | collective-permute-done | bytes 30752 | tf_op jit(solution)/shard_map/ppermute | solution.py:568
  80.5 4.6 %all-to-all-done.3 = bf16[128,4,128]{2,1,0:T(4,128)(2,1)S(1)} async-done(((bf16[128,4,128]{2,1,0:T(4,128)(2,1)}), bf16[128,4,128]{2,1,0:T(4,128)(2,1)S(1)}, u32[]{:S(2)}, u32[]{:S(2)}) %all-to-all-start.3) | async-done | bytes 131104 | tf_op jit(solution)/shard_map/all_to_all | solution.py:559
  85.1 1.8 %sweep_last.1 = (f32[3,160,128]{2,1,0:T(8,128)S(1)}, f32[60,128]{1,0:T(8,128)S(1)}, f32[60,128]{1,0:T(8,128)S(1)}, f32[512,128]{1,0:T(8,128)}, f32[128,128]{1,0:...) custom-call(bf16[512,128]{1,0:T(8,128)(2,1)S(1)} %bitcast.79, ...), custom_call_target="tpu_custom_call" | custom-call | flops 4000000 | bytes 2367488 | tf_op jit(solution)/shard_map/sweep_last/pallas_call | solution.py:546
  87.0 4.0 %all-to-all-start.4 = ((f32[128,4,128]{2,1,0:T(4,128)}), f32[128,4,128]{2,1,0:T(4,128)S(1)}, u32[]{:S(2)}, u32[]{:S(2)}) async-start(f32[128,4,128]{2,1,0:T(4,128)} %bitcast.18), calls=%async_computation.4 | async-start | bytes 524288 | tf_op jit(solution)/shard_map/all_to_all | solution.py:559
  91.0 1.6 collective-permute-start.8
  92.9 1.1 collective-permute-done.8.refs_2_
  93.9 3.1 %collective-permute-done.9.refs_3_ = f32[60,128]{1,0:T(8,128)S(1)} collective-permute-done((f32[60,128]{1,0:T(8,128)S(1)}, f32[60,128]{1,0:T(8,128)S(1)}, u32[]{:S(2)}, u32[]{:S(2)}) %collective-permute-start.9) | collective-permute-done | bytes 30752 | tf_op jit(solution)/shard_map/ppermute | solution.py:568
  97.0 5.4 %all-to-all-done.4 = f32[128,4,128]{2,1,0:T(4,128)S(1)} async-done(((f32[128,4,128]{2,1,0:T(4,128)}), f32[128,4,128]{2,1,0:T(4,128)S(1)}, u32[]{:S(2)}, u32[]{:S(2)}) %all-to-all-start.4) | async-done | bytes 262176 | tf_op jit(solution)/shard_map/all_to_all | solution.py:559
  102.5 1.7 %sweep_after.1 = (f32[3,160,128]{2,1,0:T(8,128)S(1)}, f32[60,128]{1,0:T(8,128)S(1)}, f32[60,128]{1,0:T(8,128)S(1)}, bf16[512,128]{1,0:T(8,128)(2,1)}, f32[128,12...) custom-call(f32[512,128]{1,0:T(8,128)S(1)} %bitcast.77, ...), custom_call_target="tpu_custom_call" | custom-call | flops 4000000 | bytes 2252800 | tf_op jit(solution)/shard_map/sweep_after/pallas_call | solution.py:546
  104.2 4.1 %all-to-all-start.5 = ((bf16[128,4,128]{2,1,0:T(4,128)(2,1)}), bf16[128,4,128]{2,1,0:T(4,128)(2,1)S(1)}, u32[]{:S(2)}, u32[]{:S(2)}) async-start(bf16[128,4,128]{2,1,0:T(4,128)(2,1)} %bitcast.20), calls=%async_computation.5 | async-start | bytes 262144 | tf_op jit(solution)/shard_map/all_to_all | solution.py:559
  108.2 1.7 %collective-permute-start.10 = (f32[60,128]{1,0:T(8,128)S(1)}, f32[60,128]{1,0:T(8,128)S(1)}, u32[]{:S(2)}, u32[]{:S(2)}) collective-permute-start(f32[60,128]{1,0:T(8,128)S(1)} %get-tuple-element.119), channel_id=1, source_target_pairs={{0,16},{16,32},{32,48},{48,64},{64,80},{80,96},{96,112},{112,0},{1... | collective-permute-start | bytes 92168 | tf_op jit(solution)/shard_map/ppermute | solution.py:567
  110.2 0.8 collective-permute-done.10.refs_2_
  111.0 2.9 %collective-permute-done.11.refs_3_ = f32[60,128]{1,0:T(8,128)S(1)} collective-permute-done((f32[60,128]{1,0:T(8,128)S(1)}, f32[60,128]{1,0:T(8,128)S(1)}, u32[]{:S(2)}, u32[]{:S(2)}) %collective-permute-start.11) | collective-permute-done | bytes 30752 | tf_op jit(solution)/shard_map/ppermute | solution.py:568
  113.9 4.7 %all-to-all-done.5 = bf16[128,4,128]{2,1,0:T(4,128)(2,1)S(1)} async-done(((bf16[128,4,128]{2,1,0:T(4,128)(2,1)}), bf16[128,4,128]{2,1,0:T(4,128)(2,1)S(1)}, u32[]{:S(2)}, u32[]{:S(2)}) %all-to-all-start.5) | async-done | bytes 131104 | tf_op jit(solution)/shard_map/all_to_all | solution.py:559
  118.6 1.7 %sweep_plain.5 = (f32[3,160,128]{2,1,0:T(8,128)S(1)}, f32[60,128]{1,0:T(8,128)S(1)}, f32[60,128]{1,0:T(8,128)S(1)}, bf16[512,128]{1,0:T(8,128)(2,1)}, f32[128,12...) custom-call(bf16[512,128]{1,0:T(8,128)(2,1)S(1)} %bitcast.82, f32[3,160,128]{2,1,0:T(8,128)S(1)} %interior.13.refs_1_, ...), custom_call_target="tpu_custom_call" | custom-call | flops 4000000 | bytes 2121728 | tf_op jit(solution)/shard_map/sweep_plain/pallas_call | solution.py:546
  120.3 4.0 %all-to-all-start.6 = ((bf16[128,4,128]{2,1,0:T(4,128)(2,1)}), bf16[128,4,128]{2,1,0:T(4,128)(2,1)S(1)}, u32[]{:S(2)}, u32[]{:S(2)}) async-start(bf16[128,4,128]{2,1,0:T(4,128)(2,1)} %bitcast.22), calls=%async_computation.6 | async-start | bytes 262144 | tf_op jit(solution)/shard_map/all_to_all | solution.py:559
  124.3 1.6 collective-permute-start.12
  126.2 0.8 collective-permute-done.12.refs_2_
  127.0 2.9 %collective-permute-done.13.refs_3_ = f32[60,128]{1,0:T(8,128)S(1)} collective-permute-done((f32[60,128]{1,0:T(8,128)S(1)}, f32[60,128]{1,0:T(8,128)S(1)}, u32[]{:S(2)}, u32[]{:S(2)}) %collective-permute-start.13) | collective-permute-done | bytes 30752 | tf_op jit(solution)/shard_map/ppermute | solution.py:568
  129.9 4.6 %all-to-all-done.6 = bf16[128,4,128]{2,1,0:T(4,128)(2,1)S(1)} async-done(((bf16[128,4,128]{2,1,0:T(4,128)(2,1)}), bf16[128,4,128]{2,1,0:T(4,128)(2,1)S(1)}, u32[]{:S(2)}, u32[]{:S(2)}) %all-to-all-start.6) | async-done | bytes 131104 | tf_op jit(solution)/shard_map/all_to_all | solution.py:559
  134.5 1.7 %sweep_keep.3 = (f32[3,160,128]{2,1,0:T(8,128)S(1)}, f32[60,128]{1,0:T(8,128)S(1)}, f32[60,128]{1,0:T(8,128)S(1)}, bf16[512,128]{1,0:T(8,128)(2,1)}, f32[128,128...) custom-call(bf16[512,128]{1,0:T(8,128)(2,1)S(1)} %bitcast.80, ...), custom_call_target="tpu_custom_call" | custom-call | flops 4000000 | bytes 2121728 | tf_op jit(solution)/shard_map/sweep_keep/pallas_call | solution.py:546
  136.3 4.0 %all-to-all-start.7 = ((bf16[128,4,128]{2,1,0:T(4,128)(2,1)}), bf16[128,4,128]{2,1,0:T(4,128)(2,1)S(1)}, u32[]{:S(2)}, u32[]{:S(2)}) async-start(bf16[128,4,128]{2,1,0:T(4,128)(2,1)} %bitcast.24), calls=%async_computation.7 | async-start | bytes 262144 | tf_op jit(solution)/shard_map/all_to_all | solution.py:559
  140.3 1.6 collective-permute-start.14
  143.0 2.9 %collective-permute-done.15.refs_3_ = f32[60,128]{1,0:T(8,128)S(1)} collective-permute-done((f32[60,128]{1,0:T(8,128)S(1)}, f32[60,128]{1,0:T(8,128)S(1)}, u32[]{:S(2)}, u32[]{:S(2)}) %collective-permute-start.15) | collective-permute-done | bytes 30752 | tf_op jit(solution)/shard_map/ppermute | solution.py:568
  145.9 4.6 %all-to-all-done.7 = bf16[128,4,128]{2,1,0:T(4,128)(2,1)S(1)} async-done(((bf16[128,4,128]{2,1,0:T(4,128)(2,1)}), bf16[128,4,128]{2,1,0:T(4,128)(2,1)S(1)}, u32[]{:S(2)}, u32[]{:S(2)}) %all-to-all-start.7) | async-done | bytes 131104 | tf_op jit(solution)/shard_map/all_to_all | solution.py:559
  151.2 13.6 %all_to_all.99 = f32[128,1,128]{2,1,0:T(1,128)S(1)} all-to-all(f32[128,1,128]{2,1,0:T(1,128)S(1)} %bitcast.95), channel_id=1, replica_groups=mesh['gx'=8,'gy'=16] {'gx','gy'}, dimensions={0} | all-to-all | bytes 131072 | tf_op jit(solution)/shard_map/all_to_all | solution.py:559
  164.8 0.8 finish.1
  (49 shorter events, 4.2 us)
Async XLA Ops:
  3.8 11.6 %copy-start.13 = (f32[60,128]{1,0:T(8,128)S(1)}, f32[60,128]{1,0:T(8,128)}, u32[]{:S(2)}) copy-start(f32[60,128]{1,0:T(8,128)} %get-tuple-element.77) | copy-start | bytes 92164
  3.8 13.2 %copy-start.12 = (f32[60,128]{1,0:T(8,128)S(1)}, f32[60,128]{1,0:T(8,128)}, u32[]{:S(2)}) copy-start(f32[60,128]{1,0:T(8,128)} %get-tuple-element.78) | copy-start | bytes 92164
  3.8 13.2 %copy-start.9 = (s32[1,8,128]{2,1,0:T(8,128)S(1)}, s32[1,8,128]{2,1,0:T(8,128)}, u32[]{:S(2)}) copy-start(s32[1,8,128]{2,1,0:T(8,128)} %param.16) | copy-start | bytes 12292
  3.8 13.3 %copy-start.10 = (f32[3,160,128]{2,1,0:T(8,128)S(1)}, f32[3,160,128]{2,1,0:T(8,128)}, u32[]{:S(2)}) copy-start(f32[3,160,128]{2,1,0:T(8,128)} %get-tuple-element.76.weighted) | copy-start | bytes 737284
  3.8 30.8 %all-to-all-start = ((bf16[128,32,128]{2,1,0:T(8,128)(2,1)}), bf16[128,32,128]{2,1,0:T(8,128)(2,1)S(1)}, u32[]{:S(2)}, u32[]{:S(2)}) async-start(bf16[128,32,128]{2,1,0:T(8,128)(2,1)} %bitcast.97), calls=%async_computation | async-start | bytes 2097152 | tf_op jit(solution)/shard_map/all_to_all | solution.py:559
  15.3 21.5 %collective-permute-start = (f32[60,128]{1,0:T(8,128)S(1)}, f32[60,128]{1,0:T(8,128)S(1)}, u32[]{:S(2)}, u32[]{:S(2)}) collective-permute-start(f32[60,128]{1,0:T(8,128)S(1)} %copy-done.13), channel_id=1, source_target_pairs={{0,16},{16,32},{32,48},{48,64},{64,80},{80,96},{96,112},{112,0},{1... | collective-permute-start | bytes 92168 | tf_op jit(solution)/shard_map/ppermute | solution.py:567
  17.0 0.9 copy-start
  17.0 19.8 %collective-permute-start.1 = (f32[60,128]{1,0:T(8,128)S(1)}, f32[60,128]{1,0:T(8,128)S(1)}, u32[]{:S(2)}, u32[]{:S(2)}) collective-permute-start(f32[60,128]{1,0:T(8,128)S(1)} %copy-done.12), channel_id=1, source_target_pairs={{16,0},{32,16},{48,32},{64,48},{80,64},{96,80},{112,96},{0,112},{1... | collective-permute-start | bytes 92168 | tf_op jit(solution)/shard_map/ppermute | solution.py:568
  17.9 16.7 %copy-start.8 = (f32[4,8,128]{2,1,0:T(8,128)S(1)}, f32[4,8,128]{2,1,0:T(8,128)}, u32[]{:S(2)}) copy-start(f32[4,8,128]{2,1,0:T(8,128)} %get-tuple-element.74.fixed.refs_18_) | copy-start | bytes 49156
  34.6 2.2 %copy-start.1 = (bf16[9,20,8,128]{3,2,1,0:T(8,128)(2,1)S(1)}, bf16[9,20,8,128]{3,2,1,0:T(8,128)(2,1)}, u32[]{:S(2)}) copy-start(bf16[9,20,8,128]{3,2,1,0:T(8,128)(2,1)} %param.11) | copy-start | bytes 1105924
  34.6 2.2 %copy-start.2 = (bf16[9,20,8,128]{3,2,1,0:T(8,128)(2,1)S(1)}, bf16[9,20,8,128]{3,2,1,0:T(8,128)(2,1)}, u32[]{:S(2)}) copy-start(bf16[9,20,8,128]{3,2,1,0:T(8,128)(2,1)} %param.12) | copy-start | bytes 1105924
  34.6 2.2 %copy-start.3 = (f32[3,20,8,128]{3,2,1,0:T(8,128)S(1)}, f32[3,20,8,128]{3,2,1,0:T(8,128)}, u32[]{:S(2)}) copy-start(f32[3,20,8,128]{3,2,1,0:T(8,128)} %param.10) | copy-start | bytes 737284
  34.6 2.2 %copy-start.4 = (bf16[128,160]{1,0:T(8,128)(2,1)S(1)}, bf16[128,160]{1,0:T(8,128)(2,1)}, u32[]{:S(2)}) copy-start(bf16[128,160]{1,0:T(8,128)(2,1)} %get-tuple-element.82.refs_11_) | copy-start | bytes 122884
  34.6 2.2 %copy-start.5 = (s32[128,128]{1,0:T(8,128)S(1)}, s32[128,128]{1,0:T(8,128)}, u32[]{:S(2)}) copy-start(s32[128,128]{1,0:T(8,128)} %get-tuple-element.84.refs_13_) | copy-start | bytes 196612
  34.6 2.2 %copy-start.6 = (f32[128,128]{1,0:T(8,128)S(1)}, f32[128,128]{1,0:T(8,128)}, u32[]{:S(2)}) copy-start(f32[128,128]{1,0:T(8,128)} %get-tuple-element.85.refs_14_) | copy-start | bytes 196612
  34.6 2.2 %copy-start.7 = (bf16[160,128]{1,0:T(8,128)(2,1)S(1)}, bf16[160,128]{1,0:T(8,128)(2,1)}, u32[]{:S(2)}) copy-start(bf16[160,128]{1,0:T(8,128)(2,1)} %get-tuple-element.83.refs_12_) | copy-start | bytes 122884
  34.7 2.2 %copy-start.11 = (f32[128,128]{1,0:T(8,128)S(1)}, f32[128,128]{1,0:T(8,128)}, u32[]{:S(2)}) copy-start(f32[128,128]{1,0:T(8,128)} %get-tuple-element.79.refs_4_) | copy-start | bytes 196612
  38.6 14.6 %all-to-all-start.1 = ((bf16[128,4,128]{2,1,0:T(4,128)(2,1)}), bf16[128,4,128]{2,1,0:T(4,128)(2,1)S(1)}, u32[]{:S(2)}, u32[]{:S(2)}) async-start(bf16[128,4,128]{2,1,0:T(4,128)(2,1)} %bitcast.12), calls=%async_computation.1 | async-start | bytes 262144 | tf_op jit(solution)/shard_map/all_to_all | solution.py:559
  42.9 2.7 %collective-permute-start.2 = (f32[60,128]{1,0:T(8,128)S(1)}, f32[60,128]{1,0:T(8,128)S(1)}, u32[]{:S(2)}, u32[]{:S(2)}) collective-permute-start(f32[60,128]{1,0:T(8,128)S(1)} %get-tuple-element.90), channel_id=1, source_target_pairs={{0,16},{16,32},{32,48},{48,64},{64,80},{80,96},{96,112},{112,0},{1... | collective-permute-start | bytes 92168 | tf_op jit(solution)/shard_map/ppermute | solution.py:567
  44.6 3.9 %collective-permute-start.3 = (f32[60,128]{1,0:T(8,128)S(1)}, f32[60,128]{1,0:T(8,128)S(1)}, u32[]{:S(2)}, u32[]{:S(2)}) collective-permute-start(f32[60,128]{1,0:T(8,128)S(1)} %get-tuple-element.91), channel_id=1, source_target_pairs={{16,0},{32,16},{48,32},{64,48},{80,64},{96,80},{112,96},{0,112},{1... | collective-permute-start | bytes 92168 | tf_op jit(solution)/shard_map/ppermute | solution.py:568
  54.9 14.2 %all-to-all-start.2 = ((bf16[128,4,128]{2,1,0:T(4,128)(2,1)}), bf16[128,4,128]{2,1,0:T(4,128)(2,1)S(1)}, u32[]{:S(2)}, u32[]{:S(2)}) async-start(bf16[128,4,128]{2,1,0:T(4,128)(2,1)} %bitcast.14), calls=%async_computation.2 | async-start | bytes 262144 | tf_op jit(solution)/shard_map/all_to_all | solution.py:559
  59.0 2.7 %collective-permute-start.4 = (f32[60,128]{1,0:T(8,128)S(1)}, f32[60,128]{1,0:T(8,128)S(1)}, u32[]{:S(2)}, u32[]{:S(2)}) collective-permute-start(f32[60,128]{1,0:T(8,128)S(1)} %get-tuple-element.97), channel_id=1, source_target_pairs={{0,16},{16,32},{32,48},{48,64},{64,80},{80,96},{96,112},{112,0},{1... | collective-permute-start | bytes 92168 | tf_op jit(solution)/shard_map/ppermute | solution.py:567
  60.6 3.9 %collective-permute-start.5 = (f32[60,128]{1,0:T(8,128)S(1)}, f32[60,128]{1,0:T(8,128)S(1)}, u32[]{:S(2)}, u32[]{:S(2)}) collective-permute-start(f32[60,128]{1,0:T(8,128)S(1)} %get-tuple-element.98), channel_id=1, source_target_pairs={{16,0},{32,16},{48,32},{64,48},{80,64},{96,80},{112,96},{0,112},{1... | collective-permute-start | bytes 92168 | tf_op jit(solution)/shard_map/ppermute | solution.py:568
  70.9 14.2 %all-to-all-start.3 = ((bf16[128,4,128]{2,1,0:T(4,128)(2,1)}), bf16[128,4,128]{2,1,0:T(4,128)(2,1)S(1)}, u32[]{:S(2)}, u32[]{:S(2)}) async-start(bf16[128,4,128]{2,1,0:T(4,128)(2,1)} %bitcast.16), calls=%async_computation.3 | async-start | bytes 262144 | tf_op jit(solution)/shard_map/all_to_all | solution.py:559
  74.9 2.7 %collective-permute-start.6 = (f32[60,128]{1,0:T(8,128)S(1)}, f32[60,128]{1,0:T(8,128)S(1)}, u32[]{:S(2)}, u32[]{:S(2)}) collective-permute-start(f32[60,128]{1,0:T(8,128)S(1)} %get-tuple-element.104), channel_id=1, source_target_pairs={{0,16},{16,32},{32,48},{48,64},{64,80},{80,96},{96,112},{112,0},{1... | collective-permute-start | bytes 92168 | tf_op jit(solution)/shard_map/ppermute | solution.py:567
  76.6 3.9 %collective-permute-start.7 = (f32[60,128]{1,0:T(8,128)S(1)}, f32[60,128]{1,0:T(8,128)S(1)}, u32[]{:S(2)}, u32[]{:S(2)}) collective-permute-start(f32[60,128]{1,0:T(8,128)S(1)} %get-tuple-element.105), channel_id=1, source_target_pairs={{16,0},{32,16},{48,32},{64,48},{80,64},{96,80},{112,96},{0,112},{1... | collective-permute-start | bytes 92168 | tf_op jit(solution)/shard_map/ppermute | solution.py:568
  87.0 15.5 %all-to-all-start.4 = ((f32[128,4,128]{2,1,0:T(4,128)}), f32[128,4,128]{2,1,0:T(4,128)S(1)}, u32[]{:S(2)}, u32[]{:S(2)}) async-start(f32[128,4,128]{2,1,0:T(4,128)} %bitcast.18), calls=%async_computation.4 | async-start | bytes 524288 | tf_op jit(solution)/shard_map/all_to_all | solution.py:559
  91.0 3.0 %collective-permute-start.8 = (f32[60,128]{1,0:T(8,128)S(1)}, f32[60,128]{1,0:T(8,128)S(1)}, u32[]{:S(2)}, u32[]{:S(2)}) collective-permute-start(f32[60,128]{1,0:T(8,128)S(1)} %get-tuple-element.112), channel_id=1, source_target_pairs={{0,16},{16,32},{32,48},{48,64},{64,80},{80,96},{96,112},{112,0},{1... | collective-permute-start | bytes 92168 | tf_op jit(solution)/shard_map/ppermute | solution.py:567
  92.6 4.4 %collective-permute-start.9 = (f32[60,128]{1,0:T(8,128)S(1)}, f32[60,128]{1,0:T(8,128)S(1)}, u32[]{:S(2)}, u32[]{:S(2)}) collective-permute-start(f32[60,128]{1,0:T(8,128)S(1)} %get-tuple-element.113), channel_id=1, source_target_pairs={{16,0},{32,16},{48,32},{64,48},{80,64},{96,80},{112,96},{0,112},{1... | collective-permute-start | bytes 92168 | tf_op jit(solution)/shard_map/ppermute | solution.py:568
  104.2 14.4 %all-to-all-start.5 = ((bf16[128,4,128]{2,1,0:T(4,128)(2,1)}), bf16[128,4,128]{2,1,0:T(4,128)(2,1)S(1)}, u32[]{:S(2)}, u32[]{:S(2)}) async-start(bf16[128,4,128]{2,1,0:T(4,128)(2,1)} %bitcast.20), calls=%async_computation.5 | async-start | bytes 262144 | tf_op jit(solution)/shard_map/all_to_all | solution.py:559
  108.2 2.7 %collective-permute-start.10 = (f32[60,128]{1,0:T(8,128)S(1)}, f32[60,128]{1,0:T(8,128)S(1)}, u32[]{:S(2)}, u32[]{:S(2)}) collective-permute-start(f32[60,128]{1,0:T(8,128)S(1)} %get-tuple-element.119), channel_id=1, source_target_pairs={{0,16},{16,32},{32,48},{48,64},{64,80},{80,96},{96,112},{112,0},{1... | collective-permute-start | bytes 92168 | tf_op jit(solution)/shard_map/ppermute | solution.py:567
  109.9 3.9 %collective-permute-start.11 = (f32[60,128]{1,0:T(8,128)S(1)}, f32[60,128]{1,0:T(8,128)S(1)}, u32[]{:S(2)}, u32[]{:S(2)}) collective-permute-start(f32[60,128]{1,0:T(8,128)S(1)} %get-tuple-element.120), channel_id=1, source_target_pairs={{16,0},{32,16},{48,32},{64,48},{80,64},{96,80},{112,96},{0,112},{1... | collective-permute-start | bytes 92168 | tf_op jit(solution)/shard_map/ppermute | solution.py:568
  120.3 14.2 %all-to-all-start.6 = ((bf16[128,4,128]{2,1,0:T(4,128)(2,1)}), bf16[128,4,128]{2,1,0:T(4,128)(2,1)S(1)}, u32[]{:S(2)}, u32[]{:S(2)}) async-start(bf16[128,4,128]{2,1,0:T(4,128)(2,1)} %bitcast.22), calls=%async_computation.6 | async-start | bytes 262144 | tf_op jit(solution)/shard_map/all_to_all | solution.py:559
  124.3 2.7 %collective-permute-start.12 = (f32[60,128]{1,0:T(8,128)S(1)}, f32[60,128]{1,0:T(8,128)S(1)}, u32[]{:S(2)}, u32[]{:S(2)}) collective-permute-start(f32[60,128]{1,0:T(8,128)S(1)} %get-tuple-element.126), channel_id=1, source_target_pairs={{0,16},{16,32},{32,48},{48,64},{64,80},{80,96},{96,112},{112,0},{1... | collective-permute-start | bytes 92168 | tf_op jit(solution)/shard_map/ppermute | solution.py:567
  126.0 3.9 %collective-permute-start.13 = (f32[60,128]{1,0:T(8,128)S(1)}, f32[60,128]{1,0:T(8,128)S(1)}, u32[]{:S(2)}, u32[]{:S(2)}) collective-permute-start(f32[60,128]{1,0:T(8,128)S(1)} %get-tuple-element.127), channel_id=1, source_target_pairs={{16,0},{32,16},{48,32},{64,48},{80,64},{96,80},{112,96},{0,112},{1... | collective-permute-start | bytes 92168 | tf_op jit(solution)/shard_map/ppermute | solution.py:568
  136.3 14.2 %all-to-all-start.7 = ((bf16[128,4,128]{2,1,0:T(4,128)(2,1)}), bf16[128,4,128]{2,1,0:T(4,128)(2,1)S(1)}, u32[]{:S(2)}, u32[]{:S(2)}) async-start(bf16[128,4,128]{2,1,0:T(4,128)(2,1)} %bitcast.24), calls=%async_computation.7 | async-start | bytes 262144 | tf_op jit(solution)/shard_map/all_to_all | solution.py:559
  140.3 2.7 %collective-permute-start.14 = (f32[60,128]{1,0:T(8,128)S(1)}, f32[60,128]{1,0:T(8,128)S(1)}, u32[]{:S(2)}, u32[]{:S(2)}) collective-permute-start(f32[60,128]{1,0:T(8,128)S(1)} %get-tuple-element.133), channel_id=1, source_target_pairs={{0,16},{16,32},{32,48},{48,64},{64,80},{80,96},{96,112},{112,0},{1... | collective-permute-start | bytes 92168 | tf_op jit(solution)/shard_map/ppermute | solution.py:567
  141.9 3.9 %collective-permute-start.15 = (f32[60,128]{1,0:T(8,128)S(1)}, f32[60,128]{1,0:T(8,128)S(1)}, u32[]{:S(2)}, u32[]{:S(2)}) collective-permute-start(f32[60,128]{1,0:T(8,128)S(1)} %get-tuple-element.134), channel_id=1, source_target_pairs={{16,0},{32,16},{48,32},{64,48},{80,64},{96,80},{112,96},{0,112},{1... | collective-permute-start | bytes 92168 | tf_op jit(solution)/shard_map/ppermute | solution.py:568

commit v8 on v7

--- a/solution.py
+++ b/solution.py
@@ -249,7 +249,6 @@
     number = index[...]
     own[field(1), :], own[field(3), :] = halves(to_columns(segment_values(given, number)))
     own[field(4), :], own[field(5), :] = halves(to_columns(segment_values(partial, number)))
-    own[field(6), :] = jnp.zeros((PEERS, 128), F32)
     own[field(7), :] = jnp.zeros((PEERS, 128), F32)
     base = cells[0:1, :]
     row = lax.shift_right_logical(base, 7)
@@ -268,10 +267,12 @@
     start[...] = begin
     weights = jnp.where(is_slot(lanes((PEERS, 128))), info, 0.0)
     weight[...] = weights
-    high, low = halves(live)
-    common = jnp.concatenate([low, number.astype(F32)], axis=0).astype(BF16)
-    for d in range(PEERS):
-        message[pl.ds(32 * d + 16, 16), :] = common
+    own[field(6), :] = halves(weights)[1]
+    high = halves(live)[0]
+    order = number.astype(F32)
+    common = jnp.concatenate([high, order], axis=0).astype(BF16)
+    for d in range(0, PEERS, 2):
+        message[pl.ds(24 * d + 32, 16), :] = common
     for copy in copies[6:8]:
         copy.wait()
     for t in range(CHUNKS):
@@ -289,9 +290,9 @@
         values = [weighted[n, chunk(t), :] for n in range(3)]
         borders(values, mobility, trans, weighted, along, t)
     send_borders(trans, weighted, along, toward_low, toward_high, own, pad, 8)
-    for d in range(PEERS):
-        both = jnp.concatenate([own[pl.ds(8 * d, 8), :], high], axis=0)
-        message[pl.ds(32 * d, 16), :] = both.astype(BF16)
+    for d in range(0, PEERS, 2):
+        two = [own[pl.ds(8 * d, 8), :], high, order, own[pl.ds(8 * d + 8, 8), :]]
+        message[pl.ds(24 * d, 32), :] = jnp.concatenate(two, axis=0).astype(BF16)
 
 
 def well_tables(index, table):
@@ -306,19 +307,19 @@
     wide[...] = arrived[...].astype(F32)
 
     def part(n):
-        return wide[pl.ds(n, PEERS, stride=32), :]
+        return wide[pl.ds(n, PEERS, stride=24), :]
 
     lane = lanes((PEERS, 128))
     mine = lane == me()
     for k in range(CAP):
-        turned[k] = (part(8 + k) + part(16 + k)).T
+        turned[k] = part(8 + k).T
     total = part(4) + part(5)
     for k in range(CAP):
-        target = jnp.sum(jnp.where(mine, part(24 + k), 0.0), axis=1, keepdims=True)
+        target = jnp.sum(jnp.where(mine, part(16 + k), 0.0), axis=1, keepdims=True)
         target = jnp.broadcast_to(target, (PEERS, 128))
         found = jnp.zeros((PEERS, 128), F32)
         for m in range(CAP):
-            found += jnp.where(part(24 + m) == target, turned[m], 0.0)
+            found += jnp.where(part(16 + m) == target, turned[m], 0.0)
         place = 60 + k if k < 4 else 120 + k
         total += jnp.where(lane == place, jnp.sum(found, axis=1, keepdims=True), 0.0)
     slot = is_slot(lane)
@@ -328,6 +329,7 @@
     message[block(2), :] = part(2)
     message[block(3), :] = part(3)
     pi = jnp.concatenate([turned[k, pl.ds(me(), 1), :] for k in range(CAP)], axis=0)
+    pi += to_rows(part(6))
     weight[...] = pi
     number = index[...]
     total = fixed[3] + into_segments(pi, number, table[...])
@@ -586,7 +588,7 @@
         cell_setup,
         [((PEERS, ROWS), BF16), ((ROWS, PEERS), BF16),
          ((PEERS, 128), jnp.int32), PAIRS, PAIRS, ((4, 8, 128), F32), CELLS, EDGE, EDGE,
-         ((32 * PEERS, 128), BF16)],
+         ((24 * PEERS, 128), BF16)],
         inputs,
         SCRATCH + (pltpu.VMEM((8 * PEERS, 128), F32),)
         + tuple(pltpu.VMEM(a.shape, a.dtype) for a in inputs) + (pltpu.SemaphoreType.DMA((10,)),),
@@ -607,7 +609,7 @@
         well_setup,
         [MESSAGE, TILE, TILE, TILE, TILE],
         [arrived, index, table, constants],
-        [pltpu.VMEM((32 * PEERS, 128), F32), pltpu.VMEM((CAP, PEERS, 128), F32)],
+        [pltpu.VMEM((24 * PEERS, 128), F32), pltpu.VMEM((CAP, PEERS, 128), F32)],
         name="well_setup",
     )
     fixed.update(own_weight=own_weight, table=table, fixed=constants, diagonal=diagonal)

time: 166 us -> 162 us (0.976)
  waiting for transfers between devices: 76.3 us -> 73.7 us
    all_to_all x8, waiting for transfers between devices: 49.9 us -> 47.3 us  [exchange(): lax.all_to_all(message, AXES, split_axis=0, concat_axis=0, tiled=True)]
where the time goes in v8:
time: 162 us
  waiting for transfers between devices  73.7 us (45%)
  starting transfers between devices  52.9 us (33%)
  Pallas kernels  19.8 us (12%)
  blocking collectives  13.6 us (8%)
    all_to_all x8, waiting for transfers between devices, exchange(): lax.all_to_all(message, AXES, split_axis=0, concat_axis=0, tiled=True)  47.3 us
    all_to_all x8, starting transfers between devices, exchange(): lax.all_to_all(message, AXES, split_axis=0, concat_axis=0, tiled=True)  39.6 us
    ppermute x8, waiting for transfers between devices, neighbours(): lax.ppermute(toward_low, 'gx', down)  20.5 us
    pallas_call x20, Pallas kernels, call(): pl.pallas_call(body, out_shape=[jax.ShapeDtypeStruct(*out) for out in out...  19.8 us
    all_to_all x1, blocking collectives, exchange(): lax.all_to_all(message, AXES, split_axis=0, concat_axis=0, tiled=True)  13.6 us
    ppermute x8, starting transfers between devices, neighbours(): lax.ppermute(toward_high, 'gx', up)  13.2 us
    ppermute x8, waiting for transfers between devices, neighbours(): lax.ppermute(toward_high, 'gx', up)  5.87 us
  transfers between devices with their start and end apart: 24, of which 22 were waited for; matrix products, arithmetic and copies ran while one was open for 0% of the time, Pallas kernels for 2%

profile of v8, /device:TPU:1, one launch (start us, length us, event | category | flops | bytes accessed | tf_op | source)
XLA Modules:
  0.0 161.8 jit_solution(10416552258056073009)
XLA Ops:
  0.6 3.0 %cell_setup.1 = (bf16[128,160]{1,0:T(8,128)(2,1)}, bf16[160,128]{1,0:T(8,128)(2,1)}, s32[128,128]{1,0:T(8,128)}, f32[128,128]{1,0:T(8,128)}, f32[128,128]{1,0:T(...) custom-call(f32[3,160,128]{2,1,0:T(8,128)} %bitcast.67, ...), custom_call_target="tpu_custom_call" | custom-call | flops 4000000 | bytes 1121280 | tf_op jit(solution)/shard_map/cell_setup/pallas_call | solution.py:548
  3.7 11.5 %all-to-all-start = ((bf16[128,24,128]{2,1,0:T(8,128)(2,1)}), bf16[128,24,128]{2,1,0:T(8,128)(2,1)S(1)}, u32[]{:S(2)}, u32[]{:S(2)}) async-start(bf16[128,24,128]{2,1,0:T(8,128)(2,1)} %bitcast.97), calls=%async_computation | async-start | bytes 1572864 | tf_op jit(solution)/shard_map/all_to_all | solution.py:561
  15.2 1.6 %collective-permute-start = (f32[60,128]{1,0:T(8,128)S(1)}, f32[60,128]{1,0:T(8,128)S(1)}, u32[]{:S(2)}, u32[]{:S(2)}) collective-permute-start(f32[60,128]{1,0:T(8,128)S(1)} %copy-done.13), channel_id=1, source_target_pairs={{0,16},{16,32},{32,48},{48,64},{64,80},{80,96},{96,112},{112,0},{1... | collective-permute-start | bytes 92168 | tf_op jit(solution)/shard_map/ppermute | solution.py:569
  17.0 0.8 copy-done
  18.0 14.0 %all-to-all-done = bf16[128,24,128]{2,1,0:T(8,128)(2,1)S(1)} async-done(((bf16[128,24,128]{2,1,0:T(8,128)(2,1)}), bf16[128,24,128]{2,1,0:T(8,128)(2,1)S(1)}, u32[]{:S(2)}, u32[]{:S(2)}) %all-to-all-start) | async-done | bytes 786464 | tf_op jit(solution)/shard_map/all_to_all | solution.py:561
  32.0 1.2 well_setup.1
  33.3 1.7 %sweep_plain.3 = (f32[3,160,128]{2,1,0:T(8,128)S(1)}, f32[60,128]{1,0:T(8,128)S(1)}, f32[60,128]{1,0:T(8,128)S(1)}, bf16[512,128]{1,0:T(8,128)(2,1)}, f32[128,12...) custom-call(f32[512,128]{1,0:T(8,128)S(1)} %get-tuple-element.75.refs_0_, ...), custom_call_target="tpu_custom_call" | custom-call | flops 4000000 | bytes 2252800 | tf_op jit(solution)/shard_map/sweep_plain/pallas_call | solution.py:548
  35.1 4.1 %all-to-all-start.1 = ((bf16[128,4,128]{2,1,0:T(4,128)(2,1)}), bf16[128,4,128]{2,1,0:T(4,128)(2,1)S(1)}, u32[]{:S(2)}, u32[]{:S(2)}) async-start(bf16[128,4,128]{2,1,0:T(4,128)(2,1)} %bitcast.12), calls=%async_computation.1 | async-start | bytes 262144 | tf_op jit(solution)/shard_map/all_to_all | solution.py:561
  39.1 1.7 %collective-permute-start.2 = (f32[60,128]{1,0:T(8,128)S(1)}, f32[60,128]{1,0:T(8,128)S(1)}, u32[]{:S(2)}, u32[]{:S(2)}) collective-permute-start(f32[60,128]{1,0:T(8,128)S(1)} %get-tuple-element.90), channel_id=1, source_target_pairs={{0,16},{16,32},{32,48},{48,64},{64,80},{80,96},{96,112},{112,0},{1... | collective-permute-start | bytes 92168 | tf_op jit(solution)/shard_map/ppermute | solution.py:569
  41.1 0.8 collective-permute-done.2.refs_2_
  41.9 2.9 %collective-permute-done.3.refs_3_ = f32[60,128]{1,0:T(8,128)S(1)} collective-permute-done((f32[60,128]{1,0:T(8,128)S(1)}, f32[60,128]{1,0:T(8,128)S(1)}, u32[]{:S(2)}, u32[]{:S(2)}) %collective-permute-start.3) | collective-permute-done | bytes 30752 | tf_op jit(solution)/shard_map/ppermute | solution.py:570
  44.8 4.7 %all-to-all-done.1 = bf16[128,4,128]{2,1,0:T(4,128)(2,1)S(1)} async-done(((bf16[128,4,128]{2,1,0:T(4,128)(2,1)}), bf16[128,4,128]{2,1,0:T(4,128)(2,1)S(1)}, u32[]{:S(2)}, u32[]{:S(2)}) %all-to-all-start.1) | async-done | bytes 131104 | tf_op jit(solution)/shard_map/all_to_all | solution.py:561
  49.5 1.7 %sweep_plain.4 = (f32[3,160,128]{2,1,0:T(8,128)S(1)}, f32[60,128]{1,0:T(8,128)S(1)}, f32[60,128]{1,0:T(8,128)S(1)}, bf16[512,128]{1,0:T(8,128)(2,1)}, f32[128,12...) custom-call(bf16[512,128]{1,0:T(8,128)(2,1)S(1)} %bitcast.81, f32[3,160,128]{2,1,0:T(8,128)S(1)} %interior.9.refs_1_, ...), custom_call_target="tpu_custom_call" | custom-call | flops 4000000 | bytes 2121728 | tf_op jit(solution)/shard_map/sweep_plain/pallas_call | solution.py:548
  51.2 4.0 %all-to-all-start.2 = ((bf16[128,4,128]{2,1,0:T(4,128)(2,1)}), bf16[128,4,128]{2,1,0:T(4,128)(2,1)S(1)}, u32[]{:S(2)}, u32[]{:S(2)}) async-start(bf16[128,4,128]{2,1,0:T(4,128)(2,1)} %bitcast.14), calls=%async_computation.2 | async-start | bytes 262144 | tf_op jit(solution)/shard_map/all_to_all | solution.py:561
  55.2 1.6 %collective-permute-start.4 = (f32[60,128]{1,0:T(8,128)S(1)}, f32[60,128]{1,0:T(8,128)S(1)}, u32[]{:S(2)}, u32[]{:S(2)}) collective-permute-start(f32[60,128]{1,0:T(8,128)S(1)} %get-tuple-element.97), channel_id=1, source_target_pairs={{0,16},{16,32},{32,48},{48,64},{64,80},{80,96},{96,112},{112,0},{1... | collective-permute-start | bytes 92168 | tf_op jit(solution)/shard_map/ppermute | solution.py:569
  57.1 0.8 collective-permute-done.4.refs_2_
  57.9 2.9 %collective-permute-done.5.refs_3_ = f32[60,128]{1,0:T(8,128)S(1)} collective-permute-done((f32[60,128]{1,0:T(8,128)S(1)}, f32[60,128]{1,0:T(8,128)S(1)}, u32[]{:S(2)}, u32[]{:S(2)}) %collective-permute-start.5) | collective-permute-done | bytes 30752 | tf_op jit(solution)/shard_map/ppermute | solution.py:570
  60.8 4.6 %all-to-all-done.2 = bf16[128,4,128]{2,1,0:T(4,128)(2,1)S(1)} async-done(((bf16[128,4,128]{2,1,0:T(4,128)(2,1)}), bf16[128,4,128]{2,1,0:T(4,128)(2,1)S(1)}, u32[]{:S(2)}, u32[]{:S(2)}) %all-to-all-start.2) | async-done | bytes 131104 | tf_op jit(solution)/shard_map/all_to_all | solution.py:561
  65.4 1.7 %sweep_keep.2 = (f32[3,160,128]{2,1,0:T(8,128)S(1)}, f32[60,128]{1,0:T(8,128)S(1)}, f32[60,128]{1,0:T(8,128)S(1)}, bf16[512,128]{1,0:T(8,128)(2,1)}, f32[128,128...) custom-call(bf16[512,128]{1,0:T(8,128)(2,1)S(1)} %bitcast.78, ...), custom_call_target="tpu_custom_call" | custom-call | flops 4000000 | bytes 2121728 | tf_op jit(solution)/shard_map/sweep_keep/pallas_call | solution.py:548
  67.2 4.0 %all-to-all-start.3 = ((bf16[128,4,128]{2,1,0:T(4,128)(2,1)}), bf16[128,4,128]{2,1,0:T(4,128)(2,1)S(1)}, u32[]{:S(2)}, u32[]{:S(2)}) async-start(bf16[128,4,128]{2,1,0:T(4,128)(2,1)} %bitcast.16), calls=%async_computation.3 | async-start | bytes 262144 | tf_op jit(solution)/shard_map/all_to_all | solution.py:561
  71.2 1.6 %collective-permute-start.6 = (f32[60,128]{1,0:T(8,128)S(1)}, f32[60,128]{1,0:T(8,128)S(1)}, u32[]{:S(2)}, u32[]{:S(2)}) collective-permute-start(f32[60,128]{1,0:T(8,128)S(1)} %get-tuple-element.104), channel_id=1, source_target_pairs={{0,16},{16,32},{32,48},{48,64},{64,80},{80,96},{96,112},{112,0},{1... | collective-permute-start | bytes 92168 | tf_op jit(solution)/shard_map/ppermute | solution.py:569
  73.1 0.8 collective-permute-done.6.refs_2_
  73.9 2.9 %collective-permute-done.7.refs_3_ = f32[60,128]{1,0:T(8,128)S(1)} collective-permute-done((f32[60,128]{1,0:T(8,128)S(1)}, f32[60,128]{1,0:T(8,128)S(1)}, u32[]{:S(2)}, u32[]{:S(2)}) %collective-permute-start.7) | collective-permute-done | bytes 30752 | tf_op jit(solution)/shard_map/ppermute | solution.py:570
  76.8 4.6 %all-to-all-done.3 = bf16[128,4,128]{2,1,0:T(4,128)(2,1)S(1)} async-done(((bf16[128,4,128]{2,1,0:T(4,128)(2,1)}), bf16[128,4,128]{2,1,0:T(4,128)(2,1)S(1)}, u32[]{:S(2)}, u32[]{:S(2)}) %all-to-all-start.3) | async-done | bytes 131104 | tf_op jit(solution)/shard_map/all_to_all | solution.py:561
  81.4 1.8 %sweep_last.1 = (f32[3,160,128]{2,1,0:T(8,128)S(1)}, f32[60,128]{1,0:T(8,128)S(1)}, f32[60,128]{1,0:T(8,128)S(1)}, f32[512,128]{1,0:T(8,128)}, f32[128,128]{1,0:...) custom-call(bf16[512,128]{1,0:T(8,128)(2,1)S(1)} %bitcast.79, ...), custom_call_target="tpu_custom_call" | custom-call | flops 4000000 | bytes 2367488 | tf_op jit(solution)/shard_map/sweep_last/pallas_call | solution.py:548
  83.2 4.0 %all-to-all-start.4 = ((f32[128,4,128]{2,1,0:T(4,128)}), f32[128,4,128]{2,1,0:T(4,128)S(1)}, u32[]{:S(2)}, u32[]{:S(2)}) async-start(f32[128,4,128]{2,1,0:T(4,128)} %bitcast.18), calls=%async_computation.4 | async-start | bytes 524288 | tf_op jit(solution)/shard_map/all_to_all | solution.py:561
  87.3 1.6 %collective-permute-start.8 = (f32[60,128]{1,0:T(8,128)S(1)}, f32[60,128]{1,0:T(8,128)S(1)}, u32[]{:S(2)}, u32[]{:S(2)}) collective-permute-start(f32[60,128]{1,0:T(8,128)S(1)} %get-tuple-element.112), channel_id=1, source_target_pairs={{0,16},{16,32},{32,48},{48,64},{64,80},{80,96},{96,112},{112,0},{1... | collective-permute-start | bytes 92168 | tf_op jit(solution)/shard_map/ppermute | solution.py:569
  89.1 1.1 collective-permute-done.8.refs_2_
  90.2 3.1 %collective-permute-done.9.refs_3_ = f32[60,128]{1,0:T(8,128)S(1)} collective-permute-done((f32[60,128]{1,0:T(8,128)S(1)}, f32[60,128]{1,0:T(8,128)S(1)}, u32[]{:S(2)}, u32[]{:S(2)}) %collective-permute-start.9) | collective-permute-done | bytes 30752 | tf_op jit(solution)/shard_map/ppermute | solution.py:570
  93.3 5.4 %all-to-all-done.4 = f32[128,4,128]{2,1,0:T(4,128)S(1)} async-done(((f32[128,4,128]{2,1,0:T(4,128)}), f32[128,4,128]{2,1,0:T(4,128)S(1)}, u32[]{:S(2)}, u32[]{:S(2)}) %all-to-all-start.4) | async-done | bytes 262176 | tf_op jit(solution)/shard_map/all_to_all | solution.py:561
  98.7 1.7 %sweep_after.1 = (f32[3,160,128]{2,1,0:T(8,128)S(1)}, f32[60,128]{1,0:T(8,128)S(1)}, f32[60,128]{1,0:T(8,128)S(1)}, bf16[512,128]{1,0:T(8,128)(2,1)}, f32[128,12...) custom-call(f32[512,128]{1,0:T(8,128)S(1)} %bitcast.77, ...), custom_call_target="tpu_custom_call" | custom-call | flops 4000000 | bytes 2252800 | tf_op jit(solution)/shard_map/sweep_after/pallas_call | solution.py:548
  100.4 4.0 %all-to-all-start.5 = ((bf16[128,4,128]{2,1,0:T(4,128)(2,1)}), bf16[128,4,128]{2,1,0:T(4,128)(2,1)S(1)}, u32[]{:S(2)}, u32[]{:S(2)}) async-start(bf16[128,4,128]{2,1,0:T(4,128)(2,1)} %bitcast.20), calls=%async_computation.5 | async-start | bytes 262144 | tf_op jit(solution)/shard_map/all_to_all | solution.py:561
  104.5 1.6 %collective-permute-start.10 = (f32[60,128]{1,0:T(8,128)S(1)}, f32[60,128]{1,0:T(8,128)S(1)}, u32[]{:S(2)}, u32[]{:S(2)}) collective-permute-start(f32[60,128]{1,0:T(8,128)S(1)} %get-tuple-element.119), channel_id=1, source_target_pairs={{0,16},{16,32},{32,48},{48,64},{64,80},{80,96},{96,112},{112,0},{1... | collective-permute-start | bytes 92168 | tf_op jit(solution)/shard_map/ppermute | solution.py:569
  106.3 0.8 collective-permute-done.10.refs_2_
  107.1 2.9 %collective-permute-done.11.refs_3_ = f32[60,128]{1,0:T(8,128)S(1)} collective-permute-done((f32[60,128]{1,0:T(8,128)S(1)}, f32[60,128]{1,0:T(8,128)S(1)}, u32[]{:S(2)}, u32[]{:S(2)}) %collective-permute-start.11) | collective-permute-done | bytes 30752 | tf_op jit(solution)/shard_map/ppermute | solution.py:570
  110.0 4.7 %all-to-all-done.5 = bf16[128,4,128]{2,1,0:T(4,128)(2,1)S(1)} async-done(((bf16[128,4,128]{2,1,0:T(4,128)(2,1)}), bf16[128,4,128]{2,1,0:T(4,128)(2,1)S(1)}, u32[]{:S(2)}, u32[]{:S(2)}) %all-to-all-start.5) | async-done | bytes 131104 | tf_op jit(solution)/shard_map/all_to_all | solution.py:561
  114.7 1.7 %sweep_plain.5 = (f32[3,160,128]{2,1,0:T(8,128)S(1)}, f32[60,128]{1,0:T(8,128)S(1)}, f32[60,128]{1,0:T(8,128)S(1)}, bf16[512,128]{1,0:T(8,128)(2,1)}, f32[128,12...) custom-call(bf16[512,128]{1,0:T(8,128)(2,1)S(1)} %bitcast.82, f32[3,160,128]{2,1,0:T(8,128)S(1)} %interior.13.refs_1_, ...), custom_call_target="tpu_custom_call" | custom-call | flops 4000000 | bytes 2121728 | tf_op jit(solution)/shard_map/sweep_plain/pallas_call | solution.py:548
  116.4 4.0 %all-to-all-start.6 = ((bf16[128,4,128]{2,1,0:T(4,128)(2,1)}), bf16[128,4,128]{2,1,0:T(4,128)(2,1)S(1)}, u32[]{:S(2)}, u32[]{:S(2)}) async-start(bf16[128,4,128]{2,1,0:T(4,128)(2,1)} %bitcast.22), calls=%async_computation.6 | async-start | bytes 262144 | tf_op jit(solution)/shard_map/all_to_all | solution.py:561
  120.4 1.6 %collective-permute-start.12 = (f32[60,128]{1,0:T(8,128)S(1)}, f32[60,128]{1,0:T(8,128)S(1)}, u32[]{:S(2)}, u32[]{:S(2)}) collective-permute-start(f32[60,128]{1,0:T(8,128)S(1)} %get-tuple-element.126), channel_id=1, source_target_pairs={{0,16},{16,32},{32,48},{48,64},{64,80},{80,96},{96,112},{112,0},{1... | collective-permute-start | bytes 92168 | tf_op jit(solution)/shard_map/ppermute | solution.py:569
  123.1 2.9 %collective-permute-done.13.refs_3_ = f32[60,128]{1,0:T(8,128)S(1)} collective-permute-done((f32[60,128]{1,0:T(8,128)S(1)}, f32[60,128]{1,0:T(8,128)S(1)}, u32[]{:S(2)}, u32[]{:S(2)}) %collective-permute-start.13) | collective-permute-done | bytes 30752 | tf_op jit(solution)/shard_map/ppermute | solution.py:570
  126.0 4.6 %all-to-all-done.6 = bf16[128,4,128]{2,1,0:T(4,128)(2,1)S(1)} async-done(((bf16[128,4,128]{2,1,0:T(4,128)(2,1)}), bf16[128,4,128]{2,1,0:T(4,128)(2,1)S(1)}, u32[]{:S(2)}, u32[]{:S(2)}) %all-to-all-start.6) | async-done | bytes 131104 | tf_op jit(solution)/shard_map/all_to_all | solution.py:561
  130.6 1.7 %sweep_keep.3 = (f32[3,160,128]{2,1,0:T(8,128)S(1)}, f32[60,128]{1,0:T(8,128)S(1)}, f32[60,128]{1,0:T(8,128)S(1)}, bf16[512,128]{1,0:T(8,128)(2,1)}, f32[128,128...) custom-call(bf16[512,128]{1,0:T(8,128)(2,1)S(1)} %bitcast.80, ...), custom_call_target="tpu_custom_call" | custom-call | flops 4000000 | bytes 2121728 | tf_op jit(solution)/shard_map/sweep_keep/pallas_call | solution.py:548
  132.4 4.0 %all-to-all-start.7 = ((bf16[128,4,128]{2,1,0:T(4,128)(2,1)}), bf16[128,4,128]{2,1,0:T(4,128)(2,1)S(1)}, u32[]{:S(2)}, u32[]{:S(2)}) async-start(bf16[128,4,128]{2,1,0:T(4,128)(2,1)} %bitcast.24), calls=%async_computation.7 | async-start | bytes 262144 | tf_op jit(solution)/shard_map/all_to_all | solution.py:561
  136.4 1.6 %collective-permute-start.14 = (f32[60,128]{1,0:T(8,128)S(1)}, f32[60,128]{1,0:T(8,128)S(1)}, u32[]{:S(2)}, u32[]{:S(2)}) collective-permute-start(f32[60,128]{1,0:T(8,128)S(1)} %get-tuple-element.133), channel_id=1, source_target_pairs={{0,16},{16,32},{32,48},{48,64},{64,80},{80,96},{96,112},{112,0},{1... | collective-permute-start | bytes 92168 | tf_op jit(solution)/shard_map/ppermute | solution.py:569
  139.1 2.9 %collective-permute-done.15.refs_3_ = f32[60,128]{1,0:T(8,128)S(1)} collective-permute-done((f32[60,128]{1,0:T(8,128)S(1)}, f32[60,128]{1,0:T(8,128)S(1)}, u32[]{:S(2)}, u32[]{:S(2)}) %collective-permute-start.15) | collective-permute-done | bytes 30752 | tf_op jit(solution)/shard_map/ppermute | solution.py:570
  142.0 4.6 %all-to-all-done.7 = bf16[128,4,128]{2,1,0:T(4,128)(2,1)S(1)} async-done(((bf16[128,4,128]{2,1,0:T(4,128)(2,1)}), bf16[128,4,128]{2,1,0:T(4,128)(2,1)S(1)}, u32[]{:S(2)}, u32[]{:S(2)}) %all-to-all-start.7) | async-done | bytes 131104 | tf_op jit(solution)/shard_map/all_to_all | solution.py:561
  147.3 13.6 %all_to_all.99 = f32[128,1,128]{2,1,0:T(1,128)S(1)} all-to-all(f32[128,1,128]{2,1,0:T(1,128)S(1)} %bitcast.95), channel_id=1, replica_groups=mesh['gx'=8,'gy'=16] {'gx','gy'}, dimensions={0} | all-to-all | bytes 131072 | tf_op jit(solution)/shard_map/all_to_all | solution.py:561
  160.9 0.8 finish.1
  (49 shorter events, 4.2 us)
Async XLA Ops:
  3.7 11.6 %copy-start.13 = (f32[60,128]{1,0:T(8,128)S(1)}, f32[60,128]{1,0:T(8,128)}, u32[]{:S(2)}) copy-start(f32[60,128]{1,0:T(8,128)} %get-tuple-element.77) | copy-start | bytes 92164
  3.7 13.2 %copy-start.12 = (f32[60,128]{1,0:T(8,128)S(1)}, f32[60,128]{1,0:T(8,128)}, u32[]{:S(2)}) copy-start(f32[60,128]{1,0:T(8,128)} %get-tuple-element.78) | copy-start | bytes 92164
  3.7 13.2 %copy-start.9 = (s32[1,8,128]{2,1,0:T(8,128)S(1)}, s32[1,8,128]{2,1,0:T(8,128)}, u32[]{:S(2)}) copy-start(s32[1,8,128]{2,1,0:T(8,128)} %param.16) | copy-start | bytes 12292
  3.7 13.3 %copy-start.10 = (f32[3,160,128]{2,1,0:T(8,128)S(1)}, f32[3,160,128]{2,1,0:T(8,128)}, u32[]{:S(2)}) copy-start(f32[3,160,128]{2,1,0:T(8,128)} %get-tuple-element.76.weighted) | copy-start | bytes 737284
  3.7 28.3 %all-to-all-start = ((bf16[128,24,128]{2,1,0:T(8,128)(2,1)}), bf16[128,24,128]{2,1,0:T(8,128)(2,1)S(1)}, u32[]{:S(2)}, u32[]{:S(2)}) async-start(bf16[128,24,128]{2,1,0:T(8,128)(2,1)} %bitcast.97), calls=%async_computation | async-start | bytes 1572864 | tf_op jit(solution)/shard_map/all_to_all | solution.py:561
  15.2 18.0 %collective-permute-start = (f32[60,128]{1,0:T(8,128)S(1)}, f32[60,128]{1,0:T(8,128)S(1)}, u32[]{:S(2)}, u32[]{:S(2)}) collective-permute-start(f32[60,128]{1,0:T(8,128)S(1)} %copy-done.13), channel_id=1, source_target_pairs={{0,16},{16,32},{32,48},{48,64},{64,80},{80,96},{96,112},{112,0},{1... | collective-permute-start | bytes 92168 | tf_op jit(solution)/shard_map/ppermute | solution.py:569
  16.9 0.9 copy-start
  16.9 16.4 %collective-permute-start.1 = (f32[60,128]{1,0:T(8,128)S(1)}, f32[60,128]{1,0:T(8,128)S(1)}, u32[]{:S(2)}, u32[]{:S(2)}) collective-permute-start(f32[60,128]{1,0:T(8,128)S(1)} %copy-done.12), channel_id=1, source_target_pairs={{16,0},{32,16},{48,32},{64,48},{80,64},{96,80},{112,96},{0,112},{1... | collective-permute-start | bytes 92168 | tf_op jit(solution)/shard_map/ppermute | solution.py:570
  17.8 14.2 %copy-start.8 = (f32[4,8,128]{2,1,0:T(8,128)S(1)}, f32[4,8,128]{2,1,0:T(8,128)}, u32[]{:S(2)}) copy-start(f32[4,8,128]{2,1,0:T(8,128)} %get-tuple-element.74.fixed.refs_18_) | copy-start | bytes 49156
  17.8 15.5 %copy-start.5 = (s32[128,128]{1,0:T(8,128)S(1)}, s32[128,128]{1,0:T(8,128)}, u32[]{:S(2)}) copy-start(s32[128,128]{1,0:T(8,128)} %get-tuple-element.84.refs_13_) | copy-start | bytes 196612
  17.8 15.5 %copy-start.6 = (f32[128,128]{1,0:T(8,128)S(1)}, f32[128,128]{1,0:T(8,128)}, u32[]{:S(2)}) copy-start(f32[128,128]{1,0:T(8,128)} %get-tuple-element.85.refs_14_) | copy-start | bytes 196612
  17.8 15.5 %copy-start.11 = (f32[128,128]{1,0:T(8,128)S(1)}, f32[128,128]{1,0:T(8,128)}, u32[]{:S(2)}) copy-start(f32[128,128]{1,0:T(8,128)} %get-tuple-element.79.refs_4_) | copy-start | bytes 196612
  32.0 1.3 copy-start.7
  32.0 1.3 copy-start.1
  32.0 1.3 copy-start.2
  32.0 1.3 copy-start.3
  32.0 1.3 copy-start.4
  35.1 14.4 %all-to-all-start.1 = ((bf16[128,4,128]{2,1,0:T(4,128)(2,1)}), bf16[128,4,128]{2,1,0:T(4,128)(2,1)S(1)}, u32[]{:S(2)}, u32[]{:S(2)}) async-start(bf16[128,4,128]{2,1,0:T(4,128)(2,1)} %bitcast.12), calls=%async_computation.1 | async-start | bytes 262144 | tf_op jit(solution)/shard_map/all_to_all | solution.py:561
  39.1 2.7 %collective-permute-start.2 = (f32[60,128]{1,0:T(8,128)S(1)}, f32[60,128]{1,0:T(8,128)S(1)}, u32[]{:S(2)}, u32[]{:S(2)}) collective-permute-start(f32[60,128]{1,0:T(8,128)S(1)} %get-tuple-element.90), channel_id=1, source_target_pairs={{0,16},{16,32},{32,48},{48,64},{64,80},{80,96},{96,112},{112,0},{1... | collective-permute-start | bytes 92168 | tf_op jit(solution)/shard_map/ppermute | solution.py:569
  40.8 3.9 %collective-permute-start.3 = (f32[60,128]{1,0:T(8,128)S(1)}, f32[60,128]{1,0:T(8,128)S(1)}, u32[]{:S(2)}, u32[]{:S(2)}) collective-permute-start(f32[60,128]{1,0:T(8,128)S(1)} %get-tuple-element.91), channel_id=1, source_target_pairs={{16,0},{32,16},{48,32},{64,48},{80,64},{96,80},{112,96},{0,112},{1... | collective-permute-start | bytes 92168 | tf_op jit(solution)/shard_map/ppermute | solution.py:570
  51.2 14.2 %all-to-all-start.2 = ((bf16[128,4,128]{2,1,0:T(4,128)(2,1)}), bf16[128,4,128]{2,1,0:T(4,128)(2,1)S(1)}, u32[]{:S(2)}, u32[]{:S(2)}) async-start(bf16[128,4,128]{2,1,0:T(4,128)(2,1)} %bitcast.14), calls=%async_computation.2 | async-start | bytes 262144 | tf_op jit(solution)/shard_map/all_to_all | solution.py:561
  55.2 2.7 %collective-permute-start.4 = (f32[60,128]{1,0:T(8,128)S(1)}, f32[60,128]{1,0:T(8,128)S(1)}, u32[]{:S(2)}, u32[]{:S(2)}) collective-permute-start(f32[60,128]{1,0:T(8,128)S(1)} %get-tuple-element.97), channel_id=1, source_target_pairs={{0,16},{16,32},{32,48},{48,64},{64,80},{80,96},{96,112},{112,0},{1... | collective-permute-start | bytes 92168 | tf_op jit(solution)/shard_map/ppermute | solution.py:569
  56.9 3.9 %collective-permute-start.5 = (f32[60,128]{1,0:T(8,128)S(1)}, f32[60,128]{1,0:T(8,128)S(1)}, u32[]{:S(2)}, u32[]{:S(2)}) collective-permute-start(f32[60,128]{1,0:T(8,128)S(1)} %get-tuple-element.98), channel_id=1, source_target_pairs={{16,0},{32,16},{48,32},{64,48},{80,64},{96,80},{112,96},{0,112},{1... | collective-permute-start | bytes 92168 | tf_op jit(solution)/shard_map/ppermute | solution.py:570
  67.2 14.2 %all-to-all-start.3 = ((bf16[128,4,128]{2,1,0:T(4,128)(2,1)}), bf16[128,4,128]{2,1,0:T(4,128)(2,1)S(1)}, u32[]{:S(2)}, u32[]{:S(2)}) async-start(bf16[128,4,128]{2,1,0:T(4,128)(2,1)} %bitcast.16), calls=%async_computation.3 | async-start | bytes 262144 | tf_op jit(solution)/shard_map/all_to_all | solution.py:561
  71.2 2.7 %collective-permute-start.6 = (f32[60,128]{1,0:T(8,128)S(1)}, f32[60,128]{1,0:T(8,128)S(1)}, u32[]{:S(2)}, u32[]{:S(2)}) collective-permute-start(f32[60,128]{1,0:T(8,128)S(1)} %get-tuple-element.104), channel_id=1, source_target_pairs={{0,16},{16,32},{32,48},{48,64},{64,80},{80,96},{96,112},{112,0},{1... | collective-permute-start | bytes 92168 | tf_op jit(solution)/shard_map/ppermute | solution.py:569
  72.8 3.9 %collective-permute-start.7 = (f32[60,128]{1,0:T(8,128)S(1)}, f32[60,128]{1,0:T(8,128)S(1)}, u32[]{:S(2)}, u32[]{:S(2)}) collective-permute-start(f32[60,128]{1,0:T(8,128)S(1)} %get-tuple-element.105), channel_id=1, source_target_pairs={{16,0},{32,16},{48,32},{64,48},{80,64},{96,80},{112,96},{0,112},{1... | collective-permute-start | bytes 92168 | tf_op jit(solution)/shard_map/ppermute | solution.py:570
  83.2 15.5 %all-to-all-start.4 = ((f32[128,4,128]{2,1,0:T(4,128)}), f32[128,4,128]{2,1,0:T(4,128)S(1)}, u32[]{:S(2)}, u32[]{:S(2)}) async-start(f32[128,4,128]{2,1,0:T(4,128)} %bitcast.18), calls=%async_computation.4 | async-start | bytes 524288 | tf_op jit(solution)/shard_map/all_to_all | solution.py:561
  87.3 3.0 %collective-permute-start.8 = (f32[60,128]{1,0:T(8,128)S(1)}, f32[60,128]{1,0:T(8,128)S(1)}, u32[]{:S(2)}, u32[]{:S(2)}) collective-permute-start(f32[60,128]{1,0:T(8,128)S(1)} %get-tuple-element.112), channel_id=1, source_target_pairs={{0,16},{16,32},{32,48},{48,64},{64,80},{80,96},{96,112},{112,0},{1... | collective-permute-start | bytes 92168 | tf_op jit(solution)/shard_map/ppermute | solution.py:569
  88.9 4.4 %collective-permute-start.9 = (f32[60,128]{1,0:T(8,128)S(1)}, f32[60,128]{1,0:T(8,128)S(1)}, u32[]{:S(2)}, u32[]{:S(2)}) collective-permute-start(f32[60,128]{1,0:T(8,128)S(1)} %get-tuple-element.113), channel_id=1, source_target_pairs={{16,0},{32,16},{48,32},{64,48},{80,64},{96,80},{112,96},{0,112},{1... | collective-permute-start | bytes 92168 | tf_op jit(solution)/shard_map/ppermute | solution.py:570
  100.4 14.3 %all-to-all-start.5 = ((bf16[128,4,128]{2,1,0:T(4,128)(2,1)}), bf16[128,4,128]{2,1,0:T(4,128)(2,1)S(1)}, u32[]{:S(2)}, u32[]{:S(2)}) async-start(bf16[128,4,128]{2,1,0:T(4,128)(2,1)} %bitcast.20), calls=%async_computation.5 | async-start | bytes 262144 | tf_op jit(solution)/shard_map/all_to_all | solution.py:561
  104.5 2.7 %collective-permute-start.10 = (f32[60,128]{1,0:T(8,128)S(1)}, f32[60,128]{1,0:T(8,128)S(1)}, u32[]{:S(2)}, u32[]{:S(2)}) collective-permute-start(f32[60,128]{1,0:T(8,128)S(1)} %get-tuple-element.119), channel_id=1, source_target_pairs={{0,16},{16,32},{32,48},{48,64},{64,80},{80,96},{96,112},{112,0},{1... | collective-permute-start | bytes 92168 | tf_op jit(solution)/shard_map/ppermute | solution.py:569
  106.1 3.9 %collective-permute-start.11 = (f32[60,128]{1,0:T(8,128)S(1)}, f32[60,128]{1,0:T(8,128)S(1)}, u32[]{:S(2)}, u32[]{:S(2)}) collective-permute-start(f32[60,128]{1,0:T(8,128)S(1)} %get-tuple-element.120), channel_id=1, source_target_pairs={{16,0},{32,16},{48,32},{64,48},{80,64},{96,80},{112,96},{0,112},{1... | collective-permute-start | bytes 92168 | tf_op jit(solution)/shard_map/ppermute | solution.py:570
  116.4 14.2 %all-to-all-start.6 = ((bf16[128,4,128]{2,1,0:T(4,128)(2,1)}), bf16[128,4,128]{2,1,0:T(4,128)(2,1)S(1)}, u32[]{:S(2)}, u32[]{:S(2)}) async-start(bf16[128,4,128]{2,1,0:T(4,128)(2,1)} %bitcast.22), calls=%async_computation.6 | async-start | bytes 262144 | tf_op jit(solution)/shard_map/all_to_all | solution.py:561
  120.4 2.7 %collective-permute-start.12 = (f32[60,128]{1,0:T(8,128)S(1)}, f32[60,128]{1,0:T(8,128)S(1)}, u32[]{:S(2)}, u32[]{:S(2)}) collective-permute-start(f32[60,128]{1,0:T(8,128)S(1)} %get-tuple-element.126), channel_id=1, source_target_pairs={{0,16},{16,32},{32,48},{48,64},{64,80},{80,96},{96,112},{112,0},{1... | collective-permute-start | bytes 92168 | tf_op jit(solution)/shard_map/ppermute | solution.py:569
  122.1 3.9 %collective-permute-start.13 = (f32[60,128]{1,0:T(8,128)S(1)}, f32[60,128]{1,0:T(8,128)S(1)}, u32[]{:S(2)}, u32[]{:S(2)}) collective-permute-start(f32[60,128]{1,0:T(8,128)S(1)} %get-tuple-element.127), channel_id=1, source_target_pairs={{16,0},{32,16},{48,32},{64,48},{80,64},{96,80},{112,96},{0,112},{1... | collective-permute-start | bytes 92168 | tf_op jit(solution)/shard_map/ppermute | solution.py:570
  132.4 14.2 %all-to-all-start.7 = ((bf16[128,4,128]{2,1,0:T(4,128)(2,1)}), bf16[128,4,128]{2,1,0:T(4,128)(2,1)S(1)}, u32[]{:S(2)}, u32[]{:S(2)}) async-start(bf16[128,4,128]{2,1,0:T(4,128)(2,1)} %bitcast.24), calls=%async_computation.7 | async-start | bytes 262144 | tf_op jit(solution)/shard_map/all_to_all | solution.py:561
  136.4 2.7 %collective-permute-start.14 = (f32[60,128]{1,0:T(8,128)S(1)}, f32[60,128]{1,0:T(8,128)S(1)}, u32[]{:S(2)}, u32[]{:S(2)}) collective-permute-start(f32[60,128]{1,0:T(8,128)S(1)} %get-tuple-element.133), channel_id=1, source_target_pairs={{0,16},{16,32},{32,48},{48,64},{64,80},{80,96},{96,112},{112,0},{1... | collective-permute-start | bytes 92168 | tf_op jit(solution)/shard_map/ppermute | solution.py:569
  138.0 3.9 %collective-permute-start.15 = (f32[60,128]{1,0:T(8,128)S(1)}, f32[60,128]{1,0:T(8,128)S(1)}, u32[]{:S(2)}, u32[]{:S(2)}) collective-permute-start(f32[60,128]{1,0:T(8,128)S(1)} %get-tuple-element.134), channel_id=1, source_target_pairs={{16,0},{32,16},{48,32},{64,48},{80,64},{96,80},{112,96},{0,112},{1... | collective-permute-start | bytes 92168 | tf_op jit(solution)/shard_map/ppermute | solution.py:570

commit v9 on v8

--- a/solution.py
+++ b/solution.py
@@ -26,21 +26,19 @@
     return lax.broadcasted_iota(jnp.int32, shape, 0)
 
 
-def split3(x):
-    high = x.astype(BF16)
-    rest = x - high.astype(F32)
-    mid = rest.astype(BF16)
-    low = (rest - mid.astype(F32)).astype(BF16)
-    return high, mid, low
+def halves(x):
+    high = x.astype(BF16).astype(F32)
+    return high, x - high
 
 
 def pick_rows(onehot, x):
-    high, mid, low = split3(x)
-
     def dot(part):
-        return lax.dot_general(onehot, part, (((1,), (0,)), ((), ())), preferred_element_type=F32)
-
-    return (dot(low) + dot(mid)) + dot(high)
+        return lax.dot_general(
+            onehot, part.astype(BF16), (((1,), (0,)), ((), ())), preferred_element_type=F32
+        )
+
+    high, low = halves(x)
+    return dot(low) + dot(high)
 
 
 def is_slot(lane):
@@ -69,19 +67,18 @@
 
 
 def into_segments(values, index, table):
-    parts = [part.astype(F32) for part in split3(values)]
+    parts = halves(values)
     sub = subs((16, 128))
     upper = (index >= 128).astype(jnp.int32)
     tiles = []
     for k in range(CAP):
         row = [jnp.broadcast_to(part[k : k + 1], (16, 128)) for part in parts]
         mine = jnp.broadcast_to(upper[k : k + 1], (16, 128)) == (sub & 1)
-        tile = jnp.where(sub < 2, row[0], jnp.where(sub < 4, row[1], row[2]))
-        tiles.append(jnp.where(mine & (sub < 6), tile, 0.0).astype(BF16))
+        tile = jnp.where(sub < 2, row[0], row[1])
+        tiles.append(jnp.where(mine & (sub < 4), tile, 0.0).astype(BF16))
     left = jnp.concatenate(tiles, axis=1)
     out = lax.dot_general(left, table, (((1,), (1,)), ((), ())), preferred_element_type=F32)[:8]
-    total = (pltpu.roll(out, 4, 0) + pltpu.roll(out, 6, 0)) + out
-    return jnp.where(subs((8, 128)) < 2, total, 0.0)
+    return jnp.where(subs((8, 128)) < 2, pltpu.roll(out, 6, 0) + out, 0.0)
 
 
 def previous(state):
@@ -110,11 +107,6 @@
 
 def block(n):
     return pl.ds(n, PEERS, stride=4)
-
-
-def halves(x):
-    high = x.astype(BF16).astype(F32)
-    return high, x - high
 
 
 def chunk(t):
@@ -152,16 +144,17 @@
     return [entry[3 * n] * x + entry[3 * n + 1] * y + entry[3 * n + 2] * z for n in range(3)]
 
 
-def solve(diag, rows, vector):
+def solve(diag, rows, vector, scale=None):
     a, b, c, d, e, f, g, h, i = [diag[n, rows, :].astype(F32) for n in range(9)]
     x, y, z = vector
     p, q, s = e * i - f * h, f * g - d * i, d * h - e * g
-    scale = 1.0 / (a * p + b * q + c * s)
+    if scale is None:
+        scale = 1.0 / (a * p + b * q + c * s)
     return [
         (p * x + (c * h - b * i) * y + (b * f - c * e) * z) * scale,
         (q * x + (a * i - c * g) * y + (c * d - a * f) * z) * scale,
         (s * x + (b * g - a * h) * y + (a * e - b * d) * z) * scale,
-    ]
+    ], scale
 
 
 def borders(values, mobility, trans, weighted, along, t):
@@ -226,7 +219,7 @@
 
 def cell_setup(rhs_in, diag_in, mobility_in, trans_in, cells_in, pi_in, index_in, parent_in,
                across_in, source_in,
-               rows_of, rows_to, start, weight, slots, fixed,
+               rows_of, rows_to, start, weight, slots, fixed, scale,
                weighted, toward_low, toward_high, message, along, pad, forward, own,
                rhs, diag, mobility, trans, cells, pi, index, parent, across, source, sems):
     pairs = ((cells_in, cells), (pi_in, pi), (index_in, index), (parent_in, parent),
@@ -277,7 +270,7 @@
         copy.wait()
     for t in range(CHUNKS):
         rows = chunk(t)
-        values = solve(diag, rows, [rhs[n, rows, :] for n in range(3)])
+        values, scale[rows, :] = solve(diag, rows, [rhs[n, rows, :] for n in range(3)])
         forward[rows, :] = values[0]
         for n in range(3):
             weighted[n, rows, :] = values[n]
@@ -355,7 +348,7 @@
 
 
 STEADY = ("rhs", "diag", "mobility", "trans", "rows_of", "rows_to", "start", "weight",
-          "own_weight", "table", "index", "fixed", "diagonal")
+          "own_weight", "table", "index", "fixed", "diagonal", "scale")
 MOVING = ("arrived", "near", "from_low", "from_high", "slots", "at_slots", "state")
 NEXT = ("weighted", "toward_low", "toward_high", "message", "slots", "at_slots", "state")
 MORE_IN = {
@@ -453,7 +446,7 @@
                 denom += change * change
         if not final:
             total = [fixed["rhs"][n, rows, :] + terms[n] for n in range(3)]
-            values = solve(fixed["diag"], rows, total)
+            values = solve(fixed["diag"], rows, total, fixed["scale"][rows, :])[0]
             forward[rows, :] = values[0]
             if kind == "keep":
                 for n in range(3):
@@ -583,11 +576,11 @@
     fixed = {"rhs": rhs, "diag": diag, "mobility": mobility, "trans": trans, "index": index}
     inputs = [rhs, diag, mobility, trans, perf_cell[0], perf_pi[0], index]
     inputs += [a.reshape(2, 128) for a in (seg_parent, seg_trans, seg_rhs)]
-    (rows_of, rows_to, start, weight, slots, constants, weighted, toward_low, toward_high,
+    (rows_of, rows_to, start, weight, slots, constants, scale, weighted, toward_low, toward_high,
      message) = call(
         cell_setup,
         [((PEERS, ROWS), BF16), ((ROWS, PEERS), BF16),
-         ((PEERS, 128), jnp.int32), PAIRS, PAIRS, ((4, 8, 128), F32), CELLS, EDGE, EDGE,
+         ((PEERS, 128), jnp.int32), PAIRS, PAIRS, ((4, 8, 128), F32), ((ROWS, 128), F32), CELLS, EDGE, EDGE,
          ((24 * PEERS, 128), BF16)],
         inputs,
         SCRATCH + (pltpu.VMEM((8 * PEERS, 128), F32),)
@@ -602,7 +595,7 @@
         return call(interior, [CELLS], [weighted, trans], name="interior")[0]
 
     (table,) = call(well_tables, [((128, CAP * 128), BF16)], [index], name="well_tables")
-    fixed.update(rows_of=rows_of, rows_to=rows_to, start=start, weight=weight)
+    fixed.update(rows_of=rows_of, rows_to=rows_to, start=start, weight=weight, scale=scale)
     now = {"near": inside(weighted), "slots": slots}
     now.update(neighbours(toward_low, toward_high))
     now["arrived"], own_weight, state, at_slots, diagonal = call(

time: 162 us -> 162 us (level)
  no operation moved by 1% of the time
where the time goes in v9:
time: 162 us; the launch traced here: 161 us
  waiting for transfers between devices  73.7 us (45%)
  starting transfers between devices  52.9 us (33%)
  Pallas kernels  19.3 us (12%)
  blocking collectives  13.6 us (8%)
    all_to_all x8, waiting for transfers between devices, exchange(): lax.all_to_all(message, AXES, split_axis=0, concat_axis=0, tiled=True)  47.3 us
    all_to_all x8, starting transfers between devices, exchange(): lax.all_to_all(message, AXES, split_axis=0, concat_axis=0, tiled=True)  39.6 us
    ppermute x8, waiting for transfers between devices, neighbours(): lax.ppermute(toward_low, 'gx', down)  20.5 us
    pallas_call x20, Pallas kernels, call(): pl.pallas_call(body, out_shape=[jax.ShapeDtypeStruct(*out) for out in out...  19.3 us
    all_to_all x1, blocking collectives, exchange(): lax.all_to_all(message, AXES, split_axis=0, concat_axis=0, tiled=True)  13.6 us
    ppermute x8, starting transfers between devices, neighbours(): lax.ppermute(toward_high, 'gx', up)  13.2 us
    ppermute x8, waiting for transfers between devices, neighbours(): lax.ppermute(toward_high, 'gx', up)  5.87 us
  transfers between devices with their start and end apart: 24, of which 22 were waited for; matrix products, arithmetic and copies ran while one was open for 0% of the time, Pallas kernels for 2%

profile of v9, /device:TPU:1, one launch (start us, length us, event | category | flops | bytes accessed | tf_op | source)
XLA Modules:
  0.0 161.3 jit_solution(12087211498841397035)
XLA Ops:
  0.6 3.0 %cell_setup.1 = (bf16[128,160]{1,0:T(8,128)(2,1)}, bf16[160,128]{1,0:T(8,128)(2,1)}, s32[128,128]{1,0:T(8,128)}, f32[128,128]{1,0:T(8,128)}, f32[128,128]{1,0:T(...) custom-call(f32[3,160,128]{2,1,0:T(8,128)} %bitcast.67, ...), custom_call_target="tpu_custom_call" | custom-call | flops 4000000 | bytes 1121280 | tf_op jit(solution)/shard_map/cell_setup/pallas_call | solution.py:541
  3.6 11.5 %all-to-all-start = ((bf16[128,24,128]{2,1,0:T(8,128)(2,1)}), bf16[128,24,128]{2,1,0:T(8,128)(2,1)S(1)}, u32[]{:S(2)}, u32[]{:S(2)}) async-start(bf16[128,24,128]{2,1,0:T(8,128)(2,1)} %bitcast.97), calls=%async_computation | async-start | bytes 1572864 | tf_op jit(solution)/shard_map/all_to_all | solution.py:554
  15.2 1.6 %collective-permute-start = (f32[60,128]{1,0:T(8,128)S(1)}, f32[60,128]{1,0:T(8,128)S(1)}, u32[]{:S(2)}, u32[]{:S(2)}) collective-permute-start(f32[60,128]{1,0:T(8,128)S(1)} %copy-done.14), channel_id=1, source_target_pairs={{0,16},{16,32},{32,48},{48,64},{64,80},{80,96},{96,112},{112,0},{1... | collective-permute-start | bytes 92168 | tf_op jit(solution)/shard_map/ppermute | solution.py:562
  16.9 0.8 copy-done
  18.0 14.0 %all-to-all-done = bf16[128,24,128]{2,1,0:T(8,128)(2,1)S(1)} async-done(((bf16[128,24,128]{2,1,0:T(8,128)(2,1)}), bf16[128,24,128]{2,1,0:T(8,128)(2,1)S(1)}, u32[]{:S(2)}, u32[]{:S(2)}) %all-to-all-start) | async-done | bytes 786464 | tf_op jit(solution)/shard_map/all_to_all | solution.py:554
  32.0 1.2 well_setup.1
  33.3 1.7 %sweep_plain.3 = (f32[3,160,128]{2,1,0:T(8,128)S(1)}, f32[60,128]{1,0:T(8,128)S(1)}, f32[60,128]{1,0:T(8,128)S(1)}, bf16[512,128]{1,0:T(8,128)(2,1)}, f32[128,12...) custom-call(f32[512,128]{1,0:T(8,128)S(1)} %get-tuple-element.76.refs_0_, ...), custom_call_target="tpu_custom_call" | custom-call | flops 4000000 | bytes 2334720 | tf_op jit(solution)/shard_map/sweep_plain/pallas_call | solution.py:541
  35.0 4.1 %all-to-all-start.1 = ((bf16[128,4,128]{2,1,0:T(4,128)(2,1)}), bf16[128,4,128]{2,1,0:T(4,128)(2,1)S(1)}, u32[]{:S(2)}, u32[]{:S(2)}) async-start(bf16[128,4,128]{2,1,0:T(4,128)(2,1)} %bitcast.12), calls=%async_computation.1 | async-start | bytes 262144 | tf_op jit(solution)/shard_map/all_to_all | solution.py:554
  39.0 1.7 %collective-permute-start.2 = (f32[60,128]{1,0:T(8,128)S(1)}, f32[60,128]{1,0:T(8,128)S(1)}, u32[]{:S(2)}, u32[]{:S(2)}) collective-permute-start(f32[60,128]{1,0:T(8,128)S(1)} %get-tuple-element.92), channel_id=1, source_target_pairs={{0,16},{16,32},{32,48},{48,64},{64,80},{80,96},{96,112},{112,0},{1... | collective-permute-start | bytes 92168 | tf_op jit(solution)/shard_map/ppermute | solution.py:562
  41.0 0.8 collective-permute-done.2.refs_2_
  41.8 2.9 %collective-permute-done.3.refs_3_ = f32[60,128]{1,0:T(8,128)S(1)} collective-permute-done((f32[60,128]{1,0:T(8,128)S(1)}, f32[60,128]{1,0:T(8,128)S(1)}, u32[]{:S(2)}, u32[]{:S(2)}) %collective-permute-start.3) | collective-permute-done | bytes 30752 | tf_op jit(solution)/shard_map/ppermute | solution.py:563
  44.7 4.7 %all-to-all-done.1 = bf16[128,4,128]{2,1,0:T(4,128)(2,1)S(1)} async-done(((bf16[128,4,128]{2,1,0:T(4,128)(2,1)}), bf16[128,4,128]{2,1,0:T(4,128)(2,1)S(1)}, u32[]{:S(2)}, u32[]{:S(2)}) %all-to-all-start.1) | async-done | bytes 131104 | tf_op jit(solution)/shard_map/all_to_all | solution.py:554
  49.4 1.7 %sweep_plain.4 = (f32[3,160,128]{2,1,0:T(8,128)S(1)}, f32[60,128]{1,0:T(8,128)S(1)}, f32[60,128]{1,0:T(8,128)S(1)}, bf16[512,128]{1,0:T(8,128)(2,1)}, f32[128,12...) custom-call(bf16[512,128]{1,0:T(8,128)(2,1)S(1)} %bitcast.82, f32[3,160,128]{2,1,0:T(8,128)S(1)} %interior.9.refs_1_, ...), custom_call_target="tpu_custom_call" | custom-call | flops 4000000 | bytes 2203648 | tf_op jit(solution)/shard_map/sweep_plain/pallas_call | solution.py:541
  51.0 4.0 %all-to-all-start.2 = ((bf16[128,4,128]{2,1,0:T(4,128)(2,1)}), bf16[128,4,128]{2,1,0:T(4,128)(2,1)S(1)}, u32[]{:S(2)}, u32[]{:S(2)}) async-start(bf16[128,4,128]{2,1,0:T(4,128)(2,1)} %bitcast.14), calls=%async_computation.2 | async-start | bytes 262144 | tf_op jit(solution)/shard_map/all_to_all | solution.py:554
  55.1 1.6 %collective-permute-start.4 = (f32[60,128]{1,0:T(8,128)S(1)}, f32[60,128]{1,0:T(8,128)S(1)}, u32[]{:S(2)}, u32[]{:S(2)}) collective-permute-start(f32[60,128]{1,0:T(8,128)S(1)} %get-tuple-element.99), channel_id=1, source_target_pairs={{0,16},{16,32},{32,48},{48,64},{64,80},{80,96},{96,112},{112,0},{1... | collective-permute-start | bytes 92168 | tf_op jit(solution)/shard_map/ppermute | solution.py:562
  56.9 0.8 collective-permute-done.4.refs_2_
  57.7 2.9 %collective-permute-done.5.refs_3_ = f32[60,128]{1,0:T(8,128)S(1)} collective-permute-done((f32[60,128]{1,0:T(8,128)S(1)}, f32[60,128]{1,0:T(8,128)S(1)}, u32[]{:S(2)}, u32[]{:S(2)}) %collective-permute-start.5) | collective-permute-done | bytes 30752 | tf_op jit(solution)/shard_map/ppermute | solution.py:563
  60.6 4.6 %all-to-all-done.2 = bf16[128,4,128]{2,1,0:T(4,128)(2,1)S(1)} async-done(((bf16[128,4,128]{2,1,0:T(4,128)(2,1)}), bf16[128,4,128]{2,1,0:T(4,128)(2,1)S(1)}, u32[]{:S(2)}, u32[]{:S(2)}) %all-to-all-start.2) | async-done | bytes 131104 | tf_op jit(solution)/shard_map/all_to_all | solution.py:554
  65.3 1.7 %sweep_keep.2 = (f32[3,160,128]{2,1,0:T(8,128)S(1)}, f32[60,128]{1,0:T(8,128)S(1)}, f32[60,128]{1,0:T(8,128)S(1)}, bf16[512,128]{1,0:T(8,128)(2,1)}, f32[128,128...) custom-call(bf16[512,128]{1,0:T(8,128)(2,1)S(1)} %bitcast.79, ...), custom_call_target="tpu_custom_call" | custom-call | flops 4000000 | bytes 2203648 | tf_op jit(solution)/shard_map/sweep_keep/pallas_call | solution.py:541
  66.9 4.0 %all-to-all-start.3 = ((bf16[128,4,128]{2,1,0:T(4,128)(2,1)}), bf16[128,4,128]{2,1,0:T(4,128)(2,1)S(1)}, u32[]{:S(2)}, u32[]{:S(2)}) async-start(bf16[128,4,128]{2,1,0:T(4,128)(2,1)} %bitcast.16), calls=%async_computation.3 | async-start | bytes 262144 | tf_op jit(solution)/shard_map/all_to_all | solution.py:554
  71.0 1.6 %collective-permute-start.6 = (f32[60,128]{1,0:T(8,128)S(1)}, f32[60,128]{1,0:T(8,128)S(1)}, u32[]{:S(2)}, u32[]{:S(2)}) collective-permute-start(f32[60,128]{1,0:T(8,128)S(1)} %get-tuple-element.106), channel_id=1, source_target_pairs={{0,16},{16,32},{32,48},{48,64},{64,80},{80,96},{96,112},{112,0},{1... | collective-permute-start | bytes 92168 | tf_op jit(solution)/shard_map/ppermute | solution.py:562
  72.8 0.8 collective-permute-done.6.refs_2_
  73.6 2.9 %collective-permute-done.7.refs_3_ = f32[60,128]{1,0:T(8,128)S(1)} collective-permute-done((f32[60,128]{1,0:T(8,128)S(1)}, f32[60,128]{1,0:T(8,128)S(1)}, u32[]{:S(2)}, u32[]{:S(2)}) %collective-permute-start.7) | collective-permute-done | bytes 30752 | tf_op jit(solution)/shard_map/ppermute | solution.py:563
  76.5 4.6 %all-to-all-done.3 = bf16[128,4,128]{2,1,0:T(4,128)(2,1)S(1)} async-done(((bf16[128,4,128]{2,1,0:T(4,128)(2,1)}), bf16[128,4,128]{2,1,0:T(4,128)(2,1)S(1)}, u32[]{:S(2)}, u32[]{:S(2)}) %all-to-all-start.3) | async-done | bytes 131104 | tf_op jit(solution)/shard_map/all_to_all | solution.py:554
  81.2 1.8 %sweep_last.1 = (f32[3,160,128]{2,1,0:T(8,128)S(1)}, f32[60,128]{1,0:T(8,128)S(1)}, f32[60,128]{1,0:T(8,128)S(1)}, f32[512,128]{1,0:T(8,128)}, f32[128,128]{1,0:...) custom-call(bf16[512,128]{1,0:T(8,128)(2,1)S(1)} %bitcast.80, ...), custom_call_target="tpu_custom_call" | custom-call | flops 4000000 | bytes 2449408 | tf_op jit(solution)/shard_map/sweep_last/pallas_call | solution.py:541
  82.9 4.0 %all-to-all-start.4 = ((f32[128,4,128]{2,1,0:T(4,128)}), f32[128,4,128]{2,1,0:T(4,128)S(1)}, u32[]{:S(2)}, u32[]{:S(2)}) async-start(f32[128,4,128]{2,1,0:T(4,128)} %bitcast.18), calls=%async_computation.4 | async-start | bytes 524288 | tf_op jit(solution)/shard_map/all_to_all | solution.py:554
  87.0 1.6 %collective-permute-start.8 = (f32[60,128]{1,0:T(8,128)S(1)}, f32[60,128]{1,0:T(8,128)S(1)}, u32[]{:S(2)}, u32[]{:S(2)}) collective-permute-start(f32[60,128]{1,0:T(8,128)S(1)} %get-tuple-element.114), channel_id=1, source_target_pairs={{0,16},{16,32},{32,48},{48,64},{64,80},{80,96},{96,112},{112,0},{1... | collective-permute-start | bytes 92168 | tf_op jit(solution)/shard_map/ppermute | solution.py:562
  88.8 1.1 collective-permute-done.8.refs_2_
  89.9 3.1 %collective-permute-done.9.refs_3_ = f32[60,128]{1,0:T(8,128)S(1)} collective-permute-done((f32[60,128]{1,0:T(8,128)S(1)}, f32[60,128]{1,0:T(8,128)S(1)}, u32[]{:S(2)}, u32[]{:S(2)}) %collective-permute-start.9) | collective-permute-done | bytes 30752 | tf_op jit(solution)/shard_map/ppermute | solution.py:563
  93.0 5.4 %all-to-all-done.4 = f32[128,4,128]{2,1,0:T(4,128)S(1)} async-done(((f32[128,4,128]{2,1,0:T(4,128)}), f32[128,4,128]{2,1,0:T(4,128)S(1)}, u32[]{:S(2)}, u32[]{:S(2)}) %all-to-all-start.4) | async-done | bytes 262176 | tf_op jit(solution)/shard_map/all_to_all | solution.py:554
  98.4 1.7 %sweep_after.1 = (f32[3,160,128]{2,1,0:T(8,128)S(1)}, f32[60,128]{1,0:T(8,128)S(1)}, f32[60,128]{1,0:T(8,128)S(1)}, bf16[512,128]{1,0:T(8,128)(2,1)}, f32[128,12...) custom-call(f32[512,128]{1,0:T(8,128)S(1)} %bitcast.77, ...), custom_call_target="tpu_custom_call" | custom-call | flops 4000000 | bytes 2334720 | tf_op jit(solution)/shard_map/sweep_after/pallas_call | solution.py:541
  100.1 4.0 %all-to-all-start.5 = ((bf16[128,4,128]{2,1,0:T(4,128)(2,1)}), bf16[128,4,128]{2,1,0:T(4,128)(2,1)S(1)}, u32[]{:S(2)}, u32[]{:S(2)}) async-start(bf16[128,4,128]{2,1,0:T(4,128)(2,1)} %bitcast.20), calls=%async_computation.5 | async-start | bytes 262144 | tf_op jit(solution)/shard_map/all_to_all | solution.py:554
  104.1 1.6 %collective-permute-start.10 = (f32[60,128]{1,0:T(8,128)S(1)}, f32[60,128]{1,0:T(8,128)S(1)}, u32[]{:S(2)}, u32[]{:S(2)}) collective-permute-start(f32[60,128]{1,0:T(8,128)S(1)} %get-tuple-element.121), channel_id=1, source_target_pairs={{0,16},{16,32},{32,48},{48,64},{64,80},{80,96},{96,112},{112,0},{1... | collective-permute-start | bytes 92168 | tf_op jit(solution)/shard_map/ppermute | solution.py:562
  106.0 0.8 collective-permute-done.10.refs_2_
  106.8 2.9 %collective-permute-done.11.refs_3_ = f32[60,128]{1,0:T(8,128)S(1)} collective-permute-done((f32[60,128]{1,0:T(8,128)S(1)}, f32[60,128]{1,0:T(8,128)S(1)}, u32[]{:S(2)}, u32[]{:S(2)}) %collective-permute-start.11) | collective-permute-done | bytes 30752 | tf_op jit(solution)/shard_map/ppermute | solution.py:563
  109.7 4.7 %all-to-all-done.5 = bf16[128,4,128]{2,1,0:T(4,128)(2,1)S(1)} async-done(((bf16[128,4,128]{2,1,0:T(4,128)(2,1)}), bf16[128,4,128]{2,1,0:T(4,128)(2,1)S(1)}, u32[]{:S(2)}, u32[]{:S(2)}) %all-to-all-start.5) | async-done | bytes 131104 | tf_op jit(solution)/shard_map/all_to_all | solution.py:554
  114.4 1.6 %sweep_plain.5 = (f32[3,160,128]{2,1,0:T(8,128)S(1)}, f32[60,128]{1,0:T(8,128)S(1)}, f32[60,128]{1,0:T(8,128)S(1)}, bf16[512,128]{1,0:T(8,128)(2,1)}, f32[128,12...) custom-call(bf16[512,128]{1,0:T(8,128)(2,1)S(1)} %bitcast.83, f32[3,160,128]{2,1,0:T(8,128)S(1)} %interior.13.refs_1_, ...), custom_call_target="tpu_custom_call" | custom-call | flops 4000000 | bytes 2203648 | tf_op jit(solution)/shard_map/sweep_plain/pallas_call | solution.py:541
  116.0 4.0 %all-to-all-start.6 = ((bf16[128,4,128]{2,1,0:T(4,128)(2,1)}), bf16[128,4,128]{2,1,0:T(4,128)(2,1)S(1)}, u32[]{:S(2)}, u32[]{:S(2)}) async-start(bf16[128,4,128]{2,1,0:T(4,128)(2,1)} %bitcast.22), calls=%async_computation.6 | async-start | bytes 262144 | tf_op jit(solution)/shard_map/all_to_all | solution.py:554
  120.0 1.6 %collective-permute-start.12 = (f32[60,128]{1,0:T(8,128)S(1)}, f32[60,128]{1,0:T(8,128)S(1)}, u32[]{:S(2)}, u32[]{:S(2)}) collective-permute-start(f32[60,128]{1,0:T(8,128)S(1)} %get-tuple-element.128), channel_id=1, source_target_pairs={{0,16},{16,32},{32,48},{48,64},{64,80},{80,96},{96,112},{112,0},{1... | collective-permute-start | bytes 92168 | tf_op jit(solution)/shard_map/ppermute | solution.py:562
  122.7 2.9 %collective-permute-done.13.refs_3_ = f32[60,128]{1,0:T(8,128)S(1)} collective-permute-done((f32[60,128]{1,0:T(8,128)S(1)}, f32[60,128]{1,0:T(8,128)S(1)}, u32[]{:S(2)}, u32[]{:S(2)}) %collective-permute-start.13) | collective-permute-done | bytes 30752 | tf_op jit(solution)/shard_map/ppermute | solution.py:563
  125.6 4.6 %all-to-all-done.6 = bf16[128,4,128]{2,1,0:T(4,128)(2,1)S(1)} async-done(((bf16[128,4,128]{2,1,0:T(4,128)(2,1)}), bf16[128,4,128]{2,1,0:T(4,128)(2,1)S(1)}, u32[]{:S(2)}, u32[]{:S(2)}) %all-to-all-start.6) | async-done | bytes 131104 | tf_op jit(solution)/shard_map/all_to_all | solution.py:554
  130.2 1.7 %sweep_keep.3 = (f32[3,160,128]{2,1,0:T(8,128)S(1)}, f32[60,128]{1,0:T(8,128)S(1)}, f32[60,128]{1,0:T(8,128)S(1)}, bf16[512,128]{1,0:T(8,128)(2,1)}, f32[128,128...) custom-call(bf16[512,128]{1,0:T(8,128)(2,1)S(1)} %bitcast.81, ...), custom_call_target="tpu_custom_call" | custom-call | flops 4000000 | bytes 2203648 | tf_op jit(solution)/shard_map/sweep_keep/pallas_call | solution.py:541
  131.9 4.0 %all-to-all-start.7 = ((bf16[128,4,128]{2,1,0:T(4,128)(2,1)}), bf16[128,4,128]{2,1,0:T(4,128)(2,1)S(1)}, u32[]{:S(2)}, u32[]{:S(2)}) async-start(bf16[128,4,128]{2,1,0:T(4,128)(2,1)} %bitcast.24), calls=%async_computation.7 | async-start | bytes 262144 | tf_op jit(solution)/shard_map/all_to_all | solution.py:554
  135.9 1.6 %collective-permute-start.14 = (f32[60,128]{1,0:T(8,128)S(1)}, f32[60,128]{1,0:T(8,128)S(1)}, u32[]{:S(2)}, u32[]{:S(2)}) collective-permute-start(f32[60,128]{1,0:T(8,128)S(1)} %get-tuple-element.135), channel_id=1, source_target_pairs={{0,16},{16,32},{32,48},{48,64},{64,80},{80,96},{96,112},{112,0},{1... | collective-permute-start | bytes 92168 | tf_op jit(solution)/shard_map/ppermute | solution.py:562
  138.6 2.9 %collective-permute-done.15.refs_3_ = f32[60,128]{1,0:T(8,128)S(1)} collective-permute-done((f32[60,128]{1,0:T(8,128)S(1)}, f32[60,128]{1,0:T(8,128)S(1)}, u32[]{:S(2)}, u32[]{:S(2)}) %collective-permute-start.15) | collective-permute-done | bytes 30752 | tf_op jit(solution)/shard_map/ppermute | solution.py:563
  141.5 4.6 %all-to-all-done.7 = bf16[128,4,128]{2,1,0:T(4,128)(2,1)S(1)} async-done(((bf16[128,4,128]{2,1,0:T(4,128)(2,1)}), bf16[128,4,128]{2,1,0:T(4,128)(2,1)S(1)}, u32[]{:S(2)}, u32[]{:S(2)}) %all-to-all-start.7) | async-done | bytes 131104 | tf_op jit(solution)/shard_map/all_to_all | solution.py:554
  146.8 13.6 %all_to_all.99 = f32[128,1,128]{2,1,0:T(1,128)S(1)} all-to-all(f32[128,1,128]{2,1,0:T(1,128)S(1)} %bitcast.95), channel_id=1, replica_groups=mesh['gx'=8,'gy'=16] {'gx','gy'}, dimensions={0} | all-to-all | bytes 131072 | tf_op jit(solution)/shard_map/all_to_all | solution.py:554
  160.4 0.8 finish.1
  (51 shorter events, 4.2 us)
Async XLA Ops:
  3.6 11.6 %copy-start.14 = (f32[60,128]{1,0:T(8,128)S(1)}, f32[60,128]{1,0:T(8,128)}, u32[]{:S(2)}) copy-start(f32[60,128]{1,0:T(8,128)} %get-tuple-element.78) | copy-start | bytes 92164
  3.6 13.2 %copy-start.13 = (f32[60,128]{1,0:T(8,128)S(1)}, f32[60,128]{1,0:T(8,128)}, u32[]{:S(2)}) copy-start(f32[60,128]{1,0:T(8,128)} %get-tuple-element.79) | copy-start | bytes 92164
  3.6 13.2 %copy-start.10 = (s32[1,8,128]{2,1,0:T(8,128)S(1)}, s32[1,8,128]{2,1,0:T(8,128)}, u32[]{:S(2)}) copy-start(s32[1,8,128]{2,1,0:T(8,128)} %param.16) | copy-start | bytes 12292
  3.6 13.3 %copy-start.11 = (f32[3,160,128]{2,1,0:T(8,128)S(1)}, f32[3,160,128]{2,1,0:T(8,128)}, u32[]{:S(2)}) copy-start(f32[3,160,128]{2,1,0:T(8,128)} %get-tuple-element.77.weighted) | copy-start | bytes 737284
  3.6 28.3 %all-to-all-start = ((bf16[128,24,128]{2,1,0:T(8,128)(2,1)}), bf16[128,24,128]{2,1,0:T(8,128)(2,1)S(1)}, u32[]{:S(2)}, u32[]{:S(2)}) async-start(bf16[128,24,128]{2,1,0:T(8,128)(2,1)} %bitcast.97), calls=%async_computation | async-start | bytes 1572864 | tf_op jit(solution)/shard_map/all_to_all | solution.py:554
  15.2 18.0 %collective-permute-start = (f32[60,128]{1,0:T(8,128)S(1)}, f32[60,128]{1,0:T(8,128)S(1)}, u32[]{:S(2)}, u32[]{:S(2)}) collective-permute-start(f32[60,128]{1,0:T(8,128)S(1)} %copy-done.14), channel_id=1, source_target_pairs={{0,16},{16,32},{32,48},{48,64},{64,80},{80,96},{96,112},{112,0},{1... | collective-permute-start | bytes 92168 | tf_op jit(solution)/shard_map/ppermute | solution.py:562
  16.8 0.9 copy-start
  16.8 16.4 %collective-permute-start.1 = (f32[60,128]{1,0:T(8,128)S(1)}, f32[60,128]{1,0:T(8,128)S(1)}, u32[]{:S(2)}, u32[]{:S(2)}) collective-permute-start(f32[60,128]{1,0:T(8,128)S(1)} %copy-done.13), channel_id=1, source_target_pairs={{16,0},{32,16},{48,32},{64,48},{80,64},{96,80},{112,96},{0,112},{1... | collective-permute-start | bytes 92168 | tf_op jit(solution)/shard_map/ppermute | solution.py:563
  17.7 14.2 %copy-start.9 = (f32[4,8,128]{2,1,0:T(8,128)S(1)}, f32[4,8,128]{2,1,0:T(8,128)}, u32[]{:S(2)}) copy-start(f32[4,8,128]{2,1,0:T(8,128)} %get-tuple-element.75.fixed.refs_18_) | copy-start | bytes 49156
  17.7 15.5 %copy-start.5 = (bf16[128,160]{1,0:T(8,128)(2,1)S(1)}, bf16[128,160]{1,0:T(8,128)(2,1)}, u32[]{:S(2)}) copy-start(bf16[128,160]{1,0:T(8,128)(2,1)} %get-tuple-element.83.refs_11_) | copy-start | bytes 122884
  17.7 15.5 %copy-start.6 = (s32[128,128]{1,0:T(8,128)S(1)}, s32[128,128]{1,0:T(8,128)}, u32[]{:S(2)}) copy-start(s32[128,128]{1,0:T(8,128)} %get-tuple-element.85.refs_13_) | copy-start | bytes 196612
  17.7 15.5 %copy-start.7 = (f32[128,128]{1,0:T(8,128)S(1)}, f32[128,128]{1,0:T(8,128)}, u32[]{:S(2)}) copy-start(f32[128,128]{1,0:T(8,128)} %get-tuple-element.86.refs_14_) | copy-start | bytes 196612
  17.7 15.5 %copy-start.8 = (bf16[160,128]{1,0:T(8,128)(2,1)S(1)}, bf16[160,128]{1,0:T(8,128)(2,1)}, u32[]{:S(2)}) copy-start(bf16[160,128]{1,0:T(8,128)(2,1)} %get-tuple-element.84.refs_12_) | copy-start | bytes 122884
  17.7 15.5 %copy-start.12 = (f32[128,128]{1,0:T(8,128)S(1)}, f32[128,128]{1,0:T(8,128)}, u32[]{:S(2)}) copy-start(f32[128,128]{1,0:T(8,128)} %get-tuple-element.80.refs_4_) | copy-start | bytes 196612
  31.9 1.3 copy-start.1
  31.9 1.4 copy-start.2
  31.9 1.4 copy-start.3
  31.9 1.4 copy-start.4
  35.0 14.4 %all-to-all-start.1 = ((bf16[128,4,128]{2,1,0:T(4,128)(2,1)}), bf16[128,4,128]{2,1,0:T(4,128)(2,1)S(1)}, u32[]{:S(2)}, u32[]{:S(2)}) async-start(bf16[128,4,128]{2,1,0:T(4,128)(2,1)} %bitcast.12), calls=%async_computation.1 | async-start | bytes 262144 | tf_op jit(solution)/shard_map/all_to_all | solution.py:554
  39.0 2.7 %collective-permute-start.2 = (f32[60,128]{1,0:T(8,128)S(1)}, f32[60,128]{1,0:T(8,128)S(1)}, u32[]{:S(2)}, u32[]{:S(2)}) collective-permute-start(f32[60,128]{1,0:T(8,128)S(1)} %get-tuple-element.92), channel_id=1, source_target_pairs={{0,16},{16,32},{32,48},{48,64},{64,80},{80,96},{96,112},{112,0},{1... | collective-permute-start | bytes 92168 | tf_op jit(solution)/shard_map/ppermute | solution.py:562
  40.7 3.9 %collective-permute-start.3 = (f32[60,128]{1,0:T(8,128)S(1)}, f32[60,128]{1,0:T(8,128)S(1)}, u32[]{:S(2)}, u32[]{:S(2)}) collective-permute-start(f32[60,128]{1,0:T(8,128)S(1)} %get-tuple-element.93), channel_id=1, source_target_pairs={{16,0},{32,16},{48,32},{64,48},{80,64},{96,80},{112,96},{0,112},{1... | collective-permute-start | bytes 92168 | tf_op jit(solution)/shard_map/ppermute | solution.py:563
  51.0 14.2 %all-to-all-start.2 = ((bf16[128,4,128]{2,1,0:T(4,128)(2,1)}), bf16[128,4,128]{2,1,0:T(4,128)(2,1)S(1)}, u32[]{:S(2)}, u32[]{:S(2)}) async-start(bf16[128,4,128]{2,1,0:T(4,128)(2,1)} %bitcast.14), calls=%async_computation.2 | async-start | bytes 262144 | tf_op jit(solution)/shard_map/all_to_all | solution.py:554
  55.1 2.7 %collective-permute-start.4 = (f32[60,128]{1,0:T(8,128)S(1)}, f32[60,128]{1,0:T(8,128)S(1)}, u32[]{:S(2)}, u32[]{:S(2)}) collective-permute-start(f32[60,128]{1,0:T(8,128)S(1)} %get-tuple-element.99), channel_id=1, source_target_pairs={{0,16},{16,32},{32,48},{48,64},{64,80},{80,96},{96,112},{112,0},{1... | collective-permute-start | bytes 92168 | tf_op jit(solution)/shard_map/ppermute | solution.py:562
  56.7 3.9 %collective-permute-start.5 = (f32[60,128]{1,0:T(8,128)S(1)}, f32[60,128]{1,0:T(8,128)S(1)}, u32[]{:S(2)}, u32[]{:S(2)}) collective-permute-start(f32[60,128]{1,0:T(8,128)S(1)} %get-tuple-element.100), channel_id=1, source_target_pairs={{16,0},{32,16},{48,32},{64,48},{80,64},{96,80},{112,96},{0,112},{1... | collective-permute-start | bytes 92168 | tf_op jit(solution)/shard_map/ppermute | solution.py:563
  66.9 14.2 %all-to-all-start.3 = ((bf16[128,4,128]{2,1,0:T(4,128)(2,1)}), bf16[128,4,128]{2,1,0:T(4,128)(2,1)S(1)}, u32[]{:S(2)}, u32[]{:S(2)}) async-start(bf16[128,4,128]{2,1,0:T(4,128)(2,1)} %bitcast.16), calls=%async_computation.3 | async-start | bytes 262144 | tf_op jit(solution)/shard_map/all_to_all | solution.py:554
  71.0 2.7 %collective-permute-start.6 = (f32[60,128]{1,0:T(8,128)S(1)}, f32[60,128]{1,0:T(8,128)S(1)}, u32[]{:S(2)}, u32[]{:S(2)}) collective-permute-start(f32[60,128]{1,0:T(8,128)S(1)} %get-tuple-element.106), channel_id=1, source_target_pairs={{0,16},{16,32},{32,48},{48,64},{64,80},{80,96},{96,112},{112,0},{1... | collective-permute-start | bytes 92168 | tf_op jit(solution)/shard_map/ppermute | solution.py:562
  72.6 3.9 %collective-permute-start.7 = (f32[60,128]{1,0:T(8,128)S(1)}, f32[60,128]{1,0:T(8,128)S(1)}, u32[]{:S(2)}, u32[]{:S(2)}) collective-permute-start(f32[60,128]{1,0:T(8,128)S(1)} %get-tuple-element.107), channel_id=1, source_target_pairs={{16,0},{32,16},{48,32},{64,48},{80,64},{96,80},{112,96},{0,112},{1... | collective-permute-start | bytes 92168 | tf_op jit(solution)/shard_map/ppermute | solution.py:563
  82.9 15.5 %all-to-all-start.4 = ((f32[128,4,128]{2,1,0:T(4,128)}), f32[128,4,128]{2,1,0:T(4,128)S(1)}, u32[]{:S(2)}, u32[]{:S(2)}) async-start(f32[128,4,128]{2,1,0:T(4,128)} %bitcast.18), calls=%async_computation.4 | async-start | bytes 524288 | tf_op jit(solution)/shard_map/all_to_all | solution.py:554
  87.0 3.0 %collective-permute-start.8 = (f32[60,128]{1,0:T(8,128)S(1)}, f32[60,128]{1,0:T(8,128)S(1)}, u32[]{:S(2)}, u32[]{:S(2)}) collective-permute-start(f32[60,128]{1,0:T(8,128)S(1)} %get-tuple-element.114), channel_id=1, source_target_pairs={{0,16},{16,32},{32,48},{48,64},{64,80},{80,96},{96,112},{112,0},{1... | collective-permute-start | bytes 92168 | tf_op jit(solution)/shard_map/ppermute | solution.py:562
  88.6 4.4 %collective-permute-start.9 = (f32[60,128]{1,0:T(8,128)S(1)}, f32[60,128]{1,0:T(8,128)S(1)}, u32[]{:S(2)}, u32[]{:S(2)}) collective-permute-start(f32[60,128]{1,0:T(8,128)S(1)} %get-tuple-element.115), channel_id=1, source_target_pairs={{16,0},{32,16},{48,32},{64,48},{80,64},{96,80},{112,96},{0,112},{1... | collective-permute-start | bytes 92168 | tf_op jit(solution)/shard_map/ppermute | solution.py:563
  100.1 14.3 %all-to-all-start.5 = ((bf16[128,4,128]{2,1,0:T(4,128)(2,1)}), bf16[128,4,128]{2,1,0:T(4,128)(2,1)S(1)}, u32[]{:S(2)}, u32[]{:S(2)}) async-start(bf16[128,4,128]{2,1,0:T(4,128)(2,1)} %bitcast.20), calls=%async_computation.5 | async-start | bytes 262144 | tf_op jit(solution)/shard_map/all_to_all | solution.py:554
  104.1 2.7 %collective-permute-start.10 = (f32[60,128]{1,0:T(8,128)S(1)}, f32[60,128]{1,0:T(8,128)S(1)}, u32[]{:S(2)}, u32[]{:S(2)}) collective-permute-start(f32[60,128]{1,0:T(8,128)S(1)} %get-tuple-element.121), channel_id=1, source_target_pairs={{0,16},{16,32},{32,48},{48,64},{64,80},{80,96},{96,112},{112,0},{1... | collective-permute-start | bytes 92168 | tf_op jit(solution)/shard_map/ppermute | solution.py:562
  105.8 3.9 %collective-permute-start.11 = (f32[60,128]{1,0:T(8,128)S(1)}, f32[60,128]{1,0:T(8,128)S(1)}, u32[]{:S(2)}, u32[]{:S(2)}) collective-permute-start(f32[60,128]{1,0:T(8,128)S(1)} %get-tuple-element.122), channel_id=1, source_target_pairs={{16,0},{32,16},{48,32},{64,48},{80,64},{96,80},{112,96},{0,112},{1... | collective-permute-start | bytes 92168 | tf_op jit(solution)/shard_map/ppermute | solution.py:563
  116.0 14.2 %all-to-all-start.6 = ((bf16[128,4,128]{2,1,0:T(4,128)(2,1)}), bf16[128,4,128]{2,1,0:T(4,128)(2,1)S(1)}, u32[]{:S(2)}, u32[]{:S(2)}) async-start(bf16[128,4,128]{2,1,0:T(4,128)(2,1)} %bitcast.22), calls=%async_computation.6 | async-start | bytes 262144 | tf_op jit(solution)/shard_map/all_to_all | solution.py:554
  120.0 2.7 %collective-permute-start.12 = (f32[60,128]{1,0:T(8,128)S(1)}, f32[60,128]{1,0:T(8,128)S(1)}, u32[]{:S(2)}, u32[]{:S(2)}) collective-permute-start(f32[60,128]{1,0:T(8,128)S(1)} %get-tuple-element.128), channel_id=1, source_target_pairs={{0,16},{16,32},{32,48},{48,64},{64,80},{80,96},{96,112},{112,0},{1... | collective-permute-start | bytes 92168 | tf_op jit(solution)/shard_map/ppermute | solution.py:562
  121.7 3.9 %collective-permute-start.13 = (f32[60,128]{1,0:T(8,128)S(1)}, f32[60,128]{1,0:T(8,128)S(1)}, u32[]{:S(2)}, u32[]{:S(2)}) collective-permute-start(f32[60,128]{1,0:T(8,128)S(1)} %get-tuple-element.129), channel_id=1, source_target_pairs={{16,0},{32,16},{48,32},{64,48},{80,64},{96,80},{112,96},{0,112},{1... | collective-permute-start | bytes 92168 | tf_op jit(solution)/shard_map/ppermute | solution.py:563
  131.9 14.2 %all-to-all-start.7 = ((bf16[128,4,128]{2,1,0:T(4,128)(2,1)}), bf16[128,4,128]{2,1,0:T(4,128)(2,1)S(1)}, u32[]{:S(2)}, u32[]{:S(2)}) async-start(bf16[128,4,128]{2,1,0:T(4,128)(2,1)} %bitcast.24), calls=%async_computation.7 | async-start | bytes 262144 | tf_op jit(solution)/shard_map/all_to_all | solution.py:554
  135.9 2.7 %collective-permute-start.14 = (f32[60,128]{1,0:T(8,128)S(1)}, f32[60,128]{1,0:T(8,128)S(1)}, u32[]{:S(2)}, u32[]{:S(2)}) collective-permute-start(f32[60,128]{1,0:T(8,128)S(1)} %get-tuple-element.135), channel_id=1, source_target_pairs={{0,16},{16,32},{32,48},{48,64},{64,80},{80,96},{96,112},{112,0},{1... | collective-permute-start | bytes 92168 | tf_op jit(solution)/shard_map/ppermute | solution.py:562
  137.6 3.9 %collective-permute-start.15 = (f32[60,128]{1,0:T(8,128)S(1)}, f32[60,128]{1,0:T(8,128)S(1)}, u32[]{:S(2)}, u32[]{:S(2)}) collective-permute-start(f32[60,128]{1,0:T(8,128)S(1)} %get-tuple-element.136), channel_id=1, source_target_pairs={{16,0},{32,16},{48,32},{64,48},{80,64},{96,80},{112,96},{0,112},{1... | collective-permute-start | bytes 92168 | tf_op jit(solution)/shard_map/ppermute | solution.py:563

commit v10 on v9

--- a/solution.py
+++ b/solution.py
@@ -341,6 +341,35 @@
     return numer / denom
 
 
+def parts_of(x):
+    high, rest = halves(x)
+    return (high,) + halves(rest)
+
+
+def carried(own, relayed):
+    lane = lanes((8, 128))
+    row = jnp.zeros((8, 128), F32)
+    for n, part in enumerate(parts_of(own) + parts_of(relayed)):
+        moved = pltpu.roll(part, 2 * n, 1) if n else part
+        row = jnp.where((lane >> 1) == n, moved, row)
+    return row[0:1]
+
+
+def collected(rows):
+    lane, source = lanes((PEERS, 128)), subs((PEERS, 128))
+
+    def at(shift):
+        return source == ((me() + shift) & (PEERS - 1))
+
+    direct = (lane < 6) & ~(at(1) | at(-1))
+    through = (lane >= 6) & (lane < 12) & (at(15) | at(17))
+    total = jnp.sum(jnp.where(direct | through, rows, 0.0), axis=0, keepdims=True)
+    odd = (lanes((1, 128)) & 1) == 1
+    numer = jnp.sum(jnp.where(odd, 0.0, total), axis=1, keepdims=True)
+    denom = jnp.sum(jnp.where(odd, total, 0.0), axis=1, keepdims=True)
+    return numer / denom
+
+
 def spread_pair(two):
     return jnp.concatenate(
         [jnp.broadcast_to(two[h : h + 1], (8, 128)) for h in range(2)], axis=0
@@ -352,13 +381,12 @@
 MOVING = ("arrived", "near", "from_low", "from_high", "slots", "at_slots", "state")
 NEXT = ("weighted", "toward_low", "toward_high", "message", "slots", "at_slots", "state")
 MORE_IN = {
-    "plain": (), "keep": (), "last": ("field",), "after": (),
+    "plain": (), "keep": (), "last": ("field",), "after": ("sums",), "omega": (),
     "final": ("field", "change", "seg_change", "omega"),
 }
-NARROW = ("plain", "keep", "after")
 MORE_OUT = {
-    "plain": (), "keep": ("field",), "last": ("change", "seg_change"),
-    "after": ("omega",), "final": (),
+    "plain": (), "keep": ("field",), "last": ("change", "seg_change", "sums"),
+    "after": (), "omega": ("omega",), "final": (),
 }
 
 
@@ -373,7 +401,6 @@
     extra = {name: next(take) for name in MORE_IN[kind]}
     out = {name: next(take) for name in results_of(kind)}
     along, pad, forward, wide = take
-    narrow = kind in NARROW
     weighted = out.get("weighted")
     final = kind == "final"
     gx, gy = lax.axis_index("gx"), lax.axis_index("gy")
@@ -465,33 +492,35 @@
         above = jnp.sum(numer, keepdims=True) + jnp.sum(before * change, keepdims=True)
         below = jnp.sum(denom, keepdims=True) + jnp.sum(change * change, keepdims=True)
         place = lanes((PEERS, 128))
-        sums = jnp.where(place == 60, above, jnp.where(place == 61, below, 0.0))
         if final:
-            out["message"][...] = sums
+            out["message"][...] = jnp.where(
+                place == 60, above, jnp.where(place == 61, below, 0.0)
+            )
             return
-    if kind == "after":
-        out["omega"][...] = jnp.broadcast_to(ratio(arrived[block(2), :], 60), (8, 128))
-    message = wide if narrow else out["message"]
+        sums = jnp.where(small == 0, above, jnp.where(small == 1, below, 0.0))
+        out["sums"][...] = sums
+        out["toward_high"][60:64, :] = sums[0:4]
+    if kind == "omega":
+        out["omega"][...] = jnp.broadcast_to(collected(arrived[block(0), :]), (8, 128))
+    message = wide
     advanced = state + seg_res / fixed["diagonal"][...]
     out["state"][...] = advanced
     values = segment_values(advanced, number)
     out["at_slots"][...] = values
     cells = slot_values(fixed["rows_of"][...], fixed["start"][...], forward[...])
     out["slots"][...] = cells
-    columns = to_columns(values)
-    if narrow:
-        message[block(0), :], message[block(2), :] = halves(cells)
-        message[block(1), :], message[block(3), :] = halves(columns)
-    else:
-        message[block(0), :] = cells
-        message[block(1), :] = columns
-        message[block(2), :] = sums
-        message[block(3), :] = jnp.zeros((PEERS, 128), F32)
-    send_borders(
-        fixed["trans"], weighted, along, out["toward_low"], out["toward_high"], message, pad
-    )
-    if narrow:
-        out["message"][...] = message[...].astype(BF16)
+    high, message[block(2), :] = halves(cells)
+    if kind == "after":
+        relayed = jnp.broadcast_to(now["from_low"][60:61, :], (8, 128))
+        row = jnp.broadcast_to(carried(extra["sums"][...], relayed), (PEERS, 128))
+        high = jnp.where(lanes((PEERS, 128)) < 12, row, high)
+    message[block(0), :] = high
+    message[block(1), :], message[block(3), :] = halves(to_columns(values))
+    toward_high = out["toward_high"]
+    if kind == "last":
+        toward_high = toward_high.at[pl.ds(0, 3 * NZ), :]
+    send_borders(fixed["trans"], weighted, along, out["toward_low"], toward_high, message, pad)
+    out["message"][...] = message[...].astype(BF16)
 
 
 def finish(arrived, omega, field_one, field_two, state_one, state_two, cells, segments):
@@ -517,16 +546,18 @@
 SHAPES = {
     "weighted": CELLS, "toward_low": EDGE, "toward_high": EDGE, "message": MESSAGE, "slots": PAIRS,
     "at_slots": TILE, "state": TILE, "omega": TILE, "field": CELLS, "change": CELLS,
-    "seg_change": TILE,
+    "seg_change": TILE, "sums": TILE,
 }
 
 
 def shape_of(kind, name):
+    if kind == "last" and name == "toward_high":
+        return ((64, 128), F32)
     if name != "message":
         return SHAPES[name]
     if kind == "final":
         return PAIRS
-    return (MESSAGE[0], BF16) if kind in NARROW else MESSAGE
+    return (MESSAGE[0], BF16)
 
 
 SCRATCH = (
@@ -633,10 +664,10 @@
     one = advance("keep", now)
     saved["field"] = one["field"]
     now = advance("last", one)
-    saved.update(change=now["change"], seg_change=now["seg_change"])
+    saved.update(change=now["change"], seg_change=now["seg_change"], sums=now["sums"])
     now = advance("after", now)
+    now = advance("omega", now)
     saved["omega"] = now["omega"]
-    now = advance("plain", now)
     two = advance("keep", now)
     saved["field"] = two["field"]
     sums = advance("final", two)

time: 162 us -> 161 us (level)
  transfers between devices with their start and end apart: 24 -> 24, of which waited for: 22 -> 21; matrix products, arithmetic and copies ran while one was open for 0% -> 0% of each run, Pallas kernels for 2% -> 2%
where the time goes in v10:
time: 161 us; the launch traced here: 160 us
  waiting for transfers between devices  72.4 us (45%)
  starting transfers between devices  52.9 us (33%)
  Pallas kernels  19.3 us (12%)
  blocking collectives  13.6 us (8%)
    all_to_all x8, waiting for transfers between devices, exchange(): lax.all_to_all(message, AXES, split_axis=0, concat_axis=0, tiled=True)  46.4 us
    all_to_all x8, starting transfers between devices, exchange(): lax.all_to_all(message, AXES, split_axis=0, concat_axis=0, tiled=True)  39.7 us
    ppermute x8, waiting for transfers between devices, neighbours(): lax.ppermute(toward_low, 'gx', down)  21.1 us
    pallas_call x20, Pallas kernels, call(): pl.pallas_call(body, out_shape=[jax.ShapeDtypeStruct(*out) for out in out...  19.3 us
    all_to_all x1, blocking collectives, exchange(): lax.all_to_all(message, AXES, split_axis=0, concat_axis=0, tiled=True)  13.6 us
    ppermute x8, starting transfers between devices, neighbours(): lax.ppermute(toward_high, 'gx', up)  13.2 us
    ppermute x8, waiting for transfers between devices, neighbours(): lax.ppermute(toward_high, 'gx', up)  4.79 us
  transfers between devices with their start and end apart: 24, of which 21 were waited for; matrix products, arithmetic and copies ran while one was open for 0% of the time, Pallas kernels for 2%

profile of v10, /device:TPU:1, one launch (start us, length us, event | category | flops | bytes accessed | tf_op | source)
XLA Modules:
  0.0 160.1 jit_solution(11118694737771805696)
XLA Ops:
  0.6 3.0 %cell_setup.1 = (bf16[128,160]{1,0:T(8,128)(2,1)}, bf16[160,128]{1,0:T(8,128)(2,1)}, s32[128,128]{1,0:T(8,128)}, f32[128,128]{1,0:T(8,128)}, f32[128,128]{1,0:T(...) custom-call(f32[3,160,128]{2,1,0:T(8,128)} %bitcast.67, ...), custom_call_target="tpu_custom_call" | custom-call | flops 4000000 | bytes 1121280 | tf_op jit(solution)/shard_map/cell_setup/pallas_call | solution.py:572
  3.6 11.5 %all-to-all-start = ((bf16[128,24,128]{2,1,0:T(8,128)(2,1)}), bf16[128,24,128]{2,1,0:T(8,128)(2,1)S(1)}, u32[]{:S(2)}, u32[]{:S(2)}) async-start(bf16[128,24,128]{2,1,0:T(8,128)(2,1)} %bitcast.97), calls=%async_computation | async-start | bytes 1572864 | tf_op jit(solution)/shard_map/all_to_all | solution.py:585
  15.2 1.6 %collective-permute-start = (f32[60,128]{1,0:T(8,128)S(1)}, f32[60,128]{1,0:T(8,128)S(1)}, u32[]{:S(2)}, u32[]{:S(2)}) collective-permute-start(f32[60,128]{1,0:T(8,128)S(1)} %copy-done.14), channel_id=1, source_target_pairs={{0,16},{16,32},{32,48},{48,64},{64,80},{80,96},{96,112},{112,0},{1... | collective-permute-start | bytes 92168 | tf_op jit(solution)/shard_map/ppermute | solution.py:593
  16.9 0.8 copy-done
  18.0 14.0 %all-to-all-done = bf16[128,24,128]{2,1,0:T(8,128)(2,1)S(1)} async-done(((bf16[128,24,128]{2,1,0:T(8,128)(2,1)}), bf16[128,24,128]{2,1,0:T(8,128)(2,1)S(1)}, u32[]{:S(2)}, u32[]{:S(2)}) %all-to-all-start) | async-done | bytes 786464 | tf_op jit(solution)/shard_map/all_to_all | solution.py:585
  32.0 1.2 well_setup.1
  33.3 1.7 %sweep_plain.2 = (f32[3,160,128]{2,1,0:T(8,128)S(1)}, f32[60,128]{1,0:T(8,128)S(1)}, f32[60,128]{1,0:T(8,128)S(1)}, bf16[512,128]{1,0:T(8,128)(2,1)}, f32[128,12...) custom-call(f32[512,128]{1,0:T(8,128)S(1)} %get-tuple-element.77.refs_0_, ...), custom_call_target="tpu_custom_call" | custom-call | flops 4000000 | bytes 2334720 | tf_op jit(solution)/shard_map/sweep_plain/pallas_call | solution.py:572
  35.0 4.1 %all-to-all-start.1 = ((bf16[128,4,128]{2,1,0:T(4,128)(2,1)}), bf16[128,4,128]{2,1,0:T(4,128)(2,1)S(1)}, u32[]{:S(2)}, u32[]{:S(2)}) async-start(bf16[128,4,128]{2,1,0:T(4,128)(2,1)} %bitcast.12), calls=%async_computation.1 | async-start | bytes 262144 | tf_op jit(solution)/shard_map/all_to_all | solution.py:585
  39.0 1.7 %collective-permute-start.2 = (f32[60,128]{1,0:T(8,128)S(1)}, f32[60,128]{1,0:T(8,128)S(1)}, u32[]{:S(2)}, u32[]{:S(2)}) collective-permute-start(f32[60,128]{1,0:T(8,128)S(1)} %get-tuple-element.93), channel_id=1, source_target_pairs={{0,16},{16,32},{32,48},{48,64},{64,80},{80,96},{96,112},{112,0},{1... | collective-permute-start | bytes 92168 | tf_op jit(solution)/shard_map/ppermute | solution.py:593
  41.0 0.8 collective-permute-done.2.refs_2_
  41.8 2.9 %collective-permute-done.3.refs_3_ = f32[60,128]{1,0:T(8,128)S(1)} collective-permute-done((f32[60,128]{1,0:T(8,128)S(1)}, f32[60,128]{1,0:T(8,128)S(1)}, u32[]{:S(2)}, u32[]{:S(2)}) %collective-permute-start.3) | collective-permute-done | bytes 30752 | tf_op jit(solution)/shard_map/ppermute | solution.py:594
  44.7 4.7 %all-to-all-done.1 = bf16[128,4,128]{2,1,0:T(4,128)(2,1)S(1)} async-done(((bf16[128,4,128]{2,1,0:T(4,128)(2,1)}), bf16[128,4,128]{2,1,0:T(4,128)(2,1)S(1)}, u32[]{:S(2)}, u32[]{:S(2)}) %all-to-all-start.1) | async-done | bytes 131104 | tf_op jit(solution)/shard_map/all_to_all | solution.py:585
  49.4 1.7 %sweep_plain.3 = (f32[3,160,128]{2,1,0:T(8,128)S(1)}, f32[60,128]{1,0:T(8,128)S(1)}, f32[60,128]{1,0:T(8,128)S(1)}, bf16[512,128]{1,0:T(8,128)(2,1)}, f32[128,12...) custom-call(bf16[512,128]{1,0:T(8,128)(2,1)S(1)} %bitcast.81, f32[3,160,128]{2,1,0:T(8,128)S(1)} %interior.9.refs_1_, ...), custom_call_target="tpu_custom_call" | custom-call | flops 4000000 | bytes 2203648 | tf_op jit(solution)/shard_map/sweep_plain/pallas_call | solution.py:572
  51.0 4.0 %all-to-all-start.2 = ((bf16[128,4,128]{2,1,0:T(4,128)(2,1)}), bf16[128,4,128]{2,1,0:T(4,128)(2,1)S(1)}, u32[]{:S(2)}, u32[]{:S(2)}) async-start(bf16[128,4,128]{2,1,0:T(4,128)(2,1)} %bitcast.14), calls=%async_computation.2 | async-start | bytes 262144 | tf_op jit(solution)/shard_map/all_to_all | solution.py:585
  55.1 1.6 %collective-permute-start.4 = (f32[60,128]{1,0:T(8,128)S(1)}, f32[60,128]{1,0:T(8,128)S(1)}, u32[]{:S(2)}, u32[]{:S(2)}) collective-permute-start(f32[60,128]{1,0:T(8,128)S(1)} %get-tuple-element.100), channel_id=1, source_target_pairs={{0,16},{16,32},{32,48},{48,64},{64,80},{80,96},{96,112},{112,0},{1... | collective-permute-start | bytes 92168 | tf_op jit(solution)/shard_map/ppermute | solution.py:593
  56.9 0.8 collective-permute-done.4.refs_2_
  57.7 2.9 %collective-permute-done.5.refs_3_ = f32[60,128]{1,0:T(8,128)S(1)} collective-permute-done((f32[60,128]{1,0:T(8,128)S(1)}, f32[60,128]{1,0:T(8,128)S(1)}, u32[]{:S(2)}, u32[]{:S(2)}) %collective-permute-start.5) | collective-permute-done | bytes 30752 | tf_op jit(solution)/shard_map/ppermute | solution.py:594
  60.6 4.6 %all-to-all-done.2 = bf16[128,4,128]{2,1,0:T(4,128)(2,1)S(1)} async-done(((bf16[128,4,128]{2,1,0:T(4,128)(2,1)}), bf16[128,4,128]{2,1,0:T(4,128)(2,1)S(1)}, u32[]{:S(2)}, u32[]{:S(2)}) %all-to-all-start.2) | async-done | bytes 131104 | tf_op jit(solution)/shard_map/all_to_all | solution.py:585
  65.3 1.7 %sweep_keep.2 = (f32[3,160,128]{2,1,0:T(8,128)S(1)}, f32[60,128]{1,0:T(8,128)S(1)}, f32[60,128]{1,0:T(8,128)S(1)}, bf16[512,128]{1,0:T(8,128)(2,1)}, f32[128,128...) custom-call(bf16[512,128]{1,0:T(8,128)(2,1)S(1)} %bitcast.79, ...), custom_call_target="tpu_custom_call" | custom-call | flops 4000000 | bytes 2203648 | tf_op jit(solution)/shard_map/sweep_keep/pallas_call | solution.py:572
  66.9 4.0 %all-to-all-start.3 = ((bf16[128,4,128]{2,1,0:T(4,128)(2,1)}), bf16[128,4,128]{2,1,0:T(4,128)(2,1)S(1)}, u32[]{:S(2)}, u32[]{:S(2)}) async-start(bf16[128,4,128]{2,1,0:T(4,128)(2,1)} %bitcast.16), calls=%async_computation.3 | async-start | bytes 262144 | tf_op jit(solution)/shard_map/all_to_all | solution.py:585
  71.0 1.6 %collective-permute-start.6 = (f32[60,128]{1,0:T(8,128)S(1)}, f32[60,128]{1,0:T(8,128)S(1)}, u32[]{:S(2)}, u32[]{:S(2)}) collective-permute-start(f32[60,128]{1,0:T(8,128)S(1)} %get-tuple-element.107), channel_id=1, source_target_pairs={{0,16},{16,32},{32,48},{48,64},{64,80},{80,96},{96,112},{112,0},{1... | collective-permute-start | bytes 92168 | tf_op jit(solution)/shard_map/ppermute | solution.py:593
  72.8 0.8 collective-permute-done.6.refs_2_
  73.6 2.9 %collective-permute-done.7.refs_3_ = f32[60,128]{1,0:T(8,128)S(1)} collective-permute-done((f32[60,128]{1,0:T(8,128)S(1)}, f32[60,128]{1,0:T(8,128)S(1)}, u32[]{:S(2)}, u32[]{:S(2)}) %collective-permute-start.7) | collective-permute-done | bytes 30752 | tf_op jit(solution)/shard_map/ppermute | solution.py:594
  76.5 4.6 %all-to-all-done.3 = bf16[128,4,128]{2,1,0:T(4,128)(2,1)S(1)} async-done(((bf16[128,4,128]{2,1,0:T(4,128)(2,1)}), bf16[128,4,128]{2,1,0:T(4,128)(2,1)S(1)}, u32[]{:S(2)}, u32[]{:S(2)}) %all-to-all-start.3) | async-done | bytes 131104 | tf_op jit(solution)/shard_map/all_to_all | solution.py:585
  81.2 1.8 %sweep_last.1 = (f32[3,160,128]{2,1,0:T(8,128)S(1)}, f32[60,128]{1,0:T(8,128)S(1)}, f32[64,128]{1,0:T(8,128)S(1)}, bf16[512,128]{1,0:T(8,128)(2,1)}, f32[128,128...) custom-call(bf16[512,128]{1,0:T(8,128)(2,1)S(1)} %bitcast.78, ...), custom_call_target="tpu_custom_call" | custom-call | flops 4000000 | bytes 2449408 | tf_op jit(solution)/shard_map/sweep_last/pallas_call | solution.py:572
  82.9 4.0 %all-to-all-start.4 = ((bf16[128,4,128]{2,1,0:T(4,128)(2,1)}), bf16[128,4,128]{2,1,0:T(4,128)(2,1)S(1)}, u32[]{:S(2)}, u32[]{:S(2)}) async-start(bf16[128,4,128]{2,1,0:T(4,128)(2,1)} %bitcast.18), calls=%async_computation.4 | async-start | bytes 262144 | tf_op jit(solution)/shard_map/all_to_all | solution.py:585
  86.9 1.6 %collective-permute-start.8 = (f32[64,128]{1,0:T(8,128)S(1)}, f32[64,128]{1,0:T(8,128)S(1)}, u32[]{:S(2)}, u32[]{:S(2)}) collective-permute-start(f32[64,128]{1,0:T(8,128)S(1)} %get-tuple-element.115), channel_id=1, source_target_pairs={{0,16},{16,32},{32,48},{48,64},{64,80},{80,96},{96,112},{112,0},{1... | collective-permute-start | bytes 98312 | tf_op jit(solution)/shard_map/ppermute | solution.py:593
  88.8 3.7 %collective-permute-done.9.refs_3_ = f32[60,128]{1,0:T(8,128)S(1)} collective-permute-done((f32[60,128]{1,0:T(8,128)S(1)}, f32[60,128]{1,0:T(8,128)S(1)}, u32[]{:S(2)}, u32[]{:S(2)}) %collective-permute-start.9) | collective-permute-done | bytes 30752 | tf_op jit(solution)/shard_map/ppermute | solution.py:594
  92.5 4.6 %all-to-all-done.4 = bf16[128,4,128]{2,1,0:T(4,128)(2,1)S(1)} async-done(((bf16[128,4,128]{2,1,0:T(4,128)(2,1)}), bf16[128,4,128]{2,1,0:T(4,128)(2,1)S(1)}, u32[]{:S(2)}, u32[]{:S(2)}) %all-to-all-start.4) | async-done | bytes 131104 | tf_op jit(solution)/shard_map/all_to_all | solution.py:585
  97.2 1.7 %sweep_after.1 = (f32[3,160,128]{2,1,0:T(8,128)S(1)}, f32[60,128]{1,0:T(8,128)S(1)}, f32[60,128]{1,0:T(8,128)S(1)}, bf16[512,128]{1,0:T(8,128)(2,1)}, f32[128,12...) custom-call(bf16[512,128]{1,0:T(8,128)(2,1)S(1)} %bitcast.82, f32[3,160,128]{2,1,0:T(8,128)S(1)} %interior.12.refs_1_, ...), custom_call_target="tpu_custom_call" | custom-call | flops 4000000 | bytes 2209792 | tf_op jit(solution)/shard_map/sweep_after/pallas_call | solution.py:572
  98.8 4.0 %all-to-all-start.5 = ((bf16[128,4,128]{2,1,0:T(4,128)(2,1)}), bf16[128,4,128]{2,1,0:T(4,128)(2,1)S(1)}, u32[]{:S(2)}, u32[]{:S(2)}) async-start(bf16[128,4,128]{2,1,0:T(4,128)(2,1)} %bitcast.20), calls=%async_computation.5 | async-start | bytes 262144 | tf_op jit(solution)/shard_map/all_to_all | solution.py:585
  102.8 1.6 %collective-permute-start.10 = (f32[60,128]{1,0:T(8,128)S(1)}, f32[60,128]{1,0:T(8,128)S(1)}, u32[]{:S(2)}, u32[]{:S(2)}) collective-permute-start(f32[60,128]{1,0:T(8,128)S(1)} %get-tuple-element.123), channel_id=1, source_target_pairs={{0,16},{16,32},{32,48},{48,64},{64,80},{80,96},{96,112},{112,0},{1... | collective-permute-start | bytes 92168 | tf_op jit(solution)/shard_map/ppermute | solution.py:593
  104.7 0.8 collective-permute-done.10.refs_2_
  105.5 2.9 %collective-permute-done.11.refs_3_ = f32[60,128]{1,0:T(8,128)S(1)} collective-permute-done((f32[60,128]{1,0:T(8,128)S(1)}, f32[60,128]{1,0:T(8,128)S(1)}, u32[]{:S(2)}, u32[]{:S(2)}) %collective-permute-start.11) | collective-permute-done | bytes 30752 | tf_op jit(solution)/shard_map/ppermute | solution.py:594
  108.4 4.6 %all-to-all-done.5 = bf16[128,4,128]{2,1,0:T(4,128)(2,1)S(1)} async-done(((bf16[128,4,128]{2,1,0:T(4,128)(2,1)}), bf16[128,4,128]{2,1,0:T(4,128)(2,1)S(1)}, u32[]{:S(2)}, u32[]{:S(2)}) %all-to-all-start.5) | async-done | bytes 131104 | tf_op jit(solution)/shard_map/all_to_all | solution.py:585
  113.1 1.7 %sweep_omega.1 = (f32[3,160,128]{2,1,0:T(8,128)S(1)}, f32[60,128]{1,0:T(8,128)S(1)}, f32[60,128]{1,0:T(8,128)S(1)}, bf16[512,128]{1,0:T(8,128)(2,1)}, f32[128,12...) custom-call(bf16[512,128]{1,0:T(8,128)(2,1)S(1)} %bitcast.80, ...), custom_call_target="tpu_custom_call" | custom-call | flops 4000000 | bytes 2203648 | tf_op jit(solution)/shard_map/sweep_omega/pallas_call | solution.py:572
  114.8 4.0 %all-to-all-start.6 = ((bf16[128,4,128]{2,1,0:T(4,128)(2,1)}), bf16[128,4,128]{2,1,0:T(4,128)(2,1)S(1)}, u32[]{:S(2)}, u32[]{:S(2)}) async-start(bf16[128,4,128]{2,1,0:T(4,128)(2,1)} %bitcast.22), calls=%async_computation.6 | async-start | bytes 262144 | tf_op jit(solution)/shard_map/all_to_all | solution.py:585
  118.8 1.6 %collective-permute-start.12 = (f32[60,128]{1,0:T(8,128)S(1)}, f32[60,128]{1,0:T(8,128)S(1)}, u32[]{:S(2)}, u32[]{:S(2)}) collective-permute-start(f32[60,128]{1,0:T(8,128)S(1)} %get-tuple-element.130), channel_id=1, source_target_pairs={{0,16},{16,32},{32,48},{48,64},{64,80},{80,96},{96,112},{112,0},{1... | collective-permute-start | bytes 92168 | tf_op jit(solution)/shard_map/ppermute | solution.py:593
  120.7 0.8 collective-permute-done.12.refs_2_
  121.5 2.9 %collective-permute-done.13.refs_3_ = f32[60,128]{1,0:T(8,128)S(1)} collective-permute-done((f32[60,128]{1,0:T(8,128)S(1)}, f32[60,128]{1,0:T(8,128)S(1)}, u32[]{:S(2)}, u32[]{:S(2)}) %collective-permute-start.13) | collective-permute-done | bytes 30752 | tf_op jit(solution)/shard_map/ppermute | solution.py:594
  124.4 4.6 %all-to-all-done.6 = bf16[128,4,128]{2,1,0:T(4,128)(2,1)S(1)} async-done(((bf16[128,4,128]{2,1,0:T(4,128)(2,1)}), bf16[128,4,128]{2,1,0:T(4,128)(2,1)S(1)}, u32[]{:S(2)}, u32[]{:S(2)}) %all-to-all-start.6) | async-done | bytes 131104 | tf_op jit(solution)/shard_map/all_to_all | solution.py:585
  129.0 1.7 %sweep_keep.3 = (f32[3,160,128]{2,1,0:T(8,128)S(1)}, f32[60,128]{1,0:T(8,128)S(1)}, f32[60,128]{1,0:T(8,128)S(1)}, bf16[512,128]{1,0:T(8,128)(2,1)}, f32[128,128...) custom-call(bf16[512,128]{1,0:T(8,128)(2,1)S(1)} %bitcast.83, ...), custom_call_target="tpu_custom_call" | custom-call | flops 4000000 | bytes 2203648 | tf_op jit(solution)/shard_map/sweep_keep/pallas_call | solution.py:572
  130.7 4.0 %all-to-all-start.7 = ((bf16[128,4,128]{2,1,0:T(4,128)(2,1)}), bf16[128,4,128]{2,1,0:T(4,128)(2,1)S(1)}, u32[]{:S(2)}, u32[]{:S(2)}) async-start(bf16[128,4,128]{2,1,0:T(4,128)(2,1)} %bitcast.24), calls=%async_computation.7 | async-start | bytes 262144 | tf_op jit(solution)/shard_map/all_to_all | solution.py:585
  134.7 1.6 %collective-permute-start.14 = (f32[60,128]{1,0:T(8,128)S(1)}, f32[60,128]{1,0:T(8,128)S(1)}, u32[]{:S(2)}, u32[]{:S(2)}) collective-permute-start(f32[60,128]{1,0:T(8,128)S(1)} %get-tuple-element.137), channel_id=1, source_target_pairs={{0,16},{16,32},{32,48},{48,64},{64,80},{80,96},{96,112},{112,0},{1... | collective-permute-start | bytes 92168 | tf_op jit(solution)/shard_map/ppermute | solution.py:593
  137.4 2.9 %collective-permute-done.15.refs_3_ = f32[60,128]{1,0:T(8,128)S(1)} collective-permute-done((f32[60,128]{1,0:T(8,128)S(1)}, f32[60,128]{1,0:T(8,128)S(1)}, u32[]{:S(2)}, u32[]{:S(2)}) %collective-permute-start.15) | collective-permute-done | bytes 30752 | tf_op jit(solution)/shard_map/ppermute | solution.py:594
  140.3 4.6 %all-to-all-done.7 = bf16[128,4,128]{2,1,0:T(4,128)(2,1)S(1)} async-done(((bf16[128,4,128]{2,1,0:T(4,128)(2,1)}), bf16[128,4,128]{2,1,0:T(4,128)(2,1)S(1)}, u32[]{:S(2)}, u32[]{:S(2)}) %all-to-all-start.7) | async-done | bytes 131104 | tf_op jit(solution)/shard_map/all_to_all | solution.py:585
  145.6 13.6 %all_to_all.99 = f32[128,1,128]{2,1,0:T(1,128)S(1)} all-to-all(f32[128,1,128]{2,1,0:T(1,128)S(1)} %bitcast.95), channel_id=1, replica_groups=mesh['gx'=8,'gy'=16] {'gx','gy'}, dimensions={0} | all-to-all | bytes 131072 | tf_op jit(solution)/shard_map/all_to_all | solution.py:585
  159.2 0.8 finish.1
  (51 shorter events, 3.4 us)
Async XLA Ops:
  3.6 11.6 %copy-start.14 = (f32[60,128]{1,0:T(8,128)S(1)}, f32[60,128]{1,0:T(8,128)}, u32[]{:S(2)}) copy-start(f32[60,128]{1,0:T(8,128)} %get-tuple-element.79) | copy-start | bytes 92164
  3.6 13.2 %copy-start.13 = (f32[60,128]{1,0:T(8,128)S(1)}, f32[60,128]{1,0:T(8,128)}, u32[]{:S(2)}) copy-start(f32[60,128]{1,0:T(8,128)} %get-tuple-element.80) | copy-start | bytes 92164
  3.6 13.2 %copy-start.10 = (s32[1,8,128]{2,1,0:T(8,128)S(1)}, s32[1,8,128]{2,1,0:T(8,128)}, u32[]{:S(2)}) copy-start(s32[1,8,128]{2,1,0:T(8,128)} %param.16) | copy-start | bytes 12292
  3.6 13.3 %copy-start.11 = (f32[3,160,128]{2,1,0:T(8,128)S(1)}, f32[3,160,128]{2,1,0:T(8,128)}, u32[]{:S(2)}) copy-start(f32[3,160,128]{2,1,0:T(8,128)} %get-tuple-element.78.weighted) | copy-start | bytes 737284
  3.6 28.3 %all-to-all-start = ((bf16[128,24,128]{2,1,0:T(8,128)(2,1)}), bf16[128,24,128]{2,1,0:T(8,128)(2,1)S(1)}, u32[]{:S(2)}, u32[]{:S(2)}) async-start(bf16[128,24,128]{2,1,0:T(8,128)(2,1)} %bitcast.97), calls=%async_computation | async-start | bytes 1572864 | tf_op jit(solution)/shard_map/all_to_all | solution.py:585
  15.2 18.0 %collective-permute-start = (f32[60,128]{1,0:T(8,128)S(1)}, f32[60,128]{1,0:T(8,128)S(1)}, u32[]{:S(2)}, u32[]{:S(2)}) collective-permute-start(f32[60,128]{1,0:T(8,128)S(1)} %copy-done.14), channel_id=1, source_target_pairs={{0,16},{16,32},{32,48},{48,64},{64,80},{80,96},{96,112},{112,0},{1... | collective-permute-start | bytes 92168 | tf_op jit(solution)/shard_map/ppermute | solution.py:593
  16.8 0.9 copy-start
  16.8 16.4 %collective-permute-start.1 = (f32[60,128]{1,0:T(8,128)S(1)}, f32[60,128]{1,0:T(8,128)S(1)}, u32[]{:S(2)}, u32[]{:S(2)}) collective-permute-start(f32[60,128]{1,0:T(8,128)S(1)} %copy-done.13), channel_id=1, source_target_pairs={{16,0},{32,16},{48,32},{64,48},{80,64},{96,80},{112,96},{0,112},{1... | collective-permute-start | bytes 92168 | tf_op jit(solution)/shard_map/ppermute | solution.py:594
  17.7 14.2 %copy-start.9 = (f32[4,8,128]{2,1,0:T(8,128)S(1)}, f32[4,8,128]{2,1,0:T(8,128)}, u32[]{:S(2)}) copy-start(f32[4,8,128]{2,1,0:T(8,128)} %get-tuple-element.76.fixed.refs_18_) | copy-start | bytes 49156
  17.7 15.5 %copy-start.5 = (bf16[128,160]{1,0:T(8,128)(2,1)S(1)}, bf16[128,160]{1,0:T(8,128)(2,1)}, u32[]{:S(2)}) copy-start(bf16[128,160]{1,0:T(8,128)(2,1)} %get-tuple-element.84.refs_11_) | copy-start | bytes 122884
  17.7 15.5 %copy-start.6 = (s32[128,128]{1,0:T(8,128)S(1)}, s32[128,128]{1,0:T(8,128)}, u32[]{:S(2)}) copy-start(s32[128,128]{1,0:T(8,128)} %get-tuple-element.86.refs_13_) | copy-start | bytes 196612
  17.7 15.5 %copy-start.7 = (f32[128,128]{1,0:T(8,128)S(1)}, f32[128,128]{1,0:T(8,128)}, u32[]{:S(2)}) copy-start(f32[128,128]{1,0:T(8,128)} %get-tuple-element.87.refs_14_) | copy-start | bytes 196612
  17.7 15.5 %copy-start.8 = (bf16[160,128]{1,0:T(8,128)(2,1)S(1)}, bf16[160,128]{1,0:T(8,128)(2,1)}, u32[]{:S(2)}) copy-start(bf16[160,128]{1,0:T(8,128)(2,1)} %get-tuple-element.85.refs_12_) | copy-start | bytes 122884
  17.7 15.5 %copy-start.12 = (f32[128,128]{1,0:T(8,128)S(1)}, f32[128,128]{1,0:T(8,128)}, u32[]{:S(2)}) copy-start(f32[128,128]{1,0:T(8,128)} %get-tuple-element.81.refs_4_) | copy-start | bytes 196612
  31.9 1.3 copy-start.1
  31.9 1.4 copy-start.2
  31.9 1.4 copy-start.3
  31.9 1.4 copy-start.4
  35.0 14.4 %all-to-all-start.1 = ((bf16[128,4,128]{2,1,0:T(4,128)(2,1)}), bf16[128,4,128]{2,1,0:T(4,128)(2,1)S(1)}, u32[]{:S(2)}, u32[]{:S(2)}) async-start(bf16[128,4,128]{2,1,0:T(4,128)(2,1)} %bitcast.12), calls=%async_computation.1 | async-start | bytes 262144 | tf_op jit(solution)/shard_map/all_to_all | solution.py:585
  39.0 2.7 %collective-permute-start.2 = (f32[60,128]{1,0:T(8,128)S(1)}, f32[60,128]{1,0:T(8,128)S(1)}, u32[]{:S(2)}, u32[]{:S(2)}) collective-permute-start(f32[60,128]{1,0:T(8,128)S(1)} %get-tuple-element.93), channel_id=1, source_target_pairs={{0,16},{16,32},{32,48},{48,64},{64,80},{80,96},{96,112},{112,0},{1... | collective-permute-start | bytes 92168 | tf_op jit(solution)/shard_map/ppermute | solution.py:593
  40.7 3.9 %collective-permute-start.3 = (f32[60,128]{1,0:T(8,128)S(1)}, f32[60,128]{1,0:T(8,128)S(1)}, u32[]{:S(2)}, u32[]{:S(2)}) collective-permute-start(f32[60,128]{1,0:T(8,128)S(1)} %get-tuple-element.94), channel_id=1, source_target_pairs={{16,0},{32,16},{48,32},{64,48},{80,64},{96,80},{112,96},{0,112},{1... | collective-permute-start | bytes 92168 | tf_op jit(solution)/shard_map/ppermute | solution.py:594
  51.0 14.2 %all-to-all-start.2 = ((bf16[128,4,128]{2,1,0:T(4,128)(2,1)}), bf16[128,4,128]{2,1,0:T(4,128)(2,1)S(1)}, u32[]{:S(2)}, u32[]{:S(2)}) async-start(bf16[128,4,128]{2,1,0:T(4,128)(2,1)} %bitcast.14), calls=%async_computation.2 | async-start | bytes 262144 | tf_op jit(solution)/shard_map/all_to_all | solution.py:585
  55.1 2.7 %collective-permute-start.4 = (f32[60,128]{1,0:T(8,128)S(1)}, f32[60,128]{1,0:T(8,128)S(1)}, u32[]{:S(2)}, u32[]{:S(2)}) collective-permute-start(f32[60,128]{1,0:T(8,128)S(1)} %get-tuple-element.100), channel_id=1, source_target_pairs={{0,16},{16,32},{32,48},{48,64},{64,80},{80,96},{96,112},{112,0},{1... | collective-permute-start | bytes 92168 | tf_op jit(solution)/shard_map/ppermute | solution.py:593
  56.7 3.9 %collective-permute-start.5 = (f32[60,128]{1,0:T(8,128)S(1)}, f32[60,128]{1,0:T(8,128)S(1)}, u32[]{:S(2)}, u32[]{:S(2)}) collective-permute-start(f32[60,128]{1,0:T(8,128)S(1)} %get-tuple-element.101), channel_id=1, source_target_pairs={{16,0},{32,16},{48,32},{64,48},{80,64},{96,80},{112,96},{0,112},{1... | collective-permute-start | bytes 92168 | tf_op jit(solution)/shard_map/ppermute | solution.py:594
  66.9 14.2 %all-to-all-start.3 = ((bf16[128,4,128]{2,1,0:T(4,128)(2,1)}), bf16[128,4,128]{2,1,0:T(4,128)(2,1)S(1)}, u32[]{:S(2)}, u32[]{:S(2)}) async-start(bf16[128,4,128]{2,1,0:T(4,128)(2,1)} %bitcast.16), calls=%async_computation.3 | async-start | bytes 262144 | tf_op jit(solution)/shard_map/all_to_all | solution.py:585
  71.0 2.7 %collective-permute-start.6 = (f32[60,128]{1,0:T(8,128)S(1)}, f32[60,128]{1,0:T(8,128)S(1)}, u32[]{:S(2)}, u32[]{:S(2)}) collective-permute-start(f32[60,128]{1,0:T(8,128)S(1)} %get-tuple-element.107), channel_id=1, source_target_pairs={{0,16},{16,32},{32,48},{48,64},{64,80},{80,96},{96,112},{112,0},{1... | collective-permute-start | bytes 92168 | tf_op jit(solution)/shard_map/ppermute | solution.py:593
  72.6 3.9 %collective-permute-start.7 = (f32[60,128]{1,0:T(8,128)S(1)}, f32[60,128]{1,0:T(8,128)S(1)}, u32[]{:S(2)}, u32[]{:S(2)}) collective-permute-start(f32[60,128]{1,0:T(8,128)S(1)} %get-tuple-element.108), channel_id=1, source_target_pairs={{16,0},{32,16},{48,32},{64,48},{80,64},{96,80},{112,96},{0,112},{1... | collective-permute-start | bytes 92168 | tf_op jit(solution)/shard_map/ppermute | solution.py:594
  82.9 14.2 %all-to-all-start.4 = ((bf16[128,4,128]{2,1,0:T(4,128)(2,1)}), bf16[128,4,128]{2,1,0:T(4,128)(2,1)S(1)}, u32[]{:S(2)}, u32[]{:S(2)}) async-start(bf16[128,4,128]{2,1,0:T(4,128)(2,1)} %bitcast.18), calls=%async_computation.4 | async-start | bytes 262144 | tf_op jit(solution)/shard_map/all_to_all | solution.py:585
  86.9 5.6 %collective-permute-start.8 = (f32[64,128]{1,0:T(8,128)S(1)}, f32[64,128]{1,0:T(8,128)S(1)}, u32[]{:S(2)}, u32[]{:S(2)}) collective-permute-start(f32[64,128]{1,0:T(8,128)S(1)} %get-tuple-element.115), channel_id=1, source_target_pairs={{0,16},{16,32},{32,48},{48,64},{64,80},{80,96},{96,112},{112,0},{1... | collective-permute-start | bytes 98312 | tf_op jit(solution)/shard_map/ppermute | solution.py:593
  88.6 3.9 %collective-permute-start.9 = (f32[60,128]{1,0:T(8,128)S(1)}, f32[60,128]{1,0:T(8,128)S(1)}, u32[]{:S(2)}, u32[]{:S(2)}) collective-permute-start(f32[60,128]{1,0:T(8,128)S(1)} %get-tuple-element.116), channel_id=1, source_target_pairs={{16,0},{32,16},{48,32},{64,48},{80,64},{96,80},{112,96},{0,112},{1... | collective-permute-start | bytes 92168 | tf_op jit(solution)/shard_map/ppermute | solution.py:594
  98.8 14.2 %all-to-all-start.5 = ((bf16[128,4,128]{2,1,0:T(4,128)(2,1)}), bf16[128,4,128]{2,1,0:T(4,128)(2,1)S(1)}, u32[]{:S(2)}, u32[]{:S(2)}) async-start(bf16[128,4,128]{2,1,0:T(4,128)(2,1)} %bitcast.20), calls=%async_computation.5 | async-start | bytes 262144 | tf_op jit(solution)/shard_map/all_to_all | solution.py:585
  102.8 2.7 %collective-permute-start.10 = (f32[60,128]{1,0:T(8,128)S(1)}, f32[60,128]{1,0:T(8,128)S(1)}, u32[]{:S(2)}, u32[]{:S(2)}) collective-permute-start(f32[60,128]{1,0:T(8,128)S(1)} %get-tuple-element.123), channel_id=1, source_target_pairs={{0,16},{16,32},{32,48},{48,64},{64,80},{80,96},{96,112},{112,0},{1... | collective-permute-start | bytes 92168 | tf_op jit(solution)/shard_map/ppermute | solution.py:593
  104.5 3.9 %collective-permute-start.11 = (f32[60,128]{1,0:T(8,128)S(1)}, f32[60,128]{1,0:T(8,128)S(1)}, u32[]{:S(2)}, u32[]{:S(2)}) collective-permute-start(f32[60,128]{1,0:T(8,128)S(1)} %get-tuple-element.124), channel_id=1, source_target_pairs={{16,0},{32,16},{48,32},{64,48},{80,64},{96,80},{112,96},{0,112},{1... | collective-permute-start | bytes 92168 | tf_op jit(solution)/shard_map/ppermute | solution.py:594
  114.8 14.2 %all-to-all-start.6 = ((bf16[128,4,128]{2,1,0:T(4,128)(2,1)}), bf16[128,4,128]{2,1,0:T(4,128)(2,1)S(1)}, u32[]{:S(2)}, u32[]{:S(2)}) async-start(bf16[128,4,128]{2,1,0:T(4,128)(2,1)} %bitcast.22), calls=%async_computation.6 | async-start | bytes 262144 | tf_op jit(solution)/shard_map/all_to_all | solution.py:585
  118.8 2.7 %collective-permute-start.12 = (f32[60,128]{1,0:T(8,128)S(1)}, f32[60,128]{1,0:T(8,128)S(1)}, u32[]{:S(2)}, u32[]{:S(2)}) collective-permute-start(f32[60,128]{1,0:T(8,128)S(1)} %get-tuple-element.130), channel_id=1, source_target_pairs={{0,16},{16,32},{32,48},{48,64},{64,80},{80,96},{96,112},{112,0},{1... | collective-permute-start | bytes 92168 | tf_op jit(solution)/shard_map/ppermute | solution.py:593
  120.5 3.9 %collective-permute-start.13 = (f32[60,128]{1,0:T(8,128)S(1)}, f32[60,128]{1,0:T(8,128)S(1)}, u32[]{:S(2)}, u32[]{:S(2)}) collective-permute-start(f32[60,128]{1,0:T(8,128)S(1)} %get-tuple-element.131), channel_id=1, source_target_pairs={{16,0},{32,16},{48,32},{64,48},{80,64},{96,80},{112,96},{0,112},{1... | collective-permute-start | bytes 92168 | tf_op jit(solution)/shard_map/ppermute | solution.py:594
  130.7 14.2 %all-to-all-start.7 = ((bf16[128,4,128]{2,1,0:T(4,128)(2,1)}), bf16[128,4,128]{2,1,0:T(4,128)(2,1)S(1)}, u32[]{:S(2)}, u32[]{:S(2)}) async-start(bf16[128,4,128]{2,1,0:T(4,128)(2,1)} %bitcast.24), calls=%async_computation.7 | async-start | bytes 262144 | tf_op jit(solution)/shard_map/all_to_all | solution.py:585
  134.7 2.7 %collective-permute-start.14 = (f32[60,128]{1,0:T(8,128)S(1)}, f32[60,128]{1,0:T(8,128)S(1)}, u32[]{:S(2)}, u32[]{:S(2)}) collective-permute-start(f32[60,128]{1,0:T(8,128)S(1)} %get-tuple-element.137), channel_id=1, source_target_pairs={{0,16},{16,32},{32,48},{48,64},{64,80},{80,96},{96,112},{112,0},{1... | collective-permute-start | bytes 92168 | tf_op jit(solution)/shard_map/ppermute | solution.py:593
  136.4 3.9 %collective-permute-start.15 = (f32[60,128]{1,0:T(8,128)S(1)}, f32[60,128]{1,0:T(8,128)S(1)}, u32[]{:S(2)}, u32[]{:S(2)}) collective-permute-start(f32[60,128]{1,0:T(8,128)S(1)} %get-tuple-element.138), channel_id=1, source_target_pairs={{16,0},{32,16},{48,32},{64,48},{80,64},{96,80},{112,96},{0,112},{1... | collective-permute-start | bytes 92168 | tf_op jit(solution)/shard_map/ppermute | solution.py:594

commit v11 on v10

--- a/solution.py
+++ b/solution.py
@@ -144,17 +144,17 @@
     return [entry[3 * n] * x + entry[3 * n + 1] * y + entry[3 * n + 2] * z for n in range(3)]
 
 
-def solve(diag, rows, vector, scale=None):
+def invert(diag, rows, inverse):
     a, b, c, d, e, f, g, h, i = [diag[n, rows, :].astype(F32) for n in range(9)]
-    x, y, z = vector
     p, q, s = e * i - f * h, f * g - d * i, d * h - e * g
-    if scale is None:
-        scale = 1.0 / (a * p + b * q + c * s)
-    return [
-        (p * x + (c * h - b * i) * y + (b * f - c * e) * z) * scale,
-        (q * x + (a * i - c * g) * y + (c * d - a * f) * z) * scale,
-        (s * x + (b * g - a * h) * y + (a * e - b * d) * z) * scale,
-    ], scale
+    scale = 1.0 / (a * p + b * q + c * s)
+    entries = [
+        p, c * h - b * i, b * f - c * e,
+        q, a * i - c * g, c * d - a * f,
+        s, b * g - a * h, a * e - b * d,
+    ]
+    for n, entry in enumerate(entries):
+        inverse[n, rows, :] = entry * scale
 
 
 def borders(values, mobility, trans, weighted, along, t):
@@ -219,7 +219,7 @@
 
 def cell_setup(rhs_in, diag_in, mobility_in, trans_in, cells_in, pi_in, index_in, parent_in,
                across_in, source_in,
-               rows_of, rows_to, start, weight, slots, fixed, scale,
+               rows_of, rows_to, start, weight, slots, fixed, inverse,
                weighted, toward_low, toward_high, message, along, pad, forward, own,
                rhs, diag, mobility, trans, cells, pi, index, parent, across, source, sems):
     pairs = ((cells_in, cells), (pi_in, pi), (index_in, index), (parent_in, parent),
@@ -270,7 +270,8 @@
         copy.wait()
     for t in range(CHUNKS):
         rows = chunk(t)
-        values, scale[rows, :] = solve(diag, rows, [rhs[n, rows, :] for n in range(3)])
+        invert(diag, rows, inverse)
+        values = mix(inverse, rows, [rhs[n, rows, :] for n in range(3)])
         forward[rows, :] = values[0]
         for n in range(3):
             weighted[n, rows, :] = values[n]
@@ -376,13 +377,14 @@
     )
 
 
-STEADY = ("rhs", "diag", "mobility", "trans", "rows_of", "rows_to", "start", "weight",
-          "own_weight", "table", "index", "fixed", "diagonal", "scale")
+STEADY = ("rhs", "mobility", "trans", "rows_of", "rows_to", "start", "weight",
+          "own_weight", "table", "index", "fixed", "diagonal")
 MOVING = ("arrived", "near", "from_low", "from_high", "slots", "at_slots", "state")
 NEXT = ("weighted", "toward_low", "toward_high", "message", "slots", "at_slots", "state")
 MORE_IN = {
-    "plain": (), "keep": (), "last": ("field",), "after": ("sums",), "omega": (),
-    "final": ("field", "change", "seg_change", "omega"),
+    "plain": ("inverse",), "keep": ("inverse",), "last": ("inverse", "diag", "field"),
+    "after": ("inverse", "sums"), "omega": ("inverse",),
+    "final": ("diag", "field", "change", "seg_change", "omega"),
 }
 MORE_OUT = {
     "plain": (), "keep": ("field",), "last": ("change", "seg_change", "sums"),
@@ -459,7 +461,7 @@
             value = now["near"][n, rows, :] + tx * nx + ty * ny
             terms.append(value - share * perforated[t * STEP : (t + 1) * STEP])
         if kind in ("last", "final"):
-            own = mix(fixed["diag"], rows, [extra["field"][n, rows, :] for n in range(3)])
+            own = mix(extra["diag"], rows, [extra["field"][n, rows, :] for n in range(3)])
             for n in range(3):
                 change = own[n] - terms[n]
                 before = fixed["rhs"][n, rows, :]
@@ -473,7 +475,7 @@
                 denom += change * change
         if not final:
             total = [fixed["rhs"][n, rows, :] + terms[n] for n in range(3)]
-            values = solve(fixed["diag"], rows, total, fixed["scale"][rows, :])[0]
+            values = mix(extra["inverse"], rows, total)
             forward[rows, :] = values[0]
             if kind == "keep":
                 for n in range(3):
@@ -604,14 +606,14 @@
     trans = trans.reshape(3, ROWS, 128)
     index = perf_seg[0]
 
-    fixed = {"rhs": rhs, "diag": diag, "mobility": mobility, "trans": trans, "index": index}
+    fixed = {"rhs": rhs, "mobility": mobility, "trans": trans, "index": index}
     inputs = [rhs, diag, mobility, trans, perf_cell[0], perf_pi[0], index]
     inputs += [a.reshape(2, 128) for a in (seg_parent, seg_trans, seg_rhs)]
-    (rows_of, rows_to, start, weight, slots, constants, scale, weighted, toward_low, toward_high,
+    (rows_of, rows_to, start, weight, slots, constants, inverse, weighted, toward_low, toward_high,
      message) = call(
         cell_setup,
         [((PEERS, ROWS), BF16), ((ROWS, PEERS), BF16),
-         ((PEERS, 128), jnp.int32), PAIRS, PAIRS, ((4, 8, 128), F32), ((ROWS, 128), F32), CELLS, EDGE, EDGE,
+         ((PEERS, 128), jnp.int32), PAIRS, PAIRS, ((4, 8, 128), F32), ((9, ROWS, 128), F32), CELLS, EDGE, EDGE,
          ((24 * PEERS, 128), BF16)],
         inputs,
         SCRATCH + (pltpu.VMEM((8 * PEERS, 128), F32),)
@@ -626,7 +628,7 @@
         return call(interior, [CELLS], [weighted, trans], name="interior")[0]
 
     (table,) = call(well_tables, [((128, CAP * 128), BF16)], [index], name="well_tables")
-    fixed.update(rows_of=rows_of, rows_to=rows_to, start=start, weight=weight, scale=scale)
+    fixed.update(rows_of=rows_of, rows_to=rows_to, start=start, weight=weight)
     now = {"near": inside(weighted), "slots": slots}
     now.update(neighbours(toward_low, toward_high))
     now["arrived"], own_weight, state, at_slots, diagonal = call(
@@ -638,7 +640,7 @@
     )
     fixed.update(own_weight=own_weight, table=table, fixed=constants, diagonal=diagonal)
     now.update(at_slots=at_slots, state=state)
-    saved = {}
+    saved = {"inverse": inverse, "diag": diag}
 
     def advance(kind, now):
         args = [now[name] for name in MOVING]

time: 161 us -> 166 us (1.031)
  local copies, waits for them, and re-layouts: 0.86 us -> 6.85 us
    unnamed x30 -> x56, local copies, waits for them, and re-layouts: 0.86 us -> 6.85 us
where the time goes in v11:
time: 166 us; the launch traced here: 165 us
  waiting for transfers between devices  71.7 us (43%)
  starting transfers between devices  53.5 us (32%)
  Pallas kernels  18.3 us (11%)
  blocking collectives  13.6 us (8%)
  local copies, waits for them, and re-layouts  6.85 us (4%)
    all_to_all x8, waiting for transfers between devices, exchange(): lax.all_to_all(message, AXES, split_axis=0, concat_axis=0, tiled=True)  45.8 us
    all_to_all x8, starting transfers between devices, exchange(): lax.all_to_all(message, AXES, split_axis=0, concat_axis=0, tiled=True)  40.2 us
    ppermute x8, waiting for transfers between devices, neighbours(): lax.ppermute(toward_low, 'gx', down)  21.1 us
    pallas_call x20, Pallas kernels, call(): pl.pallas_call(body, out_shape=[jax.ShapeDtypeStruct(*out) for out in out...  18.3 us
    all_to_all x1, blocking collectives, exchange(): lax.all_to_all(message, AXES, split_axis=0, concat_axis=0, tiled=True)  13.6 us
    ppermute x8, starting transfers between devices, neighbours(): lax.ppermute(toward_high, 'gx', up)  13.2 us
    unnamed x56, local copies, waits for them, and re-layouts  6.85 us
    ppermute x8, waiting for transfers between devices, neighbours(): lax.ppermute(toward_high, 'gx', up)  4.78 us
  transfers between devices with their start and end apart: 24, of which 21 were waited for; matrix products, arithmetic and copies ran while one was open for 0% of the time, Pallas kernels for 2%

profile of v11, /device:TPU:1, one launch (start us, length us, event | category | flops | bytes accessed | tf_op | source)
XLA Modules:
  0.0 165.0 jit_solution(7901373335646905839)
XLA Ops:
  0.6 3.2 %cell_setup.1 = (bf16[128,160]{1,0:T(8,128)(2,1)}, bf16[160,128]{1,0:T(8,128)(2,1)}, s32[128,128]{1,0:T(8,128)}, f32[128,128]{1,0:T(8,128)}, f32[128,128]{1,0:T(...) custom-call(f32[3,160,128]{2,1,0:T(8,128)} %bitcast.58, ...), custom_call_target="tpu_custom_call" | custom-call | flops 4000000 | bytes 1121280 | tf_op jit(solution)/shard_map/cell_setup/pallas_call | solution.py:574
  3.9 11.5 %all-to-all-start = ((bf16[128,24,128]{2,1,0:T(8,128)(2,1)}), bf16[128,24,128]{2,1,0:T(8,128)(2,1)S(1)}, u32[]{:S(2)}, u32[]{:S(2)}) async-start(bf16[128,24,128]{2,1,0:T(8,128)(2,1)} %bitcast.92), calls=%async_computation | async-start | bytes 1572864 | tf_op jit(solution)/shard_map/all_to_all | solution.py:587
  15.4 1.6 collective-permute-start
  18.2 14.0 %all-to-all-done = bf16[128,24,128]{2,1,0:T(8,128)(2,1)S(1)} async-done(((bf16[128,24,128]{2,1,0:T(8,128)(2,1)}), bf16[128,24,128]{2,1,0:T(8,128)(2,1)S(1)}, u32[]{:S(2)}, u32[]{:S(2)}) %all-to-all-start) | async-done | bytes 786464 | tf_op jit(solution)/shard_map/all_to_all | solution.py:587
  32.2 1.3 well_setup.1
  33.6 1.6 sweep_plain.2
  35.2 4.1 %all-to-all-start.1 = ((bf16[128,4,128]{2,1,0:T(4,128)(2,1)}), bf16[128,4,128]{2,1,0:T(4,128)(2,1)S(1)}, u32[]{:S(2)}, u32[]{:S(2)}) async-start(bf16[128,4,128]{2,1,0:T(4,128)(2,1)} %bitcast.12), calls=%async_computation.1 | async-start | bytes 262144 | tf_op jit(solution)/shard_map/all_to_all | solution.py:587
  39.2 1.7 %collective-permute-start.2 = (f32[60,128]{1,0:T(8,128)S(1)}, f32[60,128]{1,0:T(8,128)S(1)}, u32[]{:S(2)}, u32[]{:S(2)}) collective-permute-start(f32[60,128]{1,0:T(8,128)S(1)} %get-tuple-element.93), channel_id=1, source_target_pairs={{0,16},{16,32},{32,48},{48,64},{64,80},{80,96},{96,112},{112,0},{1... | collective-permute-start | bytes 92168 | tf_op jit(solution)/shard_map/ppermute | solution.py:595
  41.2 0.8 collective-permute-done.2.refs_2_
  42.0 2.9 %collective-permute-done.3.refs_3_ = f32[60,128]{1,0:T(8,128)S(1)} collective-permute-done((f32[60,128]{1,0:T(8,128)S(1)}, f32[60,128]{1,0:T(8,128)S(1)}, u32[]{:S(2)}, u32[]{:S(2)}) %collective-permute-start.3) | collective-permute-done | bytes 30752 | tf_op jit(solution)/shard_map/ppermute | solution.py:596
  44.9 4.7 %all-to-all-done.1 = bf16[128,4,128]{2,1,0:T(4,128)(2,1)S(1)} async-done(((bf16[128,4,128]{2,1,0:T(4,128)(2,1)}), bf16[128,4,128]{2,1,0:T(4,128)(2,1)S(1)}, u32[]{:S(2)}, u32[]{:S(2)}) %all-to-all-start.1) | async-done | bytes 131104 | tf_op jit(solution)/shard_map/all_to_all | solution.py:587
  49.6 1.6 sweep_plain.3
  51.1 4.0 %all-to-all-start.2 = ((bf16[128,4,128]{2,1,0:T(4,128)(2,1)}), bf16[128,4,128]{2,1,0:T(4,128)(2,1)S(1)}, u32[]{:S(2)}, u32[]{:S(2)}) async-start(bf16[128,4,128]{2,1,0:T(4,128)(2,1)} %bitcast.14), calls=%async_computation.2 | async-start | bytes 262144 | tf_op jit(solution)/shard_map/all_to_all | solution.py:587
  55.2 1.6 collective-permute-start.4
  57.0 0.8 collective-permute-done.4.refs_2_
  57.8 2.9 %collective-permute-done.5.refs_3_ = f32[60,128]{1,0:T(8,128)S(1)} collective-permute-done((f32[60,128]{1,0:T(8,128)S(1)}, f32[60,128]{1,0:T(8,128)S(1)}, u32[]{:S(2)}, u32[]{:S(2)}) %collective-permute-start.5) | collective-permute-done | bytes 30752 | tf_op jit(solution)/shard_map/ppermute | solution.py:596
  60.7 4.6 %all-to-all-done.2 = bf16[128,4,128]{2,1,0:T(4,128)(2,1)S(1)} async-done(((bf16[128,4,128]{2,1,0:T(4,128)(2,1)}), bf16[128,4,128]{2,1,0:T(4,128)(2,1)S(1)}, u32[]{:S(2)}, u32[]{:S(2)}) %all-to-all-start.2) | async-done | bytes 131104 | tf_op jit(solution)/shard_map/all_to_all | solution.py:587
  65.4 1.6 sweep_keep.2
  66.9 4.0 %all-to-all-start.3 = ((bf16[128,4,128]{2,1,0:T(4,128)(2,1)}), bf16[128,4,128]{2,1,0:T(4,128)(2,1)S(1)}, u32[]{:S(2)}, u32[]{:S(2)}) async-start(bf16[128,4,128]{2,1,0:T(4,128)(2,1)} %bitcast.16), calls=%async_computation.3 | async-start | bytes 262144 | tf_op jit(solution)/shard_map/all_to_all | solution.py:587
  71.0 1.6 collective-permute-start.6
  72.9 0.8 collective-permute-done.6.refs_2_
  73.7 2.9 %collective-permute-done.7.refs_3_ = f32[60,128]{1,0:T(8,128)S(1)} collective-permute-done((f32[60,128]{1,0:T(8,128)S(1)}, f32[60,128]{1,0:T(8,128)S(1)}, u32[]{:S(2)}, u32[]{:S(2)}) %collective-permute-start.7) | collective-permute-done | bytes 30752 | tf_op jit(solution)/shard_map/ppermute | solution.py:596
  76.6 4.6 %all-to-all-done.3 = bf16[128,4,128]{2,1,0:T(4,128)(2,1)S(1)} async-done(((bf16[128,4,128]{2,1,0:T(4,128)(2,1)}), bf16[128,4,128]{2,1,0:T(4,128)(2,1)S(1)}, u32[]{:S(2)}, u32[]{:S(2)}) %all-to-all-start.3) | async-done | bytes 131104 | tf_op jit(solution)/shard_map/all_to_all | solution.py:587
  81.2 1.7 %sweep_last.1 = (f32[3,160,128]{2,1,0:T(8,128)S(1)}, f32[60,128]{1,0:T(8,128)S(1)}, f32[64,128]{1,0:T(8,128)S(1)}, bf16[512,128]{1,0:T(8,128)(2,1)}, f32[128,128...) custom-call(bf16[512,128]{1,0:T(8,128)(2,1)S(1)} %bitcast.71, ...), custom_call_target="tpu_custom_call" | custom-call | flops 4000000 | bytes 3104768 | tf_op jit(solution)/shard_map/sweep_last/pallas_call | solution.py:574
  83.5 4.0 %all-to-all-start.4 = ((bf16[128,4,128]{2,1,0:T(4,128)(2,1)}), bf16[128,4,128]{2,1,0:T(4,128)(2,1)S(1)}, u32[]{:S(2)}, u32[]{:S(2)}) async-start(bf16[128,4,128]{2,1,0:T(4,128)(2,1)} %bitcast.18), calls=%async_computation.4 | async-start | bytes 262144 | tf_op jit(solution)/shard_map/all_to_all | solution.py:587
  87.5 1.6 collective-permute-start.8
  89.4 3.7 %collective-permute-done.9.refs_3_ = f32[60,128]{1,0:T(8,128)S(1)} collective-permute-done((f32[60,128]{1,0:T(8,128)S(1)}, f32[60,128]{1,0:T(8,128)S(1)}, u32[]{:S(2)}, u32[]{:S(2)}) %collective-permute-start.9) | collective-permute-done | bytes 30752 | tf_op jit(solution)/shard_map/ppermute | solution.py:596
  93.1 4.6 %all-to-all-done.4 = bf16[128,4,128]{2,1,0:T(4,128)(2,1)S(1)} async-done(((bf16[128,4,128]{2,1,0:T(4,128)(2,1)}), bf16[128,4,128]{2,1,0:T(4,128)(2,1)S(1)}, u32[]{:S(2)}, u32[]{:S(2)}) %all-to-all-start.4) | async-done | bytes 131104 | tf_op jit(solution)/shard_map/all_to_all | solution.py:587
  97.8 1.6 sweep_after.1
  99.3 4.0 %all-to-all-start.5 = ((bf16[128,4,128]{2,1,0:T(4,128)(2,1)}), bf16[128,4,128]{2,1,0:T(4,128)(2,1)S(1)}, u32[]{:S(2)}, u32[]{:S(2)}) async-start(bf16[128,4,128]{2,1,0:T(4,128)(2,1)} %bitcast.20), calls=%async_computation.5 | async-start | bytes 262144 | tf_op jit(solution)/shard_map/all_to_all | solution.py:587
  103.3 1.6 collective-permute-start.10
  105.2 0.8 collective-permute-done.10.refs_2_
  106.0 2.9 %collective-permute-done.11.refs_3_ = f32[60,128]{1,0:T(8,128)S(1)} collective-permute-done((f32[60,128]{1,0:T(8,128)S(1)}, f32[60,128]{1,0:T(8,128)S(1)}, u32[]{:S(2)}, u32[]{:S(2)}) %collective-permute-start.11) | collective-permute-done | bytes 30752 | tf_op jit(solution)/shard_map/ppermute | solution.py:596
  108.9 4.6 %all-to-all-done.5 = bf16[128,4,128]{2,1,0:T(4,128)(2,1)S(1)} async-done(((bf16[128,4,128]{2,1,0:T(4,128)(2,1)}), bf16[128,4,128]{2,1,0:T(4,128)(2,1)S(1)}, u32[]{:S(2)}, u32[]{:S(2)}) %all-to-all-start.5) | async-done | bytes 131104 | tf_op jit(solution)/shard_map/all_to_all | solution.py:587
  113.5 1.6 sweep_omega.1
  115.8 4.0 %all-to-all-start.6 = ((bf16[128,4,128]{2,1,0:T(4,128)(2,1)}), bf16[128,4,128]{2,1,0:T(4,128)(2,1)S(1)}, u32[]{:S(2)}, u32[]{:S(2)}) async-start(bf16[128,4,128]{2,1,0:T(4,128)(2,1)} %bitcast.22), calls=%async_computation.6 | async-start | bytes 262144 | tf_op jit(solution)/shard_map/all_to_all | solution.py:587
  119.8 1.6 collective-permute-start.12
  121.7 0.8 collective-permute-done.12.refs_2_
  122.5 2.9 %collective-permute-done.13.refs_3_ = f32[60,128]{1,0:T(8,128)S(1)} collective-permute-done((f32[60,128]{1,0:T(8,128)S(1)}, f32[60,128]{1,0:T(8,128)S(1)}, u32[]{:S(2)}, u32[]{:S(2)}) %collective-permute-start.13) | collective-permute-done | bytes 30752 | tf_op jit(solution)/shard_map/ppermute | solution.py:596
  126.0 4.0 %all-to-all-done.6 = bf16[128,4,128]{2,1,0:T(4,128)(2,1)S(1)} async-done(((bf16[128,4,128]{2,1,0:T(4,128)(2,1)}), bf16[128,4,128]{2,1,0:T(4,128)(2,1)S(1)}, u32[]{:S(2)}, u32[]{:S(2)}) %all-to-all-start.6) | async-done | bytes 131104 | tf_op jit(solution)/shard_map/all_to_all | solution.py:587
  130.1 0.8 copy-done.18
  131.6 0.9 sweep_keep.3
  135.1 4.6 %all-to-all-start.7 = ((bf16[128,4,128]{2,1,0:T(4,128)(2,1)}), bf16[128,4,128]{2,1,0:T(4,128)(2,1)S(1)}, u32[]{:S(2)}, u32[]{:S(2)}) async-start(bf16[128,4,128]{2,1,0:T(4,128)(2,1)} %bitcast.91), calls=%async_computation.7 | async-start | bytes 262144 | tf_op jit(solution)/shard_map/all_to_all | solution.py:587
  139.7 1.6 collective-permute-start.14
  142.3 2.9 %collective-permute-done.15.refs_3_ = f32[60,128]{1,0:T(8,128)S(1)} collective-permute-done((f32[60,128]{1,0:T(8,128)S(1)}, f32[60,128]{1,0:T(8,128)S(1)}, u32[]{:S(2)}, u32[]{:S(2)}) %collective-permute-start.15) | collective-permute-done | bytes 30752 | tf_op jit(solution)/shard_map/ppermute | solution.py:596
  145.2 4.6 %all-to-all-done.7 = bf16[128,4,128]{2,1,0:T(4,128)(2,1)S(1)} async-done(((bf16[128,4,128]{2,1,0:T(4,128)(2,1)}), bf16[128,4,128]{2,1,0:T(4,128)(2,1)S(1)}, u32[]{:S(2)}, u32[]{:S(2)}) %all-to-all-start.7) | async-done | bytes 131104 | tf_op jit(solution)/shard_map/all_to_all | solution.py:587
  150.6 13.6 %all_to_all.99 = f32[128,1,128]{2,1,0:T(1,128)S(1)} all-to-all(f32[128,1,128]{2,1,0:T(1,128)S(1)} %bitcast.89), channel_id=1, replica_groups=mesh['gx'=8,'gy'=16] {'gx','gy'}, dimensions={0} | all-to-all | bytes 131072 | tf_op jit(solution)/shard_map/all_to_all | solution.py:587
  164.2 0.8 finish.1
  (77 shorter events, 9.3 us)
Async XLA Ops:
  3.9 11.6 %copy-start.27 = (f32[60,128]{1,0:T(8,128)S(1)}, f32[60,128]{1,0:T(8,128)}, u32[]{:S(2)}) copy-start(f32[60,128]{1,0:T(8,128)} %get-tuple-element.79) | copy-start | bytes 92164
  3.9 13.2 %copy-start.26 = (f32[60,128]{1,0:T(8,128)S(1)}, f32[60,128]{1,0:T(8,128)}, u32[]{:S(2)}) copy-start(f32[60,128]{1,0:T(8,128)} %get-tuple-element.80) | copy-start | bytes 92164
  3.9 13.2 %copy-start.10 = (s32[1,8,128]{2,1,0:T(8,128)S(1)}, s32[1,8,128]{2,1,0:T(8,128)}, u32[]{:S(2)}) copy-start(s32[1,8,128]{2,1,0:T(8,128)} %param.16) | copy-start | bytes 12292
  3.9 13.3 %copy-start.11 = (f32[3,160,128]{2,1,0:T(8,128)S(1)}, f32[3,160,128]{2,1,0:T(8,128)}, u32[]{:S(2)}) copy-start(f32[3,160,128]{2,1,0:T(8,128)} %get-tuple-element.78.weighted) | copy-start | bytes 737284
  3.9 28.3 %all-to-all-start = ((bf16[128,24,128]{2,1,0:T(8,128)(2,1)}), bf16[128,24,128]{2,1,0:T(8,128)(2,1)S(1)}, u32[]{:S(2)}, u32[]{:S(2)}) async-start(bf16[128,24,128]{2,1,0:T(8,128)(2,1)} %bitcast.92), calls=%async_computation | async-start | bytes 1572864 | tf_op jit(solution)/shard_map/all_to_all | solution.py:587
  15.4 18.1 %collective-permute-start = (f32[60,128]{1,0:T(8,128)S(1)}, f32[60,128]{1,0:T(8,128)S(1)}, u32[]{:S(2)}, u32[]{:S(2)}) collective-permute-start(f32[60,128]{1,0:T(8,128)S(1)} %copy-done.27), channel_id=1, source_target_pairs={{0,16},{16,32},{32,48},{48,64},{64,80},{80,96},{96,112},{112,0},{1... | collective-permute-start | bytes 92168 | tf_op jit(solution)/shard_map/ppermute | solution.py:595
  17.1 0.9 copy-start.1
  17.1 16.4 %collective-permute-start.1 = (f32[60,128]{1,0:T(8,128)S(1)}, f32[60,128]{1,0:T(8,128)S(1)}, u32[]{:S(2)}, u32[]{:S(2)}) collective-permute-start(f32[60,128]{1,0:T(8,128)S(1)} %copy-done.26), channel_id=1, source_target_pairs={{16,0},{32,16},{48,32},{64,48},{80,64},{96,80},{112,96},{0,112},{1... | collective-permute-start | bytes 92168 | tf_op jit(solution)/shard_map/ppermute | solution.py:596
  17.1 15.1 %copy-start.9 = (f32[4,8,128]{2,1,0:T(8,128)S(1)}, f32[4,8,128]{2,1,0:T(8,128)}, u32[]{:S(2)}) copy-start(f32[4,8,128]{2,1,0:T(8,128)} %get-tuple-element.76.fixed.refs_17_) | copy-start | bytes 49156
  18.0 15.5 %copy-start = (f32[9,160,128]{2,1,0:T(8,128)S(1)}, f32[9,160,128]{2,1,0:T(8,128)}, u32[]{:S(2)}) copy-start(f32[9,160,128]{2,1,0:T(8,128)} %get-tuple-element.90.refs_19_) | copy-start | bytes 2211844
  32.2 1.3 copy-start.2
  32.2 1.3 copy-start.3
  32.2 1.4 copy-start.4
  32.2 1.4 copy-start.5
  32.2 1.4 copy-start.6
  32.2 1.4 copy-start.8
  32.2 1.4 copy-start.19
  35.2 14.4 %all-to-all-start.1 = ((bf16[128,4,128]{2,1,0:T(4,128)(2,1)}), bf16[128,4,128]{2,1,0:T(4,128)(2,1)S(1)}, u32[]{:S(2)}, u32[]{:S(2)}) async-start(bf16[128,4,128]{2,1,0:T(4,128)(2,1)} %bitcast.12), calls=%async_computation.1 | async-start | bytes 262144 | tf_op jit(solution)/shard_map/all_to_all | solution.py:587
  39.2 2.7 %collective-permute-start.2 = (f32[60,128]{1,0:T(8,128)S(1)}, f32[60,128]{1,0:T(8,128)S(1)}, u32[]{:S(2)}, u32[]{:S(2)}) collective-permute-start(f32[60,128]{1,0:T(8,128)S(1)} %get-tuple-element.93), channel_id=1, source_target_pairs={{0,16},{16,32},{32,48},{48,64},{64,80},{80,96},{96,112},{112,0},{1... | collective-permute-start | bytes 92168 | tf_op jit(solution)/shard_map/ppermute | solution.py:595
  40.9 3.9 %collective-permute-start.3 = (f32[60,128]{1,0:T(8,128)S(1)}, f32[60,128]{1,0:T(8,128)S(1)}, u32[]{:S(2)}, u32[]{:S(2)}) collective-permute-start(f32[60,128]{1,0:T(8,128)S(1)} %get-tuple-element.94), channel_id=1, source_target_pairs={{16,0},{32,16},{48,32},{64,48},{80,64},{96,80},{112,96},{0,112},{1... | collective-permute-start | bytes 92168 | tf_op jit(solution)/shard_map/ppermute | solution.py:596
  51.1 14.2 %all-to-all-start.2 = ((bf16[128,4,128]{2,1,0:T(4,128)(2,1)}), bf16[128,4,128]{2,1,0:T(4,128)(2,1)S(1)}, u32[]{:S(2)}, u32[]{:S(2)}) async-start(bf16[128,4,128]{2,1,0:T(4,128)(2,1)} %bitcast.14), calls=%async_computation.2 | async-start | bytes 262144 | tf_op jit(solution)/shard_map/all_to_all | solution.py:587
  55.2 2.7 %collective-permute-start.4 = (f32[60,128]{1,0:T(8,128)S(1)}, f32[60,128]{1,0:T(8,128)S(1)}, u32[]{:S(2)}, u32[]{:S(2)}) collective-permute-start(f32[60,128]{1,0:T(8,128)S(1)} %get-tuple-element.100), channel_id=1, source_target_pairs={{0,16},{16,32},{32,48},{48,64},{64,80},{80,96},{96,112},{112,0},{1... | collective-permute-start | bytes 92168 | tf_op jit(solution)/shard_map/ppermute | solution.py:595
  56.8 3.9 %collective-permute-start.5 = (f32[60,128]{1,0:T(8,128)S(1)}, f32[60,128]{1,0:T(8,128)S(1)}, u32[]{:S(2)}, u32[]{:S(2)}) collective-permute-start(f32[60,128]{1,0:T(8,128)S(1)} %get-tuple-element.101), channel_id=1, source_target_pairs={{16,0},{32,16},{48,32},{64,48},{80,64},{96,80},{112,96},{0,112},{1... | collective-permute-start | bytes 92168 | tf_op jit(solution)/shard_map/ppermute | solution.py:596
  66.9 14.2 %all-to-all-start.3 = ((bf16[128,4,128]{2,1,0:T(4,128)(2,1)}), bf16[128,4,128]{2,1,0:T(4,128)(2,1)S(1)}, u32[]{:S(2)}, u32[]{:S(2)}) async-start(bf16[128,4,128]{2,1,0:T(4,128)(2,1)} %bitcast.16), calls=%async_computation.3 | async-start | bytes 262144 | tf_op jit(solution)/shard_map/all_to_all | solution.py:587
  71.0 10.2 %copy-start.7 = (bf16[9,20,8,128]{3,2,1,0:T(8,128)(2,1)S(1)}, bf16[9,20,8,128]{3,2,1,0:T(8,128)(2,1)}, u32[]{:S(2)}) copy-start(bf16[9,20,8,128]{3,2,1,0:T(8,128)(2,1)} %param.11) | copy-start | bytes 1105924
  71.0 2.7 %collective-permute-start.6 = (f32[60,128]{1,0:T(8,128)S(1)}, f32[60,128]{1,0:T(8,128)S(1)}, u32[]{:S(2)}, u32[]{:S(2)}) collective-permute-start(f32[60,128]{1,0:T(8,128)S(1)} %get-tuple-element.107), channel_id=1, source_target_pairs={{0,16},{16,32},{32,48},{48,64},{64,80},{80,96},{96,112},{112,0},{1... | collective-permute-start | bytes 92168 | tf_op jit(solution)/shard_map/ppermute | solution.py:595
  72.6 3.9 %collective-permute-start.7 = (f32[60,128]{1,0:T(8,128)S(1)}, f32[60,128]{1,0:T(8,128)S(1)}, u32[]{:S(2)}, u32[]{:S(2)}) collective-permute-start(f32[60,128]{1,0:T(8,128)S(1)} %get-tuple-element.108), channel_id=1, source_target_pairs={{16,0},{32,16},{48,32},{64,48},{80,64},{96,80},{112,96},{0,112},{1... | collective-permute-start | bytes 92168 | tf_op jit(solution)/shard_map/ppermute | solution.py:596
  82.8 0.7 copy-start.12
  83.5 14.2 %all-to-all-start.4 = ((bf16[128,4,128]{2,1,0:T(4,128)(2,1)}), bf16[128,4,128]{2,1,0:T(4,128)(2,1)S(1)}, u32[]{:S(2)}, u32[]{:S(2)}) async-start(bf16[128,4,128]{2,1,0:T(4,128)(2,1)} %bitcast.18), calls=%async_computation.4 | async-start | bytes 262144 | tf_op jit(solution)/shard_map/all_to_all | solution.py:587
  87.5 5.6 %collective-permute-start.8 = (f32[64,128]{1,0:T(8,128)S(1)}, f32[64,128]{1,0:T(8,128)S(1)}, u32[]{:S(2)}, u32[]{:S(2)}) collective-permute-start(f32[64,128]{1,0:T(8,128)S(1)} %get-tuple-element.115), channel_id=1, source_target_pairs={{0,16},{16,32},{32,48},{48,64},{64,80},{80,96},{96,112},{112,0},{1... | collective-permute-start | bytes 98312 | tf_op jit(solution)/shard_map/ppermute | solution.py:595
  89.2 3.9 %collective-permute-start.9 = (f32[60,128]{1,0:T(8,128)S(1)}, f32[60,128]{1,0:T(8,128)S(1)}, u32[]{:S(2)}, u32[]{:S(2)}) collective-permute-start(f32[60,128]{1,0:T(8,128)S(1)} %get-tuple-element.116), channel_id=1, source_target_pairs={{16,0},{32,16},{48,32},{64,48},{80,64},{96,80},{112,96},{0,112},{1... | collective-permute-start | bytes 92168 | tf_op jit(solution)/shard_map/ppermute | solution.py:596
  99.3 14.2 %all-to-all-start.5 = ((bf16[128,4,128]{2,1,0:T(4,128)(2,1)}), bf16[128,4,128]{2,1,0:T(4,128)(2,1)S(1)}, u32[]{:S(2)}, u32[]{:S(2)}) async-start(bf16[128,4,128]{2,1,0:T(4,128)(2,1)} %bitcast.20), calls=%async_computation.5 | async-start | bytes 262144 | tf_op jit(solution)/shard_map/all_to_all | solution.py:587
  103.3 2.7 %collective-permute-start.10 = (f32[60,128]{1,0:T(8,128)S(1)}, f32[60,128]{1,0:T(8,128)S(1)}, u32[]{:S(2)}, u32[]{:S(2)}) collective-permute-start(f32[60,128]{1,0:T(8,128)S(1)} %get-tuple-element.123), channel_id=1, source_target_pairs={{0,16},{16,32},{32,48},{48,64},{64,80},{80,96},{96,112},{112,0},{1... | collective-permute-start | bytes 92168 | tf_op jit(solution)/shard_map/ppermute | solution.py:595
  105.0 3.9 %collective-permute-start.11 = (f32[60,128]{1,0:T(8,128)S(1)}, f32[60,128]{1,0:T(8,128)S(1)}, u32[]{:S(2)}, u32[]{:S(2)}) collective-permute-start(f32[60,128]{1,0:T(8,128)S(1)} %get-tuple-element.124), channel_id=1, source_target_pairs={{16,0},{32,16},{48,32},{64,48},{80,64},{96,80},{112,96},{0,112},{1... | collective-permute-start | bytes 92168 | tf_op jit(solution)/shard_map/ppermute | solution.py:596
  115.8 14.2 %all-to-all-start.6 = ((bf16[128,4,128]{2,1,0:T(4,128)(2,1)}), bf16[128,4,128]{2,1,0:T(4,128)(2,1)S(1)}, u32[]{:S(2)}, u32[]{:S(2)}) async-start(bf16[128,4,128]{2,1,0:T(4,128)(2,1)} %bitcast.22), calls=%async_computation.6 | async-start | bytes 262144 | tf_op jit(solution)/shard_map/all_to_all | solution.py:587
  119.8 2.7 %collective-permute-start.12 = (f32[60,128]{1,0:T(8,128)S(1)}, f32[60,128]{1,0:T(8,128)S(1)}, u32[]{:S(2)}, u32[]{:S(2)}) collective-permute-start(f32[60,128]{1,0:T(8,128)S(1)} %get-tuple-element.130), channel_id=1, source_target_pairs={{0,16},{16,32},{32,48},{48,64},{64,80},{80,96},{96,112},{112,0},{1... | collective-permute-start | bytes 92168 | tf_op jit(solution)/shard_map/ppermute | solution.py:595
  121.5 3.9 %collective-permute-start.13 = (f32[60,128]{1,0:T(8,128)S(1)}, f32[60,128]{1,0:T(8,128)S(1)}, u32[]{:S(2)}, u32[]{:S(2)}) collective-permute-start(f32[60,128]{1,0:T(8,128)S(1)} %get-tuple-element.131), channel_id=1, source_target_pairs={{16,0},{32,16},{48,32},{64,48},{80,64},{96,80},{112,96},{0,112},{1... | collective-permute-start | bytes 92168 | tf_op jit(solution)/shard_map/ppermute | solution.py:596
  130.0 0.8 copy-start.18
  130.9 0.8 copy-start.21
  132.6 0.6 copy-start.15
  134.4 0.6 copy-start.14
  135.0 4.6 %copy-start.25 = (f32[60,128]{1,0:T(8,128)S(1)}, f32[60,128]{1,0:T(8,128)}, u32[]{:S(2)}) copy-start(f32[60,128]{1,0:T(8,128)} %copy-done.24) | copy-start | bytes 92164
  135.1 6.3 %copy-start.23 = (f32[60,128]{1,0:T(8,128)S(1)}, f32[60,128]{1,0:T(8,128)}, u32[]{:S(2)}) copy-start(f32[60,128]{1,0:T(8,128)} %copy-done.22) | copy-start | bytes 92164
  135.1 14.8 %all-to-all-start.7 = ((bf16[128,4,128]{2,1,0:T(4,128)(2,1)}), bf16[128,4,128]{2,1,0:T(4,128)(2,1)S(1)}, u32[]{:S(2)}, u32[]{:S(2)}) async-start(bf16[128,4,128]{2,1,0:T(4,128)(2,1)} %bitcast.91), calls=%async_computation.7 | async-start | bytes 262144 | tf_op jit(solution)/shard_map/all_to_all | solution.py:587
  139.7 2.7 %collective-permute-start.14 = (f32[60,128]{1,0:T(8,128)S(1)}, f32[60,128]{1,0:T(8,128)S(1)}, u32[]{:S(2)}, u32[]{:S(2)}) collective-permute-start(f32[60,128]{1,0:T(8,128)S(1)} %copy-done.25), channel_id=1, source_target_pairs={{0,16},{16,32},{32,48},{48,64},{64,80},{80,96},{96,112},{112,0},{1... | collective-permute-start | bytes 92168 | tf_op jit(solution)/shard_map/ppermute | solution.py:595
  141.3 3.9 %collective-permute-start.15 = (f32[60,128]{1,0:T(8,128)S(1)}, f32[60,128]{1,0:T(8,128)S(1)}, u32[]{:S(2)}, u32[]{:S(2)}) collective-permute-start(f32[60,128]{1,0:T(8,128)S(1)} %copy-done.23), channel_id=1, source_target_pairs={{16,0},{32,16},{48,32},{64,48},{80,64},{96,80},{112,96},{0,112},{1... | collective-permute-start | bytes 92168 | tf_op jit(solution)/shard_map/ppermute | solution.py:596
  141.3 8.5 %copy-start.13 = (f32[3,160,128]{2,1,0:T(8,128)S(1)}, f32[3,160,128]{2,1,0:T(8,128)}, u32[]{:S(2)}) copy-start(f32[3,160,128]{2,1,0:T(8,128)} %copy-done.12) | copy-start | bytes 737284
  141.3 8.5 %copy-start.16 = (f32[128,128]{1,0:T(8,128)S(1)}, f32[128,128]{1,0:T(8,128)}, u32[]{:S(2)}) copy-start(f32[128,128]{1,0:T(8,128)} %copy-done.15) | copy-start | bytes 196612
  (4 other events, 2.4 us)

commit v12 on v10

--- a/solution.py
+++ b/solution.py
@@ -188,7 +188,7 @@
         message[rows, :] = jnp.where(mine, message[rows, :], packed)
 
 
-def interior(weighted, trans, near):
+def interior(weighted, trans, rhs, near):
     lane = lanes((STEP, 128))
     sub = subs((STEP, 128)) & 7
     zero = jnp.zeros((8, 128), F32)
@@ -214,7 +214,7 @@
             if t + 1 < CHUNKS:
                 above = up[t + 1][0:8] * weighted[n, pl.ds(t * STEP + STEP, 8), :]
             nz = jnp.concatenate([below + pz[8:16], pz[0:8] + above], axis=0)
-            near[n, rows, :] = tx * nx + ty * ny + tz * nz
+            near[n, rows, :] = rhs[n, rows, :] + (tx * nx + ty * ny + tz * nz)
 
 
 def cell_setup(rhs_in, diag_in, mobility_in, trans_in, cells_in, pi_in, index_in, parent_in,
@@ -376,13 +376,13 @@
     )
 
 
-STEADY = ("rhs", "diag", "mobility", "trans", "rows_of", "rows_to", "start", "weight",
+STEADY = ("diag", "mobility", "trans", "rows_of", "rows_to", "start", "weight",
           "own_weight", "table", "index", "fixed", "diagonal", "scale")
 MOVING = ("arrived", "near", "from_low", "from_high", "slots", "at_slots", "state")
 NEXT = ("weighted", "toward_low", "toward_high", "message", "slots", "at_slots", "state")
 MORE_IN = {
-    "plain": (), "keep": (), "last": ("field",), "after": ("sums",), "omega": (),
-    "final": ("field", "change", "seg_change", "omega"),
+    "plain": (), "keep": (), "last": ("rhs", "field"), "after": ("sums",), "omega": (),
+    "final": ("rhs", "field", "change", "seg_change", "omega"),
 }
 MORE_OUT = {
     "plain": (), "keep": ("field",), "last": ("change", "seg_change", "sums"),
@@ -461,8 +461,8 @@
         if kind in ("last", "final"):
             own = mix(fixed["diag"], rows, [extra["field"][n, rows, :] for n in range(3)])
             for n in range(3):
-                change = own[n] - terms[n]
-                before = fixed["rhs"][n, rows, :]
+                before = extra["rhs"][n, rows, :]
+                change = (own[n] + before) - terms[n]
                 if final:
                     kept = extra["change"][n, rows, :]
                     before = before - omega * kept
@@ -472,8 +472,7 @@
                 numer += before * change
                 denom += change * change
         if not final:
-            total = [fixed["rhs"][n, rows, :] + terms[n] for n in range(3)]
-            values = solve(fixed["diag"], rows, total, fixed["scale"][rows, :])[0]
+            values = solve(fixed["diag"], rows, terms, fixed["scale"][rows, :])[0]
             forward[rows, :] = values[0]
             if kind == "keep":
                 for n in range(3):
@@ -604,7 +603,7 @@
     trans = trans.reshape(3, ROWS, 128)
     index = perf_seg[0]
 
-    fixed = {"rhs": rhs, "diag": diag, "mobility": mobility, "trans": trans, "index": index}
+    fixed = {"diag": diag, "mobility": mobility, "trans": trans, "index": index}
     inputs = [rhs, diag, mobility, trans, perf_cell[0], perf_pi[0], index]
     inputs += [a.reshape(2, 128) for a in (seg_parent, seg_trans, seg_rhs)]
     (rows_of, rows_to, start, weight, slots, constants, scale, weighted, toward_low, toward_high,
@@ -623,7 +622,7 @@
     arrived = exchange(message)
 
     def inside(weighted):
-        return call(interior, [CELLS], [weighted, trans], name="interior")[0]
+        return call(interior, [CELLS], [weighted, trans, rhs], name="interior")[0]
 
     (table,) = call(well_tables, [((128, CAP * 128), BF16)], [index], name="well_tables")
     fixed.update(rows_of=rows_of, rows_to=rows_to, start=start, weight=weight, scale=scale)
@@ -638,7 +637,7 @@
     )
     fixed.update(own_weight=own_weight, table=table, fixed=constants, diagonal=diagonal)
     now.update(at_slots=at_slots, state=state)
-    saved = {}
+    saved = {"rhs": rhs}
 
     def advance(kind, now):
         args = [now[name] for name in MOVING]

time: 161 us -> 160 us (level)
  no operation moved by 1% of the time
where the time goes in v12:
time: 160 us
  waiting for transfers between devices  72.4 us (45%)
  starting transfers between devices  52.9 us (33%)
  Pallas kernels  19.2 us (12%)
  blocking collectives  13.6 us (8%)
    all_to_all x8, waiting for transfers between devices, exchange(): lax.all_to_all(message, AXES, split_axis=0, concat_axis=0, tiled=True)  46.5 us
    all_to_all x8, starting transfers between devices, exchange(): lax.all_to_all(message, AXES, split_axis=0, concat_axis=0, tiled=True)  39.7 us
    ppermute x8, waiting for transfers between devices, neighbours(): lax.ppermute(toward_low, 'gx', down)  21.1 us
    pallas_call x20, Pallas kernels, call(): pl.pallas_call(body, out_shape=[jax.ShapeDtypeStruct(*out) for out in out...  19.2 us
    all_to_all x1, blocking collectives, exchange(): lax.all_to_all(message, AXES, split_axis=0, concat_axis=0, tiled=True)  13.6 us
    ppermute x8, starting transfers between devices, neighbours(): lax.ppermute(toward_high, 'gx', up)  13.2 us
    ppermute x8, waiting for transfers between devices, neighbours(): lax.ppermute(toward_high, 'gx', up)  4.78 us
  transfers between devices with their start and end apart: 24, of which 21 were waited for; matrix products, arithmetic and copies ran while one was open for 0% of the time, Pallas kernels for 2%

profile of v12, /device:TPU:1, one launch (start us, length us, event | category | flops | bytes accessed | tf_op | source)
XLA Modules:
  0.0 160.0 jit_solution(10994615504273057948)
XLA Ops:
  0.6 3.0 %cell_setup.1 = (bf16[128,160]{1,0:T(8,128)(2,1)}, bf16[160,128]{1,0:T(8,128)(2,1)}, s32[128,128]{1,0:T(8,128)}, f32[128,128]{1,0:T(8,128)}, f32[128,128]{1,0:T(...) custom-call(f32[3,160,128]{2,1,0:T(8,128)} %bitcast.67, ...), custom_call_target="tpu_custom_call" | custom-call | flops 4000000 | bytes 1121280 | tf_op jit(solution)/shard_map/cell_setup/pallas_call | solution.py:571
  3.7 11.5 %all-to-all-start = ((bf16[128,24,128]{2,1,0:T(8,128)(2,1)}), bf16[128,24,128]{2,1,0:T(8,128)(2,1)S(1)}, u32[]{:S(2)}, u32[]{:S(2)}) async-start(bf16[128,24,128]{2,1,0:T(8,128)(2,1)} %bitcast.99), calls=%async_computation | async-start | bytes 1572864 | tf_op jit(solution)/shard_map/all_to_all | solution.py:584
  15.2 1.6 %collective-permute-start = (f32[60,128]{1,0:T(8,128)S(1)}, f32[60,128]{1,0:T(8,128)S(1)}, u32[]{:S(2)}, u32[]{:S(2)}) collective-permute-start(f32[60,128]{1,0:T(8,128)S(1)} %copy-done.14), channel_id=1, source_target_pairs={{0,16},{16,32},{32,48},{48,64},{64,80},{80,96},{96,112},{112,0},{1... | collective-permute-start | bytes 92168 | tf_op jit(solution)/shard_map/ppermute | solution.py:592
  16.9 0.8 copy-done
  18.0 14.0 %all-to-all-done = bf16[128,24,128]{2,1,0:T(8,128)(2,1)S(1)} async-done(((bf16[128,24,128]{2,1,0:T(8,128)(2,1)}), bf16[128,24,128]{2,1,0:T(8,128)(2,1)S(1)}, u32[]{:S(2)}, u32[]{:S(2)}) %all-to-all-start) | async-done | bytes 786464 | tf_op jit(solution)/shard_map/all_to_all | solution.py:584
  32.0 1.2 well_setup.1
  33.4 1.6 %sweep_plain.2 = (f32[3,160,128]{2,1,0:T(8,128)S(1)}, f32[60,128]{1,0:T(8,128)S(1)}, f32[60,128]{1,0:T(8,128)S(1)}, bf16[512,128]{1,0:T(8,128)(2,1)}, f32[128,12...) custom-call(f32[512,128]{1,0:T(8,128)S(1)} %get-tuple-element.77.refs_0_, ...), custom_call_target="tpu_custom_call" | custom-call | flops 4000000 | bytes 2088960 | tf_op jit(solution)/shard_map/sweep_plain/pallas_call | solution.py:571
  35.0 4.1 %all-to-all-start.1 = ((bf16[128,4,128]{2,1,0:T(4,128)(2,1)}), bf16[128,4,128]{2,1,0:T(4,128)(2,1)S(1)}, u32[]{:S(2)}, u32[]{:S(2)}) async-start(bf16[128,4,128]{2,1,0:T(4,128)(2,1)} %bitcast.12), calls=%async_computation.1 | async-start | bytes 262144 | tf_op jit(solution)/shard_map/all_to_all | solution.py:584
  39.1 1.7 %collective-permute-start.2 = (f32[60,128]{1,0:T(8,128)S(1)}, f32[60,128]{1,0:T(8,128)S(1)}, u32[]{:S(2)}, u32[]{:S(2)}) collective-permute-start(f32[60,128]{1,0:T(8,128)S(1)} %get-tuple-element.93), channel_id=1, source_target_pairs={{0,16},{16,32},{32,48},{48,64},{64,80},{80,96},{96,112},{112,0},{1... | collective-permute-start | bytes 92168 | tf_op jit(solution)/shard_map/ppermute | solution.py:592
  41.0 0.8 collective-permute-done.2.refs_2_
  41.8 2.9 %collective-permute-done.3.refs_3_ = f32[60,128]{1,0:T(8,128)S(1)} collective-permute-done((f32[60,128]{1,0:T(8,128)S(1)}, f32[60,128]{1,0:T(8,128)S(1)}, u32[]{:S(2)}, u32[]{:S(2)}) %collective-permute-start.3) | collective-permute-done | bytes 30752 | tf_op jit(solution)/shard_map/ppermute | solution.py:593
  44.7 4.7 %all-to-all-done.1 = bf16[128,4,128]{2,1,0:T(4,128)(2,1)S(1)} async-done(((bf16[128,4,128]{2,1,0:T(4,128)(2,1)}), bf16[128,4,128]{2,1,0:T(4,128)(2,1)S(1)}, u32[]{:S(2)}, u32[]{:S(2)}) %all-to-all-start.1) | async-done | bytes 131104 | tf_op jit(solution)/shard_map/all_to_all | solution.py:584
  49.4 1.6 %sweep_plain.3 = (f32[3,160,128]{2,1,0:T(8,128)S(1)}, f32[60,128]{1,0:T(8,128)S(1)}, f32[60,128]{1,0:T(8,128)S(1)}, bf16[512,128]{1,0:T(8,128)(2,1)}, f32[128,12...) custom-call(bf16[512,128]{1,0:T(8,128)(2,1)S(1)} %bitcast.83, f32[3,160,128]{2,1,0:T(8,128)S(1)} %interior.9.refs_1_, ...), custom_call_target="tpu_custom_call" | custom-call | flops 4000000 | bytes 1957888 | tf_op jit(solution)/shard_map/sweep_plain/pallas_call | solution.py:571
  51.0 4.0 %all-to-all-start.2 = ((bf16[128,4,128]{2,1,0:T(4,128)(2,1)}), bf16[128,4,128]{2,1,0:T(4,128)(2,1)S(1)}, u32[]{:S(2)}, u32[]{:S(2)}) async-start(bf16[128,4,128]{2,1,0:T(4,128)(2,1)} %bitcast.14), calls=%async_computation.2 | async-start | bytes 262144 | tf_op jit(solution)/shard_map/all_to_all | solution.py:584
  55.1 1.6 %collective-permute-start.4 = (f32[60,128]{1,0:T(8,128)S(1)}, f32[60,128]{1,0:T(8,128)S(1)}, u32[]{:S(2)}, u32[]{:S(2)}) collective-permute-start(f32[60,128]{1,0:T(8,128)S(1)} %get-tuple-element.100), channel_id=1, source_target_pairs={{0,16},{16,32},{32,48},{48,64},{64,80},{80,96},{96,112},{112,0},{1... | collective-permute-start | bytes 92168 | tf_op jit(solution)/shard_map/ppermute | solution.py:592
  56.9 0.8 collective-permute-done.4.refs_2_
  57.7 2.9 %collective-permute-done.5.refs_3_ = f32[60,128]{1,0:T(8,128)S(1)} collective-permute-done((f32[60,128]{1,0:T(8,128)S(1)}, f32[60,128]{1,0:T(8,128)S(1)}, u32[]{:S(2)}, u32[]{:S(2)}) %collective-permute-start.5) | collective-permute-done | bytes 30752 | tf_op jit(solution)/shard_map/ppermute | solution.py:593
  60.6 4.6 %all-to-all-done.2 = bf16[128,4,128]{2,1,0:T(4,128)(2,1)S(1)} async-done(((bf16[128,4,128]{2,1,0:T(4,128)(2,1)}), bf16[128,4,128]{2,1,0:T(4,128)(2,1)S(1)}, u32[]{:S(2)}, u32[]{:S(2)}) %all-to-all-start.2) | async-done | bytes 131104 | tf_op jit(solution)/shard_map/all_to_all | solution.py:584
  65.3 1.6 %sweep_keep.2 = (f32[3,160,128]{2,1,0:T(8,128)S(1)}, f32[60,128]{1,0:T(8,128)S(1)}, f32[60,128]{1,0:T(8,128)S(1)}, bf16[512,128]{1,0:T(8,128)(2,1)}, f32[128,128...) custom-call(bf16[512,128]{1,0:T(8,128)(2,1)S(1)} %bitcast.81, ...), custom_call_target="tpu_custom_call" | custom-call | flops 4000000 | bytes 1957888 | tf_op jit(solution)/shard_map/sweep_keep/pallas_call | solution.py:571
  66.9 4.0 %all-to-all-start.3 = ((bf16[128,4,128]{2,1,0:T(4,128)(2,1)}), bf16[128,4,128]{2,1,0:T(4,128)(2,1)S(1)}, u32[]{:S(2)}, u32[]{:S(2)}) async-start(bf16[128,4,128]{2,1,0:T(4,128)(2,1)} %bitcast.16), calls=%async_computation.3 | async-start | bytes 262144 | tf_op jit(solution)/shard_map/all_to_all | solution.py:584
  70.9 1.6 %collective-permute-start.6 = (f32[60,128]{1,0:T(8,128)S(1)}, f32[60,128]{1,0:T(8,128)S(1)}, u32[]{:S(2)}, u32[]{:S(2)}) collective-permute-start(f32[60,128]{1,0:T(8,128)S(1)} %get-tuple-element.107), channel_id=1, source_target_pairs={{0,16},{16,32},{32,48},{48,64},{64,80},{80,96},{96,112},{112,0},{1... | collective-permute-start | bytes 92168 | tf_op jit(solution)/shard_map/ppermute | solution.py:592
  72.8 0.8 collective-permute-done.6.refs_2_
  73.6 2.9 %collective-permute-done.7.refs_3_ = f32[60,128]{1,0:T(8,128)S(1)} collective-permute-done((f32[60,128]{1,0:T(8,128)S(1)}, f32[60,128]{1,0:T(8,128)S(1)}, u32[]{:S(2)}, u32[]{:S(2)}) %collective-permute-start.7) | collective-permute-done | bytes 30752 | tf_op jit(solution)/shard_map/ppermute | solution.py:593
  76.5 4.6 %all-to-all-done.3 = bf16[128,4,128]{2,1,0:T(4,128)(2,1)S(1)} async-done(((bf16[128,4,128]{2,1,0:T(4,128)(2,1)}), bf16[128,4,128]{2,1,0:T(4,128)(2,1)S(1)}, u32[]{:S(2)}, u32[]{:S(2)}) %all-to-all-start.3) | async-done | bytes 131104 | tf_op jit(solution)/shard_map/all_to_all | solution.py:584
  81.1 1.7 %sweep_last.1 = (f32[3,160,128]{2,1,0:T(8,128)S(1)}, f32[60,128]{1,0:T(8,128)S(1)}, f32[64,128]{1,0:T(8,128)S(1)}, bf16[512,128]{1,0:T(8,128)(2,1)}, f32[128,128...) custom-call(bf16[512,128]{1,0:T(8,128)(2,1)S(1)} %bitcast.80, ...), custom_call_target="tpu_custom_call" | custom-call | flops 4000000 | bytes 2449408 | tf_op jit(solution)/shard_map/sweep_last/pallas_call | solution.py:571
  82.9 4.0 %all-to-all-start.4 = ((bf16[128,4,128]{2,1,0:T(4,128)(2,1)}), bf16[128,4,128]{2,1,0:T(4,128)(2,1)S(1)}, u32[]{:S(2)}, u32[]{:S(2)}) async-start(bf16[128,4,128]{2,1,0:T(4,128)(2,1)} %bitcast.18), calls=%async_computation.4 | async-start | bytes 262144 | tf_op jit(solution)/shard_map/all_to_all | solution.py:584
  86.9 1.6 %collective-permute-start.8 = (f32[64,128]{1,0:T(8,128)S(1)}, f32[64,128]{1,0:T(8,128)S(1)}, u32[]{:S(2)}, u32[]{:S(2)}) collective-permute-start(f32[64,128]{1,0:T(8,128)S(1)} %get-tuple-element.115), channel_id=1, source_target_pairs={{0,16},{16,32},{32,48},{48,64},{64,80},{80,96},{96,112},{112,0},{1... | collective-permute-start | bytes 98312 | tf_op jit(solution)/shard_map/ppermute | solution.py:592
  88.8 3.7 %collective-permute-done.9.refs_3_ = f32[60,128]{1,0:T(8,128)S(1)} collective-permute-done((f32[60,128]{1,0:T(8,128)S(1)}, f32[60,128]{1,0:T(8,128)S(1)}, u32[]{:S(2)}, u32[]{:S(2)}) %collective-permute-start.9) | collective-permute-done | bytes 30752 | tf_op jit(solution)/shard_map/ppermute | solution.py:593
  92.5 4.6 %all-to-all-done.4 = bf16[128,4,128]{2,1,0:T(4,128)(2,1)S(1)} async-done(((bf16[128,4,128]{2,1,0:T(4,128)(2,1)}), bf16[128,4,128]{2,1,0:T(4,128)(2,1)S(1)}, u32[]{:S(2)}, u32[]{:S(2)}) %all-to-all-start.4) | async-done | bytes 131104 | tf_op jit(solution)/shard_map/all_to_all | solution.py:584
  97.1 1.6 %sweep_after.1 = (f32[3,160,128]{2,1,0:T(8,128)S(1)}, f32[60,128]{1,0:T(8,128)S(1)}, f32[60,128]{1,0:T(8,128)S(1)}, bf16[512,128]{1,0:T(8,128)(2,1)}, f32[128,12...) custom-call(bf16[512,128]{1,0:T(8,128)(2,1)S(1)} %bitcast.84, f32[3,160,128]{2,1,0:T(8,128)S(1)} %interior.12.refs_1_, ...), custom_call_target="tpu_custom_call" | custom-call | flops 4000000 | bytes 1964032 | tf_op jit(solution)/shard_map/sweep_after/pallas_call | solution.py:571
  98.7 4.0 %all-to-all-start.5 = ((bf16[128,4,128]{2,1,0:T(4,128)(2,1)}), bf16[128,4,128]{2,1,0:T(4,128)(2,1)S(1)}, u32[]{:S(2)}, u32[]{:S(2)}) async-start(bf16[128,4,128]{2,1,0:T(4,128)(2,1)} %bitcast.20), calls=%async_computation.5 | async-start | bytes 262144 | tf_op jit(solution)/shard_map/all_to_all | solution.py:584
  102.8 1.6 %collective-permute-start.10 = (f32[60,128]{1,0:T(8,128)S(1)}, f32[60,128]{1,0:T(8,128)S(1)}, u32[]{:S(2)}, u32[]{:S(2)}) collective-permute-start(f32[60,128]{1,0:T(8,128)S(1)} %get-tuple-element.123), channel_id=1, source_target_pairs={{0,16},{16,32},{32,48},{48,64},{64,80},{80,96},{96,112},{112,0},{1... | collective-permute-start | bytes 92168 | tf_op jit(solution)/shard_map/ppermute | solution.py:592
  104.6 0.8 collective-permute-done.10.refs_2_
  105.4 2.9 %collective-permute-done.11.refs_3_ = f32[60,128]{1,0:T(8,128)S(1)} collective-permute-done((f32[60,128]{1,0:T(8,128)S(1)}, f32[60,128]{1,0:T(8,128)S(1)}, u32[]{:S(2)}, u32[]{:S(2)}) %collective-permute-start.11) | collective-permute-done | bytes 30752 | tf_op jit(solution)/shard_map/ppermute | solution.py:593
  108.3 4.6 %all-to-all-done.5 = bf16[128,4,128]{2,1,0:T(4,128)(2,1)S(1)} async-done(((bf16[128,4,128]{2,1,0:T(4,128)(2,1)}), bf16[128,4,128]{2,1,0:T(4,128)(2,1)S(1)}, u32[]{:S(2)}, u32[]{:S(2)}) %all-to-all-start.5) | async-done | bytes 131104 | tf_op jit(solution)/shard_map/all_to_all | solution.py:584
  113.0 1.7 %sweep_omega.1 = (f32[3,160,128]{2,1,0:T(8,128)S(1)}, f32[60,128]{1,0:T(8,128)S(1)}, f32[60,128]{1,0:T(8,128)S(1)}, bf16[512,128]{1,0:T(8,128)(2,1)}, f32[128,12...) custom-call(bf16[512,128]{1,0:T(8,128)(2,1)S(1)} %bitcast.82, ...), custom_call_target="tpu_custom_call" | custom-call | flops 4000000 | bytes 1957888 | tf_op jit(solution)/shard_map/sweep_omega/pallas_call | solution.py:571
  114.7 4.0 %all-to-all-start.6 = ((bf16[128,4,128]{2,1,0:T(4,128)(2,1)}), bf16[128,4,128]{2,1,0:T(4,128)(2,1)S(1)}, u32[]{:S(2)}, u32[]{:S(2)}) async-start(bf16[128,4,128]{2,1,0:T(4,128)(2,1)} %bitcast.22), calls=%async_computation.6 | async-start | bytes 262144 | tf_op jit(solution)/shard_map/all_to_all | solution.py:584
  118.7 1.6 %collective-permute-start.12 = (f32[60,128]{1,0:T(8,128)S(1)}, f32[60,128]{1,0:T(8,128)S(1)}, u32[]{:S(2)}, u32[]{:S(2)}) collective-permute-start(f32[60,128]{1,0:T(8,128)S(1)} %get-tuple-element.130), channel_id=1, source_target_pairs={{0,16},{16,32},{32,48},{48,64},{64,80},{80,96},{96,112},{112,0},{1... | collective-permute-start | bytes 92168 | tf_op jit(solution)/shard_map/ppermute | solution.py:592
  120.6 0.8 collective-permute-done.12.refs_2_
  121.4 2.9 %collective-permute-done.13.refs_3_ = f32[60,128]{1,0:T(8,128)S(1)} collective-permute-done((f32[60,128]{1,0:T(8,128)S(1)}, f32[60,128]{1,0:T(8,128)S(1)}, u32[]{:S(2)}, u32[]{:S(2)}) %collective-permute-start.13) | collective-permute-done | bytes 30752 | tf_op jit(solution)/shard_map/ppermute | solution.py:593
  124.3 4.6 %all-to-all-done.6 = bf16[128,4,128]{2,1,0:T(4,128)(2,1)S(1)} async-done(((bf16[128,4,128]{2,1,0:T(4,128)(2,1)}), bf16[128,4,128]{2,1,0:T(4,128)(2,1)S(1)}, u32[]{:S(2)}, u32[]{:S(2)}) %all-to-all-start.6) | async-done | bytes 131104 | tf_op jit(solution)/shard_map/all_to_all | solution.py:584
  128.9 1.6 %sweep_keep.3 = (f32[3,160,128]{2,1,0:T(8,128)S(1)}, f32[60,128]{1,0:T(8,128)S(1)}, f32[60,128]{1,0:T(8,128)S(1)}, bf16[512,128]{1,0:T(8,128)(2,1)}, f32[128,128...) custom-call(bf16[512,128]{1,0:T(8,128)(2,1)S(1)} %bitcast.85, ...), custom_call_target="tpu_custom_call" | custom-call | flops 4000000 | bytes 1957888 | tf_op jit(solution)/shard_map/sweep_keep/pallas_call | solution.py:571
  130.6 4.0 %all-to-all-start.7 = ((bf16[128,4,128]{2,1,0:T(4,128)(2,1)}), bf16[128,4,128]{2,1,0:T(4,128)(2,1)S(1)}, u32[]{:S(2)}, u32[]{:S(2)}) async-start(bf16[128,4,128]{2,1,0:T(4,128)(2,1)} %bitcast.24), calls=%async_computation.7 | async-start | bytes 262144 | tf_op jit(solution)/shard_map/all_to_all | solution.py:584
  134.6 1.6 %collective-permute-start.14 = (f32[60,128]{1,0:T(8,128)S(1)}, f32[60,128]{1,0:T(8,128)S(1)}, u32[]{:S(2)}, u32[]{:S(2)}) collective-permute-start(f32[60,128]{1,0:T(8,128)S(1)} %get-tuple-element.137), channel_id=1, source_target_pairs={{0,16},{16,32},{32,48},{48,64},{64,80},{80,96},{96,112},{112,0},{1... | collective-permute-start | bytes 92168 | tf_op jit(solution)/shard_map/ppermute | solution.py:592
  137.3 2.9 %collective-permute-done.15.refs_3_ = f32[60,128]{1,0:T(8,128)S(1)} collective-permute-done((f32[60,128]{1,0:T(8,128)S(1)}, f32[60,128]{1,0:T(8,128)S(1)}, u32[]{:S(2)}, u32[]{:S(2)}) %collective-permute-start.15) | collective-permute-done | bytes 30752 | tf_op jit(solution)/shard_map/ppermute | solution.py:593
  140.2 4.6 %all-to-all-done.7 = bf16[128,4,128]{2,1,0:T(4,128)(2,1)S(1)} async-done(((bf16[128,4,128]{2,1,0:T(4,128)(2,1)}), bf16[128,4,128]{2,1,0:T(4,128)(2,1)S(1)}, u32[]{:S(2)}, u32[]{:S(2)}) %all-to-all-start.7) | async-done | bytes 131104 | tf_op jit(solution)/shard_map/all_to_all | solution.py:584
  145.5 13.6 %all_to_all.99 = f32[128,1,128]{2,1,0:T(1,128)S(1)} all-to-all(f32[128,1,128]{2,1,0:T(1,128)S(1)} %bitcast.97), channel_id=1, replica_groups=mesh['gx'=8,'gy'=16] {'gx','gy'}, dimensions={0} | all-to-all | bytes 131072 | tf_op jit(solution)/shard_map/all_to_all | solution.py:584
  159.1 0.8 finish.1
  (51 shorter events, 3.4 us)
Async XLA Ops:
  3.6 11.6 %copy-start.14 = (f32[60,128]{1,0:T(8,128)S(1)}, f32[60,128]{1,0:T(8,128)}, u32[]{:S(2)}) copy-start(f32[60,128]{1,0:T(8,128)} %get-tuple-element.79) | copy-start | bytes 92164
  3.6 13.2 %copy-start.13 = (f32[60,128]{1,0:T(8,128)S(1)}, f32[60,128]{1,0:T(8,128)}, u32[]{:S(2)}) copy-start(f32[60,128]{1,0:T(8,128)} %get-tuple-element.80) | copy-start | bytes 92164
  3.6 13.2 %copy-start.10 = (s32[1,8,128]{2,1,0:T(8,128)S(1)}, s32[1,8,128]{2,1,0:T(8,128)}, u32[]{:S(2)}) copy-start(s32[1,8,128]{2,1,0:T(8,128)} %param.16) | copy-start | bytes 12292
  3.6 13.3 %copy-start.3 = (f32[3,20,8,128]{3,2,1,0:T(8,128)S(1)}, f32[3,20,8,128]{3,2,1,0:T(8,128)}, u32[]{:S(2)}) copy-start(f32[3,20,8,128]{3,2,1,0:T(8,128)} %param.10) | copy-start | bytes 737284
  3.6 13.3 %copy-start.11 = (f32[3,160,128]{2,1,0:T(8,128)S(1)}, f32[3,160,128]{2,1,0:T(8,128)}, u32[]{:S(2)}) copy-start(f32[3,160,128]{2,1,0:T(8,128)} %get-tuple-element.78.weighted) | copy-start | bytes 737284
  3.7 28.3 %all-to-all-start = ((bf16[128,24,128]{2,1,0:T(8,128)(2,1)}), bf16[128,24,128]{2,1,0:T(8,128)(2,1)S(1)}, u32[]{:S(2)}, u32[]{:S(2)}) async-start(bf16[128,24,128]{2,1,0:T(8,128)(2,1)} %bitcast.99), calls=%async_computation | async-start | bytes 1572864 | tf_op jit(solution)/shard_map/all_to_all | solution.py:584
  15.2 18.1 %collective-permute-start = (f32[60,128]{1,0:T(8,128)S(1)}, f32[60,128]{1,0:T(8,128)S(1)}, u32[]{:S(2)}, u32[]{:S(2)}) collective-permute-start(f32[60,128]{1,0:T(8,128)S(1)} %copy-done.14), channel_id=1, source_target_pairs={{0,16},{16,32},{32,48},{48,64},{64,80},{80,96},{96,112},{112,0},{1... | collective-permute-start | bytes 92168 | tf_op jit(solution)/shard_map/ppermute | solution.py:592
  16.8 0.9 copy-start
  16.8 16.4 %collective-permute-start.1 = (f32[60,128]{1,0:T(8,128)S(1)}, f32[60,128]{1,0:T(8,128)S(1)}, u32[]{:S(2)}, u32[]{:S(2)}) collective-permute-start(f32[60,128]{1,0:T(8,128)S(1)} %copy-done.13), channel_id=1, source_target_pairs={{16,0},{32,16},{48,32},{64,48},{80,64},{96,80},{112,96},{0,112},{1... | collective-permute-start | bytes 92168 | tf_op jit(solution)/shard_map/ppermute | solution.py:593
  17.7 14.2 %copy-start.9 = (f32[4,8,128]{2,1,0:T(8,128)S(1)}, f32[4,8,128]{2,1,0:T(8,128)}, u32[]{:S(2)}) copy-start(f32[4,8,128]{2,1,0:T(8,128)} %get-tuple-element.76.fixed.refs_17_) | copy-start | bytes 49156
  17.7 15.5 %copy-start.12 = (f32[128,128]{1,0:T(8,128)S(1)}, f32[128,128]{1,0:T(8,128)}, u32[]{:S(2)}) copy-start(f32[128,128]{1,0:T(8,128)} %get-tuple-element.81.refs_4_) | copy-start | bytes 196612
  31.9 1.3 copy-start.1
  31.9 1.3 copy-start.2
  32.0 1.4 copy-start.4
  32.0 1.4 copy-start.5
  32.0 1.4 copy-start.6
  32.0 1.4 copy-start.7
  32.0 1.4 copy-start.8
  35.0 14.4 %all-to-all-start.1 = ((bf16[128,4,128]{2,1,0:T(4,128)(2,1)}), bf16[128,4,128]{2,1,0:T(4,128)(2,1)S(1)}, u32[]{:S(2)}, u32[]{:S(2)}) async-start(bf16[128,4,128]{2,1,0:T(4,128)(2,1)} %bitcast.12), calls=%async_computation.1 | async-start | bytes 262144 | tf_op jit(solution)/shard_map/all_to_all | solution.py:584
  39.1 2.7 %collective-permute-start.2 = (f32[60,128]{1,0:T(8,128)S(1)}, f32[60,128]{1,0:T(8,128)S(1)}, u32[]{:S(2)}, u32[]{:S(2)}) collective-permute-start(f32[60,128]{1,0:T(8,128)S(1)} %get-tuple-element.93), channel_id=1, source_target_pairs={{0,16},{16,32},{32,48},{48,64},{64,80},{80,96},{96,112},{112,0},{1... | collective-permute-start | bytes 92168 | tf_op jit(solution)/shard_map/ppermute | solution.py:592
  40.8 3.9 %collective-permute-start.3 = (f32[60,128]{1,0:T(8,128)S(1)}, f32[60,128]{1,0:T(8,128)S(1)}, u32[]{:S(2)}, u32[]{:S(2)}) collective-permute-start(f32[60,128]{1,0:T(8,128)S(1)} %get-tuple-element.94), channel_id=1, source_target_pairs={{16,0},{32,16},{48,32},{64,48},{80,64},{96,80},{112,96},{0,112},{1... | collective-permute-start | bytes 92168 | tf_op jit(solution)/shard_map/ppermute | solution.py:593
  51.0 14.2 %all-to-all-start.2 = ((bf16[128,4,128]{2,1,0:T(4,128)(2,1)}), bf16[128,4,128]{2,1,0:T(4,128)(2,1)S(1)}, u32[]{:S(2)}, u32[]{:S(2)}) async-start(bf16[128,4,128]{2,1,0:T(4,128)(2,1)} %bitcast.14), calls=%async_computation.2 | async-start | bytes 262144 | tf_op jit(solution)/shard_map/all_to_all | solution.py:584
  55.1 2.7 %collective-permute-start.4 = (f32[60,128]{1,0:T(8,128)S(1)}, f32[60,128]{1,0:T(8,128)S(1)}, u32[]{:S(2)}, u32[]{:S(2)}) collective-permute-start(f32[60,128]{1,0:T(8,128)S(1)} %get-tuple-element.100), channel_id=1, source_target_pairs={{0,16},{16,32},{32,48},{48,64},{64,80},{80,96},{96,112},{112,0},{1... | collective-permute-start | bytes 92168 | tf_op jit(solution)/shard_map/ppermute | solution.py:592
  56.7 3.9 %collective-permute-start.5 = (f32[60,128]{1,0:T(8,128)S(1)}, f32[60,128]{1,0:T(8,128)S(1)}, u32[]{:S(2)}, u32[]{:S(2)}) collective-permute-start(f32[60,128]{1,0:T(8,128)S(1)} %get-tuple-element.101), channel_id=1, source_target_pairs={{16,0},{32,16},{48,32},{64,48},{80,64},{96,80},{112,96},{0,112},{1... | collective-permute-start | bytes 92168 | tf_op jit(solution)/shard_map/ppermute | solution.py:593
  66.9 14.2 %all-to-all-start.3 = ((bf16[128,4,128]{2,1,0:T(4,128)(2,1)}), bf16[128,4,128]{2,1,0:T(4,128)(2,1)S(1)}, u32[]{:S(2)}, u32[]{:S(2)}) async-start(bf16[128,4,128]{2,1,0:T(4,128)(2,1)} %bitcast.16), calls=%async_computation.3 | async-start | bytes 262144 | tf_op jit(solution)/shard_map/all_to_all | solution.py:584
  70.9 2.7 %collective-permute-start.6 = (f32[60,128]{1,0:T(8,128)S(1)}, f32[60,128]{1,0:T(8,128)S(1)}, u32[]{:S(2)}, u32[]{:S(2)}) collective-permute-start(f32[60,128]{1,0:T(8,128)S(1)} %get-tuple-element.107), channel_id=1, source_target_pairs={{0,16},{16,32},{32,48},{48,64},{64,80},{80,96},{96,112},{112,0},{1... | collective-permute-start | bytes 92168 | tf_op jit(solution)/shard_map/ppermute | solution.py:592
  72.6 3.9 %collective-permute-start.7 = (f32[60,128]{1,0:T(8,128)S(1)}, f32[60,128]{1,0:T(8,128)S(1)}, u32[]{:S(2)}, u32[]{:S(2)}) collective-permute-start(f32[60,128]{1,0:T(8,128)S(1)} %get-tuple-element.108), channel_id=1, source_target_pairs={{16,0},{32,16},{48,32},{64,48},{80,64},{96,80},{112,96},{0,112},{1... | collective-permute-start | bytes 92168 | tf_op jit(solution)/shard_map/ppermute | solution.py:593
  82.9 14.2 %all-to-all-start.4 = ((bf16[128,4,128]{2,1,0:T(4,128)(2,1)}), bf16[128,4,128]{2,1,0:T(4,128)(2,1)S(1)}, u32[]{:S(2)}, u32[]{:S(2)}) async-start(bf16[128,4,128]{2,1,0:T(4,128)(2,1)} %bitcast.18), calls=%async_computation.4 | async-start | bytes 262144 | tf_op jit(solution)/shard_map/all_to_all | solution.py:584
  86.9 5.6 %collective-permute-start.8 = (f32[64,128]{1,0:T(8,128)S(1)}, f32[64,128]{1,0:T(8,128)S(1)}, u32[]{:S(2)}, u32[]{:S(2)}) collective-permute-start(f32[64,128]{1,0:T(8,128)S(1)} %get-tuple-element.115), channel_id=1, source_target_pairs={{0,16},{16,32},{32,48},{48,64},{64,80},{80,96},{96,112},{112,0},{1... | collective-permute-start | bytes 98312 | tf_op jit(solution)/shard_map/ppermute | solution.py:592
  88.5 3.9 %collective-permute-start.9 = (f32[60,128]{1,0:T(8,128)S(1)}, f32[60,128]{1,0:T(8,128)S(1)}, u32[]{:S(2)}, u32[]{:S(2)}) collective-permute-start(f32[60,128]{1,0:T(8,128)S(1)} %get-tuple-element.116), channel_id=1, source_target_pairs={{16,0},{32,16},{48,32},{64,48},{80,64},{96,80},{112,96},{0,112},{1... | collective-permute-start | bytes 92168 | tf_op jit(solution)/shard_map/ppermute | solution.py:593
  98.7 14.2 %all-to-all-start.5 = ((bf16[128,4,128]{2,1,0:T(4,128)(2,1)}), bf16[128,4,128]{2,1,0:T(4,128)(2,1)S(1)}, u32[]{:S(2)}, u32[]{:S(2)}) async-start(bf16[128,4,128]{2,1,0:T(4,128)(2,1)} %bitcast.20), calls=%async_computation.5 | async-start | bytes 262144 | tf_op jit(solution)/shard_map/all_to_all | solution.py:584
  102.8 2.7 %collective-permute-start.10 = (f32[60,128]{1,0:T(8,128)S(1)}, f32[60,128]{1,0:T(8,128)S(1)}, u32[]{:S(2)}, u32[]{:S(2)}) collective-permute-start(f32[60,128]{1,0:T(8,128)S(1)} %get-tuple-element.123), channel_id=1, source_target_pairs={{0,16},{16,32},{32,48},{48,64},{64,80},{80,96},{96,112},{112,0},{1... | collective-permute-start | bytes 92168 | tf_op jit(solution)/shard_map/ppermute | solution.py:592
  104.4 3.9 %collective-permute-start.11 = (f32[60,128]{1,0:T(8,128)S(1)}, f32[60,128]{1,0:T(8,128)S(1)}, u32[]{:S(2)}, u32[]{:S(2)}) collective-permute-start(f32[60,128]{1,0:T(8,128)S(1)} %get-tuple-element.124), channel_id=1, source_target_pairs={{16,0},{32,16},{48,32},{64,48},{80,64},{96,80},{112,96},{0,112},{1... | collective-permute-start | bytes 92168 | tf_op jit(solution)/shard_map/ppermute | solution.py:593
  114.7 14.2 %all-to-all-start.6 = ((bf16[128,4,128]{2,1,0:T(4,128)(2,1)}), bf16[128,4,128]{2,1,0:T(4,128)(2,1)S(1)}, u32[]{:S(2)}, u32[]{:S(2)}) async-start(bf16[128,4,128]{2,1,0:T(4,128)(2,1)} %bitcast.22), calls=%async_computation.6 | async-start | bytes 262144 | tf_op jit(solution)/shard_map/all_to_all | solution.py:584
  118.7 2.7 %collective-permute-start.12 = (f32[60,128]{1,0:T(8,128)S(1)}, f32[60,128]{1,0:T(8,128)S(1)}, u32[]{:S(2)}, u32[]{:S(2)}) collective-permute-start(f32[60,128]{1,0:T(8,128)S(1)} %get-tuple-element.130), channel_id=1, source_target_pairs={{0,16},{16,32},{32,48},{48,64},{64,80},{80,96},{96,112},{112,0},{1... | collective-permute-start | bytes 92168 | tf_op jit(solution)/shard_map/ppermute | solution.py:592
  120.4 3.9 %collective-permute-start.13 = (f32[60,128]{1,0:T(8,128)S(1)}, f32[60,128]{1,0:T(8,128)S(1)}, u32[]{:S(2)}, u32[]{:S(2)}) collective-permute-start(f32[60,128]{1,0:T(8,128)S(1)} %get-tuple-element.131), channel_id=1, source_target_pairs={{16,0},{32,16},{48,32},{64,48},{80,64},{96,80},{112,96},{0,112},{1... | collective-permute-start | bytes 92168 | tf_op jit(solution)/shard_map/ppermute | solution.py:593
  130.6 14.2 %all-to-all-start.7 = ((bf16[128,4,128]{2,1,0:T(4,128)(2,1)}), bf16[128,4,128]{2,1,0:T(4,128)(2,1)S(1)}, u32[]{:S(2)}, u32[]{:S(2)}) async-start(bf16[128,4,128]{2,1,0:T(4,128)(2,1)} %bitcast.24), calls=%async_computation.7 | async-start | bytes 262144 | tf_op jit(solution)/shard_map/all_to_all | solution.py:584
  134.6 2.7 %collective-permute-start.14 = (f32[60,128]{1,0:T(8,128)S(1)}, f32[60,128]{1,0:T(8,128)S(1)}, u32[]{:S(2)}, u32[]{:S(2)}) collective-permute-start(f32[60,128]{1,0:T(8,128)S(1)} %get-tuple-element.137), channel_id=1, source_target_pairs={{0,16},{16,32},{32,48},{48,64},{64,80},{80,96},{96,112},{112,0},{1... | collective-permute-start | bytes 92168 | tf_op jit(solution)/shard_map/ppermute | solution.py:592
  136.2 3.9 %collective-permute-start.15 = (f32[60,128]{1,0:T(8,128)S(1)}, f32[60,128]{1,0:T(8,128)S(1)}, u32[]{:S(2)}, u32[]{:S(2)}) collective-permute-start(f32[60,128]{1,0:T(8,128)S(1)} %get-tuple-element.138), channel_id=1, source_target_pairs={{16,0},{32,16},{48,32},{64,48},{80,64},{96,80},{112,96},{0,112},{1... | collective-permute-start | bytes 92168 | tf_op jit(solution)/shard_map/ppermute | solution.py:593

commit v13 on v10

--- a/solution.py
+++ b/solution.py
@@ -169,18 +169,17 @@
     toward_low[...] = along[pl.ds(0, 3 * NZ, stride=CX), :]
     toward_high[...] = along[pl.ds(CX - 1, 3 * NZ, stride=CX), :]
     small = lanes((8, 128))
-    high = jnp.zeros((8, 128), F32)
-    low = jnp.zeros((8, 128), F32)
+    packed = jnp.zeros((8, 128), F32)
     for t in range(CHUNKS):
         ty = trans[1, chunk(t), :].astype(F32)
         for n in range(3):
             py = ty * weighted[n, chunk(t), :]
             for half in range(2):
                 j = n * NZ + 2 * t + half
-                moved = pltpu.roll(py[8 * half : 8 * half + 8], j + 1, 1)
-                high = jnp.where(small == j, moved, high)
-                low = jnp.where(small == j + 1, moved, low)
-    low = pltpu.roll(low, 127, 1)
+                moved = pltpu.roll(py[8 * half : 8 * half + 8], 2 * j + 1, 1)
+                packed = jnp.where((small >> 1) == j, moved, packed)
+    high = jnp.take_along_axis(packed, (2 * small) & 127, axis=1)
+    low = jnp.take_along_axis(packed, (2 * small + 1) & 127, axis=1)
     mine = is_slot(lanes((4, 128)))
     for shift, tile in ((1, high), (-1, low)):
         rows = peer_rows(shift, pitch)

time: 161 us -> 161 us (level)
  no operation moved by 1% of the time
where the time goes in v13:
time: 161 us; the launch traced here: 160 us
  waiting for transfers between devices  72.4 us (45%)
  starting transfers between devices  52.9 us (33%)
  Pallas kernels  19.4 us (12%)
  blocking collectives  13.6 us (8%)
    all_to_all x8, waiting for transfers between devices, exchange(): lax.all_to_all(message, AXES, split_axis=0, concat_axis=0, tiled=True)  46.4 us
    all_to_all x8, starting transfers between devices, exchange(): lax.all_to_all(message, AXES, split_axis=0, concat_axis=0, tiled=True)  39.7 us
    ppermute x8, waiting for transfers between devices, neighbours(): lax.ppermute(toward_low, 'gx', down)  21.1 us
    pallas_call x20, Pallas kernels, call(): pl.pallas_call(body, out_shape=[jax.ShapeDtypeStruct(*out) for out in out...  19.4 us
    all_to_all x1, blocking collectives, exchange(): lax.all_to_all(message, AXES, split_axis=0, concat_axis=0, tiled=True)  13.6 us
    ppermute x8, starting transfers between devices, neighbours(): lax.ppermute(toward_high, 'gx', up)  13.2 us
    ppermute x8, waiting for transfers between devices, neighbours(): lax.ppermute(toward_high, 'gx', up)  4.79 us
  transfers between devices with their start and end apart: 24, of which 21 were waited for; matrix products, arithmetic and copies ran while one was open for 0% of the time, Pallas kernels for 2%

profile of v13, /device:TPU:1, one launch (start us, length us, event | category | flops | bytes accessed | tf_op | source)
XLA Modules:
  0.0 160.1 jit_solution(8814961628243685154)
XLA Ops:
  0.6 3.0 %cell_setup.1 = (bf16[128,160]{1,0:T(8,128)(2,1)}, bf16[160,128]{1,0:T(8,128)(2,1)}, s32[128,128]{1,0:T(8,128)}, f32[128,128]{1,0:T(8,128)}, f32[128,128]{1,0:T(...) custom-call(f32[3,160,128]{2,1,0:T(8,128)} %bitcast.67, ...), custom_call_target="tpu_custom_call" | custom-call | flops 4000000 | bytes 1121280 | tf_op jit(solution)/shard_map/cell_setup/pallas_call | solution.py:571
  3.6 11.5 %all-to-all-start = ((bf16[128,24,128]{2,1,0:T(8,128)(2,1)}), bf16[128,24,128]{2,1,0:T(8,128)(2,1)S(1)}, u32[]{:S(2)}, u32[]{:S(2)}) async-start(bf16[128,24,128]{2,1,0:T(8,128)(2,1)} %bitcast.97), calls=%async_computation | async-start | bytes 1572864 | tf_op jit(solution)/shard_map/all_to_all | solution.py:584
  15.2 1.6 %collective-permute-start = (f32[60,128]{1,0:T(8,128)S(1)}, f32[60,128]{1,0:T(8,128)S(1)}, u32[]{:S(2)}, u32[]{:S(2)}) collective-permute-start(f32[60,128]{1,0:T(8,128)S(1)} %copy-done.14), channel_id=1, source_target_pairs={{0,16},{16,32},{32,48},{48,64},{64,80},{80,96},{96,112},{112,0},{1... | collective-permute-start | bytes 92168 | tf_op jit(solution)/shard_map/ppermute | solution.py:592
  16.9 0.8 copy-done
  18.0 14.0 %all-to-all-done = bf16[128,24,128]{2,1,0:T(8,128)(2,1)S(1)} async-done(((bf16[128,24,128]{2,1,0:T(8,128)(2,1)}), bf16[128,24,128]{2,1,0:T(8,128)(2,1)S(1)}, u32[]{:S(2)}, u32[]{:S(2)}) %all-to-all-start) | async-done | bytes 786464 | tf_op jit(solution)/shard_map/all_to_all | solution.py:584
  32.0 1.2 well_setup.1
  33.3 1.7 %sweep_plain.2 = (f32[3,160,128]{2,1,0:T(8,128)S(1)}, f32[60,128]{1,0:T(8,128)S(1)}, f32[60,128]{1,0:T(8,128)S(1)}, bf16[512,128]{1,0:T(8,128)(2,1)}, f32[128,12...) custom-call(f32[512,128]{1,0:T(8,128)S(1)} %get-tuple-element.77.refs_0_, ...), custom_call_target="tpu_custom_call" | custom-call | flops 4000000 | bytes 2334720 | tf_op jit(solution)/shard_map/sweep_plain/pallas_call | solution.py:571
  35.0 4.1 %all-to-all-start.1 = ((bf16[128,4,128]{2,1,0:T(4,128)(2,1)}), bf16[128,4,128]{2,1,0:T(4,128)(2,1)S(1)}, u32[]{:S(2)}, u32[]{:S(2)}) async-start(bf16[128,4,128]{2,1,0:T(4,128)(2,1)} %bitcast.12), calls=%async_computation.1 | async-start | bytes 262144 | tf_op jit(solution)/shard_map/all_to_all | solution.py:584
  39.0 1.7 %collective-permute-start.2 = (f32[60,128]{1,0:T(8,128)S(1)}, f32[60,128]{1,0:T(8,128)S(1)}, u32[]{:S(2)}, u32[]{:S(2)}) collective-permute-start(f32[60,128]{1,0:T(8,128)S(1)} %get-tuple-element.93), channel_id=1, source_target_pairs={{0,16},{16,32},{32,48},{48,64},{64,80},{80,96},{96,112},{112,0},{1... | collective-permute-start | bytes 92168 | tf_op jit(solution)/shard_map/ppermute | solution.py:592
  41.0 0.8 collective-permute-done.2.refs_2_
  41.8 2.9 %collective-permute-done.3.refs_3_ = f32[60,128]{1,0:T(8,128)S(1)} collective-permute-done((f32[60,128]{1,0:T(8,128)S(1)}, f32[60,128]{1,0:T(8,128)S(1)}, u32[]{:S(2)}, u32[]{:S(2)}) %collective-permute-start.3) | collective-permute-done | bytes 30752 | tf_op jit(solution)/shard_map/ppermute | solution.py:593
  44.7 4.7 %all-to-all-done.1 = bf16[128,4,128]{2,1,0:T(4,128)(2,1)S(1)} async-done(((bf16[128,4,128]{2,1,0:T(4,128)(2,1)}), bf16[128,4,128]{2,1,0:T(4,128)(2,1)S(1)}, u32[]{:S(2)}, u32[]{:S(2)}) %all-to-all-start.1) | async-done | bytes 131104 | tf_op jit(solution)/shard_map/all_to_all | solution.py:584
  49.4 1.7 %sweep_plain.3 = (f32[3,160,128]{2,1,0:T(8,128)S(1)}, f32[60,128]{1,0:T(8,128)S(1)}, f32[60,128]{1,0:T(8,128)S(1)}, bf16[512,128]{1,0:T(8,128)(2,1)}, f32[128,12...) custom-call(bf16[512,128]{1,0:T(8,128)(2,1)S(1)} %bitcast.81, f32[3,160,128]{2,1,0:T(8,128)S(1)} %interior.9.refs_1_, ...), custom_call_target="tpu_custom_call" | custom-call | flops 4000000 | bytes 2203648 | tf_op jit(solution)/shard_map/sweep_plain/pallas_call | solution.py:571
  51.1 4.0 %all-to-all-start.2 = ((bf16[128,4,128]{2,1,0:T(4,128)(2,1)}), bf16[128,4,128]{2,1,0:T(4,128)(2,1)S(1)}, u32[]{:S(2)}, u32[]{:S(2)}) async-start(bf16[128,4,128]{2,1,0:T(4,128)(2,1)} %bitcast.14), calls=%async_computation.2 | async-start | bytes 262144 | tf_op jit(solution)/shard_map/all_to_all | solution.py:584
  55.1 1.6 %collective-permute-start.4 = (f32[60,128]{1,0:T(8,128)S(1)}, f32[60,128]{1,0:T(8,128)S(1)}, u32[]{:S(2)}, u32[]{:S(2)}) collective-permute-start(f32[60,128]{1,0:T(8,128)S(1)} %get-tuple-element.100), channel_id=1, source_target_pairs={{0,16},{16,32},{32,48},{48,64},{64,80},{80,96},{96,112},{112,0},{1... | collective-permute-start | bytes 92168 | tf_op jit(solution)/shard_map/ppermute | solution.py:592
  56.9 0.8 collective-permute-done.4.refs_2_
  57.7 2.9 %collective-permute-done.5.refs_3_ = f32[60,128]{1,0:T(8,128)S(1)} collective-permute-done((f32[60,128]{1,0:T(8,128)S(1)}, f32[60,128]{1,0:T(8,128)S(1)}, u32[]{:S(2)}, u32[]{:S(2)}) %collective-permute-start.5) | collective-permute-done | bytes 30752 | tf_op jit(solution)/shard_map/ppermute | solution.py:593
  60.7 4.6 %all-to-all-done.2 = bf16[128,4,128]{2,1,0:T(4,128)(2,1)S(1)} async-done(((bf16[128,4,128]{2,1,0:T(4,128)(2,1)}), bf16[128,4,128]{2,1,0:T(4,128)(2,1)S(1)}, u32[]{:S(2)}, u32[]{:S(2)}) %all-to-all-start.2) | async-done | bytes 131104 | tf_op jit(solution)/shard_map/all_to_all | solution.py:584
  65.3 1.7 %sweep_keep.2 = (f32[3,160,128]{2,1,0:T(8,128)S(1)}, f32[60,128]{1,0:T(8,128)S(1)}, f32[60,128]{1,0:T(8,128)S(1)}, bf16[512,128]{1,0:T(8,128)(2,1)}, f32[128,128...) custom-call(bf16[512,128]{1,0:T(8,128)(2,1)S(1)} %bitcast.79, ...), custom_call_target="tpu_custom_call" | custom-call | flops 4000000 | bytes 2203648 | tf_op jit(solution)/shard_map/sweep_keep/pallas_call | solution.py:571
  66.9 4.0 %all-to-all-start.3 = ((bf16[128,4,128]{2,1,0:T(4,128)(2,1)}), bf16[128,4,128]{2,1,0:T(4,128)(2,1)S(1)}, u32[]{:S(2)}, u32[]{:S(2)}) async-start(bf16[128,4,128]{2,1,0:T(4,128)(2,1)} %bitcast.16), calls=%async_computation.3 | async-start | bytes 262144 | tf_op jit(solution)/shard_map/all_to_all | solution.py:584
  71.0 1.6 %collective-permute-start.6 = (f32[60,128]{1,0:T(8,128)S(1)}, f32[60,128]{1,0:T(8,128)S(1)}, u32[]{:S(2)}, u32[]{:S(2)}) collective-permute-start(f32[60,128]{1,0:T(8,128)S(1)} %get-tuple-element.107), channel_id=1, source_target_pairs={{0,16},{16,32},{32,48},{48,64},{64,80},{80,96},{96,112},{112,0},{1... | collective-permute-start | bytes 92168 | tf_op jit(solution)/shard_map/ppermute | solution.py:592
  72.8 0.8 collective-permute-done.6.refs_2_
  73.6 2.9 %collective-permute-done.7.refs_3_ = f32[60,128]{1,0:T(8,128)S(1)} collective-permute-done((f32[60,128]{1,0:T(8,128)S(1)}, f32[60,128]{1,0:T(8,128)S(1)}, u32[]{:S(2)}, u32[]{:S(2)}) %collective-permute-start.7) | collective-permute-done | bytes 30752 | tf_op jit(solution)/shard_map/ppermute | solution.py:593
  76.5 4.6 %all-to-all-done.3 = bf16[128,4,128]{2,1,0:T(4,128)(2,1)S(1)} async-done(((bf16[128,4,128]{2,1,0:T(4,128)(2,1)}), bf16[128,4,128]{2,1,0:T(4,128)(2,1)S(1)}, u32[]{:S(2)}, u32[]{:S(2)}) %all-to-all-start.3) | async-done | bytes 131104 | tf_op jit(solution)/shard_map/all_to_all | solution.py:584
  81.2 1.8 %sweep_last.1 = (f32[3,160,128]{2,1,0:T(8,128)S(1)}, f32[60,128]{1,0:T(8,128)S(1)}, f32[64,128]{1,0:T(8,128)S(1)}, bf16[512,128]{1,0:T(8,128)(2,1)}, f32[128,128...) custom-call(bf16[512,128]{1,0:T(8,128)(2,1)S(1)} %bitcast.78, ...), custom_call_target="tpu_custom_call" | custom-call | flops 4000000 | bytes 2449408 | tf_op jit(solution)/shard_map/sweep_last/pallas_call | solution.py:571
  82.9 4.0 %all-to-all-start.4 = ((bf16[128,4,128]{2,1,0:T(4,128)(2,1)}), bf16[128,4,128]{2,1,0:T(4,128)(2,1)S(1)}, u32[]{:S(2)}, u32[]{:S(2)}) async-start(bf16[128,4,128]{2,1,0:T(4,128)(2,1)} %bitcast.18), calls=%async_computation.4 | async-start | bytes 262144 | tf_op jit(solution)/shard_map/all_to_all | solution.py:584
  87.0 1.6 %collective-permute-start.8 = (f32[64,128]{1,0:T(8,128)S(1)}, f32[64,128]{1,0:T(8,128)S(1)}, u32[]{:S(2)}, u32[]{:S(2)}) collective-permute-start(f32[64,128]{1,0:T(8,128)S(1)} %get-tuple-element.115), channel_id=1, source_target_pairs={{0,16},{16,32},{32,48},{48,64},{64,80},{80,96},{96,112},{112,0},{1... | collective-permute-start | bytes 98312 | tf_op jit(solution)/shard_map/ppermute | solution.py:592
  88.8 3.7 %collective-permute-done.9.refs_3_ = f32[60,128]{1,0:T(8,128)S(1)} collective-permute-done((f32[60,128]{1,0:T(8,128)S(1)}, f32[60,128]{1,0:T(8,128)S(1)}, u32[]{:S(2)}, u32[]{:S(2)}) %collective-permute-start.9) | collective-permute-done | bytes 30752 | tf_op jit(solution)/shard_map/ppermute | solution.py:593
  92.5 4.6 %all-to-all-done.4 = bf16[128,4,128]{2,1,0:T(4,128)(2,1)S(1)} async-done(((bf16[128,4,128]{2,1,0:T(4,128)(2,1)}), bf16[128,4,128]{2,1,0:T(4,128)(2,1)S(1)}, u32[]{:S(2)}, u32[]{:S(2)}) %all-to-all-start.4) | async-done | bytes 131104 | tf_op jit(solution)/shard_map/all_to_all | solution.py:584
  97.2 1.6 %sweep_after.1 = (f32[3,160,128]{2,1,0:T(8,128)S(1)}, f32[60,128]{1,0:T(8,128)S(1)}, f32[60,128]{1,0:T(8,128)S(1)}, bf16[512,128]{1,0:T(8,128)(2,1)}, f32[128,12...) custom-call(bf16[512,128]{1,0:T(8,128)(2,1)S(1)} %bitcast.82, f32[3,160,128]{2,1,0:T(8,128)S(1)} %interior.12.refs_1_, ...), custom_call_target="tpu_custom_call" | custom-call | flops 4000000 | bytes 2209792 | tf_op jit(solution)/shard_map/sweep_after/pallas_call | solution.py:571
  98.8 4.0 %all-to-all-start.5 = ((bf16[128,4,128]{2,1,0:T(4,128)(2,1)}), bf16[128,4,128]{2,1,0:T(4,128)(2,1)S(1)}, u32[]{:S(2)}, u32[]{:S(2)}) async-start(bf16[128,4,128]{2,1,0:T(4,128)(2,1)} %bitcast.20), calls=%async_computation.5 | async-start | bytes 262144 | tf_op jit(solution)/shard_map/all_to_all | solution.py:584
  102.8 1.6 %collective-permute-start.10 = (f32[60,128]{1,0:T(8,128)S(1)}, f32[60,128]{1,0:T(8,128)S(1)}, u32[]{:S(2)}, u32[]{:S(2)}) collective-permute-start(f32[60,128]{1,0:T(8,128)S(1)} %get-tuple-element.123), channel_id=1, source_target_pairs={{0,16},{16,32},{32,48},{48,64},{64,80},{80,96},{96,112},{112,0},{1... | collective-permute-start | bytes 92168 | tf_op jit(solution)/shard_map/ppermute | solution.py:592
  104.7 0.8 collective-permute-done.10.refs_2_
  105.5 2.9 %collective-permute-done.11.refs_3_ = f32[60,128]{1,0:T(8,128)S(1)} collective-permute-done((f32[60,128]{1,0:T(8,128)S(1)}, f32[60,128]{1,0:T(8,128)S(1)}, u32[]{:S(2)}, u32[]{:S(2)}) %collective-permute-start.11) | collective-permute-done | bytes 30752 | tf_op jit(solution)/shard_map/ppermute | solution.py:593
  108.4 4.6 %all-to-all-done.5 = bf16[128,4,128]{2,1,0:T(4,128)(2,1)S(1)} async-done(((bf16[128,4,128]{2,1,0:T(4,128)(2,1)}), bf16[128,4,128]{2,1,0:T(4,128)(2,1)S(1)}, u32[]{:S(2)}, u32[]{:S(2)}) %all-to-all-start.5) | async-done | bytes 131104 | tf_op jit(solution)/shard_map/all_to_all | solution.py:584
  113.1 1.8 %sweep_omega.1 = (f32[3,160,128]{2,1,0:T(8,128)S(1)}, f32[60,128]{1,0:T(8,128)S(1)}, f32[60,128]{1,0:T(8,128)S(1)}, bf16[512,128]{1,0:T(8,128)(2,1)}, f32[128,12...) custom-call(bf16[512,128]{1,0:T(8,128)(2,1)S(1)} %bitcast.80, ...), custom_call_target="tpu_custom_call" | custom-call | flops 4000000 | bytes 2203648 | tf_op jit(solution)/shard_map/sweep_omega/pallas_call | solution.py:571
  114.8 4.0 %all-to-all-start.6 = ((bf16[128,4,128]{2,1,0:T(4,128)(2,1)}), bf16[128,4,128]{2,1,0:T(4,128)(2,1)S(1)}, u32[]{:S(2)}, u32[]{:S(2)}) async-start(bf16[128,4,128]{2,1,0:T(4,128)(2,1)} %bitcast.22), calls=%async_computation.6 | async-start | bytes 262144 | tf_op jit(solution)/shard_map/all_to_all | solution.py:584
  118.8 1.6 %collective-permute-start.12 = (f32[60,128]{1,0:T(8,128)S(1)}, f32[60,128]{1,0:T(8,128)S(1)}, u32[]{:S(2)}, u32[]{:S(2)}) collective-permute-start(f32[60,128]{1,0:T(8,128)S(1)} %get-tuple-element.130), channel_id=1, source_target_pairs={{0,16},{16,32},{32,48},{48,64},{64,80},{80,96},{96,112},{112,0},{1... | collective-permute-start | bytes 92168 | tf_op jit(solution)/shard_map/ppermute | solution.py:592
  121.5 2.9 %collective-permute-done.13.refs_3_ = f32[60,128]{1,0:T(8,128)S(1)} collective-permute-done((f32[60,128]{1,0:T(8,128)S(1)}, f32[60,128]{1,0:T(8,128)S(1)}, u32[]{:S(2)}, u32[]{:S(2)}) %collective-permute-start.13) | collective-permute-done | bytes 30752 | tf_op jit(solution)/shard_map/ppermute | solution.py:593
  124.4 4.6 %all-to-all-done.6 = bf16[128,4,128]{2,1,0:T(4,128)(2,1)S(1)} async-done(((bf16[128,4,128]{2,1,0:T(4,128)(2,1)}), bf16[128,4,128]{2,1,0:T(4,128)(2,1)S(1)}, u32[]{:S(2)}, u32[]{:S(2)}) %all-to-all-start.6) | async-done | bytes 131104 | tf_op jit(solution)/shard_map/all_to_all | solution.py:584
  129.0 1.7 %sweep_keep.3 = (f32[3,160,128]{2,1,0:T(8,128)S(1)}, f32[60,128]{1,0:T(8,128)S(1)}, f32[60,128]{1,0:T(8,128)S(1)}, bf16[512,128]{1,0:T(8,128)(2,1)}, f32[128,128...) custom-call(bf16[512,128]{1,0:T(8,128)(2,1)S(1)} %bitcast.83, ...), custom_call_target="tpu_custom_call" | custom-call | flops 4000000 | bytes 2203648 | tf_op jit(solution)/shard_map/sweep_keep/pallas_call | solution.py:571
  130.7 4.0 %all-to-all-start.7 = ((bf16[128,4,128]{2,1,0:T(4,128)(2,1)}), bf16[128,4,128]{2,1,0:T(4,128)(2,1)S(1)}, u32[]{:S(2)}, u32[]{:S(2)}) async-start(bf16[128,4,128]{2,1,0:T(4,128)(2,1)} %bitcast.24), calls=%async_computation.7 | async-start | bytes 262144 | tf_op jit(solution)/shard_map/all_to_all | solution.py:584
  134.7 1.6 %collective-permute-start.14 = (f32[60,128]{1,0:T(8,128)S(1)}, f32[60,128]{1,0:T(8,128)S(1)}, u32[]{:S(2)}, u32[]{:S(2)}) collective-permute-start(f32[60,128]{1,0:T(8,128)S(1)} %get-tuple-element.137), channel_id=1, source_target_pairs={{0,16},{16,32},{32,48},{48,64},{64,80},{80,96},{96,112},{112,0},{1... | collective-permute-start | bytes 92168 | tf_op jit(solution)/shard_map/ppermute | solution.py:592
  136.6 0.8 collective-permute-done.14.refs_2_
  137.4 2.9 %collective-permute-done.15.refs_3_ = f32[60,128]{1,0:T(8,128)S(1)} collective-permute-done((f32[60,128]{1,0:T(8,128)S(1)}, f32[60,128]{1,0:T(8,128)S(1)}, u32[]{:S(2)}, u32[]{:S(2)}) %collective-permute-start.15) | collective-permute-done | bytes 30752 | tf_op jit(solution)/shard_map/ppermute | solution.py:593
  140.3 4.6 %all-to-all-done.7 = bf16[128,4,128]{2,1,0:T(4,128)(2,1)S(1)} async-done(((bf16[128,4,128]{2,1,0:T(4,128)(2,1)}), bf16[128,4,128]{2,1,0:T(4,128)(2,1)S(1)}, u32[]{:S(2)}, u32[]{:S(2)}) %all-to-all-start.7) | async-done | bytes 131104 | tf_op jit(solution)/shard_map/all_to_all | solution.py:584
  145.6 13.6 %all_to_all.99 = f32[128,1,128]{2,1,0:T(1,128)S(1)} all-to-all(f32[128,1,128]{2,1,0:T(1,128)S(1)} %bitcast.95), channel_id=1, replica_groups=mesh['gx'=8,'gy'=16] {'gx','gy'}, dimensions={0} | all-to-all | bytes 131072 | tf_op jit(solution)/shard_map/all_to_all | solution.py:584
  159.2 0.8 finish.1
  (51 shorter events, 3.4 us)
Async XLA Ops:
  3.6 11.6 %copy-start.14 = (f32[60,128]{1,0:T(8,128)S(1)}, f32[60,128]{1,0:T(8,128)}, u32[]{:S(2)}) copy-start(f32[60,128]{1,0:T(8,128)} %get-tuple-element.79) | copy-start | bytes 92164
  3.6 13.2 %copy-start.13 = (f32[60,128]{1,0:T(8,128)S(1)}, f32[60,128]{1,0:T(8,128)}, u32[]{:S(2)}) copy-start(f32[60,128]{1,0:T(8,128)} %get-tuple-element.80) | copy-start | bytes 92164
  3.6 13.2 %copy-start.10 = (s32[1,8,128]{2,1,0:T(8,128)S(1)}, s32[1,8,128]{2,1,0:T(8,128)}, u32[]{:S(2)}) copy-start(s32[1,8,128]{2,1,0:T(8,128)} %param.16) | copy-start | bytes 12292
  3.6 13.3 %copy-start.11 = (f32[3,160,128]{2,1,0:T(8,128)S(1)}, f32[3,160,128]{2,1,0:T(8,128)}, u32[]{:S(2)}) copy-start(f32[3,160,128]{2,1,0:T(8,128)} %get-tuple-element.78.weighted) | copy-start | bytes 737284
  3.6 28.3 %all-to-all-start = ((bf16[128,24,128]{2,1,0:T(8,128)(2,1)}), bf16[128,24,128]{2,1,0:T(8,128)(2,1)S(1)}, u32[]{:S(2)}, u32[]{:S(2)}) async-start(bf16[128,24,128]{2,1,0:T(8,128)(2,1)} %bitcast.97), calls=%async_computation | async-start | bytes 1572864 | tf_op jit(solution)/shard_map/all_to_all | solution.py:584
  15.2 18.0 %collective-permute-start = (f32[60,128]{1,0:T(8,128)S(1)}, f32[60,128]{1,0:T(8,128)S(1)}, u32[]{:S(2)}, u32[]{:S(2)}) collective-permute-start(f32[60,128]{1,0:T(8,128)S(1)} %copy-done.14), channel_id=1, source_target_pairs={{0,16},{16,32},{32,48},{48,64},{64,80},{80,96},{96,112},{112,0},{1... | collective-permute-start | bytes 92168 | tf_op jit(solution)/shard_map/ppermute | solution.py:592
  16.8 0.9 copy-start
  16.8 16.4 %collective-permute-start.1 = (f32[60,128]{1,0:T(8,128)S(1)}, f32[60,128]{1,0:T(8,128)S(1)}, u32[]{:S(2)}, u32[]{:S(2)}) collective-permute-start(f32[60,128]{1,0:T(8,128)S(1)} %copy-done.13), channel_id=1, source_target_pairs={{16,0},{32,16},{48,32},{64,48},{80,64},{96,80},{112,96},{0,112},{1... | collective-permute-start | bytes 92168 | tf_op jit(solution)/shard_map/ppermute | solution.py:593
  17.7 14.2 %copy-start.9 = (f32[4,8,128]{2,1,0:T(8,128)S(1)}, f32[4,8,128]{2,1,0:T(8,128)}, u32[]{:S(2)}) copy-start(f32[4,8,128]{2,1,0:T(8,128)} %get-tuple-element.76.fixed.refs_18_) | copy-start | bytes 49156
  17.7 15.5 %copy-start.5 = (bf16[128,160]{1,0:T(8,128)(2,1)S(1)}, bf16[128,160]{1,0:T(8,128)(2,1)}, u32[]{:S(2)}) copy-start(bf16[128,160]{1,0:T(8,128)(2,1)} %get-tuple-element.84.refs_11_) | copy-start | bytes 122884
  17.7 15.5 %copy-start.6 = (s32[128,128]{1,0:T(8,128)S(1)}, s32[128,128]{1,0:T(8,128)}, u32[]{:S(2)}) copy-start(s32[128,128]{1,0:T(8,128)} %get-tuple-element.86.refs_13_) | copy-start | bytes 196612
  17.7 15.5 %copy-start.7 = (f32[128,128]{1,0:T(8,128)S(1)}, f32[128,128]{1,0:T(8,128)}, u32[]{:S(2)}) copy-start(f32[128,128]{1,0:T(8,128)} %get-tuple-element.87.refs_14_) | copy-start | bytes 196612
  17.7 15.5 %copy-start.8 = (bf16[160,128]{1,0:T(8,128)(2,1)S(1)}, bf16[160,128]{1,0:T(8,128)(2,1)}, u32[]{:S(2)}) copy-start(bf16[160,128]{1,0:T(8,128)(2,1)} %get-tuple-element.85.refs_12_) | copy-start | bytes 122884
  17.7 15.5 %copy-start.12 = (f32[128,128]{1,0:T(8,128)S(1)}, f32[128,128]{1,0:T(8,128)}, u32[]{:S(2)}) copy-start(f32[128,128]{1,0:T(8,128)} %get-tuple-element.81.refs_4_) | copy-start | bytes 196612
  31.9 1.3 copy-start.1
  31.9 1.4 copy-start.2
  31.9 1.4 copy-start.3
  31.9 1.4 copy-start.4
  35.0 14.4 %all-to-all-start.1 = ((bf16[128,4,128]{2,1,0:T(4,128)(2,1)}), bf16[128,4,128]{2,1,0:T(4,128)(2,1)S(1)}, u32[]{:S(2)}, u32[]{:S(2)}) async-start(bf16[128,4,128]{2,1,0:T(4,128)(2,1)} %bitcast.12), calls=%async_computation.1 | async-start | bytes 262144 | tf_op jit(solution)/shard_map/all_to_all | solution.py:584
  39.0 2.7 %collective-permute-start.2 = (f32[60,128]{1,0:T(8,128)S(1)}, f32[60,128]{1,0:T(8,128)S(1)}, u32[]{:S(2)}, u32[]{:S(2)}) collective-permute-start(f32[60,128]{1,0:T(8,128)S(1)} %get-tuple-element.93), channel_id=1, source_target_pairs={{0,16},{16,32},{32,48},{48,64},{64,80},{80,96},{96,112},{112,0},{1... | collective-permute-start | bytes 92168 | tf_op jit(solution)/shard_map/ppermute | solution.py:592
  40.8 3.9 %collective-permute-start.3 = (f32[60,128]{1,0:T(8,128)S(1)}, f32[60,128]{1,0:T(8,128)S(1)}, u32[]{:S(2)}, u32[]{:S(2)}) collective-permute-start(f32[60,128]{1,0:T(8,128)S(1)} %get-tuple-element.94), channel_id=1, source_target_pairs={{16,0},{32,16},{48,32},{64,48},{80,64},{96,80},{112,96},{0,112},{1... | collective-permute-start | bytes 92168 | tf_op jit(solution)/shard_map/ppermute | solution.py:593
  51.1 14.2 %all-to-all-start.2 = ((bf16[128,4,128]{2,1,0:T(4,128)(2,1)}), bf16[128,4,128]{2,1,0:T(4,128)(2,1)S(1)}, u32[]{:S(2)}, u32[]{:S(2)}) async-start(bf16[128,4,128]{2,1,0:T(4,128)(2,1)} %bitcast.14), calls=%async_computation.2 | async-start | bytes 262144 | tf_op jit(solution)/shard_map/all_to_all | solution.py:584
  55.1 2.7 %collective-permute-start.4 = (f32[60,128]{1,0:T(8,128)S(1)}, f32[60,128]{1,0:T(8,128)S(1)}, u32[]{:S(2)}, u32[]{:S(2)}) collective-permute-start(f32[60,128]{1,0:T(8,128)S(1)} %get-tuple-element.100), channel_id=1, source_target_pairs={{0,16},{16,32},{32,48},{48,64},{64,80},{80,96},{96,112},{112,0},{1... | collective-permute-start | bytes 92168 | tf_op jit(solution)/shard_map/ppermute | solution.py:592
  56.7 3.9 %collective-permute-start.5 = (f32[60,128]{1,0:T(8,128)S(1)}, f32[60,128]{1,0:T(8,128)S(1)}, u32[]{:S(2)}, u32[]{:S(2)}) collective-permute-start(f32[60,128]{1,0:T(8,128)S(1)} %get-tuple-element.101), channel_id=1, source_target_pairs={{16,0},{32,16},{48,32},{64,48},{80,64},{96,80},{112,96},{0,112},{1... | collective-permute-start | bytes 92168 | tf_op jit(solution)/shard_map/ppermute | solution.py:593
  66.9 14.2 %all-to-all-start.3 = ((bf16[128,4,128]{2,1,0:T(4,128)(2,1)}), bf16[128,4,128]{2,1,0:T(4,128)(2,1)S(1)}, u32[]{:S(2)}, u32[]{:S(2)}) async-start(bf16[128,4,128]{2,1,0:T(4,128)(2,1)} %bitcast.16), calls=%async_computation.3 | async-start | bytes 262144 | tf_op jit(solution)/shard_map/all_to_all | solution.py:584
  71.0 2.7 %collective-permute-start.6 = (f32[60,128]{1,0:T(8,128)S(1)}, f32[60,128]{1,0:T(8,128)S(1)}, u32[]{:S(2)}, u32[]{:S(2)}) collective-permute-start(f32[60,128]{1,0:T(8,128)S(1)} %get-tuple-element.107), channel_id=1, source_target_pairs={{0,16},{16,32},{32,48},{48,64},{64,80},{80,96},{96,112},{112,0},{1... | collective-permute-start | bytes 92168 | tf_op jit(solution)/shard_map/ppermute | solution.py:592
  72.6 3.9 %collective-permute-start.7 = (f32[60,128]{1,0:T(8,128)S(1)}, f32[60,128]{1,0:T(8,128)S(1)}, u32[]{:S(2)}, u32[]{:S(2)}) collective-permute-start(f32[60,128]{1,0:T(8,128)S(1)} %get-tuple-element.108), channel_id=1, source_target_pairs={{16,0},{32,16},{48,32},{64,48},{80,64},{96,80},{112,96},{0,112},{1... | collective-permute-start | bytes 92168 | tf_op jit(solution)/shard_map/ppermute | solution.py:593
  82.9 14.2 %all-to-all-start.4 = ((bf16[128,4,128]{2,1,0:T(4,128)(2,1)}), bf16[128,4,128]{2,1,0:T(4,128)(2,1)S(1)}, u32[]{:S(2)}, u32[]{:S(2)}) async-start(bf16[128,4,128]{2,1,0:T(4,128)(2,1)} %bitcast.18), calls=%async_computation.4 | async-start | bytes 262144 | tf_op jit(solution)/shard_map/all_to_all | solution.py:584
  87.0 5.6 %collective-permute-start.8 = (f32[64,128]{1,0:T(8,128)S(1)}, f32[64,128]{1,0:T(8,128)S(1)}, u32[]{:S(2)}, u32[]{:S(2)}) collective-permute-start(f32[64,128]{1,0:T(8,128)S(1)} %get-tuple-element.115), channel_id=1, source_target_pairs={{0,16},{16,32},{32,48},{48,64},{64,80},{80,96},{96,112},{112,0},{1... | collective-permute-start | bytes 98312 | tf_op jit(solution)/shard_map/ppermute | solution.py:592
  88.6 3.9 %collective-permute-start.9 = (f32[60,128]{1,0:T(8,128)S(1)}, f32[60,128]{1,0:T(8,128)S(1)}, u32[]{:S(2)}, u32[]{:S(2)}) collective-permute-start(f32[60,128]{1,0:T(8,128)S(1)} %get-tuple-element.116), channel_id=1, source_target_pairs={{16,0},{32,16},{48,32},{64,48},{80,64},{96,80},{112,96},{0,112},{1... | collective-permute-start | bytes 92168 | tf_op jit(solution)/shard_map/ppermute | solution.py:593
  98.8 14.2 %all-to-all-start.5 = ((bf16[128,4,128]{2,1,0:T(4,128)(2,1)}), bf16[128,4,128]{2,1,0:T(4,128)(2,1)S(1)}, u32[]{:S(2)}, u32[]{:S(2)}) async-start(bf16[128,4,128]{2,1,0:T(4,128)(2,1)} %bitcast.20), calls=%async_computation.5 | async-start | bytes 262144 | tf_op jit(solution)/shard_map/all_to_all | solution.py:584
  102.8 2.7 %collective-permute-start.10 = (f32[60,128]{1,0:T(8,128)S(1)}, f32[60,128]{1,0:T(8,128)S(1)}, u32[]{:S(2)}, u32[]{:S(2)}) collective-permute-start(f32[60,128]{1,0:T(8,128)S(1)} %get-tuple-element.123), channel_id=1, source_target_pairs={{0,16},{16,32},{32,48},{48,64},{64,80},{80,96},{96,112},{112,0},{1... | collective-permute-start | bytes 92168 | tf_op jit(solution)/shard_map/ppermute | solution.py:592
  104.5 3.9 %collective-permute-start.11 = (f32[60,128]{1,0:T(8,128)S(1)}, f32[60,128]{1,0:T(8,128)S(1)}, u32[]{:S(2)}, u32[]{:S(2)}) collective-permute-start(f32[60,128]{1,0:T(8,128)S(1)} %get-tuple-element.124), channel_id=1, source_target_pairs={{16,0},{32,16},{48,32},{64,48},{80,64},{96,80},{112,96},{0,112},{1... | collective-permute-start | bytes 92168 | tf_op jit(solution)/shard_map/ppermute | solution.py:593
  114.8 14.2 %all-to-all-start.6 = ((bf16[128,4,128]{2,1,0:T(4,128)(2,1)}), bf16[128,4,128]{2,1,0:T(4,128)(2,1)S(1)}, u32[]{:S(2)}, u32[]{:S(2)}) async-start(bf16[128,4,128]{2,1,0:T(4,128)(2,1)} %bitcast.22), calls=%async_computation.6 | async-start | bytes 262144 | tf_op jit(solution)/shard_map/all_to_all | solution.py:584
  118.8 2.7 %collective-permute-start.12 = (f32[60,128]{1,0:T(8,128)S(1)}, f32[60,128]{1,0:T(8,128)S(1)}, u32[]{:S(2)}, u32[]{:S(2)}) collective-permute-start(f32[60,128]{1,0:T(8,128)S(1)} %get-tuple-element.130), channel_id=1, source_target_pairs={{0,16},{16,32},{32,48},{48,64},{64,80},{80,96},{96,112},{112,0},{1... | collective-permute-start | bytes 92168 | tf_op jit(solution)/shard_map/ppermute | solution.py:592
  120.5 3.9 %collective-permute-start.13 = (f32[60,128]{1,0:T(8,128)S(1)}, f32[60,128]{1,0:T(8,128)S(1)}, u32[]{:S(2)}, u32[]{:S(2)}) collective-permute-start(f32[60,128]{1,0:T(8,128)S(1)} %get-tuple-element.131), channel_id=1, source_target_pairs={{16,0},{32,16},{48,32},{64,48},{80,64},{96,80},{112,96},{0,112},{1... | collective-permute-start | bytes 92168 | tf_op jit(solution)/shard_map/ppermute | solution.py:593
  130.7 14.2 %all-to-all-start.7 = ((bf16[128,4,128]{2,1,0:T(4,128)(2,1)}), bf16[128,4,128]{2,1,0:T(4,128)(2,1)S(1)}, u32[]{:S(2)}, u32[]{:S(2)}) async-start(bf16[128,4,128]{2,1,0:T(4,128)(2,1)} %bitcast.24), calls=%async_computation.7 | async-start | bytes 262144 | tf_op jit(solution)/shard_map/all_to_all | solution.py:584
  134.7 2.7 %collective-permute-start.14 = (f32[60,128]{1,0:T(8,128)S(1)}, f32[60,128]{1,0:T(8,128)S(1)}, u32[]{:S(2)}, u32[]{:S(2)}) collective-permute-start(f32[60,128]{1,0:T(8,128)S(1)} %get-tuple-element.137), channel_id=1, source_target_pairs={{0,16},{16,32},{32,48},{48,64},{64,80},{80,96},{96,112},{112,0},{1... | collective-permute-start | bytes 92168 | tf_op jit(solution)/shard_map/ppermute | solution.py:592
  136.4 3.9 %collective-permute-start.15 = (f32[60,128]{1,0:T(8,128)S(1)}, f32[60,128]{1,0:T(8,128)S(1)}, u32[]{:S(2)}, u32[]{:S(2)}) collective-permute-start(f32[60,128]{1,0:T(8,128)S(1)} %get-tuple-element.138), channel_id=1, source_target_pairs={{16,0},{32,16},{48,32},{64,48},{80,64},{96,80},{112,96},{0,112},{1... | collective-permute-start | bytes 92168 | tf_op jit(solution)/shard_map/ppermute | solution.py:593
